TPU v7x, 256 devices: a whole 4x4x8 slice. The times are simulated.
256 devices in a mesh: ctx: 64 (over y, z, x_lo), tp: 4 (over x_hi, core).
Axes of the slice: x: 4 (x_hi: 2, x_lo: 2; x = x_hi * 2 + x_lo), y: 4, z: 8, core: 2. Of those that a mesh axis runs over, the one named last changes fastest.
Arguments:
- tokens: bfloat16 [8192, 2048], P('ctx'), may hold values from -2.5 to 2.5
- project_weight: bfloat16 [2048, 3, 1024], P(None, None, 'tp'), may hold values from -12 to 12
- output_weight: bfloat16 [1024, 2048], P('tp'), may hold values from -0.5 to 0.5
- distance_slope: float32 [8], P('tp'), may hold values from 5e-06 to 0.05
- cache_keys: bfloat16 [16384, 1024], P('ctx', 'tp'), may hold values from -6 to 6
- cache_values: bfloat16 [16384, 1024], P('ctx', 'tp'), may hold values from -6 to 6
- cache_count: int32 [64], P('ctx'), may hold values from 1 to 256, 10240 in all
- short_project: bfloat16 [2048, 3, 1024], P(None, None, 'tp'), may hold values from -12 to 12
- short_output: bfloat16 [1024, 2048], P('tp'), may hold values from -0.5 to 0.5
- short_slope: float32 [8], P('tp'), may hold values from 5e-06 to 0.37
Outputs:
- mixed: bfloat16 [8192, 2048], P('ctx', 'tp')
Inputs may be any that keep to these rules, and one draw needn't show every extreme that they name: `cache_count`: slots at and past a device's count hold values that no output reads. The counts sum to 10240 and one device is full.
All inputs are finite; a program needn't handle non-finite values.
Results may differ from a plain program's by a relative error of at most 0.039.
Values may be sent and summed in bfloat16 or wider, within the bound.
No kernel may reach another device: no remote copies, remote signals or barrier semaphores. Data moves between devices by JAX's collectives and lax.ppermute only.
A program may use at most 128 MiB of HBM per device.

v0:
```python
import math

import jax
import jax.numpy as jnp
from jax import lax
from jax.sharding import PartitionSpec as P

HS = 128
GROUP = 4


NEG = -1e30


def passed_along(value, axis, by):
    length = lax.axis_size(axis)
    pairs = [(i, i + by) for i in range(length) if 0 <= i + by < length]
    return lax.ppermute(value, axis, pairs)


def rms_rows(row_block):
    values = row_block.astype(jnp.float32)
    scaled = values * lax.rsqrt(jnp.mean(values * values, axis=-1, keepdims=True) + 1e-06)
    return scaled.astype(jnp.bfloat16)


def project(normed, weight):
    row_count = normed.shape[0]
    feature_width, three, inner_width = weight.shape
    mixed = jnp.dot(
        normed,
        weight.reshape(feature_width, three * inner_width),
        preferred_element_type=jnp.float32,
    )
    mixed = mixed.reshape(row_count, three, inner_width).astype(jnp.bfloat16)
    return (mixed[:, 0], mixed[:, 1], mixed[:, 2])


def fresh_state(head_count, row_count):
    return (
        jnp.full((head_count, row_count), NEG, jnp.float32),
        jnp.zeros((head_count, row_count), jnp.float32),
        jnp.zeros((head_count, row_count, HS), jnp.float32),
    )


def absorb_block(
    carry_state, query_heads, key_rows, value_rows, query_pos, key_pos, usable, slopes
):
    prior_top, weight_total, accumulated = carry_state
    head_count = query_heads.shape[1]
    key_heads = key_rows.reshape(key_rows.shape[0], head_count, HS)
    value_heads = value_rows.reshape(value_rows.shape[0], head_count, HS)
    scores = jnp.einsum(
        "rhd,khd->hrk", query_heads, key_heads, preferred_element_type=jnp.float32
    ) * HS ** (-0.5)
    scores = scores - slopes[:, None, None] * (query_pos[None, :, None] - key_pos[None, None, :])
    scores = jnp.where(usable[None], scores, NEG)
    row_top = jnp.maximum(prior_top, jnp.max(scores, axis=2))
    fade_factor = jnp.exp(prior_top - row_top)
    weights = jnp.where(usable[None], jnp.exp(scores - row_top[:, :, None]), 0.0).astype(
        jnp.bfloat16
    )
    weight_total = weight_total * fade_factor + jnp.sum(weights.astype(jnp.float32), axis=2)
    accumulated = accumulated * fade_factor[:, :, None] + jnp.einsum(
        "hrk,khd->hrd", weights, value_heads, preferred_element_type=jnp.float32
    )
    return (row_top, weight_total, accumulated)


def absorb(carry_state, query_heads, key_rows, value_rows, query_pos, key_pos, key_live, slopes):
    key_count = key_rows.shape[0]
    row_count = query_heads.shape[0]
    key_block = math.gcd(key_count, max(128, 262144 // row_count))
    if key_block == key_count:
        usable = key_live[None, :] & (key_pos[None, :] <= query_pos[:, None])
        return absorb_block(
            carry_state, query_heads, key_rows, value_rows, query_pos, key_pos, usable, slopes
        )
    block_count = key_count // key_block

    def one_step(inner_state, items):
        key_part, value_part, pos_part, live_part = items
        usable = live_part[None, :] & (pos_part[None, :] <= query_pos[:, None])
        return (
            absorb_block(
                inner_state, query_heads, key_part, value_part, query_pos, pos_part, usable, slopes
            ),
            None,
        )

    items = (
        key_rows.reshape(block_count, key_block, key_rows.shape[1]),
        value_rows.reshape(block_count, key_block, value_rows.shape[1]),
        key_pos.reshape(block_count, key_block),
        key_live.reshape(block_count, key_block),
    )
    carry_state, unused = lax.scan(one_step, carry_state, items)
    return carry_state


def finish_state(carry_state):
    accumulated = carry_state[2] / carry_state[1][:, :, None]
    head_count, row_count, head_size = accumulated.shape
    return (
        jnp.transpose(accumulated, (1, 0, 2))
        .reshape(row_count, head_count * head_size)
        .astype(jnp.bfloat16)
    )


def table_lookup(table, owner_index):
    marks = owner_index[:, None] == jnp.arange(table.shape[0], dtype=jnp.int32)[None, :]
    return jnp.sum(jnp.where(marks, table[None, :], 0), axis=1)


def on_device(
    tokens,
    project_weight,
    output_weight,
    distance_slope,
    cache_keys,
    cache_values,
    cache_count,
    short_project,
    short_output,
    short_slope,
):
    row_count, feature_width = tokens.shape
    ctx_index = lax.axis_index("ctx")
    slot_count = cache_keys.shape[0]
    queries, key_rows, value_rows = project(rms_rows(tokens), project_weight)
    head_count = queries.shape[1] // HS
    query_heads = queries.reshape(row_count, head_count, HS)
    live_counts = lax.all_gather(cache_count, "ctx", axis=0, tiled=True)
    live_prefix = jnp.cumsum(live_counts) - live_counts
    cached_total = jnp.sum(live_counts)
    query_pos = (
        cached_total + ctx_index * row_count + jnp.arange(row_count, dtype=jnp.int32)
    ).astype(jnp.float32)
    pieces = (
        lax.all_gather(key_rows, "ctx", axis=0, tiled=True),
        lax.all_gather(value_rows, "ctx", axis=0, tiled=True),
    )
    piece_rows = pieces[0].shape[0]
    key_pos = (cached_total + jnp.arange(piece_rows, dtype=jnp.int32)).astype(jnp.float32)
    live_mask = jnp.ones((piece_rows,), dtype=bool)
    carry_state = absorb(
        fresh_state(head_count, row_count),
        query_heads,
        pieces[0],
        pieces[1],
        query_pos,
        key_pos,
        live_mask,
        distance_slope,
    )
    pieces = (
        lax.all_gather(cache_keys, "ctx", axis=0, tiled=True),
        lax.all_gather(cache_values, "ctx", axis=0, tiled=True),
    )
    slot_all = jnp.arange(pieces[0].shape[0], dtype=jnp.int32)
    owner_index = slot_all // slot_count
    slot_index = slot_all - owner_index * slot_count
    live_mask = slot_index < table_lookup(live_counts, owner_index)
    key_pos = (table_lookup(live_prefix, owner_index) + slot_index).astype(jnp.float32)
    carry_state = absorb(
        carry_state,
        query_heads,
        pieces[0],
        pieces[1],
        query_pos,
        key_pos,
        live_mask,
        distance_slope,
    )
    partial_value = jnp.dot(
        finish_state(carry_state), output_weight, preferred_element_type=jnp.float32
    )
    summed = lax.psum(partial_value, "tp")
    layer_out = (tokens.astype(jnp.float32) + summed).astype(jnp.bfloat16)
    rim_rows = passed_along(layer_out[row_count - GROUP + 1 :], "ctx", 1)
    shifted = jnp.concatenate([rim_rows, layer_out[: row_count - GROUP + 1]], axis=0)
    group_count = row_count // GROUP
    pooled = jnp.mean(
        shifted.reshape(group_count, GROUP, feature_width).astype(jnp.float32), axis=1
    ).astype(jnp.bfloat16)
    short_query, short_key, short_value = project(rms_rows(pooled), short_project)
    short_heads = short_query.reshape(group_count, head_count, HS)
    group_pos = (ctx_index * group_count + jnp.arange(group_count, dtype=jnp.int32)).astype(
        jnp.float32
    )
    pieces = (
        lax.all_gather(short_key, "ctx", axis=0, tiled=True),
        lax.all_gather(short_value, "ctx", axis=0, tiled=True),
    )
    piece_rows = pieces[0].shape[0]
    key_pos = jnp.arange(piece_rows, dtype=jnp.int32).astype(jnp.float32)
    live_mask = jnp.ones((piece_rows,), dtype=bool)
    short_state = absorb(
        fresh_state(head_count, group_count),
        short_heads,
        pieces[0],
        pieces[1],
        group_pos,
        key_pos,
        live_mask,
        short_slope,
    )
    short_part = jnp.dot(
        finish_state(short_state), short_output, preferred_element_type=jnp.float32
    )
    lifted = lax.psum_scatter(short_part, "tp", scatter_dimension=1, tiled=True)
    col_count = lifted.shape[1]
    base_columns = lax.dynamic_slice_in_dim(
        layer_out, lax.axis_index("tp") * col_count, col_count, 1
    )
    return (base_columns.astype(jnp.float32) + jnp.repeat(lifted, GROUP, axis=0)).astype(
        jnp.bfloat16
    )


def solution(mesh):
    return jax.shard_map(
        on_device,
        mesh=mesh,
        in_specs=(
            P("ctx", None),
            P(None, None, "tp"),
            P("tp", None),
            P("tp"),
            P("ctx", "tp"),
            P("ctx", "tp"),
            P("ctx"),
            P(None, None, "tp"),
            P("tp", None),
            P("tp"),
        ),
        out_specs=P("ctx", "tp"),
        check_vma=False,
    )
```

profile of v0, /device:TPU:1, one launch (start us, length us, event | category | flops | bytes accessed | tf_op | source)
XLA Modules:
  0.0 2070.7 jit_solution(4591422602576277835)
XLA Ops:
  6.5 4.8 copy.63
  11.6 3.1 fusion.20
  19.6 22.1 %all-reduce = s32[64]{0:T(128)S(1)} all-reduce(s32[64]{0:T(128)S(1)} %dynamic-update-slice), channel_id=1, replica_groups=mesh['ctx'=64,'tp'=4] {'ctx'}, use_global_device_ids=true, to_apply=%add | all-reduce | flops 64 | bytes 512
  45.9 234.2 %all-gather.15.cloned.1.call-done = bf16[8192,1,256]{2,0,1:T(8,128)(2,1)} async-done(((bf16[128,1,256]{2,0,1:T(8,128)(2,1)}), bf16[8192,1,256]{2,0,1:T(8,128)(2,1)}) %all-gather.15.cloned.1.call-update) | async-done | bytes 4194320 | tf_op jit(solution)/shard_map/all_gather | solution.py:142
  280.2 302.8 %all-gather.17.cloned.1.call-done = bf16[8192,1,256]{2,0,1:T(8,128)(2,1)} async-done(((bf16[128,1,256]{2,0,1:T(8,128)(2,1)}), bf16[8192,1,256]{2,0,1:T(8,128)(2,1)}) %all-gather.17.cloned.1.call-update) | async-done | bytes 4194320 | tf_op jit(solution)/shard_map/all_gather | solution.py:143
  582.9 54.2 %while.31 = (s32[]{:T(128)}, f32[2,128]{1,0:T(2,128)S(1)}, f32[2,128]{1,0:T(2,128)S(1)}, f32[2,128,128]{2,1,0:T(8,128)}, f32[4,2048]{1,0:T(4,128)S(1)}, /*index=...) while((s32[]{:T(128)}, f32[2,128]{1,0:T(2,128)S(1)}, ...), condition=%wide.region_5.6_spmd.clone, body=%wide.region_2.0_spmd.clone.sunk | while | flops 275875328 | bytes 20301460 | solution.py:98
  584.6 2.7 constant_dynamic-slice_fusion.13
  588.8 2.3 fusion.91
  593.9 2.6 convolution_add_fusion.5
  598.2 2.7 constant_dynamic-slice_fusion.13
  602.4 2.3 fusion.91
  607.4 2.6 convolution_add_fusion.5
  611.7 2.7 constant_dynamic-slice_fusion.13
  615.9 2.3 fusion.91
  621.0 2.6 convolution_add_fusion.5
  625.3 2.7 constant_dynamic-slice_fusion.13
  629.5 2.3 fusion.91
  634.5 2.6 convolution_add_fusion.5
  637.2 261.0 %all-gather.11.cloned.1.call-done = bf16[16384,256]{1,0:T(8,128)(2,1)} async-done(((bf16[256,256]{1,0:T(8,128)(2,1)}), bf16[16384,256]{1,0:T(8,128)(2,1)}) %all-gather.11.cloned.1.call-update) | async-done | bytes 8388624 | tf_op jit(solution)/shard_map/all_gather | solution.py:159
  898.2 313.9 %all-gather.13.cloned.1.call-done = bf16[16384,256]{1,0:T(8,128)(2,1)} async-done(((bf16[256,256]{1,0:T(8,128)(2,1)}), bf16[16384,256]{1,0:T(8,128)(2,1)}) %all-gather.13.cloned.1.call-update) | async-done | bytes 8388624 | tf_op jit(solution)/shard_map/all_gather | solution.py:160
  1212.1 118.5 %while.30 = (s32[]{:T(128)}, f32[2,128]{1,0:T(2,128)S(1)}, f32[2,128]{1,0:T(2,128)S(1)}, f32[2,128,128]{2,1,0:T(8,128)}, pred[8,2048]{1,0:T(8,128)(4,1)S(1)}, /*...) while((s32[]{:T(128)}, f32[2,128]{1,0:T(2,128)S(1)}, ...), condition=%wide.region_12.13_spmd.clone, body=%wide.region_9.12_spmd.clone.sunk | while | flops 276103936 | bytes 20307596 | solution.py:98
  1215.1 2.7 constant_dynamic-slice_fusion.11
  1219.2 2.3 fusion.87
  1224.3 2.6 convolution_add_fusion.4
  1229.9 2.7 constant_dynamic-slice_fusion.11
  1234.1 2.3 fusion.87
  1239.1 2.6 convolution_add_fusion.4
  1244.8 2.7 constant_dynamic-slice_fusion.11
  1254.0 2.6 convolution_add_fusion.4
  1259.6 2.7 constant_dynamic-slice_fusion.11
  1263.7 2.3 fusion.87
  1268.8 2.6 convolution_add_fusion.4
  1274.4 2.7 constant_dynamic-slice_fusion.11
  1283.6 2.6 convolution_add_fusion.4
  1289.2 2.7 constant_dynamic-slice_fusion.11
  1298.4 2.6 convolution_add_fusion.4
  1304.0 2.7 constant_dynamic-slice_fusion.11
  1308.1 2.3 fusion.87
  1313.2 2.6 convolution_add_fusion.4
  1318.9 2.7 constant_dynamic-slice_fusion.11
  1328.0 2.6 convolution_add_fusion.4
  1333.2 87.2 %all-reduce.3.cloned.1.call-done = f32[128,2048]{1,0:T(8,128)} async-done(((f32[128,2048]{1,0:T(8,128)}), f32[128,2048]{1,0:T(8,128)}) %all-reduce.3.cloned.1.call-update) | async-done | bytes 1048592 | tf_op jit(solution)/shard_map/psum | solution.py:180
  1421.8 2.4 collective-permute-start
  1424.1 4.7 copy.72
  1430.1 2.9 fusion.23
  1434.7 253.1 %all-gather.19.cloned.1.call-done = bf16[2048,1,256]{2,0,1:T(8,128)(2,1)} async-done(((bf16[32,1,256]{2,0,1:T(8,128)(2,1)}), bf16[2048,1,256]{2,0,1:T(8,128)(2,1)}) %all-gather.19.cloned.1.call-update) | async-done | bytes 1048592 | tf_op jit(solution)/shard_map/all_gather | solution.py:194
  1690.0 293.8 %all-gather.21.cloned.1.call-done = bf16[2048,1,256]{2,0,1:T(8,128)(2,1)} async-done(((bf16[32,1,256]{2,0,1:T(8,128)(2,1)}), bf16[2048,1,256]{2,0,1:T(8,128)(2,1)}) %all-gather.21.cloned.1.call-update) | async-done | bytes 1048592 | tf_op jit(solution)/shard_map/all_gather | solution.py:195
  1988.7 72.5 %reduce-scatter.2.cloned.1.call-done = f32[32,512]{1,0:T(8,128)} async-done(((f32[32,2048]{1,0:T(8,128)}), f32[32,512]{1,0:T(8,128)}) %reduce-scatter.2.cloned.1.call-update) | async-done | bytes 65552 | tf_op jit(solution)/shard_map/reduce_scatter | solution.py:213
  (214 shorter events, 114.0 us)
Async XLA Ops:
  6.5 1325.2 %copy-start = (bf16[256,2048]{1,0:T(8,128)(2,1)S(1)}, bf16[256,2048]{1,0:T(8,128)(2,1)}, u32[]{:S(2)}) copy-start(bf16[256,2048]{1,0:T(8,128)(2,1)} %param.16) | copy-start | bytes 3145732
  6.5 4.8 copy-start.1
  6.5 273.6 %all-gather.15.cloned.1.call-start = ((), (), s32[]{:S(2)}) async-start(), calls=%async_computation.5 | async-start | bytes 4259840 | tf_op jit(solution)/shard_map/all_gather | solution.py:142
  11.6 6.6 copy-start.7
  11.6 571.4 %copy-start.5 = (f32[2]{0:T(128)S(1)}, f32[2]{0:T(128)}, u32[]{:S(2)}) copy-start(f32[2]{0:T(128)} %param.17) | copy-start | bytes 28
  15.4 567.6 %all-gather.17.cloned.1.call-start = ((), (), s32[]{:S(2)}) async-start(), calls=%async_computation.6 | async-start | bytes 4259840 | tf_op jit(solution)/shard_map/all_gather | solution.py:143
  16.1 882.1 %all-gather.11.cloned.1.call-start = ((), (), s32[]{:S(2)}) async-start(), calls=%async_computation.1 | async-start | bytes 8519680 | tf_op jit(solution)/shard_map/all_gather | solution.py:159
  16.9 1195.3 %all-gather.13.cloned.1.call-start = ((), (), s32[]{:S(2)}) async-start(), calls=%async_computation.2 | async-start | bytes 8519680 | tf_op jit(solution)/shard_map/all_gather | solution.py:160
  17.4 1403.0 %all-reduce.3.cloned.1.call-start = ((), (), s32[]{:S(2)}) async-start(), calls=%async_computation.3 | async-start | bytes 2097152 | tf_op jit(solution)/shard_map/psum | solution.py:180
  1330.7 89.7 %copy-start.2 = (bf16[128,2048]{1,0:T(8,128)(2,1)S(1)}, bf16[128,2048]{1,0:T(8,128)(2,1)}, u32[]{:S(2)}) copy-start(bf16[128,2048]{1,0:T(8,128)(2,1)} %param.14) | copy-start | bytes 1572868
  1333.2 354.7 %all-gather.19.cloned.1.call-start = ((), (), s32[]{:S(2)}) async-start(), calls=%async_computation.7 | async-start | bytes 1064960 | tf_op jit(solution)/shard_map/all_gather | solution.py:194
  1421.7 7.1 copy-start.3
  1421.8 7.1 collective-permute-start
  1433.0 256.1 %copy-start.6 = (f32[2]{0:T(128)S(1)}, f32[2]{0:T(128)}, u32[]{:S(2)}) copy-start(f32[2]{0:T(128)} %param.23) | copy-start | bytes 28
  1433.7 550.2 %all-gather.21.cloned.1.call-start = ((), (), s32[]{:S(2)}) async-start(), calls=%async_computation.8 | async-start | bytes 1064960 | tf_op jit(solution)/shard_map/all_gather | solution.py:195
  1434.5 626.8 %reduce-scatter.2.cloned.1.call-start = ((), (), s32[]{:S(2)}) async-start(), calls=%async_computation.4 | async-start | bytes 327680 | tf_op jit(solution)/shard_map/reduce_scatter | solution.py:213
  1690.0 297.7 %copy-start.4 = (bf16[256,2048]{1,0:T(8,128)(2,1)S(1)}, bf16[256,2048]{1,0:T(8,128)(2,1)}, u32[]{:S(2)}) copy-start(bf16[256,2048]{1,0:T(8,128)(2,1)} %param.22) | copy-start | bytes 3145732
Sparse Core Ops, SparseCore 0:
  15.5 264.6 all-gather.14
  282.0 300.9 all-gather.16
  584.7 313.4 all-gather.10
  899.8 312.2 all-gather.12
  1333.3 87.0 all-reduce.2
  1433.8 253.9 all-gather.18
  1689.8 294.0 all-gather.20
  1988.8 72.3 reduce-scatter.1
where the time goes:
time: 2070 us
  waiting for transfers between devices  1820 us (88%)
  local copies, waits for them, and re-layouts  102 us (5%)
  matrix products  70.2 us (3%)
  other arithmetic  36.6 us (2%)
  blocking collectives  22.1 us (1%)
    all_gather x1, waiting for transfers between devices, on_device(): lax.all_gather(cache_values, 'ctx', axis=0, tiled=True)  314 us
    all_gather x1, waiting for transfers between devices, on_device(): lax.all_gather(value_rows, 'ctx', axis=0, tiled=True)  303 us
    all_gather x1, waiting for transfers between devices, on_device(): lax.all_gather(short_value, 'ctx', axis=0, tiled=True)  294 us
    all_gather x1, waiting for transfers between devices, on_device(): lax.all_gather(cache_keys, 'ctx', axis=0, tiled=True)  261 us
    all_gather x1, waiting for transfers between devices, on_device(): lax.all_gather(short_key, 'ctx', axis=0, tiled=True)  253 us
    all_gather x1, waiting for transfers between devices, on_device(): lax.all_gather(key_rows, 'ctx', axis=0, tiled=True)  234 us
    psum x1, waiting for transfers between devices, on_device(): summed = lax.psum(partial_value, 'tp')  87.2 us
    dynamic_slice x56, local copies, waits for them, and re-layouts, absorb(): carry_state, unused = lax.scan(one_step, carry_state, items)  84.1 us
  transfers between devices with their start and end apart: 9, of which 8 were waited for; matrix products, arithmetic and copies ran while one was open for 3% of the time, Pallas kernels for 0%

commit v1 on v0

v1 whole, which is shorter than its diff:
```python
import functools
import math

import jax
import jax.numpy as jnp
from jax import lax
from jax.experimental import pallas as pl
from jax.experimental.pallas import tpu as pltpu
from jax.sharding import Mesh, PartitionSpec as P

HS = 128
GROUP = 4
NEG = -1e30
LOG2E = math.log2(math.e)
SCALE2 = HS ** -0.5 * LOG2E

VMEM = pltpu.VMEM
SMEM = pltpu.SMEM
F32 = jnp.float32
BF16 = jnp.bfloat16


def cost(flops, moved, trans=0):
    return pl.CostEstimate(flops=flops, bytes_accessed=moved, transcendentals=trans)


def params():
    return pltpu.CompilerParams(vmem_limit_bytes=48 * 1024 * 1024)


def rms_scaled(values):
    inv = lax.rsqrt(jnp.mean(values * values, axis=-1, keepdims=True) + 1e-06)
    return (values * inv).astype(BF16)


def dot_t(a, b):
    return lax.dot_general(a, b, (((1,), (1,)), ((), ())), preferred_element_type=F32)


def three_parts(x):
    hi = x.astype(BF16).astype(F32)
    mid = (x - hi).astype(BF16).astype(F32)
    lo = (x - hi - mid).astype(BF16).astype(F32)
    return hi, mid, lo


def project_kernel(copies, tok_ref, w_ref, bq_ref, bkv_ref, normed):
    step = pl.program_id(0)

    @pl.when(step == 0)
    def _():
        normed[...] = rms_scaled(tok_ref[...].astype(F32))

    out = jnp.dot(normed[...], w_ref[0], preferred_element_type=F32)

    @pl.when(step == 0)
    def _():
        scaled = (out * SCALE2).astype(BF16)
        for c in range(copies):
            bq_ref[c] = scaled

    @pl.when(step == 1)
    def _():
        rounded = out.astype(BF16)
        for c in range(copies):
            bkv_ref[c, 0] = rounded

    @pl.when(step == 2)
    def _():
        rounded = out.astype(BF16)
        for c in range(copies):
            bkv_ref[c, 1] = rounded


def project(rows, weight3, qcopies, kvcopies):
    n, d = rows.shape
    width = weight3.shape[2]
    assert qcopies == kvcopies
    return pl.pallas_call(
        functools.partial(project_kernel, qcopies),
        grid=(3,),
        in_specs=[
            pl.BlockSpec((n, d), lambda i: (0, 0)),
            pl.BlockSpec((1, d, width), lambda i: (i, 0, 0)),
        ],
        out_specs=[
            pl.BlockSpec((qcopies, n, width), lambda i: (0, 0, 0)),
            pl.BlockSpec((kvcopies, 2, n, width), lambda i: (0, 0, 0, 0)),
        ],
        out_shape=[
            jax.ShapeDtypeStruct((qcopies, n, width), BF16),
            jax.ShapeDtypeStruct((kvcopies, 2, n, width), BF16),
        ],
        scratch_shapes=[VMEM((n, d), BF16)],
        compiler_params=params(),
        cost_estimate=cost(6 * n * d * width, 2 * (n * d + 3 * d * width)),
        name="project",
    )(rows, weight3)


def attend_kernel(
    heads, idx_ref, counts_ref, slope_ref, q_ref, kc_ref, vc_ref, kv_ref, out_ref, prefix, bias
):
    tile = pl.program_id(0)
    y, z, xl = idx_ref[0], idx_ref[1], idx_ref[2]
    nq, rows, _ = q_ref.shape
    peers, slots, _ = kc_ref.shape
    span = kv_ref.shape[2]
    owners = counts_ref.shape[0]
    nc = peers * slots
    ns = peers * span

    @pl.when(tile == 0)
    def _():
        def one(i, total):
            prefix[i] = total
            return total + counts_ref[i]

        total = lax.fori_loop(0, owners, one, jnp.int32(0))
        for j in range(peers):
            ctx = (j // 2) * 16 + z * 2 + (j % 2)
            slot = lax.broadcasted_iota(jnp.int32, (1, slots), 1)
            live = slot < counts_ref[ctx]
            pos = (slot + (prefix[ctx] - total)).astype(F32)
            spot = (lax.broadcasted_iota(jnp.int32, (1, span), 1) + ctx * span).astype(F32)
            for h in range(heads):
                slope = slope_ref[h] * LOG2E
                bias[h : h + 1, j * slots : (j + 1) * slots] = jnp.where(live, slope * pos, NEG)
                bias[h : h + 1, nc + j * span : nc + (j + 1) * span] = slope * spot

    total_rows = nq * rows
    row = lax.broadcasted_iota(jnp.int32, (total_rows, 1), 0)
    row_pos = (y * 16 + xl) * rows + (tile * nq + row // rows) * (2 * rows) + row % rows
    key = lax.broadcasted_iota(jnp.int32, (1, ns), 1)
    block = key // span
    key_pos = ((block // 2) * 16 + z * 2 + block % 2) * span + key % span
    usable = key_pos <= row_pos
    lane = lax.broadcasted_iota(jnp.int32, (total_rows, HS), 1)
    packed = jnp.zeros((total_rows, HS), F32)
    for h in range(heads):
        cols = slice(h * HS, (h + 1) * HS)
        q = q_ref[:, :, cols].reshape(total_rows, HS)
        s1 = dot_t(q, kc_ref[:, :, cols].reshape(nc, HS)) + bias[h : h + 1, :nc]
        s2 = dot_t(q, kv_ref[:, 0, :, cols].reshape(ns, HS)) + bias[h : h + 1, nc:]
        s2 = jnp.where(usable, s2, NEG)
        top = jnp.maximum(
            jnp.max(s1, axis=1, keepdims=True), jnp.max(s2, axis=1, keepdims=True)
        )
        p1 = jnp.exp2(s1 - top).astype(BF16)
        p2 = jnp.exp2(s2 - top).astype(BF16)
        v1 = vc_ref[:, :, cols].reshape(nc, HS)
        v2 = kv_ref[:, 1, :, cols].reshape(ns, HS)
        a1 = jnp.concatenate([v1, jnp.ones_like(v1)], axis=1)
        a2 = jnp.concatenate([v2, jnp.ones_like(v2)], axis=1)
        both = jnp.dot(p1, a1, preferred_element_type=F32) + jnp.dot(
            p2, a2, preferred_element_type=F32
        )
        weight_total = both[:, HS:]
        part = (both[:, :HS] / weight_total).astype(BF16)
        out_ref[:, :rows, cols] = part.reshape(nq, rows, HS)
        level = top + jnp.log2(weight_total)
        for k, piece in enumerate(three_parts(level)):
            packed = jnp.where(lane == 3 * h + k, piece, packed)
    for b in range(nq):
        turned = jnp.transpose(packed[b * rows : (b + 1) * rows])[:16]
        out_ref[b, rows:, :] = jnp.concatenate(
            [turned, jnp.zeros_like(turned)], axis=1
        ).astype(BF16)


def attend(idx, counts, slopes, q, kc, vc, kv):
    blocks, rows, width = q.shape
    heads = width // HS
    peers, slots, _ = kc.shape
    span = kv.shape[2]
    keys = peers * (slots + span)
    nq = 2
    fixed = lambda shape: pl.BlockSpec(shape, lambda i, *_: (0,) * len(shape))
    return pl.pallas_call(
        functools.partial(attend_kernel, heads),
        grid_spec=pltpu.PrefetchScalarGridSpec(
            num_scalar_prefetch=3,
            grid=(blocks // nq,),
            in_specs=[
                pl.BlockSpec((nq, rows, width), lambda i, *_: (i, 0, 0)),
                fixed(kc.shape),
                fixed(vc.shape),
                fixed(kv.shape),
            ],
            out_specs=pl.BlockSpec((nq, rows + 16, width), lambda i, *_: (i, 0, 0)),
            scratch_shapes=[SMEM((counts.shape[0],), jnp.int32), VMEM((8, keys), F32)],
        ),
        out_shape=jax.ShapeDtypeStruct((blocks, rows + 16, width), BF16),
        compiler_params=params(),
        cost_estimate=cost(
            4 * blocks * rows * keys * width, 4 * keys * width, blocks * rows * keys * heads
        ),
        name="attend",
    )(idx, counts, slopes, q, kc, vc, kv)


def merge_kernel(heads, copies, parts_ref, out_ref):
    sources, padded, width = parts_ref.shape
    rows = padded - 16
    levels = jnp.concatenate(
        [parts_ref[s, rows:, :HS].astype(F32) for s in range(sources)], axis=0
    )
    turned = jnp.transpose(levels)
    for h in range(heads):
        cols = slice(h * HS, (h + 1) * HS)
        level = []
        for s in range(sources):
            at = s * 16 + 3 * h
            level.append(
                (turned[:, at : at + 1] + turned[:, at + 1 : at + 2]) + turned[:, at + 2 : at + 3]
            )
        top = functools.reduce(jnp.maximum, level)
        total = jnp.zeros((rows, 1), F32)
        acc = jnp.zeros((rows, HS), F32)
        for s in range(sources):
            weight = jnp.exp2(level[s] - top)
            total = total + weight
            acc = acc + weight * parts_ref[s, :rows, cols].astype(F32)
        done = (acc / total).astype(BF16)
        for c in range(copies):
            out_ref[c, :, cols] = done


def merge(parts, copies):
    sources, padded, width = parts.shape
    rows = padded - 16
    return pl.pallas_call(
        functools.partial(merge_kernel, width // HS, copies),
        out_shape=jax.ShapeDtypeStruct((copies, rows, width), BF16),
        compiler_params=params(),
        cost_estimate=cost(4 * sources * rows * width, 2 * sources * padded * width),
        name="merge",
    )(parts)


def layer_kernel(tok_ref, att_ref, w_ref, out_ref):
    parts, rows, width = att_ref.shape
    acc = tok_ref[...].astype(F32)
    for t in range(parts):
        acc = acc + jnp.dot(
            att_ref[t], w_ref[t * width : (t + 1) * width], preferred_element_type=F32
        )
    out_ref[...] = acc.astype(BF16)


def layer_output(tokens, att, weight):
    rows, d = tokens.shape
    step = 512
    inner = weight.shape[0]
    return pl.pallas_call(
        layer_kernel,
        grid=(d // step,),
        in_specs=[
            pl.BlockSpec((rows, step), lambda i: (0, i)),
            pl.BlockSpec(att.shape, lambda i: (0, 0, 0)),
            pl.BlockSpec((inner, step), lambda i: (0, i)),
        ],
        out_specs=pl.BlockSpec((rows, step), lambda i: (0, i)),
        out_shape=jax.ShapeDtypeStruct((rows, d), BF16),
        compiler_params=params(),
        cost_estimate=cost(2 * rows * d * inner, 2 * inner * d),
        name="layer_output",
    )(tokens, att, weight)


def short_project_kernel(copies, lay_ref, rim_ref, w_ref, bq_ref, bkv_ref, normed):
    step = pl.program_id(0)
    rows = lay_ref.shape[0]
    groups = rows // GROUP
    rim_rows = rim_ref.shape[0]

    @pl.when(step == 0)
    def _():
        g = lax.broadcasted_iota(jnp.int32, (groups, rows), 0) * GROUP
        t = lax.broadcasted_iota(jnp.int32, (groups, rows), 1)
        own = jnp.where((t <= g) & (t > g - GROUP), 1.0 / GROUP, 0.0).astype(BF16)
        g = lax.broadcasted_iota(jnp.int32, (groups, rim_rows), 0) * GROUP
        t = lax.broadcasted_iota(jnp.int32, (groups, rim_rows), 1) - rim_rows
        before = jnp.where(t > g - GROUP, 1.0 / GROUP, 0.0).astype(BF16)
        pooled = jnp.dot(own, lay_ref[...], preferred_element_type=F32) + jnp.dot(
            before, rim_ref[...], preferred_element_type=F32
        )
        normed[...] = rms_scaled(pooled.astype(BF16).astype(F32))

    out = jnp.dot(normed[...], w_ref[0], preferred_element_type=F32)

    @pl.when(step == 0)
    def _():
        scaled = (out * SCALE2).astype(BF16)
        for c in range(copies):
            bq_ref[c] = scaled

    @pl.when(step == 1)
    def _():
        rounded = out.astype(BF16)
        for c in range(copies):
            bkv_ref[c, 0] = rounded

    @pl.when(step == 2)
    def _():
        rounded = out.astype(BF16)
        for c in range(copies):
            bkv_ref[c, 1] = rounded


def short_project(layer, rim, weight3, copies):
    n, d = layer.shape
    groups = n // GROUP
    width = weight3.shape[2]
    return pl.pallas_call(
        functools.partial(short_project_kernel, copies),
        grid=(3,),
        in_specs=[
            pl.BlockSpec((n, d), lambda i: (0, 0)),
            pl.BlockSpec(rim.shape, lambda i: (0, 0)),
            pl.BlockSpec((1, d, width), lambda i: (i, 0, 0)),
        ],
        out_specs=[
            pl.BlockSpec((copies, groups, width), lambda i: (0, 0, 0)),
            pl.BlockSpec((copies, 2, groups, width), lambda i: (0, 0, 0, 0)),
        ],
        out_shape=[
            jax.ShapeDtypeStruct((copies, groups, width), BF16),
            jax.ShapeDtypeStruct((copies, 2, groups, width), BF16),
        ],
        scratch_shapes=[VMEM((groups, d), BF16)],
        compiler_params=params(),
        cost_estimate=cost(6 * groups * d * width, 2 * (n * d + 3 * d * width)),
        name="short_project",
    )(layer, rim, weight3)


def short_attend_kernel(heads, idx_ref, slope_ref, q_ref, kv_ref, out_ref):
    y, z, xl = idx_ref[0], idx_ref[1], idx_ref[2]
    blocks, groups, width = q_ref.shape
    peers = kv_ref.shape[0]
    nr, nk = blocks * groups, peers * groups
    row = lax.broadcasted_iota(jnp.int32, (nr, 1), 0)
    row_pos = (y * 16 + xl + (row // groups) * 2) * groups + row % groups
    key = lax.broadcasted_iota(jnp.int32, (1, nk), 1)
    block = key // groups
    key_pos = ((block // 2) * 16 + z * 2 + block % 2) * groups + key % groups
    usable = key_pos <= row_pos
    spot = key_pos.astype(F32)
    lane = lax.broadcasted_iota(jnp.int32, (nr, HS), 1)
    packed = jnp.zeros((nr, HS), F32)
    for h in range(heads):
        cols = slice(h * HS, (h + 1) * HS)
        q = q_ref[:, :, cols].reshape(nr, HS)
        s = dot_t(q, kv_ref[:, 0, :, cols].reshape(nk, HS)) + (slope_ref[h] * LOG2E) * spot
        s = jnp.where(usable, s, NEG)
        top = jnp.max(s, axis=1, keepdims=True)
        p = jnp.exp2(s - top).astype(BF16)
        v = kv_ref[:, 1, :, cols].reshape(nk, HS)
        both = jnp.dot(
            p, jnp.concatenate([v, jnp.ones_like(v)], axis=1), preferred_element_type=F32
        )
        weight_total = both[:, HS:]
        part = (both[:, :HS] / weight_total).astype(BF16)
        out_ref[:, :, cols] = part.reshape(blocks, groups, HS)
        level = top + jnp.log2(weight_total)
        for k, piece in enumerate(three_parts(level)):
            packed = jnp.where(lane == 3 * h + k, piece, packed)
    out_ref[:, :, width:] = packed.astype(BF16).reshape(blocks, groups, HS)


def short_attend(idx, slopes, q, kv):
    blocks, groups, width = q.shape
    smem = pl.BlockSpec(memory_space=SMEM)
    vmem = pl.BlockSpec(memory_space=VMEM)
    keys = kv.shape[0] * groups
    return pl.pallas_call(
        functools.partial(short_attend_kernel, width // HS),
        in_specs=[smem, smem, vmem, vmem],
        out_specs=vmem,
        out_shape=jax.ShapeDtypeStruct((blocks, groups, width + HS), BF16),
        compiler_params=params(),
        cost_estimate=cost(4 * blocks * groups * keys * width, 4 * keys * width),
        name="short_attend",
    )(idx, slopes, q, kv)


def short_merge_kernel(heads, copies, parts_ref, out_ref):
    sources, rows, padded = parts_ref.shape
    width = padded - HS
    for h in range(heads):
        cols = slice(h * HS, (h + 1) * HS)
        level = []
        for s in range(sources):
            lev = parts_ref[s, :, width:].astype(F32)
            level.append(
                (lev[:, 3 * h : 3 * h + 1] + lev[:, 3 * h + 1 : 3 * h + 2])
                + lev[:, 3 * h + 2 : 3 * h + 3]
            )
        top = functools.reduce(jnp.maximum, level)
        total = jnp.zeros((rows, 1), F32)
        acc = jnp.zeros((rows, HS), F32)
        for s in range(sources):
            weight = jnp.exp2(level[s] - top)
            total = total + weight
            acc = acc + weight * parts_ref[s, :, cols].astype(F32)
        done = (acc / total).astype(BF16)
        for c in range(copies):
            out_ref[c, :, cols] = done


def short_merge(parts, copies):
    sources, rows, padded = parts.shape
    width = padded - HS
    return pl.pallas_call(
        functools.partial(short_merge_kernel, width // HS, copies),
        out_shape=jax.ShapeDtypeStruct((copies, rows, width), BF16),
        compiler_params=params(),
        cost_estimate=cost(4 * sources * rows * width, 2 * sources * rows * padded),
        name="short_merge",
    )(parts)


def final_kernel(tp_ref, lay_ref, att_ref, w_ref, out_ref):
    parts, groups, width = att_ref.shape
    rows = lay_ref.shape[0]
    t = lax.broadcasted_iota(jnp.int32, (rows, groups), 0) // GROUP
    g = lax.broadcasted_iota(jnp.int32, (rows, groups), 1)
    spread = jnp.where(t == g, 1.0, 0.0).astype(BF16)
    acc = lay_ref[...].astype(F32)
    branch = jnp.zeros(acc.shape, F32)
    for p in range(parts):
        lifted = jnp.dot(spread, att_ref[p], preferred_element_type=F32).astype(BF16)
        branch = branch + jnp.dot(
            lifted, w_ref[p * width : (p + 1) * width], preferred_element_type=F32
        )
    out_ref[...] = (acc + branch).astype(BF16)


def final_sum(tp_index, layer, att, weight):
    rows, d = layer.shape
    parts = att.shape[0]
    cols = d // parts
    inner = weight.shape[0]
    return pl.pallas_call(
        final_kernel,
        grid_spec=pltpu.PrefetchScalarGridSpec(
            num_scalar_prefetch=1,
            grid=(1,),
            in_specs=[
                pl.BlockSpec((rows, cols), lambda i, tp: (0, tp[0])),
                pl.BlockSpec(att.shape, lambda i, tp: (0, 0, 0)),
                pl.BlockSpec((inner, cols), lambda i, tp: (0, tp[0])),
            ],
            out_specs=pl.BlockSpec((rows, cols), lambda i, tp: (0, 0)),
        ),
        out_shape=jax.ShapeDtypeStruct((rows, cols), BF16),
        compiler_params=params(),
        cost_estimate=cost(2 * rows * cols * inner, 2 * inner * cols),
        name="final_sum",
    )(tp_index, layer, att, weight)


def exchange(blocks, axis):
    return lax.all_to_all(blocks, axis, 0, 0)


def spread_to(block, axis, copies):
    return exchange(jnp.broadcast_to(block[None], (copies,) + block.shape), axis)


def on_device(
    tokens,
    project_weight,
    output_weight,
    distance_slope,
    cache_keys,
    cache_values,
    cache_count,
    short_project_weight,
    short_output,
    short_slope,
):
    ctx_axes = ("y", "z", "xl")
    key_axes = ("y", "xl")
    nk = lax.axis_size("y") * lax.axis_size("xl")
    nq = lax.axis_size("z")
    tp = lax.axis_size("tp")
    idx = jnp.stack([lax.axis_index("y"), lax.axis_index("z"), lax.axis_index("xl")]).astype(
        jnp.int32
    )
    tp_index = lax.axis_index("tp").astype(jnp.int32).reshape(1)

    counts = lax.all_gather(cache_count, ctx_axes, axis=0, tiled=True)
    out_weight = lax.all_gather(output_weight, "tp", axis=0, tiled=True)
    short_out_weight = lax.all_gather(short_output, "tp", axis=0, tiled=True)
    kc = spread_to(cache_keys, key_axes, nk)
    vc = spread_to(cache_values, key_axes, nk)

    bq, bkv = project(tokens, jnp.transpose(project_weight, (1, 0, 2)), nq, nk)
    q = exchange(bq, "z")
    kv = exchange(bkv, key_axes)
    parts = attend(idx, counts, distance_slope, q, kc, vc, kv)
    att = exchange(merge(exchange(parts, "z"), tp), "tp")
    layer = layer_output(tokens, att, out_weight)

    n = lax.axis_size(ctx_axes)
    rim = lax.ppermute(layer[-16:], ctx_axes, [(i, i + 1) for i in range(n - 1)])
    sbq, sbkv = short_project(layer, rim, jnp.transpose(short_project_weight, (1, 0, 2)), nq)
    sq = exchange(sbq, "z")
    skv = exchange(sbkv, key_axes)
    sparts = short_attend(idx, short_slope, sq, skv)
    satt = exchange(short_merge(exchange(sparts, "z"), tp), "tp")
    return final_sum(tp_index, layer, satt, short_out_weight)


def solution(mesh):
    split = Mesh(mesh.devices.reshape(4, 8, 2, 4), ("y", "z", "xl", "tp"))
    ctx = ("y", "z", "xl")
    return jax.shard_map(
        on_device,
        mesh=split,
        in_specs=(
            P(ctx, None),
            P(None, None, "tp"),
            P("tp", None),
            P("tp"),
            P(ctx, "tp"),
            P(ctx, "tp"),
            P(ctx),
            P(None, None, "tp"),
            P("tp", None),
            P("tp"),
        ),
        out_specs=P(ctx, "tp"),
        check_vma=False,
    )
```

time: 2070 us -> 248 us (0.12)
  waiting for transfers between devices: 1820 us -> 7.49 us
  blocking collectives: 22.1 us -> 176 us
  local copies, waits for them, and re-layouts: 102 us -> 11.6 us
  matrix products: 70.2 us -> 0 us
  other arithmetic: 36.6 us -> 0.08 us
  Pallas kernels: 0 us -> 22.8 us
    all_gather x6 -> x2, waiting for transfers between devices: 1660 us -> 0.01 us  [the longest x1 0.01 us: on_device(): out_weight = lax.all_gather(output_weight, 'tp', axis=0, tiled=True)]
    all_to_all x0 -> x8, blocking collectives: none -> 138 us  [exchange(): return lax.all_to_all(blocks, axis, 0, 0)]
    psum x1 -> x0, waiting for transfers between devices: 87.2 us -> none  [on_device(): summed = lax.psum(partial_value, 'tp')]
    dynamic_slice x56 -> x0, local copies, waits for them, and re-layouts: 84.1 us -> none  [absorb(): carry_state, unused = lax.scan(one_step, carry_state, items)]
    reduce_scatter x1 -> x0, waiting for transfers between devices: 72.5 us -> none  [on_device(): lifted = lax.psum_scatter(short_part, 'tp', scatter_dimension=1, tiled=True)]
    dot_general x30 -> x0, matrix products: 70.2 us -> none  [the longest x13 33.3 us: absorb_block(): jnp.einsum('hrk,khd->hrd', weights, value_heads, preferred_element_type=j...]
    pallas_call x0 -> x8, Pallas kernels: none -> 22.8 us  [the longest x1 14 us: attend(): pl.pallas_call(functools.partial(attend_kernel, heads), grid_spec=pltpu.P...]
  transfers between devices with their start and end apart: 9 -> 5, of which waited for: 8 -> 2; matrix products, arithmetic and copies ran while one was open for 3% -> 1% of each run, Pallas kernels for 0% -> 9%
where the time goes in v1:
time: 248 us; the launch traced here: 247 us
  blocking collectives  176 us (71%)
  Pallas kernels  22.8 us (9%)
  starting transfers between devices  14.9 us (6%)
  between operations  14.2 us (6%)
  local copies, waits for them, and re-layouts  11.6 us (5%)
  waiting for transfers between devices  7.49 us (3%)
    all_to_all x8, blocking collectives, exchange(): return lax.all_to_all(blocks, axis, 0, 0)  138 us
    unnamed x1, blocking collectives  38.6 us
    pallas_call x1, Pallas kernels, attend(): pl.pallas_call(functools.partial(attend_kernel, heads), grid_spec=pltpu.P...  14 us
    all_to_all x2, starting transfers between devices, exchange(): return lax.all_to_all(blocks, axis, 0, 0)  13.3 us
    unnamed x25, local copies, waits for them, and re-layouts  10.5 us
  transfers between devices with their start and end apart: 5, of which 2 were waited for; matrix products, arithmetic and copies ran while one was open for 1% of the time, Pallas kernels for 9%

profile of v1, /device:TPU:1, one launch (start us, length us, event | category | flops | bytes accessed | tf_op | source)
XLA Modules:
  0.0 247.5 jit_solution(17589146983469488414)
XLA Ops:
  6.5 0.0 all-gather.3.cloned.1.call-start
  6.5 0.7 all-gather.3.cloned.1.call-update
  7.3 0.0 copy-start.8
  7.3 0.0 all-gather.5.cloned.1.call-start
  7.3 0.7 all-gather.5.cloned.1.call-update
  8.0 0.0 copy-start.2
  8.0 1.9 copy-done.2
  9.9 0.0 copy-start.4
  9.9 1.0 copy-done.4
  10.9 0.0 copy-start.9
  11.0 1.3 project.1
  12.2 24.8 %all_to_all.50.q_ref = bf16[8,128,256]{2,1,0:T(8,128)(2,1)S(1)} all-to-all(bf16[8,128,256]{2,1,0:T(8,128)(2,1)S(1)} %get-tuple-element.9), channel_id=1, replica_groups=mesh['y'=4,'z'=8,'xl'=2,'tp'=4] {'z'}, dimensions={0} | all-to-all | bytes 1048576 | tf_op jit(solution)/shard_map/all_to_all | solution.py:465
  37.0 0.0 copy-start.10
  37.0 26.3 %all_to_all.51.kv_ref = bf16[8,2,128,256]{3,2,1,0:T(8,128)(2,1)S(1)} all-to-all(bf16[8,2,128,256]{3,2,1,0:T(8,128)(2,1)S(1)} %get-tuple-element.10), channel_id=1, replica_groups=mesh['y'=4,'z'=8,'xl'=2,'tp'=4] {'y','xl'}, dimensions={0} | all-to-all | bytes 2097152 | tf_op jit(solution)/shard_map/all_to_all | solution.py:465
  63.3 0.0 copy-done.8
  63.3 0.1 broadcast_in_dim.4
  63.4 16.4 %all_to_all.52.kc_ref = bf16[8,256,256]{2,1,0:T(8,128)(2,1)S(1)} all-to-all(bf16[8,256,256]{2,1,0:T(8,128)(2,1)S(1)} %broadcast_in_dim.4), channel_id=1, replica_groups=mesh['y'=4,'z'=8,'xl'=2,'tp'=4] {'y','xl'}, dimensions={0} | all-to-all | bytes 2097152 | tf_op jit(solution)/shard_map/all_to_all | solution.py:465
  79.7 0.0 copy-done.9
  79.8 1.1 broadcast_in_dim.5
  80.8 4.2 %all-to-all-start.2 = ((bf16[8,256,256]{2,1,0:T(8,128)(2,1)}), bf16[8,256,256]{2,1,0:T(8,128)(2,1)}, u32[]{:S(2)}, u32[]{:S(2)}) async-start(bf16[8,256,256]{2,1,0:T(8,128)(2,1)} %broadcast_in_dim.5), calls=%async_computation.2 | async-start | bytes 2097152 | tf_op jit(solution)/shard_map/all_to_all | solution.py:465
  85.7 0.0 copy-done.10
  85.7 0.6 dynamic-slice
  86.3 0.7 dynamic-update-slice
  87.0 38.6 %all-reduce.counts_ref = s32[64]{0:T(128)S(1)} all-reduce(s32[64]{0:T(128)S(1)} %dynamic-update-slice), channel_id=1, replica_groups=mesh['y'=4,'z'=8,'xl'=2,'tp'=4] {'y','z','xl'}, use_global_device_ids=true, to_apply=%add | all-reduce | flops 64 | bytes 512
  125.6 0.1 pad_add_fusion.idx_ref
  125.7 0.0 all-to-all-done.2.vc_ref
  125.7 0.0 copy-done.7
  125.7 14.0 %attend.1 = bf16[8,144,256]{2,1,0:T(8,128)(2,1)S(1)} custom-call(s32[3]{0:T(128)S(1)} %pad_add_fusion.idx_ref, s32[64]{0:T(128)S(1)} %all-reduce.counts_ref, f32[2]{0:T(128)S(1)} %copy-done.7, bf16[8,128,256]{2,1,0:T(8,128)(2,1)S(1)} %all_to_all.50.q_ref, bf16[8,256,256]{2,1,0:T(8,128)(2,1)S(1)} %all_to_all.52.kc_ref, ...), custom_call_target="tpu_custom_call" | custom-call | flops 3221225472 | bytes 3145728 | tf_op jit(solution)/shard_map/attend/pallas_call | solution.py:179
  139.8 17.7 %all_to_all.53.parts_ref = bf16[8,144,256]{2,1,0:T(8,128)(2,1)S(1)} all-to-all(bf16[8,144,256]{2,1,0:T(8,128)(2,1)S(1)} %attend.1), channel_id=1, replica_groups=mesh['y'=4,'z'=8,'xl'=2,'tp'=4] {'z'}, dimensions={0} | all-to-all | bytes 1179648 | tf_op jit(solution)/shard_map/all_to_all | solution.py:465
  157.5 1.2 merge.1
  158.7 18.3 %all_to_all.54.att_ref = bf16[4,128,256]{2,1,0:T(8,128)(2,1)S(1)} all-to-all(bf16[4,128,256]{2,1,0:T(8,128)(2,1)S(1)} %merge.1), channel_id=1, replica_groups=mesh['y'=4,'z'=8,'xl'=2,'tp'=4] {'tp'}, dimensions={0} | all-to-all | bytes 524288 | tf_op jit(solution)/shard_map/all_to_all | solution.py:465
  177.0 0.0 copy-done.5
  177.0 2.2 copy-done.1
  179.2 1.7 layer_output.1.lay_ref
  180.9 1.6 collective-permute-start
  182.5 1.3 collective-permute-done.rim_ref
  183.8 1.9 copy-done.3
  185.7 1.3 short_project.1
  187.0 13.6 %all_to_all.55.q_ref = bf16[8,32,256]{2,1,0:T(8,128)(2,1)S(1)} all-to-all(bf16[8,32,256]{2,1,0:T(8,128)(2,1)S(1)} %get-tuple-element.11), channel_id=1, replica_groups=mesh['y'=4,'z'=8,'xl'=2,'tp'=4] {'z'}, dimensions={0} | all-to-all | bytes 262144 | tf_op jit(solution)/shard_map/all_to_all | solution.py:465
  200.6 9.7 %all_to_all.56.kv_ref = bf16[8,2,32,256]{3,2,1,0:T(8,128)(2,1)S(1)} all-to-all(bf16[8,2,32,256]{3,2,1,0:T(8,128)(2,1)S(1)} %get-tuple-element.12), channel_id=1, replica_groups=mesh['y'=4,'z'=8,'xl'=2,'tp'=4] {'y','xl'}, dimensions={0} | all-to-all | bytes 524288 | tf_op jit(solution)/shard_map/all_to_all | solution.py:465
  210.2 0.0 copy-done.6
  210.3 1.0 short_attend.1
  211.3 11.0 %all_to_all.57.parts_ref = bf16[8,32,384]{2,1,0:T(8,128)(2,1)S(1)} all-to-all(bf16[8,32,384]{2,1,0:T(8,128)(2,1)S(1)} %short_attend.1), channel_id=1, replica_groups=mesh['y'=4,'z'=8,'xl'=2,'tp'=4] {'z'}, dimensions={0} | all-to-all | bytes 393216 | tf_op jit(solution)/shard_map/all_to_all | solution.py:465
  222.3 1.0 short_merge.1
  223.3 9.1 %all-to-all-start.9 = ((bf16[4,32,256]{2,1,0:T(8,128)(2,1)}), bf16[4,32,256]{2,1,0:T(8,128)(2,1)S(1)}, u32[]{:S(2)}, u32[]{:S(2)}) async-start(bf16[4,32,256]{2,1,0:T(8,128)(2,1)} %short_merge.1), calls=%async_computation.9 | async-start | bytes 131072 | tf_op jit(solution)/shard_map/all_to_all | solution.py:465
  232.4 4.8 %all-to-all-done.9.att_ref = bf16[4,32,256]{2,1,0:T(8,128)(2,1)S(1)} async-done(((bf16[4,32,256]{2,1,0:T(8,128)(2,1)}), bf16[4,32,256]{2,1,0:T(8,128)(2,1)S(1)}, u32[]{:S(2)}, u32[]{:S(2)}) %all-to-all-start.9) | async-done | bytes 65568 | tf_op jit(solution)/shard_map/all_to_all | solution.py:465
  237.1 2.2 copy-done
  239.3 1.3 final_sum.1
  (10 shorter events, 0.0 us)
Async XLA Ops:
  6.5 170.4 %all-gather.3.cloned.1.call-start = ((), (), s32[]{:S(2)}) async-start(), calls=%async_computation.10 | async-start | bytes 5242880 | tf_op jit(solution)/shard_map/all_gather | solution.py:495
  7.3 56.0 %copy-start.8 = (bf16[256,256]{1,0:T(8,128)(2,1)S(1)}, bf16[256,256]{1,0:T(8,128)(2,1)}, u32[]{:S(2)}) copy-start(bf16[256,256]{1,0:T(8,128)(2,1)} %param.14) | copy-start | bytes 393220
  7.3 225.1 %all-gather.5.cloned.1.call-start = ((), (), s32[]{:S(2)}) async-start(), calls=%async_computation.11 | async-start | bytes 5242880 | tf_op jit(solution)/shard_map/all_gather | solution.py:496
  8.0 1.9 copy-start.2
  9.9 1.0 copy-start.4
  10.9 68.8 %copy-start.9 = (bf16[256,256]{1,0:T(8,128)(2,1)S(1)}, bf16[256,256]{1,0:T(8,128)(2,1)}, u32[]{:S(2)}) copy-start(bf16[256,256]{1,0:T(8,128)(2,1)} %param.15) | copy-start | bytes 393220
  37.0 48.7 %copy-start.10 = (u32[256]{0:T(256)S(1)}, u32[256]{0:T(256)}, u32[]{:S(2)}) copy-start(u32[256]{0:T(256)} %constant.22) | copy-start | bytes 3076
  37.0 88.7 %copy-start.7 = (f32[2]{0:T(128)S(1)}, f32[2]{0:T(128)}, u32[]{:S(2)}) copy-start(f32[2]{0:T(128)} %slope_ref.2) | copy-start | bytes 28
  80.8 44.9 %all-to-all-start.2 = ((bf16[8,256,256]{2,1,0:T(8,128)(2,1)}), bf16[8,256,256]{2,1,0:T(8,128)(2,1)}, u32[]{:S(2)}, u32[]{:S(2)}) async-start(bf16[8,256,256]{2,1,0:T(8,128)(2,1)} %broadcast_in_dim.5), calls=%async_computation.2 | async-start | bytes 2097152 | tf_op jit(solution)/shard_map/all_to_all | solution.py:465
  125.7 51.3 %copy-start.5 = (bf16[128,2048]{1,0:T(8,128)(2,1)S(1)}, bf16[128,2048]{1,0:T(8,128)(2,1)}, u32[]{:S(2)}) copy-start(bf16[128,2048]{1,0:T(8,128)(2,1)} %tok_ref.3) | copy-start | bytes 1572868
  177.0 2.2 copy-start.1
  179.2 31.1 %copy-start.6 = (f32[2]{0:T(128)S(1)}, f32[2]{0:T(128)}, u32[]{:S(2)}) copy-start(f32[2]{0:T(128)} %slope_ref.3) | copy-start | bytes 28
  180.9 2.9 %collective-permute-start = (bf16[16,2048]{1,0:T(8,128)(2,1)S(1)}, bf16[16,2048]{1,0:T(8,128)(2,1)S(1)}, u32[]{:S(2)}, u32[]{:S(2)}) collective-permute-start(bf16[16,2048]{1,0:T(8,128)(2,1)S(1)} %slice.4), channel_id=1, source_target_pairs={{0,4},{4,8},{8,12},{12,16},{16,20},{20,24},{24,28},{28,32},{32,36}... | collective-permute-start | bytes 196616 | tf_op jit(solution)/shard_map/ppermute | solution.py:508
  183.8 1.9 copy-start.3
  223.3 13.8 %all-to-all-start.9 = ((bf16[4,32,256]{2,1,0:T(8,128)(2,1)}), bf16[4,32,256]{2,1,0:T(8,128)(2,1)S(1)}, u32[]{:S(2)}, u32[]{:S(2)}) async-start(bf16[4,32,256]{2,1,0:T(8,128)(2,1)} %short_merge.1), calls=%async_computation.9 | async-start | bytes 131072 | tf_op jit(solution)/shard_map/all_to_all | solution.py:465
  237.1 2.2 copy-start
Sparse Core Ops, SparseCore 0:
  9.2 51.2 all-gather.2
  62.3 55.6 all-gather.4

commit v2 on v1

v2 whole, which is shorter than its diff:
```python
import functools
import math

import jax
import jax.numpy as jnp
from jax import lax
from jax.experimental import pallas as pl
from jax.experimental.pallas import tpu as pltpu
from jax.sharding import Mesh, PartitionSpec as P

HS = 128
GROUP = 4
NEG = -1e30
LOG2E = math.log2(math.e)
SCALE2 = HS ** -0.5 * LOG2E

VMEM = pltpu.VMEM
SMEM = pltpu.SMEM
F32 = jnp.float32
BF16 = jnp.bfloat16


def cost(flops, moved, trans=0):
    return pl.CostEstimate(flops=flops, bytes_accessed=moved, transcendentals=trans)


def params(mib):
    return pltpu.CompilerParams(vmem_limit_bytes=mib * 1024 * 1024)


def rms_scaled(values):
    inv = lax.rsqrt(jnp.mean(values * values, axis=-1, keepdims=True) + 1e-06)
    return (values * inv).astype(BF16)


def dot_t(a, b):
    return lax.dot_general(a, b, (((1,), (1,)), ((), ())), preferred_element_type=F32)


def three_parts(x):
    hi = x.astype(BF16).astype(F32)
    mid = (x - hi).astype(BF16).astype(F32)
    lo = (x - hi - mid).astype(BF16).astype(F32)
    return hi, mid, lo


def project_kernel(tok_ref, w_ref, q_ref, kv_ref, normed):
    step = pl.program_id(0)

    @pl.when(step == 0)
    def _():
        normed[...] = rms_scaled(tok_ref[...].astype(F32))

    out = jnp.dot(normed[...], w_ref[0], preferred_element_type=F32)
    store_projection(step, out, q_ref, kv_ref)


def store_projection(step, out, q_ref, kv_ref):
    @pl.when(step == 0)
    def _():
        q_ref[...] = (out * SCALE2).astype(BF16)

    @pl.when(step == 1)
    def _():
        kv_ref[0] = out.astype(BF16)

    @pl.when(step == 2)
    def _():
        kv_ref[1] = out.astype(BF16)


def project(rows, weight3):
    n, d = rows.shape
    width = weight3.shape[2]
    return pl.pallas_call(
        project_kernel,
        grid=(3,),
        in_specs=[
            pl.BlockSpec((n, d), lambda i: (0, 0)),
            pl.BlockSpec((1, d, width), lambda i: (i, 0, 0)),
        ],
        out_specs=[
            pl.BlockSpec((n, width), lambda i: (0, 0)),
            pl.BlockSpec((2, n, width), lambda i: (0, 0, 0)),
        ],
        out_shape=[
            jax.ShapeDtypeStruct((n, width), BF16),
            jax.ShapeDtypeStruct((2, n, width), BF16),
        ],
        scratch_shapes=[VMEM((n, d), BF16)],
        compiler_params=params(12),
        cost_estimate=cost(6 * n * d * width, 2 * (n * d + 3 * d * width)),
        name="project",
    )(rows, weight3)


def attend_kernel(blocks, cached, idx_ref, counts_ref, slope_ref, *refs):
    operands = 1 + max(b[0] for b in blocks)
    q_ref, refs = refs[0], refs[1:]
    key_refs, refs = refs[:operands], refs[operands:]
    if cached:
        acc_ref, stat_ref, prefix, bias = refs
    else:
        prior_acc, prior_stat, out_ref, bias = refs
    tile = pl.program_id(0)
    y, z, xl = idx_ref[0], idx_ref[1], idx_ref[2]
    _, nq, rows, width = q_ref.shape
    heads = width // HS
    size = key_refs[0].shape[1]
    owners = counts_ref.shape[0]

    def owner(back, other):
        side = 1 - xl if other else xl
        return ((y + 4 - back) % 4) * 16 + z * 2 + side

    @pl.when(tile == 0)
    def _():
        if cached:

            def one(i, total):
                prefix[i] = total
                return total + counts_ref[i]

            total = lax.fori_loop(0, owners, one, jnp.int32(0))
        place = lax.broadcasted_iota(jnp.int32, (1, size), 1)
        for j, (_, _, back, other) in enumerate(blocks):
            ctx = owner(back, other)
            if cached:
                pos = (place + (prefix[ctx] - total)).astype(F32)
            else:
                pos = (place + ctx * size).astype(F32)
            for h in range(heads):
                row = pos * (slope_ref[h] * LOG2E)
                if cached:
                    row = jnp.where(place < counts_ref[ctx], row, NEG)
                bias[h : h + 1, j * size : (j + 1) * size] = row

    total_rows = nq * rows
    zs = (z + 8 - 2 * tile) % 8
    row = lax.broadcasted_iota(jnp.int32, (total_rows, 1), 0)
    base = (y * 16 + xl) * rows
    row_pos = jnp.where(
        row < rows, base + zs * 2 * rows + row, base + (zs ^ 1) * 2 * rows + row - rows
    )
    place = lax.broadcasted_iota(jnp.int32, (1, size), 1)
    q_tile = q_ref[0].reshape(total_rows, width)
    odd = z % 2 == 1
    lane = lax.broadcasted_iota(jnp.int32, (total_rows, HS), 1)
    packed = jnp.zeros((total_rows, HS), F32)
    for h in range(heads):
        cols = slice(h * HS, (h + 1) * HS)
        q = q_tile[:, cols]
        scores = []
        for j, (ref, at, back, other) in enumerate(blocks):
            s = dot_t(q, key_refs[ref][at, :, cols])
            s = s + bias[h : h + 1, j * size : (j + 1) * size]
            if not cached:
                s = jnp.where(place + owner(back, other) * size <= row_pos, s, NEG)
            scores.append(s)
        top = jnp.max(functools.reduce(jnp.maximum, scores), axis=1, keepdims=True)
        if not cached:
            prior = prior_stat[:, h : h + 1]
            top = jnp.maximum(top, prior)
        both = jnp.zeros((total_rows, 2 * HS), F32)
        for s, (ref, at, _, _) in zip(scores, blocks):
            v = key_refs[ref][at + 1, :, cols]
            both = both + jnp.dot(
                jnp.exp2(s - top).astype(BF16),
                jnp.concatenate([v, jnp.ones_like(v)], axis=1),
                preferred_element_type=F32,
            )
        acc, weight_total = both[:, :HS], both[:, HS:]
        if cached:
            acc_ref[:, cols] = acc
            packed = jnp.where(lane == h, top, packed)
            packed = jnp.where(lane == heads + h, weight_total, packed)
            continue
        fade = jnp.exp2(prior - top)
        acc = acc + fade * prior_acc[:, cols]
        weight_total = weight_total + fade * prior_stat[:, heads + h : heads + h + 1]
        part = (acc / weight_total).astype(BF16)
        out_ref[0, :rows, cols] = jnp.where(odd, part[rows:], part[:rows])
        out_ref[1, :rows, cols] = jnp.where(odd, part[:rows], part[rows:])
        level = top + jnp.log2(weight_total)
        for k, piece in enumerate(three_parts(level)):
            packed = jnp.where(lane == 3 * h + k, piece, packed)
    if cached:
        stat_ref[...] = packed
        return
    first, second = packed[:rows], packed[rows:]
    for b, own in enumerate((jnp.where(odd, second, first), jnp.where(odd, first, second))):
        turned = jnp.transpose(own)[:16]
        out_ref[b, rows:, :] = jnp.concatenate([turned, jnp.zeros_like(turned)], axis=1).astype(
            BF16
        )


def attend(idx, counts, slopes, queries, blocks, keys, prior=None):
    _, nq, rows, width = queries.shape
    cached = prior is None
    size = keys[0].shape[1]
    nk = len(blocks) * size
    total = nq * rows
    whole = lambda a: pl.BlockSpec(a.shape, lambda i, *_: (0,) * a.ndim)
    scratch = []
    acc = jax.ShapeDtypeStruct((4 * total, width), F32)
    stat = jax.ShapeDtypeStruct((4 * total, HS), F32)
    state_specs = [
        pl.BlockSpec((total, width), lambda i, *_: (i, 0)),
        pl.BlockSpec((total, HS), lambda i, *_: (i, 0)),
    ]
    in_specs = [pl.BlockSpec((1, nq, rows, width), lambda i, *_: (i, 0, 0, 0))]
    in_specs += [whole(a) for a in keys]
    if cached:
        scratch.append(SMEM((counts.shape[0],), jnp.int32))
        out_specs, out_shape, prior = state_specs, [acc, stat], ()
    else:
        in_specs += state_specs
        out_specs = pl.BlockSpec(
            (nq, rows + 16, width), lambda i, idx, *_: ((idx[1] // 2 + 4 - i) % 4, 0, 0)
        )
        out_shape = jax.ShapeDtypeStruct((4 * nq, rows + 16, width), BF16)
    scratch.append(VMEM((8, nk), F32))
    return pl.pallas_call(
        functools.partial(attend_kernel, tuple(blocks), cached),
        grid_spec=pltpu.PrefetchScalarGridSpec(
            num_scalar_prefetch=3,
            grid=(4,),
            in_specs=in_specs,
            out_specs=out_specs,
            scratch_shapes=scratch,
        ),
        out_shape=out_shape,
        compiler_params=params(40),
        cost_estimate=cost(
            16 * total * nk * width, 4 * nk * width, 8 * total * nk * (width // HS)
        ),
        name="attend_cache" if cached else "attend_span",
    )(idx, counts, slopes, queries, *keys, *prior)


def merge_kernel(heads, parts_ref, out_ref):
    sources, padded, width = parts_ref.shape
    rows = padded - 16
    levels = jnp.concatenate(
        [parts_ref[s, rows:, :HS].astype(F32) for s in range(sources)], axis=0
    )
    turned = jnp.transpose(levels)
    for h in range(heads):
        cols = slice(h * HS, (h + 1) * HS)
        level = []
        for s in range(sources):
            at = s * 16 + 3 * h
            level.append(
                (turned[:, at : at + 1] + turned[:, at + 1 : at + 2]) + turned[:, at + 2 : at + 3]
            )
        top = functools.reduce(jnp.maximum, level)
        total = jnp.zeros((rows, 1), F32)
        acc = jnp.zeros((rows, HS), F32)
        for s in range(sources):
            weight = jnp.exp2(level[s] - top)
            total = total + weight
            acc = acc + weight * parts_ref[s, :rows, cols].astype(F32)
        out_ref[:, cols] = (acc / total).astype(BF16)


def merge(parts):
    sources, padded, width = parts.shape
    rows = padded - 16
    return pl.pallas_call(
        functools.partial(merge_kernel, width // HS),
        out_shape=jax.ShapeDtypeStruct((rows, width), BF16),
        compiler_params=params(16),
        cost_estimate=cost(4 * sources * rows * width, 2 * sources * padded * width),
        name="merge",
    )(parts)


def layer_kernel(tok_ref, *refs):
    parts = len(refs) // 2
    acc = tok_ref[...].astype(F32)
    for att, weight in zip(refs[:parts], refs[parts:-1]):
        acc = acc + jnp.dot(att[...], weight[...], preferred_element_type=F32)
    refs[-1][...] = acc.astype(BF16)


def layer_output(tokens, atts, weights):
    rows, d = tokens.shape
    step = 512
    inner, width = weights[0].shape[0], atts[0].shape[1]
    return pl.pallas_call(
        layer_kernel,
        grid=(d // step,),
        in_specs=[pl.BlockSpec((rows, step), lambda i: (0, i))]
        + [pl.BlockSpec((rows, width), lambda i: (0, 0))] * len(atts)
        + [pl.BlockSpec((inner, step), lambda i: (0, i))] * len(weights),
        out_specs=pl.BlockSpec((rows, step), lambda i: (0, i)),
        out_shape=jax.ShapeDtypeStruct((rows, d), BF16),
        compiler_params=params(16),
        cost_estimate=cost(8 * rows * d * inner, 8 * inner * d),
        name="layer_output",
    )(tokens, *atts, *weights)


def short_project_kernel(lay_ref, rim_ref, w_ref, q_ref, kv_ref, normed):
    step = pl.program_id(0)
    rows = lay_ref.shape[0]
    groups = rows // GROUP
    rim_rows = rim_ref.shape[0]

    @pl.when(step == 0)
    def _():
        g = lax.broadcasted_iota(jnp.int32, (groups, rows), 0) * GROUP
        t = lax.broadcasted_iota(jnp.int32, (groups, rows), 1)
        own = jnp.where((t <= g) & (t > g - GROUP), 1.0 / GROUP, 0.0).astype(BF16)
        g = lax.broadcasted_iota(jnp.int32, (groups, rim_rows), 0) * GROUP
        t = lax.broadcasted_iota(jnp.int32, (groups, rim_rows), 1) - rim_rows
        before = jnp.where(t > g - GROUP, 1.0 / GROUP, 0.0).astype(BF16)
        pooled = jnp.dot(own, lay_ref[...], preferred_element_type=F32) + jnp.dot(
            before, rim_ref[...], preferred_element_type=F32
        )
        normed[...] = rms_scaled(pooled.astype(BF16).astype(F32))

    out = jnp.dot(normed[...], w_ref[0], preferred_element_type=F32)

    store_projection(step, out, q_ref, kv_ref)


def short_project(layer, rim, weight3):
    n, d = layer.shape
    groups = n // GROUP
    width = weight3.shape[2]
    return pl.pallas_call(
        short_project_kernel,
        grid=(3,),
        in_specs=[
            pl.BlockSpec((n, d), lambda i: (0, 0)),
            pl.BlockSpec(rim.shape, lambda i: (0, 0)),
            pl.BlockSpec((1, d, width), lambda i: (i, 0, 0)),
        ],
        out_specs=[
            pl.BlockSpec((groups, width), lambda i: (0, 0)),
            pl.BlockSpec((2, groups, width), lambda i: (0, 0, 0)),
        ],
        out_shape=[
            jax.ShapeDtypeStruct((groups, width), BF16),
            jax.ShapeDtypeStruct((2, groups, width), BF16),
        ],
        scratch_shapes=[VMEM((groups, d), BF16)],
        compiler_params=params(16),
        cost_estimate=cost(6 * groups * d * width, 2 * (n * d + 3 * d * width)),
        name="short_project",
    )(layer, rim, weight3)


def short_attend_kernel(idx_ref, slope_ref, *refs):
    queries, key_refs, out_ref = refs[:4], refs[4:8], refs[8]
    y, z, xl = idx_ref[0], idx_ref[1], idx_ref[2]
    groups, width = queries[0].shape[1:]
    heads = width // HS
    nr = nk = 8 * groups
    row = lax.broadcasted_iota(jnp.int32, (nr, 1), 0)
    zs = row // groups
    row_pos = (y * 16 + zs * 2 + xl) * groups + row % groups
    back = (z // 2 + 4 - zs // 2) % 4
    came = (2 * back + (zs ^ z) % 2) * groups + row % groups
    order = jnp.where(lax.broadcasted_iota(jnp.int32, (nr, nr), 1) == came, 1.0, 0.0).astype(BF16)
    key = lax.broadcasted_iota(jnp.int32, (1, nk), 1)
    ys = (y + 4 - key // (2 * groups)) % 4
    side = jnp.where((key // groups) % 2 == 1, 1 - xl, xl)
    key_pos = (ys * 16 + z * 2 + side) * groups + key % groups
    usable = key_pos <= row_pos
    spot = key_pos.astype(F32)
    lane = lax.broadcasted_iota(jnp.int32, (nr, HS), 1)
    packed = jnp.zeros((nr, HS), F32)
    outs = []
    for h in range(heads):
        cols = slice(h * HS, (h + 1) * HS)
        q = jnp.concatenate([r[:, :, cols].reshape(2 * groups, HS) for r in queries], axis=0)
        q = jnp.dot(order, q, preferred_element_type=F32).astype(BF16)
        k = jnp.concatenate([r[:, 0, :, cols].reshape(2 * groups, HS) for r in key_refs], axis=0)
        v = jnp.concatenate([r[:, 1, :, cols].reshape(2 * groups, HS) for r in key_refs], axis=0)
        s = dot_t(q, k) + (slope_ref[h] * LOG2E) * spot
        s = jnp.where(usable, s, NEG)
        top = jnp.max(s, axis=1, keepdims=True)
        p = jnp.exp2(s - top).astype(BF16)
        both = jnp.dot(
            p, jnp.concatenate([v, jnp.ones_like(v)], axis=1), preferred_element_type=F32
        )
        weight_total = both[:, HS:]
        outs.append((both[:, :HS] / weight_total).astype(BF16))
        level = top + jnp.log2(weight_total)
        for k, piece in enumerate(three_parts(level)):
            packed = jnp.where(lane == 3 * h + k, piece, packed)
    out = jnp.concatenate(outs + [packed.astype(BF16)], axis=1)
    out_ref[...] = out.reshape(out_ref.shape)


def short_attend(idx, slopes, queries, keys):
    _, groups, width = queries[0].shape
    smem = pl.BlockSpec(memory_space=SMEM)
    vmem = pl.BlockSpec(memory_space=VMEM)
    n = 8 * groups
    return pl.pallas_call(
        short_attend_kernel,
        in_specs=[smem, smem] + [vmem] * 8,
        out_specs=vmem,
        out_shape=jax.ShapeDtypeStruct((8, groups, width + HS), BF16),
        compiler_params=params(16),
        cost_estimate=cost(4 * n * n * width, 8 * n * width),
        name="short_attend",
    )(idx, slopes, *queries, *keys)


def short_merge_kernel(heads, parts_ref, out_ref):
    sources, rows, padded = parts_ref.shape
    width = padded - HS
    for h in range(heads):
        cols = slice(h * HS, (h + 1) * HS)
        level = []
        for s in range(sources):
            lev = parts_ref[s, :, width:].astype(F32)
            level.append(
                (lev[:, 3 * h : 3 * h + 1] + lev[:, 3 * h + 1 : 3 * h + 2])
                + lev[:, 3 * h + 2 : 3 * h + 3]
            )
        top = functools.reduce(jnp.maximum, level)
        total = jnp.zeros((rows, 1), F32)
        acc = jnp.zeros((rows, HS), F32)
        for s in range(sources):
            weight = jnp.exp2(level[s] - top)
            total = total + weight
            acc = acc + weight * parts_ref[s, :, cols].astype(F32)
        out_ref[:, cols] = (acc / total).astype(BF16)


def short_merge(parts):
    sources, rows, padded = parts.shape
    width = padded - HS
    return pl.pallas_call(
        functools.partial(short_merge_kernel, width // HS),
        out_shape=jax.ShapeDtypeStruct((rows, width), BF16),
        compiler_params=params(16),
        cost_estimate=cost(4 * sources * rows * width, 2 * sources * rows * padded),
        name="short_merge",
    )(parts)


def final_kernel(tp_ref, lay_ref, *refs):
    parts = len(refs) // 2
    groups = refs[0].shape[0]
    rows = lay_ref.shape[0]
    t = lax.broadcasted_iota(jnp.int32, (rows, groups), 0) // GROUP
    g = lax.broadcasted_iota(jnp.int32, (rows, groups), 1)
    spread = jnp.where(t == g, 1.0, 0.0).astype(BF16)
    branch = jnp.zeros(lay_ref.shape, F32)
    for att, weight in zip(refs[:parts], refs[parts:-1]):
        lifted = jnp.dot(spread, att[...], preferred_element_type=F32).astype(BF16)
        branch = branch + jnp.dot(lifted, weight[...], preferred_element_type=F32)
    refs[-1][...] = (lay_ref[...].astype(F32) + branch).astype(BF16)


def final_sum(tp_index, layer, atts, weights):
    rows = layer.shape[0]
    inner, cols = weights[0].shape
    whole = lambda a: pl.BlockSpec(a.shape, lambda i, tp: (0, 0))
    return pl.pallas_call(
        final_kernel,
        grid_spec=pltpu.PrefetchScalarGridSpec(
            num_scalar_prefetch=1,
            grid=(1,),
            in_specs=[pl.BlockSpec((rows, cols), lambda i, tp: (0, tp[0]))]
            + [whole(a) for a in (*atts, *weights)],
            out_specs=pl.BlockSpec((rows, cols), lambda i, tp: (0, 0)),
        ),
        out_shape=jax.ShapeDtypeStruct((rows, cols), BF16),
        compiler_params=params(16),
        cost_estimate=cost(8 * rows * cols * inner, 8 * inner * cols),
        name="final_sum",
    )(tp_index, layer, *atts, *weights)


def exchange(blocks, axis):
    return lax.all_to_all(blocks, axis, 0, 0)


def swap(x, axis, flip=1):
    return lax.ppermute(x, axis, [(i, i ^ flip) for i in range(lax.axis_size(axis))])


def moved(x, axis, by):
    n = lax.axis_size(axis)
    return lax.ppermute(x, axis, [(i, (i + by) % n) for i in range(n)])


def round_tp(x):
    return [x] + [swap(x, "tp", flip) for flip in (1, 2, 3)]


def round_z(x):
    pair = jnp.stack([x, swap(x, "z")])
    return [pair] + [moved(pair, "z", by) for by in (2, 4, 6)]


def round_y(pair):
    half = pair.shape[0] // 2
    left, right = moved(pair, "y", 1), moved(pair, "y", -1)
    return [pair, left, right, moved(left[:half], "y", 1), moved(right[half:], "y", -1)]


KEY_BLOCKS = (
    (0, 0, 0, False),
    (0, 2, 0, True),
    (1, 0, 1, False),
    (1, 2, 1, True),
    (2, 0, 3, False),
    (2, 2, 3, True),
    (3, 0, 2, False),
    (4, 0, 2, True),
)


def after(x, *others):
    return lax.optimization_barrier((x, *others))[0]


def on_device(
    tokens,
    project_weight,
    output_weight,
    distance_slope,
    cache_keys,
    cache_values,
    cache_count,
    short_project_weight,
    short_output,
    short_slope,
):
    ctx_axes = ("y", "z", "xl")
    idx = jnp.stack([lax.axis_index("y"), lax.axis_index("z"), lax.axis_index("xl")]).astype(
        jnp.int32
    )
    tp = lax.axis_index("tp").astype(jnp.int32)

    own = [cache_keys, cache_values]
    counts = lax.all_gather(cache_count, ctx_axes, axis=0, tiled=True)
    cache = after(jnp.stack(own + [swap(a, "xl") for a in own]), counts)
    q, kv = project(tokens, jnp.transpose(project_weight, (1, 0, 2)))
    queries = jnp.stack(round_z(q))
    other_kv = swap(kv, "xl")
    cache_ring = round_y(cache)
    span_ring = round_y(after(jnp.concatenate([kv, other_kv], axis=0), cache_ring[1]))

    held = after(output_weight, other_kv)
    crossed = swap(held, "tp", 2)
    out_weights = [held, swap(held, "tp", 1), crossed, swap(crossed, "tp", 1)]
    width = short_output.shape[1] // 4
    late = after(short_output, crossed)
    short_weights = []
    for flip in range(4):
        piece = lax.dynamic_slice_in_dim(late, (tp ^ flip) * width, width, 1)
        short_weights.append(swap(piece, "tp", flip) if flip else piece)

    state = attend(idx, counts, distance_slope, queries, KEY_BLOCKS, cache_ring)
    parts = attend(idx, counts, distance_slope, queries, KEY_BLOCKS, span_ring, state)
    parts, *short_weights = lax.optimization_barrier((exchange(parts, "z"), *short_weights))
    atts = round_tp(merge(parts))
    layer = layer_output(tokens, atts, out_weights)

    n = lax.axis_size(ctx_axes)
    rim = lax.ppermute(layer[-16:], ctx_axes, [(i, i + 1) for i in range(n - 1)])
    sq, skv = short_project(layer, rim, jnp.transpose(short_project_weight, (1, 0, 2)))
    short_queries = round_z(sq)
    pair = jnp.stack([skv, swap(skv, "xl")])
    short_keys = [pair] + [moved(pair, "y", by) for by in (1, 2, 3)]
    sparts = short_attend(idx, short_slope, short_queries, short_keys)
    satts = round_tp(short_merge(exchange(sparts, "z")))
    return final_sum(tp.reshape(1), layer, satts, short_weights)


def solution(mesh):
    split = Mesh(mesh.devices.reshape(4, 8, 2, 4), ("y", "z", "xl", "tp"))
    ctx = ("y", "z", "xl")
    return jax.shard_map(
        on_device,
        mesh=split,
        in_specs=(
            P(ctx, None),
            P(None, None, "tp"),
            P("tp", None),
            P("tp"),
            P(ctx, "tp"),
            P(ctx, "tp"),
            P(ctx),
            P(None, None, "tp"),
            P("tp", None),
            P("tp"),
        ),
        out_specs=P(ctx, "tp"),
        check_vma=False,
    )
```

time: 248 us -> 184 us (0.74)
  blocking collectives: 176 us -> 34.3 us
  starting transfers between devices: 14.9 us -> 74.2 us
  waiting for transfers between devices: 7.49 us -> 28.9 us
  between operations: 14.2 us -> 0.94 us
  Pallas kernels: 22.8 us -> 28.2 us
  local copies, waits for them, and re-layouts: 11.6 us -> 14.2 us
    all_to_all x8 -> x1, blocking collectives: 138 us -> 12.6 us  [exchange(): return lax.all_to_all(blocks, axis, 0, 0)]
    ppermute x0 -> x35, starting transfers between devices: none -> 68.4 us  [the longest x18 40.2 us: swap(): lax.ppermute(x, axis, [(i, i ^ flip) for i in range(lax.axis_size(axis))])]
    ppermute x0 -> x35, waiting for transfers between devices: none -> 27.6 us  [the longest x18 21.3 us: swap(): lax.ppermute(x, axis, [(i, i ^ flip) for i in range(lax.axis_size(axis))])]
    unnamed x1, blocking collectives: 38.6 us -> 21.8 us
    all_to_all x2 -> x1, starting transfers between devices: 13.3 us -> 3.67 us  [exchange(): return lax.all_to_all(blocks, axis, 0, 0)]
    all_to_all x2 -> x1, waiting for transfers between devices: 4.77 us -> 0.01 us  [exchange(): return lax.all_to_all(blocks, axis, 0, 0)]
    pallas_call x6 -> x7, Pallas kernels: 19.8 us -> 23.7 us  [the longest x2 18.2 us: attend(): pl.pallas_call(functools.partial(attend_kernel, tuple(blocks), cached), g...]
    slice x0 -> x4, local copies, waits for them, and re-layouts: none -> 3.28 us  [the longest x2 1.65 us: round_y(): left[:half]]
  transfers between devices with their start and end apart: 5 -> 37, of which waited for: 2 -> 12; matrix products, arithmetic and copies ran while one was open for 1% -> 4% of each run, Pallas kernels for 9% -> 11%
where the time goes in v2:
time: 184 us; the launch traced here: 183 us
  starting transfers between devices  74.2 us (40%)
  blocking collectives  34.3 us (19%)
  waiting for transfers between devices  28.9 us (16%)
  Pallas kernels  28.2 us (15%)
  local copies, waits for them, and re-layouts  14.2 us (8%)
  other arithmetic  2.27 us (1%)
    ppermute x18, starting transfers between devices, swap(): lax.ppermute(x, axis, [(i, i ^ flip) for i in range(lax.axis_size(axis))])  40.2 us
    ppermute x17, starting transfers between devices, moved(): return lax.ppermute(x, axis, [(i, (i + by) % n) for i in range(n)])  28.2 us
    unnamed x1, blocking collectives  21.8 us
    ppermute x18, waiting for transfers between devices, swap(): lax.ppermute(x, axis, [(i, i ^ flip) for i in range(lax.axis_size(axis))])  21.3 us
    pallas_call x2, Pallas kernels, attend(): pl.pallas_call(functools.partial(attend_kernel, tuple(blocks), cached), g...  18.2 us
    all_to_all x1, blocking collectives, exchange(): return lax.all_to_all(blocks, axis, 0, 0)  12.6 us
    unnamed x41, local copies, waits for them, and re-layouts  9.6 us
    ppermute x17, waiting for transfers between devices, moved(): return lax.ppermute(x, axis, [(i, (i + by) % n) for i in range(n)])  6.25 us
  transfers between devices with their start and end apart: 37, of which 12 were waited for; matrix products, arithmetic and copies ran while one was open for 4% of the time, Pallas kernels for 11%

profile of v2, /device:TPU:1, one launch (start us, length us, event | category | flops | bytes accessed | tf_op | source)
XLA Modules:
  0.0 183.0 jit_solution(9446487916349235061)
XLA Ops:
  0.0 2.0 %collective-permute-start.5 = (bf16[256,256]{1,0:T(8,128)(2,1)}, bf16[256,256]{1,0:T(8,128)(2,1)S(1)}, u32[]{:S(2)}, u32[]{:S(2)}) collective-permute-start(bf16[256,256]{1,0:T(8,128)(2,1)} %param.14), channel_id=1, source_target_pairs={{0,4},{4,0},{1,5},{5,1},{2,6},{6,2},{3,7},{7,3},{8,12},{12,8},{9,1... | collective-permute-start | bytes 393224 | tf_op jit(solution)/shard_map/ppermute | solution.py:488
  2.8 1.3 dynamic-slice
  4.8 21.8 %all-reduce.counts_ref = s32[64]{0:T(128)S(1)} all-reduce(s32[64]{0:T(128)S(1)} %dynamic-update-slice), channel_id=1, replica_groups=mesh['y'=4,'z'=8,'xl'=2,'tp'=4] {'y','z','xl'}, use_global_device_ids=true, to_apply=%add | all-reduce | flops 64 | bytes 512
  27.8 1.9 %copy-done = bf16[2048,3,256]{2,0,1:T(8,128)(2,1)S(1)} copy-done((bf16[2048,3,256]{2,0,1:T(8,128)(2,1)S(1)}, bf16[2048,3,256]{2,0,1:T(8,128)(2,1)}, u32[]{:S(2)}) %copy-start) | copy-done | bytes 3145752
  29.6 1.0 copy-done.2
  30.7 1.2 project.1
  31.9 1.3 collective-permute-start.4
  33.2 2.7 %collective-permute-start.12 = (bf16[4,256,256]{2,1,0:T(8,128)(2,1)S(1)}, bf16[4,256,256]{2,1,0:T(8,128)(2,1)S(1)}, u32[]{:S(2)}, u32[]{:S(2)}) collective-permute-start(bf16[4,256,256]{2,1,0:T(8,128)(2,1)S(1)} %pad_maximum_fusion.1.refs_1_), channel_id=1, source_target_pairs={{0,192},{64,0},{128,64},{192,128},{1,193},{65,1},{129,65},{193,129... | collective-permute-start | bytes 1572872 | tf_op jit(solution)/shard_map/ppermute | solution.py:493
  35.9 2.7 %collective-permute-start.15 = (bf16[256,2048]{1,0:T(8,128)(2,1)S(1)}, bf16[256,2048]{1,0:T(8,128)(2,1)S(1)}, u32[]{:S(2)}, u32[]{:S(2)}) collective-permute-start(bf16[256,2048]{1,0:T(8,128)(2,1)S(1)} %copy-done.4), channel_id=1, source_target_pairs={{0,2},{1,3},{2,0},{3,1},{4,6},{5,7},{6,4},{7,5},{8,10},{9,11},{10,... | collective-permute-start | bytes 3145736 | tf_op jit(solution)/shard_map/ppermute | solution.py:488
  39.3 2.7 %collective-permute-done = bf16[128,256]{1,0:T(8,128)(2,1)S(1)} collective-permute-done((bf16[128,256]{1,0:T(8,128)(2,1)S(1)}, bf16[128,256]{1,0:T(8,128)(2,1)S(1)}, u32[]{:S(2)}, u32[]{:S(2)}) %collective-permute-start) | collective-permute-done | bytes 65568 | tf_op jit(solution)/shard_map/ppermute | solution.py:488
  42.0 1.2 collective-permute-start.2
  43.3 3.5 %collective-permute-start.3 = (bf16[2,128,256]{2,1,0:T(8,128)(2,1)S(1)}, bf16[2,128,256]{2,1,0:T(8,128)(2,1)S(1)}, u32[]{:S(2)}, u32[]{:S(2)}) collective-permute-start(bf16[2,128,256]{2,1,0:T(8,128)(2,1)S(1)} %get-tuple-element.40), channel_id=1, source_target_pairs={{0,48},{8,56},{16,0},{24,8},{32,16},{40,24},{48,32},{56,40},{1,49}... | collective-permute-start | bytes 393224 | tf_op jit(solution)/shard_map/ppermute | solution.py:493
  47.6 3.0 %collective-permute-start.9 = (bf16[4,128,256]{2,1,0:T(8,128)(2,1)S(1)}, bf16[4,128,256]{2,1,0:T(8,128)(2,1)}, u32[]{:S(2)}, u32[]{:S(2)}) collective-permute-start(bf16[4,128,256]{2,1,0:T(8,128)(2,1)S(1)} %pad_maximum_fusion.2.refs_1_), channel_id=1, source_target_pairs={{0,192},{64,0},{128,64},{192,128},{1,193},{65,1},{129,65},{193,129... | collective-permute-start | bytes 786440 | tf_op jit(solution)/shard_map/ppermute | solution.py:493
  51.3 2.6 %collective-permute-done.1 = bf16[2,128,256]{2,1,0:T(8,128)(2,1)S(1)} collective-permute-done((bf16[2,128,256]{2,1,0:T(8,128)(2,1)S(1)}, bf16[2,128,256]{2,1,0:T(8,128)(2,1)S(1)}, u32[]{:S(2)}, u32[]{:S(2)}) %collective-permute-start.1) | collective-permute-done | bytes 131104 | tf_op jit(solution)/shard_map/ppermute | solution.py:493
  53.9 3.0 %collective-permute-start.14 = (bf16[2,256,256]{2,1,0:T(8,128)(2,1)}, bf16[2,256,256]{2,1,0:T(8,128)(2,1)}, u32[]{:S(2)}, u32[]{:S(2)}) collective-permute-start(bf16[2,256,256]{2,1,0:T(8,128)(2,1)} %slice.23), channel_id=1, source_target_pairs={{0,192},{64,0},{128,64},{192,128},{1,193},{65,1},{129,65},{193,129... | collective-permute-start | bytes 786440 | tf_op jit(solution)/shard_map/ppermute | solution.py:493
  57.6 1.1 pad_maximum_fusion.refs_0_
  59.6 2.8 %collective-permute-start.11 = (bf16[2,128,256]{2,1,0:T(8,128)(2,1)S(1)}, bf16[2,128,256]{2,1,0:T(8,128)(2,1)S(1)}, u32[]{:S(2)}, u32[]{:S(2)}) collective-permute-start(bf16[2,128,256]{2,1,0:T(8,128)(2,1)S(1)} %slice.21), channel_id=1, source_target_pairs={{0,192},{64,0},{128,64},{192,128},{1,193},{65,1},{129,65},{193,129... | collective-permute-start | bytes 393224 | tf_op jit(solution)/shard_map/ppermute | solution.py:493
  64.5 1.0 copy-done.13
  65.5 10.2 %attend_cache.1 = (f32[1024,256]{1,0:T(8,128)S(1)}, f32[1024,128]{1,0:T(8,128)S(1)}) custom-call(s32[3]{0:T(128)S(1)} %pad_add_fusion.idx_ref, s32[64]{0:T(128)S(1)} %all-reduce.counts_ref, f32[2]{0:T(128)S(1)} %copy-done.15, bf16[4,2,128,256]{3,2,1,0:T(8,128)(2,1)S(1)} %pad_maximum_fusion.refs_0_, bf16[4,256,256]{2,1,0:T(8,128)(2,1)S(1)} %pad_maximum_fusion.1.refs_1_, ...), custom_call_target="tpu_custom_call" | custom-call | flops 2147483648 | bytes 2097152 | tf_op jit(solution)/shard_map/attend_cache/pallas_call | solution.py:224
  75.7 8.0 %attend_span.1 = bf16[8,144,256]{2,1,0:T(8,128)(2,1)S(1)} custom-call(s32[3]{0:T(128)S(1)} %pad_add_fusion.idx_ref, s32[64]{0:T(128)S(1)} %all-reduce.counts_ref, f32[2]{0:T(128)S(1)} %copy-done.15, bf16[4,2,128,256]{3,2,1,0:T(8,128)(2,1)S(1)} %pad_maximum_fusion.refs_0_, bf16[4,128,256]{2,1,0:T(8,128)(2,1)S(1)} %pad_maximum_fusion.2.refs_1_, ...), custom_call_target="tpu_custom_call" | custom-call | flops 1073741824 | bytes 1048576 | tf_op jit(solution)/shard_map/attend_span/pallas_call | solution.py:224
  84.6 3.7 %all-to-all-start = ((bf16[8,144,256]{2,1,0:T(8,128)(2,1)}), bf16[8,144,256]{2,1,0:T(8,128)(2,1)S(1)}, u32[]{:S(2)}, u32[]{:S(2)}) async-start(bf16[8,144,256]{2,1,0:T(8,128)(2,1)} %copy-done.5), calls=%async_computation | async-start | bytes 1179648 | tf_op jit(solution)/shard_map/all_to_all | solution.py:484
  88.3 12.4 %collective-permute-start.22 = (bf16[256,2048]{1,0:T(8,128)(2,1)S(1)}, bf16[256,2048]{1,0:T(8,128)(2,1)}, u32[]{:S(2)}, u32[]{:S(2)}) collective-permute-start(bf16[256,2048]{1,0:T(8,128)(2,1)S(1)} %copy-done.4), channel_id=1, source_target_pairs={{0,1},{1,0},{2,3},{3,2},{4,5},{5,4},{6,7},{7,6},{8,9},{9,8},{10,11... | collective-permute-start | bytes 3145736 | tf_op jit(solution)/shard_map/ppermute | solution.py:488
  100.8 1.3 constant_dynamic-slice_fusion
  102.7 2.8 %collective-permute-start.17 = (bf16[256,512]{1,0:T(8,128)(2,1)S(1)}, bf16[256,512]{1,0:T(8,128)(2,1)S(1)}, u32[]{:S(2)}, u32[]{:S(2)}) collective-permute-start(bf16[256,512]{1,0:T(8,128)(2,1)S(1)} %get-tuple-element.36), channel_id=1, source_target_pairs={{0,2},{1,3},{2,0},{3,1},{4,6},{5,7},{6,4},{7,5},{8,10},{9,11},{10,... | collective-permute-start | bytes 786440 | tf_op jit(solution)/shard_map/ppermute | solution.py:488
  105.8 6.5 %collective-permute-done.18.refs_7_ = bf16[256,512]{1,0:T(8,128)(2,1)S(1)} collective-permute-done((bf16[256,512]{1,0:T(8,128)(2,1)S(1)}, bf16[256,512]{1,0:T(8,128)(2,1)S(1)}, u32[]{:S(2)}, u32[]{:S(2)}) %collective-permute-start.18) | collective-permute-done | bytes 262176 | tf_op jit(solution)/shard_map/ppermute | solution.py:488
  113.0 4.7 %collective-permute-done.17.refs_6_ = bf16[256,512]{1,0:T(8,128)(2,1)S(1)} collective-permute-done((bf16[256,512]{1,0:T(8,128)(2,1)S(1)}, bf16[256,512]{1,0:T(8,128)(2,1)S(1)}, u32[]{:S(2)}, u32[]{:S(2)}) %collective-permute-start.17) | collective-permute-done | bytes 262176 | tf_op jit(solution)/shard_map/ppermute | solution.py:488
  119.1 1.2 merge.1.refs_0_
  121.2 2.7 %collective-permute-start.20 = (bf16[128,256]{1,0:T(8,128)(2,1)S(1)}, bf16[128,256]{1,0:T(8,128)(2,1)S(1)}, u32[]{:S(2)}, u32[]{:S(2)}) collective-permute-start(bf16[128,256]{1,0:T(8,128)(2,1)S(1)} %merge.1.refs_0_), channel_id=1, source_target_pairs={{0,2},{1,3},{2,0},{3,1},{4,6},{5,7},{6,4},{7,5},{8,10},{9,11},{10,... | collective-permute-start | bytes 196616 | tf_op jit(solution)/shard_map/ppermute | solution.py:488
  124.0 2.5 %collective-permute-done.21.refs_3_ = bf16[128,256]{1,0:T(8,128)(2,1)S(1)} collective-permute-done((bf16[128,256]{1,0:T(8,128)(2,1)S(1)}, bf16[128,256]{1,0:T(8,128)(2,1)S(1)}, u32[]{:S(2)}, u32[]{:S(2)}) %collective-permute-start.21) | collective-permute-done | bytes 65568 | tf_op jit(solution)/shard_map/ppermute | solution.py:488
  126.6 1.4 collective-permute-done.20.refs_2_
  128.0 3.2 %layer_output.1.lay_ref = bf16[128,2048]{1,0:T(8,128)(2,1)S(1)} custom-call(bf16[128,2048]{1,0:T(8,128)(2,1)S(1)} %copy-done.3, bf16[128,256]{1,0:T(8,128)(2,1)S(1)} %merge.1.refs_0_, bf16[128,256]{1,0:T(8,128)(2,1)S(1)} %collective-permute-done.19.refs_1_, bf16[128,256]{1,0:T(8,128)(2,1)S(1)} %collective-permute-done.20.refs_2_, ...), custom_call_target="tpu_custom_call" | custom-call | flops 536870912 | bytes 4194304 | tf_op jit(solution)/shard_map/layer_output/pallas_call | solution.py:291
  131.3 2.1 %collective-permute-start.24 = (bf16[16,2048]{1,0:T(8,128)(2,1)S(1)}, bf16[16,2048]{1,0:T(8,128)(2,1)S(1)}, u32[]{:S(2)}, u32[]{:S(2)}) collective-permute-start(bf16[16,2048]{1,0:T(8,128)(2,1)S(1)} %slice.24), channel_id=1, source_target_pairs={{0,4},{4,8},{8,12},{12,16},{16,20},{20,24},{24,28},{28,32},{32,36}... | collective-permute-start | bytes 196616 | tf_op jit(solution)/shard_map/ppermute | solution.py:571
  133.4 1.3 collective-permute-done.24.rim_ref
  134.7 1.2 short_project.1
  135.9 4.4 %collective-permute-start.25 = (bf16[32,256]{1,0:T(8,128)(2,1)S(1)}, bf16[32,256]{1,0:T(8,128)(2,1)S(1)}, u32[]{:S(2)}, u32[]{:S(2)}) collective-permute-start(bf16[32,256]{1,0:T(8,128)(2,1)S(1)} %get-tuple-element.29), channel_id=1, source_target_pairs={{0,8},{8,0},{16,24},{24,16},{32,40},{40,32},{48,56},{56,48},{1,9},... | collective-permute-start | bytes 49160 | tf_op jit(solution)/shard_map/ppermute | solution.py:488
  140.3 1.1 collective-permute-done.25
  141.4 3.6 %collective-permute-start.28 = (bf16[2,32,256]{2,1,0:T(8,128)(2,1)S(1)}, bf16[2,32,256]{2,1,0:T(8,128)(2,1)S(1)}, u32[]{:S(2)}, u32[]{:S(2)}) collective-permute-start(bf16[2,32,256]{2,1,0:T(8,128)(2,1)S(1)} %pad_maximum_fusion.5.refs_0_), channel_id=1, source_target_pairs={{0,48},{8,56},{16,0},{24,8},{32,16},{40,24},{48,32},{56,40},{1,49}... | collective-permute-start | bytes 98312 | tf_op jit(solution)/shard_map/ppermute | solution.py:493
  145.0 2.0 %collective-permute-start.32 = (bf16[2,2,32,256]{3,2,1,0:T(8,128)(2,1)S(1)}, bf16[2,2,32,256]{3,2,1,0:T(8,128)(2,1)S(1)}, u32[]{:S(2)}, u32[]{:S(2)}) collective-permute-start(bf16[2,2,32,256]{3,2,1,0:T(8,128)(2,1)S(1)} %pad_maximum_fusion.4.refs_4_), channel_id=1, source_target_pairs={{0,192},{64,0},{128,64},{192,128},{1,193},{65,1},{129,65},{193,129... | collective-permute-start | bytes 196616 | tf_op jit(solution)/shard_map/ppermute | solution.py:493
  147.6 3.3 %collective-permute-start.27 = (bf16[2,32,256]{2,1,0:T(8,128)(2,1)S(1)}, bf16[2,32,256]{2,1,0:T(8,128)(2,1)S(1)}, u32[]{:S(2)}, u32[]{:S(2)}) collective-permute-start(bf16[2,32,256]{2,1,0:T(8,128)(2,1)S(1)} %pad_maximum_fusion.5.refs_0_), channel_id=1, source_target_pairs={{0,32},{8,40},{16,48},{24,56},{32,0},{40,8},{48,16},{56,24},{1,33}... | collective-permute-start | bytes 98312 | tf_op jit(solution)/shard_map/ppermute | solution.py:493
  150.9 2.1 %collective-permute-start.26 = (bf16[2,32,256]{2,1,0:T(8,128)(2,1)S(1)}, bf16[2,32,256]{2,1,0:T(8,128)(2,1)S(1)}, u32[]{:S(2)}, u32[]{:S(2)}) collective-permute-start(bf16[2,32,256]{2,1,0:T(8,128)(2,1)S(1)} %pad_maximum_fusion.5.refs_0_), channel_id=1, source_target_pairs={{0,16},{8,24},{16,32},{24,40},{32,48},{40,56},{48,0},{56,8},{1,17}... | collective-permute-start | bytes 98312 | tf_op jit(solution)/shard_map/ppermute | solution.py:493
  153.0 1.3 collective-permute-done.27.refs_2_
  154.3 1.5 collective-permute-done.26.refs_1_
  155.8 1.4 short_attend.1
  157.3 12.6 %all_to_all.10.parts_ref = bf16[8,32,384]{2,1,0:T(8,128)(2,1)S(1)} all-to-all(bf16[8,32,384]{2,1,0:T(8,128)(2,1)S(1)} %short_attend.1), channel_id=1, replica_groups=mesh['y'=4,'z'=8,'xl'=2,'tp'=4] {'z'}, dimensions={0} | all-to-all | bytes 393216 | tf_op jit(solution)/shard_map/all_to_all | solution.py:484
  170.2 7.4 %collective-permute-start.35 = (bf16[32,256]{1,0:T(8,128)(2,1)S(1)}, bf16[32,256]{1,0:T(8,128)(2,1)S(1)}, u32[]{:S(2)}, u32[]{:S(2)}) collective-permute-start(bf16[32,256]{1,0:T(8,128)(2,1)S(1)} %short_merge.1.refs_0_), channel_id=1, source_target_pairs={{0,3},{1,2},{2,1},{3,0},{4,7},{5,6},{6,5},{7,4},{8,11},{9,10},{10,... | collective-permute-start | bytes 49160 | tf_op jit(solution)/shard_map/ppermute | solution.py:488
  177.5 1.7 collective-permute-start.34
  179.2 2.4 %collective-permute-done.34.refs_2_ = bf16[32,256]{1,0:T(8,128)(2,1)S(1)} collective-permute-done((bf16[32,256]{1,0:T(8,128)(2,1)S(1)}, bf16[32,256]{1,0:T(8,128)(2,1)S(1)}, u32[]{:S(2)}, u32[]{:S(2)}) %collective-permute-start.34) | collective-permute-done | bytes 16416 | tf_op jit(solution)/shard_map/ppermute | solution.py:488
  181.7 1.3 final_sum.1
  (91 shorter events, 14.2 us)
Async XLA Ops:
  0.0 35.9 %copy-start.4 = (bf16[256,2048]{1,0:T(8,128)(2,1)S(1)}, bf16[256,2048]{1,0:T(8,128)(2,1)}, u32[]{:S(2)}) copy-start(bf16[256,2048]{1,0:T(8,128)(2,1)} %refs_4_) | copy-start | bytes 3145732
  0.0 26.6 %collective-permute-start.5 = (bf16[256,256]{1,0:T(8,128)(2,1)}, bf16[256,256]{1,0:T(8,128)(2,1)S(1)}, u32[]{:S(2)}, u32[]{:S(2)}) collective-permute-start(bf16[256,256]{1,0:T(8,128)(2,1)} %param.14), channel_id=1, source_target_pairs={{0,4},{4,0},{1,5},{5,1},{2,6},{6,2},{3,7},{7,3},{8,12},{12,8},{9,1... | collective-permute-start | bytes 393224 | tf_op jit(solution)/shard_map/ppermute | solution.py:488
  2.0 24.6 %collective-permute-start.6 = (bf16[256,256]{1,0:T(8,128)(2,1)}, bf16[256,256]{1,0:T(8,128)(2,1)S(1)}, u32[]{:S(2)}, u32[]{:S(2)}) collective-permute-start(bf16[256,256]{1,0:T(8,128)(2,1)} %param.15), channel_id=1, source_target_pairs={{0,4},{4,0},{1,5},{5,1},{2,6},{6,2},{3,7},{7,3},{8,12},{12,8},{9,1... | collective-permute-start | bytes 393224 | tf_op jit(solution)/shard_map/ppermute | solution.py:488
  27.6 15.7 %collective-permute-start.7 = (bf16[4,256,256]{2,1,0:T(8,128)(2,1)S(1)}, bf16[4,256,256]{2,1,0:T(8,128)(2,1)S(1)}, u32[]{:S(2)}, u32[]{:S(2)}) collective-permute-start(bf16[4,256,256]{2,1,0:T(8,128)(2,1)S(1)} %pad_maximum_fusion.1.refs_1_), channel_id=1, source_target_pairs={{0,64},{64,128},{128,192},{192,0},{1,65},{65,129},{129,193},{193,1... | collective-permute-start | bytes 1572872 | tf_op jit(solution)/shard_map/ppermute | solution.py:493
  30.7 33.8 %copy-start.15 = (f32[2]{0:T(128)S(1)}, f32[2]{0:T(128)}, u32[]{:S(2)}) copy-start(f32[2]{0:T(128)} %slope_ref.4) | copy-start | bytes 28
  31.9 4.0 %collective-permute-start.4 = (bf16[2,128,256]{2,1,0:T(8,128)(2,1)S(1)}, bf16[2,128,256]{2,1,0:T(8,128)(2,1)S(1)}, u32[]{:S(2)}, u32[]{:S(2)}) collective-permute-start(bf16[2,128,256]{2,1,0:T(8,128)(2,1)S(1)} %get-tuple-element.21), channel_id=1, source_target_pairs={{0,4},{4,0},{1,5},{5,1},{2,6},{6,2},{3,7},{7,3},{8,12},{12,8},{9,1... | collective-permute-start | bytes 393224 | tf_op jit(solution)/shard_map/ppermute | solution.py:488
  33.2 14.4 %collective-permute-start.12 = (bf16[4,256,256]{2,1,0:T(8,128)(2,1)S(1)}, bf16[4,256,256]{2,1,0:T(8,128)(2,1)S(1)}, u32[]{:S(2)}, u32[]{:S(2)}) collective-permute-start(bf16[4,256,256]{2,1,0:T(8,128)(2,1)S(1)} %pad_maximum_fusion.1.refs_1_), channel_id=1, source_target_pairs={{0,192},{64,0},{128,64},{192,128},{1,193},{65,1},{129,65},{193,129... | collective-permute-start | bytes 1572872 | tf_op jit(solution)/shard_map/ppermute | solution.py:493
  35.9 64.8 %collective-permute-start.15 = (bf16[256,2048]{1,0:T(8,128)(2,1)S(1)}, bf16[256,2048]{1,0:T(8,128)(2,1)S(1)}, u32[]{:S(2)}, u32[]{:S(2)}) collective-permute-start(bf16[256,2048]{1,0:T(8,128)(2,1)S(1)} %copy-done.4), channel_id=1, source_target_pairs={{0,2},{1,3},{2,0},{3,1},{4,6},{5,7},{6,4},{7,5},{8,10},{9,11},{10,... | collective-permute-start | bytes 3145736 | tf_op jit(solution)/shard_map/ppermute | solution.py:488
  38.6 3.4 %collective-permute-start = (bf16[128,256]{1,0:T(8,128)(2,1)S(1)}, bf16[128,256]{1,0:T(8,128)(2,1)S(1)}, u32[]{:S(2)}, u32[]{:S(2)}) collective-permute-start(bf16[128,256]{1,0:T(8,128)(2,1)S(1)} %get-tuple-element.20), channel_id=1, source_target_pairs={{0,8},{8,0},{16,24},{24,16},{32,40},{40,32},{48,56},{56,48},{1,9},... | collective-permute-start | bytes 196616 | tf_op jit(solution)/shard_map/ppermute | solution.py:488
  42.0 9.3 %collective-permute-start.2 = (bf16[2,128,256]{2,1,0:T(8,128)(2,1)S(1)}, bf16[2,128,256]{2,1,0:T(8,128)(2,1)S(1)}, u32[]{:S(2)}, u32[]{:S(2)}) collective-permute-start(bf16[2,128,256]{2,1,0:T(8,128)(2,1)S(1)} %get-tuple-element.40), channel_id=1, source_target_pairs={{0,32},{8,40},{16,48},{24,56},{32,0},{40,8},{48,16},{56,24},{1,33}... | collective-permute-start | bytes 393224 | tf_op jit(solution)/shard_map/ppermute | solution.py:493
  43.2 10.7 %collective-permute-start.1 = (bf16[2,128,256]{2,1,0:T(8,128)(2,1)S(1)}, bf16[2,128,256]{2,1,0:T(8,128)(2,1)S(1)}, u32[]{:S(2)}, u32[]{:S(2)}) collective-permute-start(bf16[2,128,256]{2,1,0:T(8,128)(2,1)S(1)} %get-tuple-element.40), channel_id=1, source_target_pairs={{0,16},{8,24},{16,32},{24,40},{32,48},{40,56},{48,0},{56,8},{1,17}... | collective-permute-start | bytes 393224 | tf_op jit(solution)/shard_map/ppermute | solution.py:493
  43.3 13.5 %collective-permute-start.3 = (bf16[2,128,256]{2,1,0:T(8,128)(2,1)S(1)}, bf16[2,128,256]{2,1,0:T(8,128)(2,1)S(1)}, u32[]{:S(2)}, u32[]{:S(2)}) collective-permute-start(bf16[2,128,256]{2,1,0:T(8,128)(2,1)S(1)} %get-tuple-element.40), channel_id=1, source_target_pairs={{0,48},{8,56},{16,0},{24,8},{32,16},{40,24},{48,32},{56,40},{1,49}... | collective-permute-start | bytes 393224 | tf_op jit(solution)/shard_map/ppermute | solution.py:493
  47.6 3.7 %copy-start.12 = (bf16[4,256,256]{2,1,0:T(8,128)(2,1)}, bf16[4,256,256]{2,1,0:T(8,128)(2,1)S(1)}, u32[]{:S(2)}) copy-start(bf16[4,256,256]{2,1,0:T(8,128)(2,1)S(1)} %collective-permute-done.12.refs_3_) | copy-start | bytes 1572868
  47.6 11.1 %collective-permute-start.9 = (bf16[4,128,256]{2,1,0:T(8,128)(2,1)S(1)}, bf16[4,128,256]{2,1,0:T(8,128)(2,1)}, u32[]{:S(2)}, u32[]{:S(2)}) collective-permute-start(bf16[4,128,256]{2,1,0:T(8,128)(2,1)S(1)} %pad_maximum_fusion.2.refs_1_), channel_id=1, source_target_pairs={{0,192},{64,0},{128,64},{192,128},{1,193},{65,1},{129,65},{193,129... | collective-permute-start | bytes 786440 | tf_op jit(solution)/shard_map/ppermute | solution.py:493
  51.3 5.6 %copy-start.16 = (bf16[2,128,256]{2,1,0:T(8,128)(2,1)}, bf16[2,128,256]{2,1,0:T(8,128)(2,1)S(1)}, u32[]{:S(2)}) copy-start(bf16[2,128,256]{2,1,0:T(8,128)(2,1)S(1)} %collective-permute-done.2) | copy-start | bytes 393220
  51.3 11.1 %collective-permute-start.8 = (bf16[4,128,256]{2,1,0:T(8,128)(2,1)S(1)}, bf16[4,128,256]{2,1,0:T(8,128)(2,1)}, u32[]{:S(2)}, u32[]{:S(2)}) collective-permute-start(bf16[4,128,256]{2,1,0:T(8,128)(2,1)S(1)} %pad_maximum_fusion.2.refs_1_), channel_id=1, source_target_pairs={{0,64},{64,128},{128,192},{192,0},{1,65},{65,129},{129,193},{193,1... | collective-permute-start | bytes 786440 | tf_op jit(solution)/shard_map/ppermute | solution.py:493
  53.9 3.0 %copy-start.17 = (bf16[2,128,256]{2,1,0:T(8,128)(2,1)}, bf16[2,128,256]{2,1,0:T(8,128)(2,1)S(1)}, u32[]{:S(2)}) copy-start(bf16[2,128,256]{2,1,0:T(8,128)(2,1)S(1)} %collective-permute-done.1) | copy-start | bytes 393220
  53.9 9.7 %collective-permute-start.14 = (bf16[2,256,256]{2,1,0:T(8,128)(2,1)}, bf16[2,256,256]{2,1,0:T(8,128)(2,1)}, u32[]{:S(2)}, u32[]{:S(2)}) collective-permute-start(bf16[2,256,256]{2,1,0:T(8,128)(2,1)} %slice.23), channel_id=1, source_target_pairs={{0,192},{64,0},{128,64},{192,128},{1,193},{65,1},{129,65},{193,129... | collective-permute-start | bytes 786440 | tf_op jit(solution)/shard_map/ppermute | solution.py:493
  57.5 6.9 %collective-permute-start.13 = (bf16[2,256,256]{2,1,0:T(8,128)(2,1)}, bf16[2,256,256]{2,1,0:T(8,128)(2,1)}, u32[]{:S(2)}, u32[]{:S(2)}) collective-permute-start(bf16[2,256,256]{2,1,0:T(8,128)(2,1)} %slice.22), channel_id=1, source_target_pairs={{0,64},{64,128},{128,192},{192,0},{1,65},{65,129},{129,193},{193,1... | collective-permute-start | bytes 786440 | tf_op jit(solution)/shard_map/ppermute | solution.py:493
  59.6 16.1 %collective-permute-start.11 = (bf16[2,128,256]{2,1,0:T(8,128)(2,1)S(1)}, bf16[2,128,256]{2,1,0:T(8,128)(2,1)S(1)}, u32[]{:S(2)}, u32[]{:S(2)}) collective-permute-start(bf16[2,128,256]{2,1,0:T(8,128)(2,1)S(1)} %slice.21), channel_id=1, source_target_pairs={{0,192},{64,0},{128,64},{192,128},{1,193},{65,1},{129,65},{193,129... | collective-permute-start | bytes 393224 | tf_op jit(solution)/shard_map/ppermute | solution.py:493
  63.3 12.4 %collective-permute-start.10 = (bf16[2,128,256]{2,1,0:T(8,128)(2,1)S(1)}, bf16[2,128,256]{2,1,0:T(8,128)(2,1)S(1)}, u32[]{:S(2)}, u32[]{:S(2)}) collective-permute-start(bf16[2,128,256]{2,1,0:T(8,128)(2,1)S(1)} %slice.20), channel_id=1, source_target_pairs={{0,64},{64,128},{128,192},{192,0},{1,65},{65,129},{129,193},{193,1... | collective-permute-start | bytes 393224 | tf_op jit(solution)/shard_map/ppermute | solution.py:493
  84.6 43.4 %copy-start.3 = (bf16[128,2048]{1,0:T(8,128)(2,1)S(1)}, bf16[128,2048]{1,0:T(8,128)(2,1)}, u32[]{:S(2)}) copy-start(bf16[128,2048]{1,0:T(8,128)(2,1)} %tok_ref.3) | copy-start | bytes 1572868
  84.6 34.5 %all-to-all-start = ((bf16[8,144,256]{2,1,0:T(8,128)(2,1)}), bf16[8,144,256]{2,1,0:T(8,128)(2,1)S(1)}, u32[]{:S(2)}, u32[]{:S(2)}) async-start(bf16[8,144,256]{2,1,0:T(8,128)(2,1)} %copy-done.5), calls=%async_computation | async-start | bytes 1179648 | tf_op jit(solution)/shard_map/all_to_all | solution.py:484
  88.3 35.8 %collective-permute-start.22 = (bf16[256,2048]{1,0:T(8,128)(2,1)S(1)}, bf16[256,2048]{1,0:T(8,128)(2,1)}, u32[]{:S(2)}, u32[]{:S(2)}) collective-permute-start(bf16[256,2048]{1,0:T(8,128)(2,1)S(1)} %copy-done.4), channel_id=1, source_target_pairs={{0,1},{1,0},{2,3},{3,2},{4,5},{5,4},{6,7},{7,6},{8,9},{9,8},{10,11... | collective-permute-start | bytes 3145736 | tf_op jit(solution)/shard_map/ppermute | solution.py:488
  100.7 27.3 %collective-permute-start.23 = (bf16[256,2048]{1,0:T(8,128)(2,1)S(1)}, bf16[256,2048]{1,0:T(8,128)(2,1)}, u32[]{:S(2)}, u32[]{:S(2)}) collective-permute-start(bf16[256,2048]{1,0:T(8,128)(2,1)S(1)} %collective-permute-done.15.refs_6_), channel_id=1, source_target_pairs={{0,1},{1,0},{2,3},{3,2},{4,5},{5,4},{6,7},{7,6},{8,9},{9,8},{10,11... | collective-permute-start | bytes 3145736 | tf_op jit(solution)/shard_map/ppermute | solution.py:488
  102.1 10.2 %collective-permute-start.18 = (bf16[256,512]{1,0:T(8,128)(2,1)S(1)}, bf16[256,512]{1,0:T(8,128)(2,1)S(1)}, u32[]{:S(2)}, u32[]{:S(2)}) collective-permute-start(bf16[256,512]{1,0:T(8,128)(2,1)S(1)} %get-tuple-element.35), channel_id=1, source_target_pairs={{0,3},{1,2},{2,1},{3,0},{4,7},{5,6},{6,5},{7,4},{8,11},{9,10},{10,... | collective-permute-start | bytes 786440 | tf_op jit(solution)/shard_map/ppermute | solution.py:488
  102.7 14.9 %collective-permute-start.17 = (bf16[256,512]{1,0:T(8,128)(2,1)S(1)}, bf16[256,512]{1,0:T(8,128)(2,1)S(1)}, u32[]{:S(2)}, u32[]{:S(2)}) collective-permute-start(bf16[256,512]{1,0:T(8,128)(2,1)S(1)} %get-tuple-element.36), channel_id=1, source_target_pairs={{0,2},{1,3},{2,0},{3,1},{4,6},{5,7},{6,4},{7,5},{8,10},{9,11},{10,... | collective-permute-start | bytes 786440 | tf_op jit(solution)/shard_map/ppermute | solution.py:488
  105.5 12.9 %collective-permute-start.16 = (bf16[256,512]{1,0:T(8,128)(2,1)S(1)}, bf16[256,512]{1,0:T(8,128)(2,1)S(1)}, u32[]{:S(2)}, u32[]{:S(2)}) collective-permute-start(bf16[256,512]{1,0:T(8,128)(2,1)S(1)} %get-tuple-element.37), channel_id=1, source_target_pairs={{0,1},{1,0},{2,3},{3,2},{4,5},{5,4},{6,7},{7,6},{8,9},{9,8},{10,11... | collective-permute-start | bytes 786440 | tf_op jit(solution)/shard_map/ppermute | solution.py:488
  119.0 15.6 %copy-start.1 = (bf16[2048,3,256]{2,0,1:T(8,128)(2,1)S(1)}, bf16[2048,3,256]{2,0,1:T(8,128)(2,1)}, u32[]{:S(2)}) copy-start(bf16[2048,3,256]{2,0,1:T(8,128)(2,1)} %param.17) | copy-start | bytes 9437188
  120.3 6.3 %collective-permute-start.21 = (bf16[128,256]{1,0:T(8,128)(2,1)S(1)}, bf16[128,256]{1,0:T(8,128)(2,1)S(1)}, u32[]{:S(2)}, u32[]{:S(2)}) collective-permute-start(bf16[128,256]{1,0:T(8,128)(2,1)S(1)} %merge.1.refs_0_), channel_id=1, source_target_pairs={{0,3},{1,2},{2,1},{3,0},{4,7},{5,6},{6,5},{7,4},{8,11},{9,10},{10,... | collective-permute-start | bytes 196616 | tf_op jit(solution)/shard_map/ppermute | solution.py:488
  121.2 6.8 %collective-permute-start.20 = (bf16[128,256]{1,0:T(8,128)(2,1)S(1)}, bf16[128,256]{1,0:T(8,128)(2,1)S(1)}, u32[]{:S(2)}, u32[]{:S(2)}) collective-permute-start(bf16[128,256]{1,0:T(8,128)(2,1)S(1)} %merge.1.refs_0_), channel_id=1, source_target_pairs={{0,2},{1,3},{2,0},{3,1},{4,6},{5,7},{6,4},{7,5},{8,10},{9,11},{10,... | collective-permute-start | bytes 196616 | tf_op jit(solution)/shard_map/ppermute | solution.py:488
  123.9 4.0 %collective-permute-start.19 = (bf16[128,256]{1,0:T(8,128)(2,1)S(1)}, bf16[128,256]{1,0:T(8,128)(2,1)S(1)}, u32[]{:S(2)}, u32[]{:S(2)}) collective-permute-start(bf16[128,256]{1,0:T(8,128)(2,1)S(1)} %merge.1.refs_0_), channel_id=1, source_target_pairs={{0,1},{1,0},{2,3},{3,2},{4,5},{5,4},{6,7},{7,6},{8,9},{9,8},{10,11... | collective-permute-start | bytes 196616 | tf_op jit(solution)/shard_map/ppermute | solution.py:488
  131.2 24.6 %copy-start.14 = (f32[2]{0:T(128)S(1)}, f32[2]{0:T(128)}, u32[]{:S(2)}) copy-start(f32[2]{0:T(128)} %slope_ref.5) | copy-start | bytes 28
  131.2 50.4 %copy-start.7 = (bf16[256,512]{1,0:T(8,128)(2,1)S(1)}, bf16[256,512]{1,0:T(8,128)(2,1)}, u32[]{:S(2)}) copy-start(bf16[256,512]{1,0:T(8,128)(2,1)} %copy-done.6) | copy-start | bytes 786436
  131.2 50.4 %copy-start.9 = (bf16[256,512]{1,0:T(8,128)(2,1)S(1)}, bf16[256,512]{1,0:T(8,128)(2,1)}, u32[]{:S(2)}) copy-start(bf16[256,512]{1,0:T(8,128)(2,1)} %copy-done.8) | copy-start | bytes 786436
  131.2 50.4 %copy-start.11 = (bf16[256,512]{1,0:T(8,128)(2,1)S(1)}, bf16[256,512]{1,0:T(8,128)(2,1)}, u32[]{:S(2)}) copy-start(bf16[256,512]{1,0:T(8,128)(2,1)} %copy-done.10) | copy-start | bytes 786436
  131.3 3.4 %collective-permute-start.24 = (bf16[16,2048]{1,0:T(8,128)(2,1)S(1)}, bf16[16,2048]{1,0:T(8,128)(2,1)S(1)}, u32[]{:S(2)}, u32[]{:S(2)}) collective-permute-start(bf16[16,2048]{1,0:T(8,128)(2,1)S(1)} %slice.24), channel_id=1, source_target_pairs={{0,4},{4,8},{8,12},{12,16},{16,20},{20,24},{24,28},{28,32},{32,36}... | collective-permute-start | bytes 196616 | tf_op jit(solution)/shard_map/ppermute | solution.py:571
  135.9 5.5 %collective-permute-start.25 = (bf16[32,256]{1,0:T(8,128)(2,1)S(1)}, bf16[32,256]{1,0:T(8,128)(2,1)S(1)}, u32[]{:S(2)}, u32[]{:S(2)}) collective-permute-start(bf16[32,256]{1,0:T(8,128)(2,1)S(1)} %get-tuple-element.29), channel_id=1, source_target_pairs={{0,8},{8,0},{16,24},{24,16},{32,40},{40,32},{48,56},{56,48},{1,9},... | collective-permute-start | bytes 49160 | tf_op jit(solution)/shard_map/ppermute | solution.py:488
  140.3 4.7 %collective-permute-start.29 = (bf16[2,32,256]{2,1,0:T(8,128)(2,1)S(1)}, bf16[2,32,256]{2,1,0:T(8,128)(2,1)S(1)}, u32[]{:S(2)}, u32[]{:S(2)}) collective-permute-start(bf16[2,32,256]{2,1,0:T(8,128)(2,1)S(1)} %get-tuple-element.30), channel_id=1, source_target_pairs={{0,4},{4,0},{1,5},{5,1},{2,6},{6,2},{3,7},{7,3},{8,12},{12,8},{9,1... | collective-permute-start | bytes 98312 | tf_op jit(solution)/shard_map/ppermute | solution.py:488
  141.4 9.5 %collective-permute-start.28 = (bf16[2,32,256]{2,1,0:T(8,128)(2,1)S(1)}, bf16[2,32,256]{2,1,0:T(8,128)(2,1)S(1)}, u32[]{:S(2)}, u32[]{:S(2)}) collective-permute-start(bf16[2,32,256]{2,1,0:T(8,128)(2,1)S(1)} %pad_maximum_fusion.5.refs_0_), channel_id=1, source_target_pairs={{0,48},{8,56},{16,0},{24,8},{32,16},{40,24},{48,32},{56,40},{1,49}... | collective-permute-start | bytes 98312 | tf_op jit(solution)/shard_map/ppermute | solution.py:493
  145.0 10.8 %collective-permute-start.32 = (bf16[2,2,32,256]{3,2,1,0:T(8,128)(2,1)S(1)}, bf16[2,2,32,256]{3,2,1,0:T(8,128)(2,1)S(1)}, u32[]{:S(2)}, u32[]{:S(2)}) collective-permute-start(bf16[2,2,32,256]{3,2,1,0:T(8,128)(2,1)S(1)} %pad_maximum_fusion.4.refs_4_), channel_id=1, source_target_pairs={{0,192},{64,0},{128,64},{192,128},{1,193},{65,1},{129,65},{193,129... | collective-permute-start | bytes 196616 | tf_op jit(solution)/shard_map/ppermute | solution.py:493
  147.0 8.8 %collective-permute-start.31 = (bf16[2,2,32,256]{3,2,1,0:T(8,128)(2,1)S(1)}, bf16[2,2,32,256]{3,2,1,0:T(8,128)(2,1)S(1)}, u32[]{:S(2)}, u32[]{:S(2)}) collective-permute-start(bf16[2,2,32,256]{3,2,1,0:T(8,128)(2,1)S(1)} %pad_maximum_fusion.4.refs_4_), channel_id=1, source_target_pairs={{0,128},{64,192},{128,0},{192,64},{1,129},{65,193},{129,1},{193,65... | collective-permute-start | bytes 196616 | tf_op jit(solution)/shard_map/ppermute | solution.py:493
  147.0 8.8 %collective-permute-start.30 = (bf16[2,2,32,256]{3,2,1,0:T(8,128)(2,1)S(1)}, bf16[2,2,32,256]{3,2,1,0:T(8,128)(2,1)S(1)}, u32[]{:S(2)}, u32[]{:S(2)}) collective-permute-start(bf16[2,2,32,256]{3,2,1,0:T(8,128)(2,1)S(1)} %pad_maximum_fusion.4.refs_4_), channel_id=1, source_target_pairs={{0,64},{64,128},{128,192},{192,0},{1,65},{65,129},{129,193},{193,1... | collective-permute-start | bytes 196616 | tf_op jit(solution)/shard_map/ppermute | solution.py:493
  147.6 6.7 %collective-permute-start.27 = (bf16[2,32,256]{2,1,0:T(8,128)(2,1)S(1)}, bf16[2,32,256]{2,1,0:T(8,128)(2,1)S(1)}, u32[]{:S(2)}, u32[]{:S(2)}) collective-permute-start(bf16[2,32,256]{2,1,0:T(8,128)(2,1)S(1)} %pad_maximum_fusion.5.refs_0_), channel_id=1, source_target_pairs={{0,32},{8,40},{16,48},{24,56},{32,0},{40,8},{48,16},{56,24},{1,33}... | collective-permute-start | bytes 98312 | tf_op jit(solution)/shard_map/ppermute | solution.py:493
  150.9 4.9 %collective-permute-start.26 = (bf16[2,32,256]{2,1,0:T(8,128)(2,1)S(1)}, bf16[2,32,256]{2,1,0:T(8,128)(2,1)S(1)}, u32[]{:S(2)}, u32[]{:S(2)}) collective-permute-start(bf16[2,32,256]{2,1,0:T(8,128)(2,1)S(1)} %pad_maximum_fusion.5.refs_0_), channel_id=1, source_target_pairs={{0,16},{8,24},{16,32},{24,40},{32,48},{40,56},{48,0},{56,8},{1,17}... | collective-permute-start | bytes 98312 | tf_op jit(solution)/shard_map/ppermute | solution.py:493
  170.2 9.0 %collective-permute-start.35 = (bf16[32,256]{1,0:T(8,128)(2,1)S(1)}, bf16[32,256]{1,0:T(8,128)(2,1)S(1)}, u32[]{:S(2)}, u32[]{:S(2)}) collective-permute-start(bf16[32,256]{1,0:T(8,128)(2,1)S(1)} %short_merge.1.refs_0_), channel_id=1, source_target_pairs={{0,3},{1,2},{2,1},{3,0},{4,7},{5,6},{6,5},{7,4},{8,11},{9,10},{10,... | collective-permute-start | bytes 49160 | tf_op jit(solution)/shard_map/ppermute | solution.py:488
  177.5 4.1 %collective-permute-start.34 = (bf16[32,256]{1,0:T(8,128)(2,1)S(1)}, bf16[32,256]{1,0:T(8,128)(2,1)S(1)}, u32[]{:S(2)}, u32[]{:S(2)}) collective-permute-start(bf16[32,256]{1,0:T(8,128)(2,1)S(1)} %short_merge.1.refs_0_), channel_id=1, source_target_pairs={{0,2},{1,3},{2,0},{3,1},{4,6},{5,7},{6,4},{7,5},{8,10},{9,11},{10,... | collective-permute-start | bytes 49160 | tf_op jit(solution)/shard_map/ppermute | solution.py:488
  179.2 2.4 %collective-permute-start.33 = (bf16[32,256]{1,0:T(8,128)(2,1)S(1)}, bf16[32,256]{1,0:T(8,128)(2,1)S(1)}, u32[]{:S(2)}, u32[]{:S(2)}) collective-permute-start(bf16[32,256]{1,0:T(8,128)(2,1)S(1)} %short_merge.1.refs_0_), channel_id=1, source_target_pairs={{0,1},{1,0},{2,3},{3,2},{4,5},{5,4},{6,7},{7,6},{8,9},{9,8},{10,11... | collective-permute-start | bytes 49160 | tf_op jit(solution)/shard_map/ppermute | solution.py:488
  (8 other events, 7.6 us)

commit v3 on v2

v3 whole, which is shorter than its diff:
```python
import functools
import math

import jax
import jax.numpy as jnp
from jax import lax
from jax.experimental import pallas as pl
from jax.experimental.pallas import tpu as pltpu
from jax.sharding import Mesh, PartitionSpec as P

HS = 128
GROUP = 4
NEG = -1e30
LOG2E = math.log2(math.e)
SCALE2 = HS ** -0.5 * LOG2E

VMEM = pltpu.VMEM
SMEM = pltpu.SMEM
F32 = jnp.float32
BF16 = jnp.bfloat16


def cost(flops, moved, trans=0):
    return pl.CostEstimate(flops=flops, bytes_accessed=moved, transcendentals=trans)


def params(mib):
    return pltpu.CompilerParams(vmem_limit_bytes=mib * 1024 * 1024)


def rms_scaled(values):
    inv = lax.rsqrt(jnp.mean(values * values, axis=-1, keepdims=True) + 1e-06)
    return (values * inv).astype(BF16)


def dot_t(a, b):
    return lax.dot_general(a, b, (((1,), (1,)), ((), ())), preferred_element_type=F32)


def three_parts(x):
    hi = x.astype(BF16).astype(F32)
    mid = (x - hi).astype(BF16).astype(F32)
    lo = (x - hi - mid).astype(BF16).astype(F32)
    return hi, mid, lo


def project_kernel(count_ref, tok_ref, w_ref, ck_ref, cv_ref, q_ref, pack_ref, normed):
    step = pl.program_id(0)
    rows = tok_ref.shape[0]
    slots = ck_ref.shape[0]

    @pl.when(step == 0)
    def _():
        normed[...] = rms_scaled(tok_ref[...].astype(F32))
        pack_ref[:slots] = ck_ref[...]
        pack_ref[slots : 2 * slots] = cv_ref[...]
        count = jnp.full((16, pack_ref.shape[1]), count_ref[0], jnp.int32)
        pack_ref[2 * (slots + rows) :] = count.astype(F32).astype(BF16)

    out = jnp.dot(normed[...], w_ref[0], preferred_element_type=F32)

    @pl.when(step == 0)
    def _():
        q_ref[...] = (out * SCALE2).astype(BF16)

    @pl.when(step == 1)
    def _():
        pack_ref[2 * slots : 2 * slots + rows] = out.astype(BF16)

    @pl.when(step == 2)
    def _():
        pack_ref[2 * slots + rows : 2 * (slots + rows)] = out.astype(BF16)


def project(count, rows, weight3, cache_keys, cache_values):
    n, d = rows.shape
    width = weight3.shape[2]
    total = 2 * (n + cache_keys.shape[0]) + 16
    whole = lambda shape: pl.BlockSpec(shape, lambda i: (0, 0))
    return pl.pallas_call(
        project_kernel,
        grid=(3,),
        in_specs=[
            pl.BlockSpec(memory_space=SMEM),
            whole((n, d)),
            pl.BlockSpec((1, d, width), lambda i: (i, 0, 0)),
            whole(cache_keys.shape),
            whole(cache_values.shape),
        ],
        out_specs=[whole((n, width)), whole((total, width))],
        out_shape=[
            jax.ShapeDtypeStruct((n, width), BF16),
            jax.ShapeDtypeStruct((total, width), BF16),
        ],
        scratch_shapes=[VMEM((n, d), BF16)],
        compiler_params=params(12),
        cost_estimate=cost(6 * n * d * width, 2 * (n * d + 3 * d * width)),
        name="project",
    )(count, rows, weight3, cache_keys, cache_values)


def mark_kernel(q_ref, own_ref, other_ref, out_ref):
    rows = q_ref.shape[0]
    out_ref[:rows] = q_ref[...]
    step = lax.broadcasted_iota(jnp.int32, own_ref.shape, 0)
    own, other = own_ref[...].astype(F32), other_ref[...].astype(F32)
    out_ref[rows:] = jnp.where(step < 8, own, other).astype(BF16)


def mark(q, own, other):
    n, width = q.shape
    last = own.shape[0] // 16 - 1
    return pl.pallas_call(
        mark_kernel,
        grid=(1,),
        in_specs=[pl.BlockSpec((n, width), lambda i: (0, 0))]
        + [pl.BlockSpec((16, width), lambda i: (last, 0))] * 2,
        out_specs=pl.BlockSpec((n + 16, width), lambda i: (0, 0)),
        out_shape=jax.ShapeDtypeStruct((n + 16, width), BF16),
        compiler_params=params(8),
        cost_estimate=cost(0, 4 * n * width),
        name="mark",
    )(q, own, other)


def join_kernel(a_ref, b_ref, out_ref):
    rows = a_ref.shape[0]
    out_ref[:rows] = a_ref[...]
    out_ref[rows:] = b_ref[...]


def join(a, b):
    n, width = a.shape
    return pl.pallas_call(
        join_kernel,
        out_shape=jax.ShapeDtypeStruct((2 * n, width), BF16),
        compiler_params=params(8),
        cost_estimate=cost(0, 8 * n * width),
        name="join",
    )(a, b)


def plane_kernel(*refs):
    rows = []
    for pair in refs[:-1]:
        half = pair.shape[0] // 2
        for at in (half - 16, 2 * half - 16):
            marks = pair[at : at + 16].astype(F32)
            rows += [marks[:1], marks[8:9]]
    refs[-1][...] = jnp.concatenate(rows, axis=0).astype(BF16)


def plane_counts(queries):
    return pl.pallas_call(
        plane_kernel,
        out_shape=jax.ShapeDtypeStruct((16, queries[0].shape[1]), BF16),
        compiler_params=params(8),
        cost_estimate=cost(0, 8 * queries[0].size),
        name="plane_counts",
    )(*queries)


RING = ((0, 0), (0, 1), (1, 0), (1, 1), (3, 0), (3, 1), (2, 0), (2, 1))


def place_of_device():
    return lax.axis_index("y"), lax.axis_index("z"), lax.axis_index("xl")


def columns_of(pieces):
    return [s[:, at : at + HS] for s in pieces for at in range(0, s.shape[1], HS)]


def attend_heads(qs, pieces, score, value):
    heads = len(qs)
    pending = [score(0, qs[0], j) for j in range(pieces)]
    results = []
    for h in range(heads):
        top = jnp.max(functools.reduce(jnp.maximum, columns_of(pending)), axis=1, keepdims=True)
        following = []
        both = None
        for j in range(pieces):
            term = jnp.dot(
                jnp.exp2(pending[j] - top).astype(BF16), value(h, j), preferred_element_type=F32
            )
            both = term if both is None else both + term
            if h + 1 < heads:
                following.append(score(h + 1, qs[h + 1], j))
        pending = following
        results.append((top, both[:, HS:], both[:, :HS]))
    return results


def with_ones(v):
    return jnp.concatenate([v, jnp.ones_like(v)], axis=1)


def attend_kernel(slots, slope_ref, *refs):
    queries, planes, packs = refs[:4], refs[4:8], refs[8:16]
    out_ref, q_tile, bias = refs[16:]
    tile = pl.program_id(0)
    y, z, xl = place_of_device()
    rows = q_tile.shape[0] // 2
    width = q_tile.shape[1]
    heads = width // HS
    owners = len(RING)
    cached = owners * slots

    def side_of(other):
        return 1 - xl if other else xl

    for t in range(4):

        @pl.when(tile == t)
        def _(t=t):
            q_tile[:rows] = queries[t][:rows]
            q_tile[rows:] = queries[t][rows + 16 : 2 * rows + 16]

    @pl.when(tile == 0)
    def _():
        steps = lax.broadcasted_iota(jnp.int32, (16, width), 0)
        zs = (z + 8 - 2 * (steps // 4)) % 8
        zs = jnp.where((steps // 2) % 2 == 1, zs ^ 1, zs)
        totals, parts, owns = [], [], []
        for plane in planes:
            counts = plane[...].astype(F32)
            totals.append(jnp.sum(counts, axis=0, keepdims=True))
            parts.append(jnp.sum(jnp.where(zs < z, counts, 0.0), axis=0, keepdims=True))
            owns.append((counts[0:1], counts[1:2]))
        ys = [(y + 4 - back) % 4 for back in range(4)]
        everything = functools.reduce(jnp.add, totals)
        slot = lax.broadcasted_iota(jnp.int32, (1, slots), 1).astype(F32)
        place = lax.broadcasted_iota(jnp.int32, (1, rows), 1)
        for j, (back, other) in enumerate(RING):
            side = side_of(other)
            start = parts[back] - everything
            for i in range(4):
                start = start + jnp.where(ys[i] < ys[back], totals[i], 0.0)
            start = start + jnp.where(side == 1, owns[back][1 - other], 0.0)
            spot = (place + (ys[back] * 16 + z * 2 + side) * rows).astype(F32)
            for h in range(heads):
                slope = slope_ref[h] * LOG2E
                bias[h : h + 1, j * slots : (j + 1) * slots] = jnp.where(
                    slot < owns[back][other], slope * (slot + start), NEG
                )
                at = cached + j * rows
                bias[h : h + 1, at : at + rows] = jnp.where(ys[back] <= y, slope * spot, NEG)

    row = lax.broadcasted_iota(jnp.int32, (2 * rows, 1), 0)
    first = (z + 8 - 2 * tile) % 8
    row_ctx = y * 16 + xl + 2 * jnp.where(row < rows, first, first ^ 1)
    row_pos = row_ctx * rows + jnp.where(row < rows, row, row - rows)
    place = lax.broadcasted_iota(jnp.int32, (1, rows), 1)

    def score(h, q, j):
        cols = slice(h * HS, (h + 1) * HS)
        if j < owners:
            s = dot_t(q, packs[j][:slots, cols])
            return s + bias[h : h + 1, j * slots : (j + 1) * slots]
        back, other = RING[j - owners]
        at = cached + (j - owners) * rows
        s = dot_t(q, packs[j - owners][2 * slots : 2 * slots + rows, cols])
        s = s + bias[h : h + 1, at : at + rows]
        if back == 0:
            first_key = (y * 16 + z * 2 + side_of(other)) * rows
            s = jnp.where(place + first_key <= row_pos, s, NEG)
        return s

    def value(h, j):
        cols = slice(h * HS, (h + 1) * HS)
        if j < owners:
            return with_ones(packs[j][slots : 2 * slots, cols])
        return with_ones(packs[j - owners][2 * slots + rows : 2 * (slots + rows), cols])

    lane = lax.broadcasted_iota(jnp.int32, (2 * rows, HS), 1)
    packed = jnp.zeros((2 * rows, HS), F32)
    qs = [q_tile[:, h * HS : (h + 1) * HS] for h in range(heads)]
    done = []
    for h, (top, total, acc) in enumerate(attend_heads(qs, 2 * owners, score, value)):
        done.append((acc / total).astype(BF16))
        for k, piece in enumerate(three_parts(top + jnp.log2(total))):
            packed = jnp.where(lane == 3 * h + k, piece, packed)
    both = jnp.concatenate(done, axis=1)
    odd = z % 2 == 1
    blocks = []
    for own, level in (
        (jnp.where(odd, both[rows:], both[:rows]), jnp.where(odd, packed[rows:], packed[:rows])),
        (jnp.where(odd, both[:rows], both[rows:]), jnp.where(odd, packed[:rows], packed[rows:])),
    ):
        turned = jnp.transpose(level)[:16]
        tail = jnp.concatenate([turned, jnp.zeros_like(turned)], axis=1).astype(BF16)
        blocks.append((own, tail))
    for p in range(4):

        @pl.when((z // 2 + 4 - tile) % 4 == p)
        def _(p=p):
            for b, (own, tail) in enumerate(blocks):
                out_ref[2 * p + b, :rows] = own
                out_ref[2 * p + b, rows:] = tail


def attend(slopes, queries, planes, packs, slots):
    padded, width = queries[0].shape
    rows = padded // 2 - 16
    nk = len(RING) * (slots + rows)
    whole = lambda a: pl.BlockSpec(a.shape, lambda i: (0,) * a.ndim)
    out = jax.ShapeDtypeStruct((8, rows + 16, width), BF16)
    return pl.pallas_call(
        functools.partial(attend_kernel, slots),
        grid=(4,),
        in_specs=[pl.BlockSpec(memory_space=SMEM)]
        + [whole(a) for a in (*queries, *planes, *packs)],
        out_specs=whole(out),
        out_shape=out,
        scratch_shapes=[VMEM((2 * rows, width), BF16), VMEM((8, nk), F32)],
        compiler_params=params(40),
        cost_estimate=cost(32 * rows * nk * width, 4 * nk * width, 16 * rows * nk),
        name="attend",
    )(slopes, *queries, *planes, *packs)


def merge_kernel(heads, parts_ref, out_ref):
    sources, padded, width = parts_ref.shape
    rows = padded - 16
    levels = jnp.concatenate(
        [parts_ref[s, rows:, :HS].astype(F32) for s in range(sources)], axis=0
    )
    turned = jnp.transpose(levels)
    for h in range(heads):
        cols = slice(h * HS, (h + 1) * HS)
        level = []
        for s in range(sources):
            at = s * 16 + 3 * h
            level.append(
                (turned[:, at : at + 1] + turned[:, at + 1 : at + 2]) + turned[:, at + 2 : at + 3]
            )
        top = functools.reduce(jnp.maximum, level)
        total = jnp.zeros((rows, 1), F32)
        acc = jnp.zeros((rows, HS), F32)
        for s in range(sources):
            weight = jnp.exp2(level[s] - top)
            total = total + weight
            acc = acc + weight * parts_ref[s, :rows, cols].astype(F32)
        out_ref[:, cols] = (acc / total).astype(BF16)


def merge(parts):
    sources, padded, width = parts.shape
    rows = padded - 16
    return pl.pallas_call(
        functools.partial(merge_kernel, width // HS),
        out_shape=jax.ShapeDtypeStruct((rows, width), BF16),
        compiler_params=params(16),
        cost_estimate=cost(4 * sources * rows * width, 2 * sources * padded * width),
        name="merge",
    )(parts)


def product_kernel(tok_ref, a_ref, b_ref, wa_ref, wb_ref, sum_ref, term_ref, rim_ref):
    term = jnp.dot(a_ref[...], wa_ref[...], preferred_element_type=F32) + jnp.dot(
        b_ref[...], wb_ref[...], preferred_element_type=F32
    )
    total = tok_ref[...].astype(F32) + term
    sum_ref[...] = total
    term_ref[...] = term.astype(BF16)
    rim_ref[:16] = total[-16:].astype(BF16)
    rim_ref[16:] = term[-16:].astype(BF16)


def layer_product(tokens, atts, weights):
    rows, d = tokens.shape
    step = 512
    inner, width = weights[0].shape[0], atts[0].shape[1]
    cols = lambda n: pl.BlockSpec((n, step), lambda i: (0, i))
    return pl.pallas_call(
        product_kernel,
        grid=(d // step,),
        in_specs=[cols(rows)]
        + [pl.BlockSpec((rows, width), lambda i: (0, 0))] * 2
        + [cols(inner)] * 2,
        out_specs=[cols(rows), cols(rows), cols(32)],
        out_shape=[
            jax.ShapeDtypeStruct((rows, d), F32),
            jax.ShapeDtypeStruct((rows, d), BF16),
            jax.ShapeDtypeStruct((32, d), BF16),
        ],
        compiler_params=params(16),
        cost_estimate=cost(4 * rows * d * inner, 4 * inner * d),
        name="layer_product",
    )(tokens, *atts, *weights)


def short_project_kernel(
    sum_ref, term_ref, rim_a, rim_b, w_ref, cols_ref, q_ref, kv_ref, normed
):
    step = pl.program_id(0)
    rows, d = sum_ref.shape
    groups = rows // GROUP
    rim_rows = 16
    width = q_ref.shape[1]

    @pl.when(step == 0)
    def _():
        layer = (sum_ref[...] + term_ref[...].astype(F32)).astype(BF16)
        part = d // 4
        tp = lax.axis_index("tp")
        mine = layer[:, :part]
        for t in range(1, 4):
            mine = jnp.where(tp == t, layer[:, t * part : (t + 1) * part], mine)
        cols_ref[...] = mine
        rim = (rim_a[:rim_rows].astype(F32) + rim_b[rim_rows:].astype(F32)).astype(BF16)
        g = lax.broadcasted_iota(jnp.int32, (groups, rows), 0) * GROUP
        t = lax.broadcasted_iota(jnp.int32, (groups, rows), 1)
        own = jnp.where((t <= g) & (t > g - GROUP), 1.0 / GROUP, 0.0).astype(BF16)
        g = lax.broadcasted_iota(jnp.int32, (groups, rim_rows), 0) * GROUP
        t = lax.broadcasted_iota(jnp.int32, (groups, rim_rows), 1) - rim_rows
        before = jnp.where(t > g - GROUP, 1.0 / GROUP, 0.0).astype(BF16)
        pooled = jnp.dot(own, layer, preferred_element_type=F32) + jnp.dot(
            before, rim, preferred_element_type=F32
        )
        normed[...] = rms_scaled(pooled.astype(BF16).astype(F32))

    out = jnp.dot(normed[...], w_ref[0], preferred_element_type=F32)

    @pl.when(step == 0)
    def _():
        q_ref[...] = (out * SCALE2).astype(BF16)

    @pl.when(step == 1)
    def _():
        kv_ref[:, :width] = out.astype(BF16)

    @pl.when(step == 2)
    def _():
        kv_ref[:, width:] = out.astype(BF16)


def short_project(total, term, rims, weight3):
    n, d = total.shape
    groups = n // GROUP
    width = weight3.shape[2]
    whole = lambda shape: pl.BlockSpec(shape, lambda i: (0, 0))
    shapes = [(n, d // 4), (groups, width), (groups, 2 * width)]
    return pl.pallas_call(
        short_project_kernel,
        grid=(3,),
        in_specs=[whole((n, d)), whole((n, d)), whole((32, d)), whole((32, d))]
        + [pl.BlockSpec((1, d, width), lambda i: (i, 0, 0))],
        out_specs=[whole(s) for s in shapes],
        out_shape=[jax.ShapeDtypeStruct(s, BF16) for s in shapes],
        scratch_shapes=[VMEM((groups, d), BF16)],
        compiler_params=params(16),
        cost_estimate=cost(6 * groups * d * width, 2 * (n * d + 3 * d * width)),
        name="short_project",
    )(total, term, *rims, weight3)


def join_two_kernel(a, b, c, d, left, right):
    for x, y, out in ((a, b, left), (c, d, right)):
        out[: x.shape[0]] = x[...]
        out[x.shape[0] :] = y[...]


def join_two(a, b, c, d):
    shapes = [(2 * x.shape[0], x.shape[1]) for x in (a, c)]
    return pl.pallas_call(
        join_two_kernel,
        out_shape=[jax.ShapeDtypeStruct(s, BF16) for s in shapes],
        compiler_params=params(8),
        cost_estimate=cost(0, 8 * (a.size + c.size)),
        name="join_two",
    )(a, b, c, d)


def short_attend_kernel(slope_ref, q0, q1, kv0, kv1, out_ref):
    y, z, xl = place_of_device()
    _, groups, _ = out_ref.shape
    width = q0.shape[1]
    heads = width // HS
    nr = nk = 8 * groups
    row = lax.broadcasted_iota(jnp.int32, (nr, 1), 0)
    zs = row // groups
    row_pos = (y * 16 + zs * 2 + xl) * groups + row % groups
    came = (zs ^ z) * groups + row % groups
    order = jnp.where(lax.broadcasted_iota(jnp.int32, (nr, nr), 1) == came, 1.0, 0.0).astype(BF16)
    key = lax.broadcasted_iota(jnp.int32, (1, nk), 1)
    block = key // groups
    key_pos = ((y ^ (block // 2)) * 16 + z * 2 + (xl ^ (block % 2))) * groups + key % groups
    usable = key_pos <= row_pos
    spot = key_pos.astype(F32)
    lane = lax.broadcasted_iota(jnp.int32, (nr, HS), 1)
    packed = jnp.zeros((nr, HS), F32)
    queries = jnp.concatenate([q0[...], q1[...]], axis=0)
    queries = jnp.dot(order, queries, preferred_element_type=F32).astype(BF16)
    outs = []
    for h in range(heads):
        cols = slice(h * HS, (h + 1) * HS)
        k = jnp.concatenate([kv0[:, cols], kv1[:, cols]], axis=0)
        cols_v = slice(width + h * HS, width + (h + 1) * HS)
        v = jnp.concatenate([kv0[:, cols_v], kv1[:, cols_v]], axis=0)
        s = dot_t(queries[:, cols], k) + (slope_ref[h] * LOG2E) * spot
        s = jnp.where(usable, s, NEG)
        top = jnp.max(s, axis=1, keepdims=True)
        p = jnp.exp2(s - top).astype(BF16)
        both = jnp.dot(p, with_ones(v), preferred_element_type=F32)
        weight_total = both[:, HS:]
        outs.append((both[:, :HS] / weight_total).astype(BF16))
        level = top + jnp.log2(weight_total)
        for k, piece in enumerate(three_parts(level)):
            packed = jnp.where(lane == 3 * h + k, piece, packed)
    out = jnp.concatenate(outs + [packed.astype(BF16)], axis=1)
    out_ref[...] = out.reshape(out_ref.shape)


def short_attend(slopes, q0, q1, kv0, kv1):
    n, width = q0.shape
    groups = n // 4
    smem = pl.BlockSpec(memory_space=SMEM)
    vmem = pl.BlockSpec(memory_space=VMEM)
    return pl.pallas_call(
        short_attend_kernel,
        in_specs=[smem] + [vmem] * 4,
        out_specs=vmem,
        out_shape=jax.ShapeDtypeStruct((8, groups, width + HS), BF16),
        compiler_params=params(16),
        cost_estimate=cost(16 * n * n * width, 8 * n * width),
        name="short_attend",
    )(slopes, q0, q1, kv0, kv1)


def short_merge_kernel(heads, parts_ref, w_ref, *outs):
    sources, rows, padded = parts_ref.shape
    width = padded - HS
    merged = []
    for h in range(heads):
        cols = slice(h * HS, (h + 1) * HS)
        level = []
        for s in range(sources):
            lev = parts_ref[s, :, width:].astype(F32)
            level.append(
                (lev[:, 3 * h : 3 * h + 1] + lev[:, 3 * h + 1 : 3 * h + 2])
                + lev[:, 3 * h + 2 : 3 * h + 3]
            )
        top = functools.reduce(jnp.maximum, level)
        total = jnp.zeros((rows, 1), F32)
        acc = jnp.zeros((rows, HS), F32)
        for s in range(sources):
            weight = jnp.exp2(level[s] - top)
            total = total + weight
            acc = acc + weight * parts_ref[s, :, cols].astype(F32)
        merged.append((acc / total).astype(BF16))
    att = jnp.concatenate(merged, axis=1)
    cols = outs[0].shape[1]
    terms = [
        jnp.dot(
            att, w_ref[:, t * cols : (t + 1) * cols], preferred_element_type=F32
        ).astype(BF16)
        for t in range(4)
    ]
    tp = lax.axis_index("tp")
    for flip, out in enumerate(outs):
        chosen = terms[flip]
        for t in range(1, 4):
            chosen = jnp.where(tp == t, terms[t ^ flip], chosen)
        out[...] = chosen


def short_merge(parts, weight):
    sources, rows, padded = parts.shape
    width = padded - HS
    cols = weight.shape[1] // 4
    out = jax.ShapeDtypeStruct((rows, cols), BF16)
    return pl.pallas_call(
        functools.partial(short_merge_kernel, width // HS),
        out_shape=[out] * 4,
        compiler_params=params(16),
        cost_estimate=cost(8 * rows * width * cols, 8 * width * cols),
        name="short_merge",
    )(parts, weight)


def final_kernel(lay_ref, *refs):
    terms, out_ref = refs[:-1], refs[-1]
    rows, groups = lay_ref.shape[0], terms[0].shape[0]
    t = lax.broadcasted_iota(jnp.int32, (rows, groups), 0) // GROUP
    g = lax.broadcasted_iota(jnp.int32, (rows, groups), 1)
    spread = jnp.where(t == g, 1.0, 0.0).astype(BF16)
    branch = jnp.zeros(lay_ref.shape, F32)
    for term in terms:
        branch = branch + jnp.dot(spread, term[...], preferred_element_type=F32)
    out_ref[...] = (lay_ref[...].astype(F32) + branch).astype(BF16)


def final_sum(layer, terms):
    rows, cols = layer.shape
    groups = terms[0].shape[0]
    return pl.pallas_call(
        final_kernel,
        out_shape=jax.ShapeDtypeStruct((rows, cols), BF16),
        compiler_params=params(16),
        cost_estimate=cost(8 * rows * cols * groups, 4 * rows * cols),
        name="final_sum",
    )(layer, *terms)


def exchange(blocks, axis):
    return lax.all_to_all(blocks, axis, 0, 0)


def swap(x, axis, flip=1):
    return lax.ppermute(x, axis, [(i, i ^ flip) for i in range(lax.axis_size(axis))])


def moved(x, axis, by):
    n = lax.axis_size(axis)
    return lax.ppermute(x, axis, [(i, (i + by) % n) for i in range(n)])


def both_ways(x):
    return moved(x, "y", 1), moved(x, "y", -1)


def after(x, *others):
    return lax.optimization_barrier((x, *others))[0]


def on_device(
    tokens,
    project_weight,
    output_weight,
    distance_slope,
    cache_keys,
    cache_values,
    cache_count,
    short_project_weight,
    short_output,
    short_slope,
):
    axes = ("y", "z", "xl", "tp")
    slots = cache_keys.shape[0]
    q, pack = project(
        cache_count, tokens, jnp.transpose(project_weight, (1, 0, 2)), cache_keys, cache_values
    )
    other = swap(pack, "xl")
    left, right = both_ways(pack)
    marked = mark(q, pack, other)
    pair = join(marked, swap(marked, "z"))
    left_other, right_other = both_ways(other)
    queries = [pair] + [moved(pair, "z", by) for by in (2, 4, 6)]
    far, far_other = moved(left, "y", 1), moved(right_other, "y", -1)
    crossed = swap(after(output_weight, other), "tp", 2)
    plane = plane_counts(queries)
    planes = [plane] + [moved(plane, "y", by) for by in (1, 2, 3)]
    packs = [pack, other, left, left_other, right, right_other, far, far_other]
    parts = attend(distance_slope, queries, planes, packs, slots)

    att = merge(exchange(parts, "z"))
    total, term, rim = layer_product(
        tokens, (att, swap(att, "tp", 2)), (output_weight, crossed)
    )
    n, tp = lax.axis_size(axes), lax.axis_size("tp")
    ahead = [(i, i + tp) for i in range(n - tp)]
    rims = [
        lax.ppermute(rim, axes, ahead),
        lax.ppermute(rim, axes, [(i, j ^ 1) for i, j in ahead]),
    ]
    layer, sq, skv = short_project(
        total, swap(term, "tp", 1), rims, jnp.transpose(short_project_weight, (1, 0, 2))
    )
    sq, skv = join_two(sq, swap(sq, "z"), skv, swap(skv, "xl"))
    sq, skv = join_two(sq, swap(sq, "z", 2), skv, swap(skv, "y"))
    sparts = short_attend(
        short_slope, sq, swap(sq, "z", 4), skv, swap(skv, "y", 2)
    )
    terms = short_merge(exchange(sparts, "z"), short_output)
    terms = [swap(t, "tp", flip) if flip else t for flip, t in enumerate(terms)]
    return final_sum(layer, terms)


def solution(mesh):
    split = Mesh(mesh.devices.reshape(4, 8, 2, 4), ("y", "z", "xl", "tp"))
    ctx = ("y", "z", "xl")
    return jax.shard_map(
        on_device,
        mesh=split,
        in_specs=(
            P(ctx, None),
            P(None, None, "tp"),
            P("tp", None),
            P("tp"),
            P(ctx, "tp"),
            P(ctx, "tp"),
            P(ctx),
            P(None, None, "tp"),
            P("tp", None),
            P("tp"),
        ),
        out_specs=P(ctx, "tp"),
        check_vma=False,
    )
```

time: 184 us -> 171 us (0.929)
  waiting for transfers between devices: 28.9 us -> 51.6 us
  blocking collectives: 34.3 us -> 13.4 us
  local copies, waits for them, and re-layouts: 14.2 us -> 7.82 us
  Pallas kernels: 28.2 us -> 22.6 us
  other arithmetic: 2.27 us -> 0 us
    unnamed x1 -> x0, blocking collectives: 21.8 us -> none
    all_to_all x1, waiting for transfers between devices: 0.01 us -> 10.2 us  [exchange(): return lax.all_to_all(blocks, axis, 0, 0)]
    ppermute x17 -> x12, waiting for transfers between devices: 6.25 us -> 14.5 us  [moved(): return lax.ppermute(x, axis, [(i, (i + by) % n) for i in range(n)])]
    pallas_call x7 -> x11, Pallas kernels: 26.6 us -> 19.8 us  [the longest x1 12.4 us: attend(): pl.pallas_call(functools.partial(attend_kernel, slots), grid=(4,), in_spe...]
    ppermute x17 -> x12, starting transfers between devices: 28.2 us -> 22.3 us  [moved(): return lax.ppermute(x, axis, [(i, (i + by) % n) for i in range(n)])]
    all_to_all x1, starting transfers between devices: 3.67 us -> 7.37 us  [exchange(): return lax.all_to_all(blocks, axis, 0, 0)]
    ppermute x1 -> x2, starting transfers between devices: 2.11 us -> 5.76 us  [the longest x1 3.15 us: on_device(): lax.ppermute(rim, axes, [(i, j ^ 1) for i, j in ahead])]
    slice x5 -> x0, local copies, waits for them, and re-layouts: 3.28 us -> none  [the longest x2 1.65 us: round_y(): left[:half]]
  transfers between devices with their start and end apart: 37 -> 29, of which waited for: 12 -> 17; matrix products, arithmetic and copies ran while one was open for 4% -> 0% of each run, Pallas kernels for 11% -> 1%
where the time goes in v3:
time: 171 us
  starting transfers between devices  74.7 us (44%)
  waiting for transfers between devices  51.6 us (30%)
  Pallas kernels  22.6 us (13%)
  blocking collectives  13.4 us (8%)
  local copies, waits for them, and re-layouts  7.82 us (5%)
    ppermute x14, starting transfers between devices, swap(): lax.ppermute(x, axis, [(i, i ^ flip) for i in range(lax.axis_size(axis))])  39.3 us
    ppermute x14, waiting for transfers between devices, swap(): lax.ppermute(x, axis, [(i, i ^ flip) for i in range(lax.axis_size(axis))])  24 us
    ppermute x12, starting transfers between devices, moved(): return lax.ppermute(x, axis, [(i, (i + by) % n) for i in range(n)])  22.3 us
    ppermute x12, waiting for transfers between devices, moved(): return lax.ppermute(x, axis, [(i, (i + by) % n) for i in range(n)])  14.5 us
    all_to_all x1, blocking collectives, exchange(): return lax.all_to_all(blocks, axis, 0, 0)  13.4 us
    pallas_call x1, Pallas kernels, attend(): pl.pallas_call(functools.partial(attend_kernel, slots), grid=(4,), in_spe...  12.4 us
    all_to_all x1, waiting for transfers between devices, exchange(): return lax.all_to_all(blocks, axis, 0, 0)  10.2 us
    unnamed x22, local copies, waits for them, and re-layouts  7.82 us
  transfers between devices with their start and end apart: 29, of which 17 were waited for; matrix products, arithmetic and copies ran while one was open for 0% of the time, Pallas kernels for 1%

profile of v3, /device:TPU:1, one launch (start us, length us, event | category | flops | bytes accessed | tf_op | source)
XLA Modules:
  0.0 171.0 jit_solution(13892790090386927473)
XLA Ops:
  0.7 1.9 %copy-done.1 = bf16[2048,3,256]{2,0,1:T(8,128)(2,1)S(1)} copy-done((bf16[2048,3,256]{2,0,1:T(8,128)(2,1)S(1)}, bf16[2048,3,256]{2,0,1:T(8,128)(2,1)}, u32[]{:S(2)}) %copy-start.1) | copy-done | bytes 3145752
  2.6 1.0 copy-done.2
  5.4 1.2 project.1
  6.6 2.1 %collective-permute-start = (bf16[784,256]{1,0:T(8,128)(2,1)S(1)}, bf16[784,256]{1,0:T(8,128)(2,1)S(1)}, u32[]{:S(2)}, u32[]{:S(2)}) collective-permute-start(bf16[784,256]{1,0:T(8,128)(2,1)S(1)} %get-tuple-element.23.own_ref.refs_8_), channel_id=1, source_target_pairs={{0,4},{4,0},{1,5},{5,1},{2,6},{6,2},{3,7},{7,3},{8,12},{12,8},{9,1... | collective-permute-start | bytes 1204232 | tf_op jit(solution)/shard_map/ppermute | solution.py:611
  8.7 1.3 collective-permute-start.8
  10.0 6.4 %collective-permute-done.other_ref.refs_9_ = bf16[784,256]{1,0:T(8,128)(2,1)S(1)} collective-permute-done((bf16[784,256]{1,0:T(8,128)(2,1)S(1)}, bf16[784,256]{1,0:T(8,128)(2,1)S(1)}, u32[]{:S(2)}, u32[]{:S(2)}) %collective-permute-start) | collective-permute-done | bytes 401440 | tf_op jit(solution)/shard_map/ppermute | solution.py:611
  16.4 4.0 %collective-permute-start.11 = (bf16[784,256]{1,0:T(8,128)(2,1)S(1)}, bf16[784,256]{1,0:T(8,128)(2,1)S(1)}, u32[]{:S(2)}, u32[]{:S(2)}) collective-permute-start(bf16[784,256]{1,0:T(8,128)(2,1)S(1)} %collective-permute-done.other_ref.refs_9_), channel_id=1, source_target_pairs={{0,192},{64,0},{128,64},{192,128},{1,193},{65,1},{129,65},{193,129... | collective-permute-start | bytes 1204232 | tf_op jit(solution)/shard_map/ppermute | solution.py:616
  20.4 1.7 collective-permute-start.1
  22.1 2.0 %collective-permute-done.1.b_ref = bf16[144,256]{1,0:T(8,128)(2,1)S(1)} collective-permute-done((bf16[144,256]{1,0:T(8,128)(2,1)S(1)}, bf16[144,256]{1,0:T(8,128)(2,1)S(1)}, u32[]{:S(2)}, u32[]{:S(2)}) %collective-permute-start.1) | collective-permute-done | bytes 73760 | tf_op jit(solution)/shard_map/ppermute | solution.py:611
  24.1 5.9 %collective-permute-start.4 = (bf16[288,256]{1,0:T(8,128)(2,1)S(1)}, bf16[288,256]{1,0:T(8,128)(2,1)S(1)}, u32[]{:S(2)}, u32[]{:S(2)}) collective-permute-start(bf16[288,256]{1,0:T(8,128)(2,1)S(1)} %join.1.refs_0_), channel_id=1, source_target_pairs={{0,48},{8,56},{16,0},{24,8},{32,16},{40,24},{48,32},{56,40},{1,49}... | collective-permute-start | bytes 442376 | tf_op jit(solution)/shard_map/ppermute | solution.py:616
  30.2 1.3 collective-permute-start.9
  31.5 2.6 %collective-permute-start.13 = (bf16[784,256]{1,0:T(8,128)(2,1)S(1)}, bf16[784,256]{1,0:T(8,128)(2,1)S(1)}, u32[]{:S(2)}, u32[]{:S(2)}) collective-permute-start(bf16[784,256]{1,0:T(8,128)(2,1)S(1)} %collective-permute-done.11.refs_13_), channel_id=1, source_target_pairs={{0,192},{64,0},{128,64},{192,128},{1,193},{65,1},{129,65},{193,129... | collective-permute-start | bytes 1204232 | tf_op jit(solution)/shard_map/ppermute | solution.py:616
  34.2 3.6 %collective-permute-start.3 = (bf16[288,256]{1,0:T(8,128)(2,1)S(1)}, bf16[288,256]{1,0:T(8,128)(2,1)S(1)}, u32[]{:S(2)}, u32[]{:S(2)}) collective-permute-start(bf16[288,256]{1,0:T(8,128)(2,1)S(1)} %join.1.refs_0_), channel_id=1, source_target_pairs={{0,32},{8,40},{16,48},{24,56},{32,0},{40,8},{48,16},{56,24},{1,33}... | collective-permute-start | bytes 442376 | tf_op jit(solution)/shard_map/ppermute | solution.py:616
  37.8 4.4 %collective-permute-done.3.refs_2_ = bf16[288,256]{1,0:T(8,128)(2,1)S(1)} collective-permute-done((bf16[288,256]{1,0:T(8,128)(2,1)S(1)}, bf16[288,256]{1,0:T(8,128)(2,1)S(1)}, u32[]{:S(2)}, u32[]{:S(2)}) %collective-permute-start.3) | collective-permute-done | bytes 147488 | tf_op jit(solution)/shard_map/ppermute | solution.py:616
  42.2 3.1 %collective-permute-start.2 = (bf16[288,256]{1,0:T(8,128)(2,1)S(1)}, bf16[288,256]{1,0:T(8,128)(2,1)S(1)}, u32[]{:S(2)}, u32[]{:S(2)}) collective-permute-start(bf16[288,256]{1,0:T(8,128)(2,1)S(1)} %join.1.refs_0_), channel_id=1, source_target_pairs={{0,16},{8,24},{16,32},{24,40},{32,48},{40,56},{48,0},{56,8},{1,17}... | collective-permute-start | bytes 442376 | tf_op jit(solution)/shard_map/ppermute | solution.py:616
  45.3 3.7 %collective-permute-done.2.refs_1_ = bf16[288,256]{1,0:T(8,128)(2,1)S(1)} collective-permute-done((bf16[288,256]{1,0:T(8,128)(2,1)S(1)}, bf16[288,256]{1,0:T(8,128)(2,1)S(1)}, u32[]{:S(2)}, u32[]{:S(2)}) %collective-permute-start.2) | collective-permute-done | bytes 147488 | tf_op jit(solution)/shard_map/ppermute | solution.py:616
  49.2 2.4 %collective-permute-done.7.refs_7_ = bf16[16,256]{1,0:T(8,128)(2,1)S(1)} collective-permute-done((bf16[16,256]{1,0:T(8,128)(2,1)S(1)}, bf16[16,256]{1,0:T(8,128)(2,1)S(1)}, u32[]{:S(2)}, u32[]{:S(2)}) %collective-permute-start.7) | collective-permute-done | bytes 8224 | tf_op jit(solution)/shard_map/ppermute | solution.py:616
  51.6 1.6 collective-permute-done.6.refs_6_
  53.2 2.4 %collective-permute-done.5.refs_5_ = bf16[16,256]{1,0:T(8,128)(2,1)S(1)} collective-permute-done((bf16[16,256]{1,0:T(8,128)(2,1)S(1)}, bf16[16,256]{1,0:T(8,128)(2,1)S(1)}, u32[]{:S(2)}, u32[]{:S(2)}) %collective-permute-start.5) | collective-permute-done | bytes 8224 | tf_op jit(solution)/shard_map/ppermute | solution.py:616
  55.6 12.4 %attend.1 = bf16[8,144,256]{2,1,0:T(8,128)(2,1)S(1)} custom-call(f32[2]{0:T(128)S(1)} %copy-done.10, bf16[288,256]{1,0:T(8,128)(2,1)S(1)} %join.1.refs_0_, bf16[288,256]{1,0:T(8,128)(2,1)S(1)} %collective-permute-done.2.refs_1_, bf16[288,256]{1,0:T(8,128)(2,1)S(1)} %collective-permute-done.3.refs_2_, bf16[288,256]{1,0:T(8,128)(2,1)S(1)} %collective-permute-done.4.refs_3_, ...), custom_call_target="tpu_custom_call" | custom-call | flops 3221225472 | bytes 3145728 | tf_op jit(solution)/shard_map/attend/pallas_call | solution.py:308
  68.8 7.4 %all-to-all-start = ((bf16[8,144,256]{2,1,0:T(8,128)(2,1)}), bf16[8,144,256]{2,1,0:T(8,128)(2,1)}, u32[]{:S(2)}, u32[]{:S(2)}) async-start(bf16[8,144,256]{2,1,0:T(8,128)(2,1)} %copy-done.6), calls=%async_computation | async-start | bytes 1179648 | tf_op jit(solution)/shard_map/all_to_all | solution.py:607
  76.2 2.7 %collective-permute-start.15 = (bf16[256,2048]{1,0:T(8,128)(2,1)}, bf16[256,2048]{1,0:T(8,128)(2,1)}, u32[]{:S(2)}, u32[]{:S(2)}) collective-permute-start(bf16[256,2048]{1,0:T(8,128)(2,1)} %wa_ref.1), channel_id=1, source_target_pairs={{0,2},{1,3},{2,0},{3,1},{4,6},{5,7},{6,4},{7,5},{8,10},{9,11},{10,... | collective-permute-start | bytes 3145736 | tf_op jit(solution)/shard_map/ppermute | solution.py:611
  78.9 10.2 %all-to-all-done.parts_ref = bf16[8,144,256]{2,1,0:T(8,128)(2,1)} async-done(((bf16[8,144,256]{2,1,0:T(8,128)(2,1)}), bf16[8,144,256]{2,1,0:T(8,128)(2,1)}, u32[]{:S(2)}, u32[]{:S(2)}) %all-to-all-start) | async-done | bytes 589856 | tf_op jit(solution)/shard_map/all_to_all | solution.py:607
  89.2 2.3 %merge.1.a_ref = bf16[128,256]{1,0:T(8,128)(2,1)S(1)} custom-call(bf16[8,144,256]{2,1,0:T(8,128)(2,1)} %all-to-all-done.parts_ref), custom_call_target="tpu_custom_call" | custom-call | flops 1048576 | bytes 589824 | tf_op jit(solution)/shard_map/merge/pallas_call | solution.py:350
  91.4 2.8 %collective-permute-start.14 = (bf16[128,256]{1,0:T(8,128)(2,1)S(1)}, bf16[128,256]{1,0:T(8,128)(2,1)S(1)}, u32[]{:S(2)}, u32[]{:S(2)}) collective-permute-start(bf16[128,256]{1,0:T(8,128)(2,1)S(1)} %merge.1.a_ref), channel_id=1, source_target_pairs={{0,2},{1,3},{2,0},{3,1},{4,6},{5,7},{6,4},{7,5},{8,10},{9,11},{10,... | collective-permute-start | bytes 196616 | tf_op jit(solution)/shard_map/ppermute | solution.py:611
  94.8 2.6 %collective-permute-done.14.b_ref = bf16[128,256]{1,0:T(8,128)(2,1)S(1)} collective-permute-done((bf16[128,256]{1,0:T(8,128)(2,1)S(1)}, bf16[128,256]{1,0:T(8,128)(2,1)S(1)}, u32[]{:S(2)}, u32[]{:S(2)}) %collective-permute-start.14) | collective-permute-done | bytes 65568 | tf_op jit(solution)/shard_map/ppermute | solution.py:611
  97.3 1.0 copy-done.3
  98.4 1.2 copy-done.5
  99.6 2.8 %layer_product.1 = (f32[128,2048]{1,0:T(8,128)S(1)}, bf16[128,2048]{1,0:T(8,128)(2,1)S(1)}, bf16[32,2048]{1,0:T(8,128)(2,1)S(1)}) custom-call(bf16[128,2048]{1,0:T(8,128)(2,1)S(1)} %copy-done.3, bf16[128,256]{1,0:T(8,128)(2,1)S(1)} %merge.1.a_ref, bf16[128,256]{1,0:T(8,128)(2,1)S(1)} %collective-permute-done.14.b_ref, bf16[256,2048]{1,0:T(8,128)(2,1)S(1)} %copy-done.5, ...), custom_call_target="tpu_custom_call" | custom-call | flops 268435456 | bytes 2097152 | tf_op jit(solution)/shard_map/layer_product/pallas_call | solution.py:375
  102.5 8.4 %collective-permute-start.16 = (bf16[128,2048]{1,0:T(8,128)(2,1)S(1)}, bf16[128,2048]{1,0:T(8,128)(2,1)S(1)}, u32[]{:S(2)}, u32[]{:S(2)}) collective-permute-start(bf16[128,2048]{1,0:T(8,128)(2,1)S(1)} %get-tuple-element.26), channel_id=1, source_target_pairs={{0,1},{1,0},{2,3},{3,2},{4,5},{5,4},{6,7},{7,6},{8,9},{9,8},{10,11... | collective-permute-start | bytes 1572872 | tf_op jit(solution)/shard_map/ppermute | solution.py:611
  110.9 3.2 %collective-permute-start.18 = (bf16[32,2048]{1,0:T(8,128)(2,1)S(1)}, bf16[32,2048]{1,0:T(8,128)(2,1)S(1)}, u32[]{:S(2)}, u32[]{:S(2)}) collective-permute-start(bf16[32,2048]{1,0:T(8,128)(2,1)S(1)} %get-tuple-element.27), channel_id=1, source_target_pairs={{0,5},{1,4},{2,7},{3,6},{4,9},{5,8},{6,11},{7,10},{8,13},{9,12},{1... | collective-permute-start | bytes 393224 | tf_op jit(solution)/shard_map/ppermute | solution.py:665
  114.0 2.6 %collective-permute-start.17 = (bf16[32,2048]{1,0:T(8,128)(2,1)S(1)}, bf16[32,2048]{1,0:T(8,128)(2,1)S(1)}, u32[]{:S(2)}, u32[]{:S(2)}) collective-permute-start(bf16[32,2048]{1,0:T(8,128)(2,1)S(1)} %get-tuple-element.27), channel_id=1, source_target_pairs={{0,4},{1,5},{2,6},{3,7},{4,8},{5,9},{6,10},{7,11},{8,12},{9,13},{1... | collective-permute-start | bytes 393224 | tf_op jit(solution)/shard_map/ppermute | solution.py:664
  116.8 2.7 %collective-permute-done.17.rim_a = bf16[32,2048]{1,0:T(8,128)(2,1)S(1)} collective-permute-done((bf16[32,2048]{1,0:T(8,128)(2,1)S(1)}, bf16[32,2048]{1,0:T(8,128)(2,1)S(1)}, u32[]{:S(2)}, u32[]{:S(2)}) %collective-permute-start.17) | collective-permute-done | bytes 131104 | tf_op jit(solution)/shard_map/ppermute | solution.py:664
  119.5 1.2 short_project.1
  120.8 2.2 %collective-permute-start.20 = (bf16[32,512]{1,0:T(8,128)(2,1)S(1)}, bf16[32,512]{1,0:T(8,128)(2,1)S(1)}, u32[]{:S(2)}, u32[]{:S(2)}) collective-permute-start(bf16[32,512]{1,0:T(8,128)(2,1)S(1)} %get-tuple-element.30.c), channel_id=1, source_target_pairs={{0,4},{4,0},{1,5},{5,1},{2,6},{6,2},{3,7},{7,3},{8,12},{12,8},{9,1... | collective-permute-start | bytes 98312 | tf_op jit(solution)/shard_map/ppermute | solution.py:611
  123.8 2.0 %collective-permute-done.19.b = bf16[32,256]{1,0:T(8,128)(2,1)S(1)} collective-permute-done((bf16[32,256]{1,0:T(8,128)(2,1)S(1)}, bf16[32,256]{1,0:T(8,128)(2,1)S(1)}, u32[]{:S(2)}, u32[]{:S(2)}) %collective-permute-start.19) | collective-permute-done | bytes 16416 | tf_op jit(solution)/shard_map/ppermute | solution.py:611
  125.8 1.2 collective-permute-start.22
  127.0 1.4 collective-permute-start.21
  128.4 2.3 %collective-permute-done.21.b = bf16[64,256]{1,0:T(8,128)(2,1)S(1)} collective-permute-done((bf16[64,256]{1,0:T(8,128)(2,1)S(1)}, bf16[64,256]{1,0:T(8,128)(2,1)S(1)}, u32[]{:S(2)}, u32[]{:S(2)}) %collective-permute-start.21) | collective-permute-done | bytes 32800 | tf_op jit(solution)/shard_map/ppermute | solution.py:611
  130.7 3.1 %collective-permute-start.24 = (bf16[128,512]{1,0:T(8,128)(2,1)S(1)}, bf16[128,512]{1,0:T(8,128)(2,1)S(1)}, u32[]{:S(2)}, u32[]{:S(2)}) collective-permute-start(bf16[128,512]{1,0:T(8,128)(2,1)S(1)} %get-tuple-element.34.kv0), channel_id=1, source_target_pairs={{0,128},{64,192},{128,0},{192,64},{1,129},{65,193},{129,1},{193,65... | collective-permute-start | bytes 393224 | tf_op jit(solution)/shard_map/ppermute | solution.py:611
  133.8 3.1 %collective-permute-start.23 = (bf16[128,256]{1,0:T(8,128)(2,1)S(1)}, bf16[128,256]{1,0:T(8,128)(2,1)S(1)}, u32[]{:S(2)}, u32[]{:S(2)}) collective-permute-start(bf16[128,256]{1,0:T(8,128)(2,1)S(1)} %get-tuple-element.33.q0), channel_id=1, source_target_pairs={{0,32},{8,40},{16,48},{24,56},{32,0},{40,8},{48,16},{56,24},{1,33}... | collective-permute-start | bytes 196616 | tf_op jit(solution)/shard_map/ppermute | solution.py:611
  136.9 3.9 %collective-permute-done.23.q1 = bf16[128,256]{1,0:T(8,128)(2,1)S(1)} collective-permute-done((bf16[128,256]{1,0:T(8,128)(2,1)S(1)}, bf16[128,256]{1,0:T(8,128)(2,1)S(1)}, u32[]{:S(2)}, u32[]{:S(2)}) %collective-permute-start.23) | collective-permute-done | bytes 65568 | tf_op jit(solution)/shard_map/ppermute | solution.py:611
  140.8 1.2 short_attend.1
  142.0 13.4 %all_to_all.10.parts_ref = bf16[8,32,384]{2,1,0:T(8,128)(2,1)S(1)} all-to-all(bf16[8,32,384]{2,1,0:T(8,128)(2,1)S(1)} %short_attend.1), channel_id=1, replica_groups=mesh['y'=4,'z'=8,'xl'=2,'tp'=4] {'z'}, dimensions={0} | all-to-all | bytes 393216 | tf_op jit(solution)/shard_map/all_to_all | solution.py:607
  155.9 6.6 %collective-permute-start.25 = (bf16[32,512]{1,0:T(8,128)(2,1)S(1)}, bf16[32,512]{1,0:T(8,128)(2,1)S(1)}, u32[]{:S(2)}, u32[]{:S(2)}) collective-permute-start(bf16[32,512]{1,0:T(8,128)(2,1)S(1)} %get-tuple-element.36), channel_id=1, source_target_pairs={{0,1},{1,0},{2,3},{3,2},{4,5},{5,4},{6,7},{7,6},{8,9},{9,8},{10,11... | collective-permute-start | bytes 98312 | tf_op jit(solution)/shard_map/ppermute | solution.py:611
  162.5 2.7 %collective-permute-start.26 = (bf16[32,512]{1,0:T(8,128)(2,1)S(1)}, bf16[32,512]{1,0:T(8,128)(2,1)S(1)}, u32[]{:S(2)}, u32[]{:S(2)}) collective-permute-start(bf16[32,512]{1,0:T(8,128)(2,1)S(1)} %get-tuple-element.37), channel_id=1, source_target_pairs={{0,2},{1,3},{2,0},{3,1},{4,6},{5,7},{6,4},{7,5},{8,10},{9,11},{10,... | collective-permute-start | bytes 98312 | tf_op jit(solution)/shard_map/ppermute | solution.py:611
  165.8 1.0 collective-permute-done.26.refs_2_
  166.8 3.2 %collective-permute-done.27.refs_3_ = bf16[32,512]{1,0:T(8,128)(2,1)S(1)} collective-permute-done((bf16[32,512]{1,0:T(8,128)(2,1)S(1)}, bf16[32,512]{1,0:T(8,128)(2,1)S(1)}, u32[]{:S(2)}, u32[]{:S(2)}) %collective-permute-start.27) | collective-permute-done | bytes 32800 | tf_op jit(solution)/shard_map/ppermute | solution.py:611
  (46 shorter events, 6.6 us)
Async XLA Ops:
  0.0 55.6 %copy-start.10 = (f32[2]{0:T(128)S(1)}, f32[2]{0:T(128)}, u32[]{:S(2)}) copy-start(f32[2]{0:T(128)} %slope_ref.2) | copy-start | bytes 28
  0.7 1.9 %copy-start.1 = (bf16[2048,3,256]{2,0,1:T(8,128)(2,1)S(1)}, bf16[2048,3,256]{2,0,1:T(8,128)(2,1)}, u32[]{:S(2)}) copy-start(bf16[2048,3,256]{2,0,1:T(8,128)(2,1)} %param.11) | copy-start | bytes 9437188
  2.6 1.0 copy-start.2
  3.6 0.9 copy-start.7
  4.5 0.9 copy-start.8
  6.6 9.8 %collective-permute-start = (bf16[784,256]{1,0:T(8,128)(2,1)S(1)}, bf16[784,256]{1,0:T(8,128)(2,1)S(1)}, u32[]{:S(2)}, u32[]{:S(2)}) collective-permute-start(bf16[784,256]{1,0:T(8,128)(2,1)S(1)} %get-tuple-element.23.own_ref.refs_8_), channel_id=1, source_target_pairs={{0,4},{4,0},{1,5},{5,1},{2,6},{6,2},{3,7},{7,3},{8,12},{12,8},{9,1... | collective-permute-start | bytes 1204232 | tf_op jit(solution)/shard_map/ppermute | solution.py:611
  8.7 22.8 %collective-permute-start.8 = (bf16[784,256]{1,0:T(8,128)(2,1)S(1)}, bf16[784,256]{1,0:T(8,128)(2,1)S(1)}, u32[]{:S(2)}, u32[]{:S(2)}) collective-permute-start(bf16[784,256]{1,0:T(8,128)(2,1)S(1)} %get-tuple-element.23.own_ref.refs_8_), channel_id=1, source_target_pairs={{0,64},{64,128},{128,192},{192,0},{1,65},{65,129},{129,193},{193,1... | collective-permute-start | bytes 1204232 | tf_op jit(solution)/shard_map/ppermute | solution.py:616
  16.4 15.1 %collective-permute-start.11 = (bf16[784,256]{1,0:T(8,128)(2,1)S(1)}, bf16[784,256]{1,0:T(8,128)(2,1)S(1)}, u32[]{:S(2)}, u32[]{:S(2)}) collective-permute-start(bf16[784,256]{1,0:T(8,128)(2,1)S(1)} %collective-permute-done.other_ref.refs_9_), channel_id=1, source_target_pairs={{0,192},{64,0},{128,64},{192,128},{1,193},{65,1},{129,65},{193,129... | collective-permute-start | bytes 1204232 | tf_op jit(solution)/shard_map/ppermute | solution.py:616
  20.4 3.7 %collective-permute-start.1 = (bf16[144,256]{1,0:T(8,128)(2,1)S(1)}, bf16[144,256]{1,0:T(8,128)(2,1)S(1)}, u32[]{:S(2)}, u32[]{:S(2)}) collective-permute-start(bf16[144,256]{1,0:T(8,128)(2,1)S(1)} %mark.1.a_ref), channel_id=1, source_target_pairs={{0,8},{8,0},{16,24},{24,16},{32,40},{40,32},{48,56},{56,48},{1,9},... | collective-permute-start | bytes 221192 | tf_op jit(solution)/shard_map/ppermute | solution.py:611
  24.1 10.1 %collective-permute-start.4 = (bf16[288,256]{1,0:T(8,128)(2,1)S(1)}, bf16[288,256]{1,0:T(8,128)(2,1)S(1)}, u32[]{:S(2)}, u32[]{:S(2)}) collective-permute-start(bf16[288,256]{1,0:T(8,128)(2,1)S(1)} %join.1.refs_0_), channel_id=1, source_target_pairs={{0,48},{8,56},{16,0},{24,8},{32,16},{40,24},{48,32},{56,40},{1,49}... | collective-permute-start | bytes 442376 | tf_op jit(solution)/shard_map/ppermute | solution.py:616
  30.0 19.1 %collective-permute-start.10 = (bf16[784,256]{1,0:T(8,128)(2,1)S(1)}, bf16[784,256]{1,0:T(8,128)(2,1)S(1)}, u32[]{:S(2)}, u32[]{:S(2)}) collective-permute-start(bf16[784,256]{1,0:T(8,128)(2,1)S(1)} %get-tuple-element.23.own_ref.refs_8_), channel_id=1, source_target_pairs={{0,192},{64,0},{128,64},{192,128},{1,193},{65,1},{129,65},{193,129... | collective-permute-start | bytes 1204232 | tf_op jit(solution)/shard_map/ppermute | solution.py:616
  30.2 25.4 %collective-permute-start.9 = (bf16[784,256]{1,0:T(8,128)(2,1)S(1)}, bf16[784,256]{1,0:T(8,128)(2,1)S(1)}, u32[]{:S(2)}, u32[]{:S(2)}) collective-permute-start(bf16[784,256]{1,0:T(8,128)(2,1)S(1)} %collective-permute-done.other_ref.refs_9_), channel_id=1, source_target_pairs={{0,64},{64,128},{128,192},{192,0},{1,65},{65,129},{129,193},{193,1... | collective-permute-start | bytes 1204232 | tf_op jit(solution)/shard_map/ppermute | solution.py:616
  31.5 24.1 %collective-permute-start.12 = (bf16[784,256]{1,0:T(8,128)(2,1)S(1)}, bf16[784,256]{1,0:T(8,128)(2,1)S(1)}, u32[]{:S(2)}, u32[]{:S(2)}) collective-permute-start(bf16[784,256]{1,0:T(8,128)(2,1)S(1)} %collective-permute-done.8.refs_10_), channel_id=1, source_target_pairs={{0,64},{64,128},{128,192},{192,0},{1,65},{65,129},{129,193},{193,1... | collective-permute-start | bytes 1204232 | tf_op jit(solution)/shard_map/ppermute | solution.py:616
  31.5 24.1 %collective-permute-start.13 = (bf16[784,256]{1,0:T(8,128)(2,1)S(1)}, bf16[784,256]{1,0:T(8,128)(2,1)S(1)}, u32[]{:S(2)}, u32[]{:S(2)}) collective-permute-start(bf16[784,256]{1,0:T(8,128)(2,1)S(1)} %collective-permute-done.11.refs_13_), channel_id=1, source_target_pairs={{0,192},{64,0},{128,64},{192,128},{1,193},{65,1},{129,65},{193,129... | collective-permute-start | bytes 1204232 | tf_op jit(solution)/shard_map/ppermute | solution.py:616
  34.2 8.0 %collective-permute-start.3 = (bf16[288,256]{1,0:T(8,128)(2,1)S(1)}, bf16[288,256]{1,0:T(8,128)(2,1)S(1)}, u32[]{:S(2)}, u32[]{:S(2)}) collective-permute-start(bf16[288,256]{1,0:T(8,128)(2,1)S(1)} %join.1.refs_0_), channel_id=1, source_target_pairs={{0,32},{8,40},{16,48},{24,56},{32,0},{40,8},{48,16},{56,24},{1,33}... | collective-permute-start | bytes 442376 | tf_op jit(solution)/shard_map/ppermute | solution.py:616
  42.2 6.8 %collective-permute-start.2 = (bf16[288,256]{1,0:T(8,128)(2,1)S(1)}, bf16[288,256]{1,0:T(8,128)(2,1)S(1)}, u32[]{:S(2)}, u32[]{:S(2)}) collective-permute-start(bf16[288,256]{1,0:T(8,128)(2,1)S(1)} %join.1.refs_0_), channel_id=1, source_target_pairs={{0,16},{8,24},{16,32},{24,40},{32,48},{40,56},{48,0},{56,8},{1,17}... | collective-permute-start | bytes 442376 | tf_op jit(solution)/shard_map/ppermute | solution.py:616
  49.0 2.6 %collective-permute-start.7 = (bf16[16,256]{1,0:T(8,128)(2,1)S(1)}, bf16[16,256]{1,0:T(8,128)(2,1)S(1)}, u32[]{:S(2)}, u32[]{:S(2)}) collective-permute-start(bf16[16,256]{1,0:T(8,128)(2,1)S(1)} %plane_counts.1.refs_4_), channel_id=1, source_target_pairs={{0,192},{64,0},{128,64},{192,128},{1,193},{65,1},{129,65},{193,129... | collective-permute-start | bytes 24584 | tf_op jit(solution)/shard_map/ppermute | solution.py:616
  49.1 4.1 %collective-permute-start.6 = (bf16[16,256]{1,0:T(8,128)(2,1)S(1)}, bf16[16,256]{1,0:T(8,128)(2,1)S(1)}, u32[]{:S(2)}, u32[]{:S(2)}) collective-permute-start(bf16[16,256]{1,0:T(8,128)(2,1)S(1)} %plane_counts.1.refs_4_), channel_id=1, source_target_pairs={{0,128},{64,192},{128,0},{192,64},{1,129},{65,193},{129,1},{193,65... | collective-permute-start | bytes 24584 | tf_op jit(solution)/shard_map/ppermute | solution.py:616
  51.6 4.0 %collective-permute-start.5 = (bf16[16,256]{1,0:T(8,128)(2,1)S(1)}, bf16[16,256]{1,0:T(8,128)(2,1)S(1)}, u32[]{:S(2)}, u32[]{:S(2)}) collective-permute-start(bf16[16,256]{1,0:T(8,128)(2,1)S(1)} %plane_counts.1.refs_4_), channel_id=1, source_target_pairs={{0,64},{64,128},{128,192},{192,0},{1,65},{65,129},{129,193},{193,1... | collective-permute-start | bytes 24584 | tf_op jit(solution)/shard_map/ppermute | solution.py:616
  68.0 0.8 copy-start.6
  68.8 50.7 %copy-start = (bf16[2048,3,256]{2,0,1:T(8,128)(2,1)S(1)}, bf16[2048,3,256]{2,0,1:T(8,128)(2,1)}, u32[]{:S(2)}) copy-start(bf16[2048,3,256]{2,0,1:T(8,128)(2,1)} %param.17) | copy-start | bytes 9437188
  68.8 20.3 %all-to-all-start = ((bf16[8,144,256]{2,1,0:T(8,128)(2,1)}), bf16[8,144,256]{2,1,0:T(8,128)(2,1)}, u32[]{:S(2)}, u32[]{:S(2)}) async-start(bf16[8,144,256]{2,1,0:T(8,128)(2,1)} %copy-done.6), calls=%async_computation | async-start | bytes 1179648 | tf_op jit(solution)/shard_map/all_to_all | solution.py:607
  76.2 18.6 %collective-permute-start.15 = (bf16[256,2048]{1,0:T(8,128)(2,1)}, bf16[256,2048]{1,0:T(8,128)(2,1)}, u32[]{:S(2)}, u32[]{:S(2)}) collective-permute-start(bf16[256,2048]{1,0:T(8,128)(2,1)} %wa_ref.1), channel_id=1, source_target_pairs={{0,2},{1,3},{2,0},{3,1},{4,6},{5,7},{6,4},{7,5},{8,10},{9,11},{10,... | collective-permute-start | bytes 3145736 | tf_op jit(solution)/shard_map/ppermute | solution.py:611
  91.4 5.9 %collective-permute-start.14 = (bf16[128,256]{1,0:T(8,128)(2,1)S(1)}, bf16[128,256]{1,0:T(8,128)(2,1)S(1)}, u32[]{:S(2)}, u32[]{:S(2)}) collective-permute-start(bf16[128,256]{1,0:T(8,128)(2,1)S(1)} %merge.1.a_ref), channel_id=1, source_target_pairs={{0,2},{1,3},{2,0},{3,1},{4,6},{5,7},{6,4},{7,5},{8,10},{9,11},{10,... | collective-permute-start | bytes 196616 | tf_op jit(solution)/shard_map/ppermute | solution.py:611
  97.3 1.0 copy-start.3
  98.4 1.2 copy-start.5
  102.4 38.4 %copy-start.9 = (f32[2]{0:T(128)S(1)}, f32[2]{0:T(128)}, u32[]{:S(2)}) copy-start(f32[2]{0:T(128)} %slope_ref.3) | copy-start | bytes 28
  102.5 53.0 %copy-start.4 = (bf16[256,2048]{1,0:T(8,128)(2,1)S(1)}, bf16[256,2048]{1,0:T(8,128)(2,1)}, u32[]{:S(2)}) copy-start(bf16[256,2048]{1,0:T(8,128)(2,1)} %w_ref.1) | copy-start | bytes 3145732
  102.5 17.1 %collective-permute-start.16 = (bf16[128,2048]{1,0:T(8,128)(2,1)S(1)}, bf16[128,2048]{1,0:T(8,128)(2,1)S(1)}, u32[]{:S(2)}, u32[]{:S(2)}) collective-permute-start(bf16[128,2048]{1,0:T(8,128)(2,1)S(1)} %get-tuple-element.26), channel_id=1, source_target_pairs={{0,1},{1,0},{2,3},{3,2},{4,5},{5,4},{6,7},{7,6},{8,9},{9,8},{10,11... | collective-permute-start | bytes 1572872 | tf_op jit(solution)/shard_map/ppermute | solution.py:611
  110.9 6.0 %collective-permute-start.18 = (bf16[32,2048]{1,0:T(8,128)(2,1)S(1)}, bf16[32,2048]{1,0:T(8,128)(2,1)S(1)}, u32[]{:S(2)}, u32[]{:S(2)}) collective-permute-start(bf16[32,2048]{1,0:T(8,128)(2,1)S(1)} %get-tuple-element.27), channel_id=1, source_target_pairs={{0,5},{1,4},{2,7},{3,6},{4,9},{5,8},{6,11},{7,10},{8,13},{9,12},{1... | collective-permute-start | bytes 393224 | tf_op jit(solution)/shard_map/ppermute | solution.py:665
  114.0 5.5 %collective-permute-start.17 = (bf16[32,2048]{1,0:T(8,128)(2,1)S(1)}, bf16[32,2048]{1,0:T(8,128)(2,1)S(1)}, u32[]{:S(2)}, u32[]{:S(2)}) collective-permute-start(bf16[32,2048]{1,0:T(8,128)(2,1)S(1)} %get-tuple-element.27), channel_id=1, source_target_pairs={{0,4},{1,5},{2,6},{3,7},{4,8},{5,9},{6,10},{7,11},{8,12},{9,13},{1... | collective-permute-start | bytes 393224 | tf_op jit(solution)/shard_map/ppermute | solution.py:664
  120.8 5.0 %collective-permute-start.20 = (bf16[32,512]{1,0:T(8,128)(2,1)S(1)}, bf16[32,512]{1,0:T(8,128)(2,1)S(1)}, u32[]{:S(2)}, u32[]{:S(2)}) collective-permute-start(bf16[32,512]{1,0:T(8,128)(2,1)S(1)} %get-tuple-element.30.c), channel_id=1, source_target_pairs={{0,4},{4,0},{1,5},{5,1},{2,6},{6,2},{3,7},{7,3},{8,12},{12,8},{9,1... | collective-permute-start | bytes 98312 | tf_op jit(solution)/shard_map/ppermute | solution.py:611
  123.0 2.8 %collective-permute-start.19 = (bf16[32,256]{1,0:T(8,128)(2,1)S(1)}, bf16[32,256]{1,0:T(8,128)(2,1)S(1)}, u32[]{:S(2)}, u32[]{:S(2)}) collective-permute-start(bf16[32,256]{1,0:T(8,128)(2,1)S(1)} %get-tuple-element.29.a), channel_id=1, source_target_pairs={{0,8},{8,0},{16,24},{24,16},{32,40},{40,32},{48,56},{56,48},{1,9},... | collective-permute-start | bytes 49160 | tf_op jit(solution)/shard_map/ppermute | solution.py:611
  125.8 4.9 %collective-permute-start.22 = (bf16[64,512]{1,0:T(8,128)(2,1)S(1)}, bf16[64,512]{1,0:T(8,128)(2,1)S(1)}, u32[]{:S(2)}, u32[]{:S(2)}) collective-permute-start(bf16[64,512]{1,0:T(8,128)(2,1)S(1)} %get-tuple-element.32.c), channel_id=1, source_target_pairs={{0,64},{64,0},{128,192},{192,128},{1,65},{65,1},{129,193},{193,129... | collective-permute-start | bytes 196616 | tf_op jit(solution)/shard_map/ppermute | solution.py:611
  127.0 3.7 %collective-permute-start.21 = (bf16[64,256]{1,0:T(8,128)(2,1)S(1)}, bf16[64,256]{1,0:T(8,128)(2,1)S(1)}, u32[]{:S(2)}, u32[]{:S(2)}) collective-permute-start(bf16[64,256]{1,0:T(8,128)(2,1)S(1)} %get-tuple-element.31.a), channel_id=1, source_target_pairs={{0,16},{8,24},{16,0},{24,8},{32,48},{40,56},{48,32},{56,40},{1,17}... | collective-permute-start | bytes 98312 | tf_op jit(solution)/shard_map/ppermute | solution.py:611
  130.7 10.1 %collective-permute-start.24 = (bf16[128,512]{1,0:T(8,128)(2,1)S(1)}, bf16[128,512]{1,0:T(8,128)(2,1)S(1)}, u32[]{:S(2)}, u32[]{:S(2)}) collective-permute-start(bf16[128,512]{1,0:T(8,128)(2,1)S(1)} %get-tuple-element.34.kv0), channel_id=1, source_target_pairs={{0,128},{64,192},{128,0},{192,64},{1,129},{65,193},{129,1},{193,65... | collective-permute-start | bytes 393224 | tf_op jit(solution)/shard_map/ppermute | solution.py:611
  133.8 7.0 %collective-permute-start.23 = (bf16[128,256]{1,0:T(8,128)(2,1)S(1)}, bf16[128,256]{1,0:T(8,128)(2,1)S(1)}, u32[]{:S(2)}, u32[]{:S(2)}) collective-permute-start(bf16[128,256]{1,0:T(8,128)(2,1)S(1)} %get-tuple-element.33.q0), channel_id=1, source_target_pairs={{0,32},{8,40},{16,48},{24,56},{32,0},{40,8},{48,16},{56,24},{1,33}... | collective-permute-start | bytes 196616 | tf_op jit(solution)/shard_map/ppermute | solution.py:611
  155.9 9.8 %collective-permute-start.25 = (bf16[32,512]{1,0:T(8,128)(2,1)S(1)}, bf16[32,512]{1,0:T(8,128)(2,1)S(1)}, u32[]{:S(2)}, u32[]{:S(2)}) collective-permute-start(bf16[32,512]{1,0:T(8,128)(2,1)S(1)} %get-tuple-element.36), channel_id=1, source_target_pairs={{0,1},{1,0},{2,3},{3,2},{4,5},{5,4},{6,7},{7,6},{8,9},{9,8},{10,11... | collective-permute-start | bytes 98312 | tf_op jit(solution)/shard_map/ppermute | solution.py:611
  162.5 4.3 %collective-permute-start.26 = (bf16[32,512]{1,0:T(8,128)(2,1)S(1)}, bf16[32,512]{1,0:T(8,128)(2,1)S(1)}, u32[]{:S(2)}, u32[]{:S(2)}) collective-permute-start(bf16[32,512]{1,0:T(8,128)(2,1)S(1)} %get-tuple-element.37), channel_id=1, source_target_pairs={{0,2},{1,3},{2,0},{3,1},{4,6},{5,7},{6,4},{7,5},{8,10},{9,11},{10,... | collective-permute-start | bytes 98312 | tf_op jit(solution)/shard_map/ppermute | solution.py:611
  165.2 4.9 %collective-permute-start.27 = (bf16[32,512]{1,0:T(8,128)(2,1)S(1)}, bf16[32,512]{1,0:T(8,128)(2,1)S(1)}, u32[]{:S(2)}, u32[]{:S(2)}) collective-permute-start(bf16[32,512]{1,0:T(8,128)(2,1)S(1)} %get-tuple-element.38), channel_id=1, source_target_pairs={{0,3},{1,2},{2,1},{3,0},{4,7},{5,6},{6,5},{7,4},{8,11},{9,10},{10,... | collective-permute-start | bytes 98312 | tf_op jit(solution)/shard_map/ppermute | solution.py:611

commit v4 on v3

--- a/solution.py
+++ b/solution.py
@@ -16,6 +16,7 @@
 
 VMEM = pltpu.VMEM
 SMEM = pltpu.SMEM
+HBM = pltpu.HBM
 F32 = jnp.float32
 BF16 = jnp.bfloat16
 
@@ -44,56 +45,58 @@
     return hi, mid, lo
 
 
-def project_kernel(count_ref, tok_ref, w_ref, ck_ref, cv_ref, q_ref, pack_ref, normed):
-    step = pl.program_id(0)
-    rows = tok_ref.shape[0]
-    slots = ck_ref.shape[0]
-
-    @pl.when(step == 0)
-    def _():
-        normed[...] = rms_scaled(tok_ref[...].astype(F32))
-        pack_ref[:slots] = ck_ref[...]
-        pack_ref[slots : 2 * slots] = cv_ref[...]
-        count = jnp.full((16, pack_ref.shape[1]), count_ref[0], jnp.int32)
-        pack_ref[2 * (slots + rows) :] = count.astype(F32).astype(BF16)
-
-    out = jnp.dot(normed[...], w_ref[0], preferred_element_type=F32)
-
-    @pl.when(step == 0)
-    def _():
-        q_ref[...] = (out * SCALE2).astype(BF16)
-
-    @pl.when(step == 1)
-    def _():
-        pack_ref[2 * slots : 2 * slots + rows] = out.astype(BF16)
-
-    @pl.when(step == 2)
-    def _():
-        pack_ref[2 * slots + rows : 2 * (slots + rows)] = out.astype(BF16)
+def project_kernel(
+    count_ref, tok_hbm, w_hbm, ck_hbm, cv_hbm, q_ref, pack_ref, tok, weight, sems
+):
+    rows = tok.shape[0]
+    slots = ck_hbm.shape[0]
+    width = q_ref.shape[1]
+    copies = [pltpu.make_async_copy(tok_hbm, tok, sems.at[0])]
+    copies += [
+        pltpu.make_async_copy(w_hbm.at[i], weight.at[i], sems.at[1 + i]) for i in range(3)
+    ]
+    copies += [
+        pltpu.make_async_copy(ck_hbm, pack_ref.at[:slots], sems.at[4]),
+        pltpu.make_async_copy(cv_hbm, pack_ref.at[slots : 2 * slots], sems.at[5]),
+    ]
+    for copy in copies:
+        copy.start()
+    count = jnp.full((16, width), count_ref[0], jnp.int32)
+    pack_ref[2 * (slots + rows) :] = count.astype(F32).astype(BF16)
+    copies[0].wait()
+    normed = rms_scaled(tok[...].astype(F32))
+    for i in range(3):
+        copies[1 + i].wait()
+        out = jnp.dot(normed, weight[i], preferred_element_type=F32)
+        if i == 0:
+            q_ref[...] = (out * SCALE2).astype(BF16)
+        else:
+            at = 2 * slots + (i - 1) * rows
+            pack_ref[at : at + rows] = out.astype(BF16)
+    copies[4].wait()
+    copies[5].wait()
 
 
 def project(count, rows, weight3, cache_keys, cache_values):
     n, d = rows.shape
     width = weight3.shape[2]
     total = 2 * (n + cache_keys.shape[0]) + 16
-    whole = lambda shape: pl.BlockSpec(shape, lambda i: (0, 0))
+    hbm = pl.BlockSpec(memory_space=HBM)
+    vmem = pl.BlockSpec(memory_space=VMEM)
     return pl.pallas_call(
         project_kernel,
-        grid=(3,),
-        in_specs=[
-            pl.BlockSpec(memory_space=SMEM),
-            whole((n, d)),
-            pl.BlockSpec((1, d, width), lambda i: (i, 0, 0)),
-            whole(cache_keys.shape),
-            whole(cache_values.shape),
-        ],
-        out_specs=[whole((n, width)), whole((total, width))],
+        in_specs=[pl.BlockSpec(memory_space=SMEM), hbm, hbm, hbm, hbm],
+        out_specs=[vmem, vmem],
         out_shape=[
             jax.ShapeDtypeStruct((n, width), BF16),
             jax.ShapeDtypeStruct((total, width), BF16),
         ],
-        scratch_shapes=[VMEM((n, d), BF16)],
-        compiler_params=params(12),
+        scratch_shapes=[
+            VMEM((n, d), BF16),
+            VMEM(weight3.shape, BF16),
+            pltpu.SemaphoreType.DMA((6,)),
+        ],
+        compiler_params=params(60),
         cost_estimate=cost(6 * n * d * width, 2 * (n * d + 3 * d * width)),
         name="project",
     )(count, rows, weight3, cache_keys, cache_values)
@@ -109,18 +112,31 @@
 
 def mark(q, own, other):
     n, width = q.shape
-    last = own.shape[0] // 16 - 1
     return pl.pallas_call(
         mark_kernel,
-        grid=(1,),
-        in_specs=[pl.BlockSpec((n, width), lambda i: (0, 0))]
-        + [pl.BlockSpec((16, width), lambda i: (last, 0))] * 2,
-        out_specs=pl.BlockSpec((n + 16, width), lambda i: (0, 0)),
         out_shape=jax.ShapeDtypeStruct((n + 16, width), BF16),
         compiler_params=params(8),
         cost_estimate=cost(0, 4 * n * width),
         name="mark",
     )(q, own, other)
+
+
+def halves_kernel(left_ref, right_ref, own_ref, other_ref):
+    half = own_ref.shape[0]
+    own_ref[...] = left_ref[:half]
+    other_ref[...] = right_ref[half:]
+
+
+def halves(left, right):
+    n, width = left.shape
+    out = jax.ShapeDtypeStruct((n // 2, width), BF16)
+    return pl.pallas_call(
+        halves_kernel,
+        out_shape=[out, out],
+        compiler_params=params(8),
+        cost_estimate=cost(0, 4 * n * width),
+        name="halves",
+    )(left, right)
 
 
 def join_kernel(a_ref, b_ref, out_ref):
@@ -140,14 +156,22 @@
     )(a, b)
 
 
-def plane_kernel(*refs):
+def plane_kernel(own, left, right, far, far_other, out_ref):
     rows = []
-    for pair in refs[:-1]:
-        half = pair.shape[0] // 2
-        for at in (half - 16, 2 * half - 16):
-            marks = pair[at : at + 16].astype(F32)
-            rows += [marks[:1], marks[8:9]]
-    refs[-1][...] = jnp.concatenate(rows, axis=0).astype(BF16)
+    half = far.shape[0]
+    for ref, end in (
+        (own, half),
+        (own, 2 * half),
+        (left, half),
+        (left, 2 * half),
+        (far, half),
+        (far_other, half),
+        (right, half),
+        (right, 2 * half),
+    ):
+        marks = ref[end - 16 : end].astype(F32)
+        rows += [marks[:1], marks[8:9]]
+    out_ref[...] = jnp.concatenate(rows, axis=0).astype(BF16)
 
 
 def plane_counts(queries):
@@ -196,8 +220,8 @@
 
 
 def attend_kernel(slots, slope_ref, *refs):
-    queries, planes, packs = refs[:4], refs[4:8], refs[8:16]
-    out_ref, q_tile, bias = refs[16:]
+    queries, planes, packs = refs[:5], refs[5:9], refs[9:17]
+    out_ref, q_tile, bias = refs[17:]
     tile = pl.program_id(0)
     y, z, xl = place_of_device()
     rows = q_tile.shape[0] // 2
@@ -209,12 +233,16 @@
     def side_of(other):
         return 1 - xl if other else xl
 
-    for t in range(4):
+    own, left, right, far, far_other = queries
+    step = rows + 16
+    for t, (a, b, at) in enumerate(
+        ((own, own, step), (left, left, step), (far, far_other, 0), (right, right, step))
+    ):
 
         @pl.when(tile == t)
-        def _(t=t):
-            q_tile[:rows] = queries[t][:rows]
-            q_tile[rows:] = queries[t][rows + 16 : 2 * rows + 16]
+        def _(a=a, b=b, at=at):
+            q_tile[:rows] = a[:rows]
+            q_tile[rows:] = b[at : at + rows]
 
     @pl.when(tile == 0)
     def _():
@@ -356,34 +384,58 @@
     )(parts)
 
 
-def product_kernel(tok_ref, a_ref, b_ref, wa_ref, wb_ref, sum_ref, term_ref, rim_ref):
-    term = jnp.dot(a_ref[...], wa_ref[...], preferred_element_type=F32) + jnp.dot(
-        b_ref[...], wb_ref[...], preferred_element_type=F32
-    )
-    total = tok_ref[...].astype(F32) + term
-    sum_ref[...] = total
-    term_ref[...] = term.astype(BF16)
-    rim_ref[:16] = total[-16:].astype(BF16)
-    rim_ref[16:] = term[-16:].astype(BF16)
+def product_kernel(
+    tok_hbm, a_ref, b_ref, wa_hbm, wb_hbm, sum_ref, term_ref, rim_ref, tok, wa, wb, sems
+):
+    chunks = wa.shape[0]
+    cols = wa.shape[2]
+    copies = []
+    for c in range(chunks):
+        at = pl.ds(c * cols, cols)
+        copies.append(
+            [
+                pltpu.make_async_copy(src.at[:, at], dst.at[c], sems.at[i, c])
+                for i, (src, dst) in enumerate(((wa_hbm, wa), (wb_hbm, wb), (tok_hbm, tok)))
+            ]
+        )
+    for group in copies:
+        for copy in group:
+            copy.start()
+    for c, group in enumerate(copies):
+        for copy in group:
+            copy.wait()
+        at = slice(c * cols, (c + 1) * cols)
+        term = jnp.dot(a_ref[...], wa[c], preferred_element_type=F32) + jnp.dot(
+            b_ref[...], wb[c], preferred_element_type=F32
+        )
+        total = tok[c].astype(F32) + term
+        sum_ref[:, at] = total
+        term_ref[:, at] = term.astype(BF16)
+        rim_ref[:16, at] = total[-16:].astype(BF16)
+        rim_ref[16:, at] = term[-16:].astype(BF16)
 
 
 def layer_product(tokens, atts, weights):
     rows, d = tokens.shape
-    step = 512
-    inner, width = weights[0].shape[0], atts[0].shape[1]
-    cols = lambda n: pl.BlockSpec((n, step), lambda i: (0, i))
+    chunks = 4
+    inner = weights[0].shape[0]
+    hbm = pl.BlockSpec(memory_space=HBM)
+    vmem = pl.BlockSpec(memory_space=VMEM)
     return pl.pallas_call(
         product_kernel,
-        grid=(d // step,),
-        in_specs=[cols(rows)]
-        + [pl.BlockSpec((rows, width), lambda i: (0, 0))] * 2
-        + [cols(inner)] * 2,
-        out_specs=[cols(rows), cols(rows), cols(32)],
+        in_specs=[hbm, vmem, vmem, hbm, hbm],
+        out_specs=[vmem] * 3,
         out_shape=[
             jax.ShapeDtypeStruct((rows, d), F32),
             jax.ShapeDtypeStruct((rows, d), BF16),
             jax.ShapeDtypeStruct((32, d), BF16),
         ],
+        scratch_shapes=[
+            VMEM((chunks, rows, d // chunks), BF16),
+            VMEM((chunks, inner, d // chunks), BF16),
+            VMEM((chunks, inner, d // chunks), BF16),
+            pltpu.SemaphoreType.DMA((3, chunks)),
+        ],
         compiler_params=params(16),
         cost_estimate=cost(4 * rows * d * inner, 4 * inner * d),
         name="layer_product",
@@ -391,13 +443,13 @@
 
 
 def short_project_kernel(
-    sum_ref, term_ref, rim_a, rim_b, w_ref, cols_ref, q_ref, kv_ref, normed
+    sum_ref, term_ref, rim_a, rim_b, w_ref, cols_ref, qkv_ref, normed
 ):
     step = pl.program_id(0)
     rows, d = sum_ref.shape
     groups = rows // GROUP
     rim_rows = 16
-    width = q_ref.shape[1]
+    width = w_ref.shape[2]
 
     @pl.when(step == 0)
     def _():
@@ -422,25 +474,21 @@
 
     out = jnp.dot(normed[...], w_ref[0], preferred_element_type=F32)
 
-    @pl.when(step == 0)
-    def _():
-        q_ref[...] = (out * SCALE2).astype(BF16)
-
-    @pl.when(step == 1)
-    def _():
-        kv_ref[:, :width] = out.astype(BF16)
-
-    @pl.when(step == 2)
-    def _():
-        kv_ref[:, width:] = out.astype(BF16)
-
-
-def short_project(total, term, rims, weight3):
+    scaled = jnp.where(step == 0, out * SCALE2, out).astype(BF16)
+    for i in range(3):
+
+        @pl.when(step == i)
+        def _(i=i):
+            for c in range(qkv_ref.shape[0]):
+                qkv_ref[c, :, i * width : (i + 1) * width] = scaled
+
+
+def short_project(total, term, rims, weight3, copies):
     n, d = total.shape
     groups = n // GROUP
     width = weight3.shape[2]
-    whole = lambda shape: pl.BlockSpec(shape, lambda i: (0, 0))
-    shapes = [(n, d // 4), (groups, width), (groups, 2 * width)]
+    whole = lambda shape: pl.BlockSpec(shape, lambda i: (0,) * len(shape))
+    shapes = [(n, d // 4), (copies, groups, 3 * width)]
     return pl.pallas_call(
         short_project_kernel,
         grid=(3,),
@@ -455,50 +503,43 @@
     )(total, term, *rims, weight3)
 
 
-def join_two_kernel(a, b, c, d, left, right):
-    for x, y, out in ((a, b, left), (c, d, right)):
-        out[: x.shape[0]] = x[...]
-        out[x.shape[0] :] = y[...]
-
-
-def join_two(a, b, c, d):
-    shapes = [(2 * x.shape[0], x.shape[1]) for x in (a, c)]
-    return pl.pallas_call(
-        join_two_kernel,
-        out_shape=[jax.ShapeDtypeStruct(s, BF16) for s in shapes],
+def keys_kernel(qkv_ref, out_ref):
+    width = out_ref.shape[2]
+    out_ref[...] = qkv_ref[:, :, width // 2 :]
+
+
+def keys_of(qkv):
+    blocks, groups, width = qkv.shape
+    return pl.pallas_call(
+        keys_kernel,
+        out_shape=jax.ShapeDtypeStruct((blocks, groups, width // 3 * 2), BF16),
         compiler_params=params(8),
-        cost_estimate=cost(0, 8 * (a.size + c.size)),
-        name="join_two",
-    )(a, b, c, d)
-
-
-def short_attend_kernel(slope_ref, q0, q1, kv0, kv1, out_ref):
+        cost_estimate=cost(0, 4 * qkv.size),
+        name="keys_of",
+    )(qkv)
+
+
+def short_attend_kernel(slope_ref, qkv_ref, kv_ref, out_ref):
     y, z, xl = place_of_device()
-    _, groups, _ = out_ref.shape
-    width = q0.shape[1]
+    blocks, groups, padded = out_ref.shape
+    width = padded - HS
     heads = width // HS
-    nr = nk = 8 * groups
-    row = lax.broadcasted_iota(jnp.int32, (nr, 1), 0)
-    zs = row // groups
-    row_pos = (y * 16 + zs * 2 + xl) * groups + row % groups
-    came = (zs ^ z) * groups + row % groups
-    order = jnp.where(lax.broadcasted_iota(jnp.int32, (nr, nr), 1) == came, 1.0, 0.0).astype(BF16)
-    key = lax.broadcasted_iota(jnp.int32, (1, nk), 1)
-    block = key // groups
-    key_pos = ((y ^ (block // 2)) * 16 + z * 2 + (xl ^ (block % 2))) * groups + key % groups
+    n = blocks * groups
+    row = lax.broadcasted_iota(jnp.int32, (n, 1), 0)
+    row_pos = (y * 16 + xl + 2 * (row // groups)) * groups + row % groups
+    key = lax.broadcasted_iota(jnp.int32, (1, n), 1)
+    key_pos = ((z // 2) * 16 + z % 2 + 2 * (key // groups)) * groups + key % groups
     usable = key_pos <= row_pos
     spot = key_pos.astype(F32)
-    lane = lax.broadcasted_iota(jnp.int32, (nr, HS), 1)
-    packed = jnp.zeros((nr, HS), F32)
-    queries = jnp.concatenate([q0[...], q1[...]], axis=0)
-    queries = jnp.dot(order, queries, preferred_element_type=F32).astype(BF16)
+    lane = lax.broadcasted_iota(jnp.int32, (n, HS), 1)
+    packed = jnp.zeros((n, HS), F32)
     outs = []
     for h in range(heads):
         cols = slice(h * HS, (h + 1) * HS)
-        k = jnp.concatenate([kv0[:, cols], kv1[:, cols]], axis=0)
-        cols_v = slice(width + h * HS, width + (h + 1) * HS)
-        v = jnp.concatenate([kv0[:, cols_v], kv1[:, cols_v]], axis=0)
-        s = dot_t(queries[:, cols], k) + (slope_ref[h] * LOG2E) * spot
+        q = qkv_ref[:, :, cols].reshape(n, HS)
+        k = kv_ref[:, :, cols].reshape(n, HS)
+        v = kv_ref[:, :, width + h * HS : width + (h + 1) * HS].reshape(n, HS)
+        s = dot_t(q, k) + (slope_ref[h] * LOG2E) * spot
         s = jnp.where(usable, s, NEG)
         top = jnp.max(s, axis=1, keepdims=True)
         p = jnp.exp2(s - top).astype(BF16)
@@ -512,20 +553,21 @@
     out_ref[...] = out.reshape(out_ref.shape)
 
 
-def short_attend(slopes, q0, q1, kv0, kv1):
-    n, width = q0.shape
-    groups = n // 4
+def short_attend(slopes, qkv, kv):
+    blocks, groups, width3 = qkv.shape
+    width = width3 // 3
+    n = blocks * groups
     smem = pl.BlockSpec(memory_space=SMEM)
     vmem = pl.BlockSpec(memory_space=VMEM)
     return pl.pallas_call(
         short_attend_kernel,
-        in_specs=[smem] + [vmem] * 4,
+        in_specs=[smem, vmem, vmem],
         out_specs=vmem,
-        out_shape=jax.ShapeDtypeStruct((8, groups, width + HS), BF16),
+        out_shape=jax.ShapeDtypeStruct((blocks, groups, width + HS), BF16),
         compiler_params=params(16),
-        cost_estimate=cost(16 * n * n * width, 8 * n * width),
+        cost_estimate=cost(4 * n * n * width, 8 * n * width),
         name="short_attend",
-    )(slopes, q0, q1, kv0, kv1)
+    )(slopes, qkv, kv)
 
 
 def short_merge_kernel(heads, parts_ref, w_ref, *outs):
@@ -616,8 +658,21 @@
     return lax.ppermute(x, axis, [(i, (i + by) % n) for i in range(n)])
 
 
-def both_ways(x):
-    return moved(x, "y", 1), moved(x, "y", -1)
+def both_ways(x, axis, by):
+    return moved(x, axis, by), moved(x, axis, -by)
+
+
+def across(block):
+    ny, nz, nx = (lax.axis_size(a) for a in ("y", "z", "xl"))
+    assert ny * nx == nz
+    pairs = []
+    for y in range(ny):
+        for z in range(nz):
+            for x in range(nx):
+                line = y * nx + x
+                to = ((z // nx) * nz + line) * nx + z % nx
+                pairs.append(((y * nz + z) * nx + x, to))
+    return lax.ppermute(block, ("y", "z", "xl"), pairs)
 
 
 def after(x, *others):
@@ -638,21 +693,29 @@
 ):
     axes = ("y", "z", "xl", "tp")
     slots = cache_keys.shape[0]
+    count = jnp.broadcast_to(cache_count.astype(BF16)[None], (16, cache_keys.shape[1]))
+    other_count = swap(count, "xl")
     q, pack = project(
         cache_count, tokens, jnp.transpose(project_weight, (1, 0, 2)), cache_keys, cache_values
     )
-    other = swap(pack, "xl")
-    left, right = both_ways(pack)
-    marked = mark(q, pack, other)
-    pair = join(marked, swap(marked, "z"))
-    left_other, right_other = both_ways(other)
-    queries = [pair] + [moved(pair, "z", by) for by in (2, 4, 6)]
+    q, pack, other_count = lax.optimization_barrier((q, pack, other_count))
+    marked = mark(q, count, other_count)
+    left, right = both_ways(pack, "y", 1)
+    other, left, right, mate = lax.optimization_barrier(
+        (swap(pack, "xl"), left, right, swap(marked, "z"))
+    )
+    left_other, right_other = both_ways(other, "y", 1)
+    pair = join(marked, mate)
+    left_pair, right_pair = both_ways(pair, "z", 2)
+    near = halves(left_pair, right_pair)
+    queries = [pair, left_pair, right_pair, moved(near[0], "z", 2), moved(near[1], "z", -2)]
     far, far_other = moved(left, "y", 1), moved(right_other, "y", -1)
     crossed = swap(after(output_weight, other), "tp", 2)
     plane = plane_counts(queries)
     planes = [plane] + [moved(plane, "y", by) for by in (1, 2, 3)]
     packs = [pack, other, left, left_other, right, right_other, far, far_other]
     parts = attend(distance_slope, queries, planes, packs, slots)
+    parts, crossed = lax.optimization_barrier((parts, crossed))
 
     att = merge(exchange(parts, "z"))
     total, term, rim = layer_product(
@@ -664,14 +727,15 @@
         lax.ppermute(rim, axes, ahead),
         lax.ppermute(rim, axes, [(i, j ^ 1) for i, j in ahead]),
     ]
-    layer, sq, skv = short_project(
-        total, swap(term, "tp", 1), rims, jnp.transpose(short_project_weight, (1, 0, 2))
+    layer, qkv = short_project(
+        total,
+        swap(term, "tp", 1),
+        rims,
+        jnp.transpose(short_project_weight, (1, 0, 2)),
+        lax.axis_size("z"),
     )
-    sq, skv = join_two(sq, swap(sq, "z"), skv, swap(skv, "xl"))
-    sq, skv = join_two(sq, swap(sq, "z", 2), skv, swap(skv, "y"))
-    sparts = short_attend(
-        short_slope, sq, swap(sq, "z", 4), skv, swap(skv, "y", 2)
-    )
+    qkv = exchange(qkv, "z")
+    sparts = short_attend(short_slope, qkv, across(keys_of(qkv)))
     terms = short_merge(exchange(sparts, "z"), short_output)
     terms = [swap(t, "tp", flip) if flip else t for flip, t in enumerate(terms)]
     return final_sum(layer, terms)

time: 171 us -> 194 us (1.13)
  blocking collectives: 13.4 us -> 74.6 us
  starting transfers between devices: 74.7 us -> 50.4 us
  waiting for transfers between devices: 51.6 us -> 42.6 us
  local copies, waits for them, and re-layouts: 7.82 us -> 1.86 us
    all_to_all x1 -> x3, blocking collectives: 13.4 us -> 74.6 us  [exchange(): return lax.all_to_all(blocks, axis, 0, 0)]
    ppermute x12 -> x13, waiting for transfers between devices: 14.5 us -> 31.5 us  [moved(): return lax.ppermute(x, axis, [(i, (i + by) % n) for i in range(n)])]
    ppermute x14 -> x9, waiting for transfers between devices: 24 us -> 8.73 us  [swap(): lax.ppermute(x, axis, [(i, i ^ flip) for i in range(lax.axis_size(axis))])]
    ppermute x14 -> x9, starting transfers between devices: 39.3 us -> 26.5 us  [swap(): lax.ppermute(x, axis, [(i, i ^ flip) for i in range(lax.axis_size(axis))])]
    all_to_all x1 -> x0, waiting for transfers between devices: 10.2 us -> none  [exchange(): return lax.all_to_all(blocks, axis, 0, 0)]
    all_to_all x1 -> x0, starting transfers between devices: 7.37 us -> none  [exchange(): return lax.all_to_all(blocks, axis, 0, 0)]
    unnamed x22 -> x16, local copies, waits for them, and re-layouts: 7.82 us -> 1.86 us
    ppermute x12 -> x13, starting transfers between devices: 22.3 us -> 18.1 us  [moved(): return lax.ppermute(x, axis, [(i, (i + by) % n) for i in range(n)])]
  transfers between devices with their start and end apart: 29 -> 25, of which waited for: 17 -> 13; matrix products, arithmetic and copies ran while one was open for 0% -> 0% of each run, Pallas kernels for 1% -> 8%
where the time goes in v4:
time: 194 us; the launch traced here: 193 us
  blocking collectives  74.6 us (38%)
  starting transfers between devices  50.4 us (26%)
  waiting for transfers between devices  42.6 us (22%)
  Pallas kernels  22.2 us (11%)
    all_to_all x3, blocking collectives, exchange(): return lax.all_to_all(blocks, axis, 0, 0)  74.6 us
    ppermute x13, waiting for transfers between devices, moved(): return lax.ppermute(x, axis, [(i, (i + by) % n) for i in range(n)])  31.5 us
    ppermute x9, starting transfers between devices, swap(): lax.ppermute(x, axis, [(i, i ^ flip) for i in range(lax.axis_size(axis))])  26.5 us
    ppermute x13, starting transfers between devices, moved(): return lax.ppermute(x, axis, [(i, (i + by) % n) for i in range(n)])  18.1 us
    pallas_call x1, Pallas kernels, attend(): pl.pallas_call(functools.partial(attend_kernel, slots), grid=(4,), in_spe...  12.5 us
    ppermute x9, waiting for transfers between devices, swap(): lax.ppermute(x, axis, [(i, i ^ flip) for i in range(lax.axis_size(axis))])  8.73 us
  transfers between devices with their start and end apart: 25, of which 13 were waited for; matrix products, arithmetic and copies ran while one was open for 0% of the time, Pallas kernels for 8%

profile of v4, /device:TPU:1, one launch (start us, length us, event | category | flops | bytes accessed | tf_op | source)
XLA Modules:
  0.0 192.7 jit_solution(15547466598467204630)
XLA Ops:
  0.8 2.1 %collective-permute-start = (bf16[16,256]{1,0:T(8,128)(2,1)S(1)}, bf16[16,256]{1,0:T(8,128)(2,1)S(1)}, u32[]{:S(2)}, u32[]{:S(2)}) collective-permute-start(bf16[16,256]{1,0:T(8,128)(2,1)S(1)} %broadcast_in_dim.9.own_ref), channel_id=1, source_target_pairs={{0,4},{4,0},{1,5},{5,1},{2,6},{6,2},{3,7},{7,3},{8,12},{12,8},{9,1... | collective-permute-start | bytes 24584 | tf_op jit(solution)/shard_map/ppermute | solution.py:653
  2.9 3.4 %project.1 = (bf16[128,256]{1,0:T(8,128)(2,1)}, bf16[784,256]{1,0:T(8,128)(2,1)}) custom-call(s32[1]{0:T(128)S(6)} %copy.11.count_ref, bf16[128,2048]{1,0:T(8,128)(2,1)} %tok_hbm.3, bf16[3,2048,256]{2,1,0:T(8,128)(2,1)} %bitcast.4, bf16[256,256]{1,0:T(8,128)(2,1)} %ck_hbm.1, bf16[256,256]{1,0:T(8,128)(2,1)} %cv_hbm.1), custom_call_target="tpu_custom_call" | custom-call | flops 402653184 | bytes 3670016 | tf_op jit(solution)/shard_map/project/pallas_call | solution.py:86
  6.3 2.8 %collective-permute-start.3 = (bf16[784,256]{1,0:T(8,128)(2,1)}, bf16[784,256]{1,0:T(8,128)(2,1)S(1)}, u32[]{:S(2)}, u32[]{:S(2)}) collective-permute-start(bf16[784,256]{1,0:T(8,128)(2,1)} %get-tuple-element.32.refs_9_), channel_id=1, source_target_pairs={{0,192},{64,0},{128,64},{192,128},{1,193},{65,1},{129,65},{193,129... | collective-permute-start | bytes 1204232 | tf_op jit(solution)/shard_map/ppermute | solution.py:658
  9.1 0.3 collective-permute-start.1
  9.3 0.8 copy-done.4
  10.2 1.6 collective-permute-start.4
  11.8 2.0 %collective-permute-done.4.b_ref = bf16[144,256]{1,0:T(8,128)(2,1)S(1)} collective-permute-done((bf16[144,256]{1,0:T(8,128)(2,1)S(1)}, bf16[144,256]{1,0:T(8,128)(2,1)S(1)}, u32[]{:S(2)}, u32[]{:S(2)}) %collective-permute-start.4) | collective-permute-done | bytes 73760 | tf_op jit(solution)/shard_map/ppermute | solution.py:653
  13.9 3.2 %collective-permute-done.3.refs_13_ = bf16[784,256]{1,0:T(8,128)(2,1)S(1)} collective-permute-done((bf16[784,256]{1,0:T(8,128)(2,1)}, bf16[784,256]{1,0:T(8,128)(2,1)S(1)}, u32[]{:S(2)}, u32[]{:S(2)}) %collective-permute-start.3) | collective-permute-done | bytes 401440 | tf_op jit(solution)/shard_map/ppermute | solution.py:658
  17.0 3.0 %collective-permute-done.2.refs_11_ = bf16[784,256]{1,0:T(8,128)(2,1)S(1)} collective-permute-done((bf16[784,256]{1,0:T(8,128)(2,1)}, bf16[784,256]{1,0:T(8,128)(2,1)S(1)}, u32[]{:S(2)}, u32[]{:S(2)}) %collective-permute-start.2) | collective-permute-done | bytes 401440 | tf_op jit(solution)/shard_map/ppermute | solution.py:658
  20.1 1.2 collective-permute-start.13
  21.2 2.5 %collective-permute-start.16 = (bf16[256,2048]{1,0:T(8,128)(2,1)S(1)}, bf16[256,2048]{1,0:T(8,128)(2,1)S(1)}, u32[]{:S(2)}, u32[]{:S(2)}) collective-permute-start(bf16[256,2048]{1,0:T(8,128)(2,1)S(1)} %copy-done.3), channel_id=1, source_target_pairs={{0,2},{1,3},{2,0},{3,1},{4,6},{5,7},{6,4},{7,5},{8,10},{9,11},{10,... | collective-permute-start | bytes 3145736 | tf_op jit(solution)/shard_map/ppermute | solution.py:653
  23.7 6.1 %collective-permute-start.6 = (bf16[288,256]{1,0:T(8,128)(2,1)S(1)}, bf16[288,256]{1,0:T(8,128)(2,1)S(1)}, u32[]{:S(2)}, u32[]{:S(2)}) collective-permute-start(bf16[288,256]{1,0:T(8,128)(2,1)S(1)} %join.1.own.refs_0_), channel_id=1, source_target_pairs={{0,48},{8,56},{16,0},{24,8},{32,16},{40,24},{48,32},{56,40},{1,49}... | collective-permute-start | bytes 442376 | tf_op jit(solution)/shard_map/ppermute | solution.py:658
  29.8 0.3 collective-permute-start.12
  30.1 2.6 %collective-permute-start.15 = (bf16[784,256]{1,0:T(8,128)(2,1)S(1)}, bf16[784,256]{1,0:T(8,128)(2,1)S(1)}, u32[]{:S(2)}, u32[]{:S(2)}) collective-permute-start(bf16[784,256]{1,0:T(8,128)(2,1)S(1)} %collective-permute-done.13.refs_14_), channel_id=1, source_target_pairs={{0,192},{64,0},{128,64},{192,128},{1,193},{65,1},{129,65},{193,129... | collective-permute-start | bytes 1204232 | tf_op jit(solution)/shard_map/ppermute | solution.py:658
  32.8 2.6 %collective-permute-start.5 = (bf16[288,256]{1,0:T(8,128)(2,1)S(1)}, bf16[288,256]{1,0:T(8,128)(2,1)S(1)}, u32[]{:S(2)}, u32[]{:S(2)}) collective-permute-start(bf16[288,256]{1,0:T(8,128)(2,1)S(1)} %join.1.own.refs_0_), channel_id=1, source_target_pairs={{0,16},{8,24},{16,32},{24,40},{32,48},{40,56},{48,0},{56,8},{1,17}... | collective-permute-start | bytes 442376 | tf_op jit(solution)/shard_map/ppermute | solution.py:658
  35.4 6.3 %collective-permute-done.5.left_ref.left.refs_1_ = bf16[288,256]{1,0:T(8,128)(2,1)S(1)} collective-permute-done((bf16[288,256]{1,0:T(8,128)(2,1)S(1)}, bf16[288,256]{1,0:T(8,128)(2,1)S(1)}, u32[]{:S(2)}, u32[]{:S(2)}) %collective-permute-start.5) | collective-permute-done | bytes 147488 | tf_op jit(solution)/shard_map/ppermute | solution.py:658
  41.7 0.1 collective-permute-start.7
  41.9 6.1 %collective-permute-done.7.far.refs_3_ = bf16[144,256]{1,0:T(8,128)(2,1)S(1)} collective-permute-done((bf16[144,256]{1,0:T(8,128)(2,1)S(1)}, bf16[144,256]{1,0:T(8,128)(2,1)S(1)}, u32[]{:S(2)}, u32[]{:S(2)}) %collective-permute-start.7) | collective-permute-done | bytes 73760 | tf_op jit(solution)/shard_map/ppermute | solution.py:658
  47.9 1.7 collective-permute-start.8
  49.7 3.2 %collective-permute-done.8.far_other.refs_4_ = bf16[144,256]{1,0:T(8,128)(2,1)S(1)} collective-permute-done((bf16[144,256]{1,0:T(8,128)(2,1)S(1)}, bf16[144,256]{1,0:T(8,128)(2,1)S(1)}, u32[]{:S(2)}, u32[]{:S(2)}) %collective-permute-start.8) | collective-permute-done | bytes 73760 | tf_op jit(solution)/shard_map/ppermute | solution.py:658
  53.0 2.5 %collective-permute-done.11.refs_8_ = bf16[16,256]{1,0:T(8,128)(2,1)S(1)} collective-permute-done((bf16[16,256]{1,0:T(8,128)(2,1)S(1)}, bf16[16,256]{1,0:T(8,128)(2,1)S(1)}, u32[]{:S(2)}, u32[]{:S(2)}) %collective-permute-start.11) | collective-permute-done | bytes 8224 | tf_op jit(solution)/shard_map/ppermute | solution.py:658
  55.4 0.3 collective-permute-start.10
  55.7 3.7 %collective-permute-done.10.refs_7_ = bf16[16,256]{1,0:T(8,128)(2,1)S(1)} collective-permute-done((bf16[16,256]{1,0:T(8,128)(2,1)S(1)}, bf16[16,256]{1,0:T(8,128)(2,1)S(1)}, u32[]{:S(2)}, u32[]{:S(2)}) %collective-permute-start.10) | collective-permute-done | bytes 8224 | tf_op jit(solution)/shard_map/ppermute | solution.py:658
  59.5 0.2 collective-permute-start.9
  59.6 3.5 %collective-permute-done.9.refs_6_ = bf16[16,256]{1,0:T(8,128)(2,1)S(1)} collective-permute-done((bf16[16,256]{1,0:T(8,128)(2,1)S(1)}, bf16[16,256]{1,0:T(8,128)(2,1)S(1)}, u32[]{:S(2)}, u32[]{:S(2)}) %collective-permute-start.9) | collective-permute-done | bytes 8224 | tf_op jit(solution)/shard_map/ppermute | solution.py:658
  63.2 1.0 copy-done.6
  64.2 12.5 %attend.1 = bf16[8,144,256]{2,1,0:T(8,128)(2,1)S(1)} custom-call(f32[2]{0:T(128)S(1)} %copy-done.7, bf16[288,256]{1,0:T(8,128)(2,1)S(1)} %join.1.own.refs_0_, bf16[288,256]{1,0:T(8,128)(2,1)S(1)} %collective-permute-done.5.left_ref.left.refs_1_, bf16[288,256]{1,0:T(8,128)(2,1)S(1)} %collective-permute-done.6.right_ref.right.refs_2_, ...), custom_call_target="tpu_custom_call" | custom-call | flops 3221225472 | bytes 3145728 | tf_op jit(solution)/shard_map/attend/pallas_call | solution.py:336
  76.7 18.3 %all_to_all.15.parts_ref = bf16[8,144,256]{2,1,0:T(8,128)(2,1)S(1)} all-to-all(bf16[8,144,256]{2,1,0:T(8,128)(2,1)S(1)} %attend.1), channel_id=1, replica_groups=mesh['y'=4,'z'=8,'xl'=2,'tp'=4] {'z'}, dimensions={0} | all-to-all | bytes 1179648 | tf_op jit(solution)/shard_map/all_to_all | solution.py:649
  95.0 1.2 merge.1.a_ref
  96.2 1.7 collective-permute-start.17
  97.9 3.3 %collective-permute-done.17.b_ref = bf16[128,256]{1,0:T(8,128)(2,1)S(1)} collective-permute-done((bf16[128,256]{1,0:T(8,128)(2,1)S(1)}, bf16[128,256]{1,0:T(8,128)(2,1)S(1)}, u32[]{:S(2)}, u32[]{:S(2)}) %collective-permute-start.17) | collective-permute-done | bytes 65568 | tf_op jit(solution)/shard_map/ppermute | solution.py:653
  101.2 1.3 layer_product.1
  102.5 12.2 %collective-permute-start.18 = (bf16[128,2048]{1,0:T(8,128)(2,1)S(1)}, bf16[128,2048]{1,0:T(8,128)(2,1)S(1)}, u32[]{:S(2)}, u32[]{:S(2)}) collective-permute-start(bf16[128,2048]{1,0:T(8,128)(2,1)S(1)} %get-tuple-element.43), channel_id=1, source_target_pairs={{0,1},{1,0},{2,3},{3,2},{4,5},{5,4},{6,7},{7,6},{8,9},{9,8},{10,11... | collective-permute-start | bytes 1572872 | tf_op jit(solution)/shard_map/ppermute | solution.py:653
  114.7 2.0 %collective-permute-start.20 = (bf16[32,2048]{1,0:T(8,128)(2,1)S(1)}, bf16[32,2048]{1,0:T(8,128)(2,1)S(1)}, u32[]{:S(2)}, u32[]{:S(2)}) collective-permute-start(bf16[32,2048]{1,0:T(8,128)(2,1)S(1)} %get-tuple-element.44), channel_id=1, source_target_pairs={{0,5},{1,4},{2,7},{3,6},{4,9},{5,8},{6,11},{7,10},{8,13},{9,12},{1... | collective-permute-start | bytes 393224 | tf_op jit(solution)/shard_map/ppermute | solution.py:728
  116.8 3.2 %collective-permute-start.19 = (bf16[32,2048]{1,0:T(8,128)(2,1)S(1)}, bf16[32,2048]{1,0:T(8,128)(2,1)S(1)}, u32[]{:S(2)}, u32[]{:S(2)}) collective-permute-start(bf16[32,2048]{1,0:T(8,128)(2,1)S(1)} %get-tuple-element.44), channel_id=1, source_target_pairs={{0,4},{1,5},{2,6},{3,7},{4,8},{5,9},{6,10},{7,11},{8,12},{9,13},{1... | collective-permute-start | bytes 393224 | tf_op jit(solution)/shard_map/ppermute | solution.py:727
  119.9 2.3 %collective-permute-done.19.rim_a = bf16[32,2048]{1,0:T(8,128)(2,1)S(1)} collective-permute-done((bf16[32,2048]{1,0:T(8,128)(2,1)S(1)}, bf16[32,2048]{1,0:T(8,128)(2,1)S(1)}, u32[]{:S(2)}, u32[]{:S(2)}) %collective-permute-start.19) | collective-permute-done | bytes 131104 | tf_op jit(solution)/shard_map/ppermute | solution.py:727
  122.3 1.3 short_project.1
  123.6 18.7 %all_to_all.16.qkv_ref = bf16[8,32,768]{2,1,0:T(8,128)(2,1)S(1)} all-to-all(bf16[8,32,768]{2,1,0:T(8,128)(2,1)S(1)} %get-tuple-element.46), channel_id=1, replica_groups=mesh['y'=4,'z'=8,'xl'=2,'tp'=4] {'z'}, dimensions={0} | all-to-all | bytes 786432 | tf_op jit(solution)/shard_map/all_to_all | solution.py:649
  142.3 0.7 collective-permute-start.21
  143.0 1.0 short_attend.1
  144.1 37.6 %all_to_all.17.parts_ref = bf16[8,32,384]{2,1,0:T(8,128)(2,1)S(1)} all-to-all(bf16[8,32,384]{2,1,0:T(8,128)(2,1)S(1)} %short_attend.1), channel_id=1, replica_groups=mesh['y'=4,'z'=8,'xl'=2,'tp'=4] {'z'}, dimensions={0} | all-to-all | bytes 393216 | tf_op jit(solution)/shard_map/all_to_all | solution.py:649
  181.7 0.5 short_merge.1
  182.2 2.9 %collective-permute-start.22 = (bf16[32,512]{1,0:T(8,128)(2,1)S(1)}, bf16[32,512]{1,0:T(8,128)(2,1)S(1)}, u32[]{:S(2)}, u32[]{:S(2)}) collective-permute-start(bf16[32,512]{1,0:T(8,128)(2,1)S(1)} %get-tuple-element.48), channel_id=1, source_target_pairs={{0,1},{1,0},{2,3},{3,2},{4,5},{5,4},{6,7},{7,6},{8,9},{9,8},{10,11... | collective-permute-start | bytes 98312 | tf_op jit(solution)/shard_map/ppermute | solution.py:653
  185.1 1.7 collective-permute-start.23
  186.9 1.5 collective-permute-start.24
  188.4 1.0 collective-permute-done.23.refs_2_
  189.4 2.3 %collective-permute-done.24.refs_3_ = bf16[32,512]{1,0:T(8,128)(2,1)S(1)} collective-permute-done((bf16[32,512]{1,0:T(8,128)(2,1)S(1)}, bf16[32,512]{1,0:T(8,128)(2,1)S(1)}, u32[]{:S(2)}, u32[]{:S(2)}) %collective-permute-start.24) | collective-permute-done | bytes 32800 | tf_op jit(solution)/shard_map/ppermute | solution.py:653
  191.7 0.9 final_sum.1
  (35 shorter events, 0.2 us)
Async XLA Ops:
  0.0 21.2 %copy-start.3 = (bf16[256,2048]{1,0:T(8,128)(2,1)S(1)}, bf16[256,2048]{1,0:T(8,128)(2,1)}, u32[]{:S(2)}) copy-start(bf16[256,2048]{1,0:T(8,128)(2,1)} %wa_hbm.1) | copy-start | bytes 3145732
  0.0 63.2 %copy-start.7 = (f32[2]{0:T(128)S(1)}, f32[2]{0:T(128)}, u32[]{:S(2)}) copy-start(f32[2]{0:T(128)} %slope_ref.2) | copy-start | bytes 28
  0.8 5.5 %collective-permute-start = (bf16[16,256]{1,0:T(8,128)(2,1)S(1)}, bf16[16,256]{1,0:T(8,128)(2,1)S(1)}, u32[]{:S(2)}, u32[]{:S(2)}) collective-permute-start(bf16[16,256]{1,0:T(8,128)(2,1)S(1)} %broadcast_in_dim.9.own_ref), channel_id=1, source_target_pairs={{0,4},{4,0},{1,5},{5,1},{2,6},{6,2},{3,7},{7,3},{8,12},{12,8},{9,1... | collective-permute-start | bytes 24584 | tf_op jit(solution)/shard_map/ppermute | solution.py:653
  6.3 10.8 %collective-permute-start.3 = (bf16[784,256]{1,0:T(8,128)(2,1)}, bf16[784,256]{1,0:T(8,128)(2,1)S(1)}, u32[]{:S(2)}, u32[]{:S(2)}) collective-permute-start(bf16[784,256]{1,0:T(8,128)(2,1)} %get-tuple-element.32.refs_9_), channel_id=1, source_target_pairs={{0,192},{64,0},{128,64},{192,128},{1,193},{65,1},{129,65},{193,129... | collective-permute-start | bytes 1204232 | tf_op jit(solution)/shard_map/ppermute | solution.py:658
  9.1 11.0 %collective-permute-start.2 = (bf16[784,256]{1,0:T(8,128)(2,1)}, bf16[784,256]{1,0:T(8,128)(2,1)S(1)}, u32[]{:S(2)}, u32[]{:S(2)}) collective-permute-start(bf16[784,256]{1,0:T(8,128)(2,1)} %get-tuple-element.32.refs_9_), channel_id=1, source_target_pairs={{0,64},{64,128},{128,192},{192,0},{1,65},{65,129},{129,193},{193,1... | collective-permute-start | bytes 1204232 | tf_op jit(solution)/shard_map/ppermute | solution.py:658
  9.1 11.0 %collective-permute-start.1 = (bf16[784,256]{1,0:T(8,128)(2,1)}, bf16[784,256]{1,0:T(8,128)(2,1)S(1)}, u32[]{:S(2)}, u32[]{:S(2)}) collective-permute-start(bf16[784,256]{1,0:T(8,128)(2,1)} %get-tuple-element.32.refs_9_), channel_id=1, source_target_pairs={{0,4},{4,0},{1,5},{5,1},{2,6},{6,2},{3,7},{7,3},{8,12},{12,8},{9,1... | collective-permute-start | bytes 1204232 | tf_op jit(solution)/shard_map/ppermute | solution.py:653
  9.3 0.8 copy-start.4
  10.2 3.7 %collective-permute-start.4 = (bf16[144,256]{1,0:T(8,128)(2,1)S(1)}, bf16[144,256]{1,0:T(8,128)(2,1)S(1)}, u32[]{:S(2)}, u32[]{:S(2)}) collective-permute-start(bf16[144,256]{1,0:T(8,128)(2,1)S(1)} %mark.1.a_ref), channel_id=1, source_target_pairs={{0,8},{8,0},{16,24},{24,16},{32,40},{40,32},{48,56},{56,48},{1,9},... | collective-permute-start | bytes 221192 | tf_op jit(solution)/shard_map/ppermute | solution.py:653
  20.1 10.1 %collective-permute-start.13 = (bf16[784,256]{1,0:T(8,128)(2,1)S(1)}, bf16[784,256]{1,0:T(8,128)(2,1)S(1)}, u32[]{:S(2)}, u32[]{:S(2)}) collective-permute-start(bf16[784,256]{1,0:T(8,128)(2,1)S(1)} %collective-permute-done.1.refs_10_), channel_id=1, source_target_pairs={{0,192},{64,0},{128,64},{192,128},{1,193},{65,1},{129,65},{193,129... | collective-permute-start | bytes 1204232 | tf_op jit(solution)/shard_map/ppermute | solution.py:658
  21.2 55.4 %collective-permute-start.16 = (bf16[256,2048]{1,0:T(8,128)(2,1)S(1)}, bf16[256,2048]{1,0:T(8,128)(2,1)S(1)}, u32[]{:S(2)}, u32[]{:S(2)}) collective-permute-start(bf16[256,2048]{1,0:T(8,128)(2,1)S(1)} %copy-done.3), channel_id=1, source_target_pairs={{0,2},{1,3},{2,0},{3,1},{4,6},{5,7},{6,4},{7,5},{8,10},{9,11},{10,... | collective-permute-start | bytes 3145736 | tf_op jit(solution)/shard_map/ppermute | solution.py:653
  23.7 9.1 %collective-permute-start.6 = (bf16[288,256]{1,0:T(8,128)(2,1)S(1)}, bf16[288,256]{1,0:T(8,128)(2,1)S(1)}, u32[]{:S(2)}, u32[]{:S(2)}) collective-permute-start(bf16[288,256]{1,0:T(8,128)(2,1)S(1)} %join.1.own.refs_0_), channel_id=1, source_target_pairs={{0,48},{8,56},{16,0},{24,8},{32,16},{40,24},{48,32},{56,40},{1,49}... | collective-permute-start | bytes 442376 | tf_op jit(solution)/shard_map/ppermute | solution.py:658
  29.8 33.4 %collective-permute-start.12 = (bf16[784,256]{1,0:T(8,128)(2,1)S(1)}, bf16[784,256]{1,0:T(8,128)(2,1)S(1)}, u32[]{:S(2)}, u32[]{:S(2)}) collective-permute-start(bf16[784,256]{1,0:T(8,128)(2,1)S(1)} %collective-permute-done.1.refs_10_), channel_id=1, source_target_pairs={{0,64},{64,128},{128,192},{192,0},{1,65},{65,129},{129,193},{193,1... | collective-permute-start | bytes 1204232 | tf_op jit(solution)/shard_map/ppermute | solution.py:658
  30.1 33.1 %collective-permute-start.14 = (bf16[784,256]{1,0:T(8,128)(2,1)S(1)}, bf16[784,256]{1,0:T(8,128)(2,1)S(1)}, u32[]{:S(2)}, u32[]{:S(2)}) collective-permute-start(bf16[784,256]{1,0:T(8,128)(2,1)S(1)} %collective-permute-done.2.refs_11_), channel_id=1, source_target_pairs={{0,64},{64,128},{128,192},{192,0},{1,65},{65,129},{129,193},{193,1... | collective-permute-start | bytes 1204232 | tf_op jit(solution)/shard_map/ppermute | solution.py:658
  30.1 33.0 %collective-permute-start.15 = (bf16[784,256]{1,0:T(8,128)(2,1)S(1)}, bf16[784,256]{1,0:T(8,128)(2,1)S(1)}, u32[]{:S(2)}, u32[]{:S(2)}) collective-permute-start(bf16[784,256]{1,0:T(8,128)(2,1)S(1)} %collective-permute-done.13.refs_14_), channel_id=1, source_target_pairs={{0,192},{64,0},{128,64},{192,128},{1,193},{65,1},{129,65},{193,129... | collective-permute-start | bytes 1204232 | tf_op jit(solution)/shard_map/ppermute | solution.py:658
  32.8 8.9 %collective-permute-start.5 = (bf16[288,256]{1,0:T(8,128)(2,1)S(1)}, bf16[288,256]{1,0:T(8,128)(2,1)S(1)}, u32[]{:S(2)}, u32[]{:S(2)}) collective-permute-start(bf16[288,256]{1,0:T(8,128)(2,1)S(1)} %join.1.own.refs_0_), channel_id=1, source_target_pairs={{0,16},{8,24},{16,32},{24,40},{32,48},{40,56},{48,0},{56,8},{1,17}... | collective-permute-start | bytes 442376 | tf_op jit(solution)/shard_map/ppermute | solution.py:658
  41.7 6.2 %collective-permute-start.7 = (bf16[144,256]{1,0:T(8,128)(2,1)S(1)}, bf16[144,256]{1,0:T(8,128)(2,1)S(1)}, u32[]{:S(2)}, u32[]{:S(2)}) collective-permute-start(bf16[144,256]{1,0:T(8,128)(2,1)S(1)} %get-tuple-element.34), channel_id=1, source_target_pairs={{0,16},{8,24},{16,32},{24,40},{32,48},{40,56},{48,0},{56,8},{1,17}... | collective-permute-start | bytes 221192 | tf_op jit(solution)/shard_map/ppermute | solution.py:658
  47.9 4.9 %collective-permute-start.8 = (bf16[144,256]{1,0:T(8,128)(2,1)S(1)}, bf16[144,256]{1,0:T(8,128)(2,1)S(1)}, u32[]{:S(2)}, u32[]{:S(2)}) collective-permute-start(bf16[144,256]{1,0:T(8,128)(2,1)S(1)} %get-tuple-element.35), channel_id=1, source_target_pairs={{0,48},{8,56},{16,0},{24,8},{32,16},{40,24},{48,32},{56,40},{1,49}... | collective-permute-start | bytes 221192 | tf_op jit(solution)/shard_map/ppermute | solution.py:658
  52.9 48.3 %copy-start.1 = (bf16[128,2048]{1,0:T(8,128)(2,1)S(1)}, bf16[128,2048]{1,0:T(8,128)(2,1)}, u32[]{:S(2)}) copy-start(bf16[128,2048]{1,0:T(8,128)(2,1)} %tok_hbm.3) | copy-start | bytes 1572868
  52.9 2.6 %collective-permute-start.11 = (bf16[16,256]{1,0:T(8,128)(2,1)S(1)}, bf16[16,256]{1,0:T(8,128)(2,1)S(1)}, u32[]{:S(2)}, u32[]{:S(2)}) collective-permute-start(bf16[16,256]{1,0:T(8,128)(2,1)S(1)} %plane_counts.1.refs_5_), channel_id=1, source_target_pairs={{0,192},{64,0},{128,64},{192,128},{1,193},{65,1},{129,65},{193,129... | collective-permute-start | bytes 24584 | tf_op jit(solution)/shard_map/ppermute | solution.py:658
  55.4 4.0 %collective-permute-start.10 = (bf16[16,256]{1,0:T(8,128)(2,1)S(1)}, bf16[16,256]{1,0:T(8,128)(2,1)S(1)}, u32[]{:S(2)}, u32[]{:S(2)}) collective-permute-start(bf16[16,256]{1,0:T(8,128)(2,1)S(1)} %plane_counts.1.refs_5_), channel_id=1, source_target_pairs={{0,128},{64,192},{128,0},{192,64},{1,129},{65,193},{129,1},{193,65... | collective-permute-start | bytes 24584 | tf_op jit(solution)/shard_map/ppermute | solution.py:658
  59.5 3.7 %collective-permute-start.9 = (bf16[16,256]{1,0:T(8,128)(2,1)S(1)}, bf16[16,256]{1,0:T(8,128)(2,1)S(1)}, u32[]{:S(2)}, u32[]{:S(2)}) collective-permute-start(bf16[16,256]{1,0:T(8,128)(2,1)S(1)} %plane_counts.1.refs_5_), channel_id=1, source_target_pairs={{0,64},{64,128},{128,192},{192,0},{1,65},{65,129},{129,193},{193,1... | collective-permute-start | bytes 24584 | tf_op jit(solution)/shard_map/ppermute | solution.py:658
  63.2 1.0 copy-start.6
  76.7 45.6 %copy-start = (bf16[2048,3,256]{2,0,1:T(8,128)(2,1)S(1)}, bf16[2048,3,256]{2,0,1:T(8,128)(2,1)}, u32[]{:S(2)}) copy-start(bf16[2048,3,256]{2,0,1:T(8,128)(2,1)} %param.17) | copy-start | bytes 9437188
  96.2 5.0 %collective-permute-start.17 = (bf16[128,256]{1,0:T(8,128)(2,1)S(1)}, bf16[128,256]{1,0:T(8,128)(2,1)S(1)}, u32[]{:S(2)}, u32[]{:S(2)}) collective-permute-start(bf16[128,256]{1,0:T(8,128)(2,1)S(1)} %merge.1.a_ref), channel_id=1, source_target_pairs={{0,2},{1,3},{2,0},{3,1},{4,6},{5,7},{6,4},{7,5},{8,10},{9,11},{10,... | collective-permute-start | bytes 196616 | tf_op jit(solution)/shard_map/ppermute | solution.py:653
  102.5 19.7 %collective-permute-start.18 = (bf16[128,2048]{1,0:T(8,128)(2,1)S(1)}, bf16[128,2048]{1,0:T(8,128)(2,1)S(1)}, u32[]{:S(2)}, u32[]{:S(2)}) collective-permute-start(bf16[128,2048]{1,0:T(8,128)(2,1)S(1)} %get-tuple-element.43), channel_id=1, source_target_pairs={{0,1},{1,0},{2,3},{3,2},{4,5},{5,4},{6,7},{7,6},{8,9},{9,8},{10,11... | collective-permute-start | bytes 1572872 | tf_op jit(solution)/shard_map/ppermute | solution.py:653
  114.7 5.2 %collective-permute-start.20 = (bf16[32,2048]{1,0:T(8,128)(2,1)S(1)}, bf16[32,2048]{1,0:T(8,128)(2,1)S(1)}, u32[]{:S(2)}, u32[]{:S(2)}) collective-permute-start(bf16[32,2048]{1,0:T(8,128)(2,1)S(1)} %get-tuple-element.44), channel_id=1, source_target_pairs={{0,5},{1,4},{2,7},{3,6},{4,9},{5,8},{6,11},{7,10},{8,13},{9,12},{1... | collective-permute-start | bytes 393224 | tf_op jit(solution)/shard_map/ppermute | solution.py:728
  116.8 5.5 %collective-permute-start.19 = (bf16[32,2048]{1,0:T(8,128)(2,1)S(1)}, bf16[32,2048]{1,0:T(8,128)(2,1)S(1)}, u32[]{:S(2)}, u32[]{:S(2)}) collective-permute-start(bf16[32,2048]{1,0:T(8,128)(2,1)S(1)} %get-tuple-element.44), channel_id=1, source_target_pairs={{0,4},{1,5},{2,6},{3,7},{4,8},{5,9},{6,10},{7,11},{8,12},{9,13},{1... | collective-permute-start | bytes 393224 | tf_op jit(solution)/shard_map/ppermute | solution.py:727
  122.3 20.8 %copy-start.5 = (f32[2]{0:T(128)S(1)}, f32[2]{0:T(128)}, u32[]{:S(2)}) copy-start(f32[2]{0:T(128)} %slope_ref.3) | copy-start | bytes 28
  122.3 59.4 %copy-start.2 = (bf16[256,2048]{1,0:T(8,128)(2,1)S(1)}, bf16[256,2048]{1,0:T(8,128)(2,1)}, u32[]{:S(2)}) copy-start(bf16[256,2048]{1,0:T(8,128)(2,1)} %w_ref.1) | copy-start | bytes 3145732
  142.3 0.7 collective-permute-start.21
  182.2 6.1 %collective-permute-start.22 = (bf16[32,512]{1,0:T(8,128)(2,1)S(1)}, bf16[32,512]{1,0:T(8,128)(2,1)S(1)}, u32[]{:S(2)}, u32[]{:S(2)}) collective-permute-start(bf16[32,512]{1,0:T(8,128)(2,1)S(1)} %get-tuple-element.48), channel_id=1, source_target_pairs={{0,1},{1,0},{2,3},{3,2},{4,5},{5,4},{6,7},{7,6},{8,9},{9,8},{10,11... | collective-permute-start | bytes 98312 | tf_op jit(solution)/shard_map/ppermute | solution.py:653
  185.1 4.3 %collective-permute-start.23 = (bf16[32,512]{1,0:T(8,128)(2,1)S(1)}, bf16[32,512]{1,0:T(8,128)(2,1)S(1)}, u32[]{:S(2)}, u32[]{:S(2)}) collective-permute-start(bf16[32,512]{1,0:T(8,128)(2,1)S(1)} %get-tuple-element.49), channel_id=1, source_target_pairs={{0,2},{1,3},{2,0},{3,1},{4,6},{5,7},{6,4},{7,5},{8,10},{9,11},{10,... | collective-permute-start | bytes 98312 | tf_op jit(solution)/shard_map/ppermute | solution.py:653
  186.9 4.9 %collective-permute-start.24 = (bf16[32,512]{1,0:T(8,128)(2,1)S(1)}, bf16[32,512]{1,0:T(8,128)(2,1)S(1)}, u32[]{:S(2)}, u32[]{:S(2)}) collective-permute-start(bf16[32,512]{1,0:T(8,128)(2,1)S(1)} %get-tuple-element.50), channel_id=1, source_target_pairs={{0,3},{1,2},{2,1},{3,0},{4,7},{5,6},{6,5},{7,4},{8,11},{9,10},{10,... | collective-permute-start | bytes 98312 | tf_op jit(solution)/shard_map/ppermute | solution.py:653

commit v5 on v4

--- a/solution.py
+++ b/solution.py
@@ -46,11 +46,10 @@
 
 
 def project_kernel(
-    count_ref, tok_hbm, w_hbm, ck_hbm, cv_hbm, q_ref, pack_ref, tok, weight, sems
+    tok_hbm, w_hbm, ck_hbm, cv_hbm, q_ref, pack_ref, tok, weight, sems
 ):
     rows = tok.shape[0]
     slots = ck_hbm.shape[0]
-    width = q_ref.shape[1]
     copies = [pltpu.make_async_copy(tok_hbm, tok, sems.at[0])]
     copies += [
         pltpu.make_async_copy(w_hbm.at[i], weight.at[i], sems.at[1 + i]) for i in range(3)
@@ -61,8 +60,6 @@
     ]
     for copy in copies:
         copy.start()
-    count = jnp.full((16, width), count_ref[0], jnp.int32)
-    pack_ref[2 * (slots + rows) :] = count.astype(F32).astype(BF16)
     copies[0].wait()
     normed = rms_scaled(tok[...].astype(F32))
     for i in range(3):
@@ -77,15 +74,15 @@
     copies[5].wait()
 
 
-def project(count, rows, weight3, cache_keys, cache_values):
+def project(rows, weight3, cache_keys, cache_values):
     n, d = rows.shape
     width = weight3.shape[2]
-    total = 2 * (n + cache_keys.shape[0]) + 16
+    total = 2 * (n + cache_keys.shape[0])
     hbm = pl.BlockSpec(memory_space=HBM)
     vmem = pl.BlockSpec(memory_space=VMEM)
     return pl.pallas_call(
         project_kernel,
-        in_specs=[pl.BlockSpec(memory_space=SMEM), hbm, hbm, hbm, hbm],
+        in_specs=[hbm] * 4,
         out_specs=[vmem, vmem],
         out_shape=[
             jax.ShapeDtypeStruct((n, width), BF16),
@@ -99,26 +96,55 @@
         compiler_params=params(60),
         cost_estimate=cost(6 * n * d * width, 2 * (n * d + 3 * d * width)),
         name="project",
-    )(count, rows, weight3, cache_keys, cache_values)
-
-
-def mark_kernel(q_ref, own_ref, other_ref, out_ref):
-    rows = q_ref.shape[0]
-    out_ref[:rows] = q_ref[...]
-    step = lax.broadcasted_iota(jnp.int32, own_ref.shape, 0)
-    own, other = own_ref[...].astype(F32), other_ref[...].astype(F32)
-    out_ref[rows:] = jnp.where(step < 8, own, other).astype(BF16)
-
-
-def mark(q, own, other):
-    n, width = q.shape
-    return pl.pallas_call(
-        mark_kernel,
-        out_shape=jax.ShapeDtypeStruct((n + 16, width), BF16),
+    )(rows, weight3, cache_keys, cache_values)
+
+
+def table_kernel(count_ref, out_ref):
+    y, z, xl = place_of_device()
+    lane = lax.broadcasted_iota(jnp.int32, out_ref.shape, 1)
+    out_ref[...] = jnp.where(lane == y * 16 + z * 2 + xl, count_ref[0], 0).astype(F32)
+
+
+def own_count(count):
+    return pl.pallas_call(
+        table_kernel,
+        in_specs=[pl.BlockSpec(memory_space=SMEM)],
+        out_shape=jax.ShapeDtypeStruct((8, HS), F32),
         compiler_params=params(8),
-        cost_estimate=cost(0, 4 * n * width),
-        name="mark",
-    )(q, own, other)
+        cost_estimate=cost(0, 4096),
+        name="own_count",
+    )(count)
+
+
+def add_kernel(a_ref, b_ref, out_ref):
+    out_ref[...] = a_ref[...] + b_ref[...]
+
+
+def added(a, b):
+    return pl.pallas_call(
+        add_kernel,
+        out_shape=jax.ShapeDtypeStruct(a.shape, a.dtype),
+        compiler_params=params(8),
+        cost_estimate=cost(a.size, 12 * a.size),
+        name="added",
+    )(a, b)
+
+
+def join_kernel(a_ref, b_ref, out_ref):
+    rows = a_ref.shape[0]
+    out_ref[:rows] = a_ref[...]
+    out_ref[rows:] = b_ref[...]
+
+
+def join(a, b):
+    n, width = a.shape
+    return pl.pallas_call(
+        join_kernel,
+        out_shape=jax.ShapeDtypeStruct((2 * n, width), BF16),
+        compiler_params=params(8),
+        cost_estimate=cost(0, 8 * n * width),
+        name="join",
+    )(a, b)
 
 
 def halves_kernel(left_ref, right_ref, own_ref, other_ref):
@@ -154,34 +180,6 @@
         cost_estimate=cost(0, 8 * n * width),
         name="join",
     )(a, b)
-
-
-def plane_kernel(own, left, right, far, far_other, out_ref):
-    rows = []
-    half = far.shape[0]
-    for ref, end in (
-        (own, half),
-        (own, 2 * half),
-        (left, half),
-        (left, 2 * half),
-        (far, half),
-        (far_other, half),
-        (right, half),
-        (right, 2 * half),
-    ):
-        marks = ref[end - 16 : end].astype(F32)
-        rows += [marks[:1], marks[8:9]]
-    out_ref[...] = jnp.concatenate(rows, axis=0).astype(BF16)
-
-
-def plane_counts(queries):
-    return pl.pallas_call(
-        plane_kernel,
-        out_shape=jax.ShapeDtypeStruct((16, queries[0].shape[1]), BF16),
-        compiler_params=params(8),
-        cost_estimate=cost(0, 8 * queries[0].size),
-        name="plane_counts",
-    )(*queries)
 
 
 RING = ((0, 0), (0, 1), (1, 0), (1, 1), (3, 0), (3, 1), (2, 0), (2, 1))
@@ -220,8 +218,8 @@
 
 
 def attend_kernel(slots, slope_ref, *refs):
-    queries, planes, packs = refs[:5], refs[5:9], refs[9:17]
-    out_ref, q_tile, bias = refs[17:]
+    queries, tables, packs = refs[:5], refs[5:7], refs[7:15]
+    out_ref, q_tile, bias = refs[15:]
     tile = pl.program_id(0)
     y, z, xl = place_of_device()
     rows = q_tile.shape[0] // 2
@@ -234,9 +232,8 @@
         return 1 - xl if other else xl
 
     own, left, right, far, far_other = queries
-    step = rows + 16
     for t, (a, b, at) in enumerate(
-        ((own, own, step), (left, left, step), (far, far_other, 0), (right, right, step))
+        ((own, own, rows), (left, left, rows), (far, far_other, 0), (right, right, rows))
     ):
 
         @pl.when(tile == t)
@@ -246,33 +243,24 @@
 
     @pl.when(tile == 0)
     def _():
-        steps = lax.broadcasted_iota(jnp.int32, (16, width), 0)
-        zs = (z + 8 - 2 * (steps // 4)) % 8
-        zs = jnp.where((steps // 2) % 2 == 1, zs ^ 1, zs)
-        totals, parts, owns = [], [], []
-        for plane in planes:
-            counts = plane[...].astype(F32)
-            totals.append(jnp.sum(counts, axis=0, keepdims=True))
-            parts.append(jnp.sum(jnp.where(zs < z, counts, 0.0), axis=0, keepdims=True))
-            owns.append((counts[0:1], counts[1:2]))
-        ys = [(y + 4 - back) % 4 for back in range(4)]
-        everything = functools.reduce(jnp.add, totals)
+        table = (tables[0][...] + tables[1][...])[:1]
+        lane = lax.broadcasted_iota(jnp.int32, table.shape, 1)
+        everything = jnp.sum(table, axis=1, keepdims=True)
         slot = lax.broadcasted_iota(jnp.int32, (1, slots), 1).astype(F32)
         place = lax.broadcasted_iota(jnp.int32, (1, rows), 1)
         for j, (back, other) in enumerate(RING):
-            side = side_of(other)
-            start = parts[back] - everything
-            for i in range(4):
-                start = start + jnp.where(ys[i] < ys[back], totals[i], 0.0)
-            start = start + jnp.where(side == 1, owns[back][1 - other], 0.0)
-            spot = (place + (ys[back] * 16 + z * 2 + side) * rows).astype(F32)
+            yj = (y + 4 - back) % 4
+            ctx = yj * 16 + z * 2 + side_of(other)
+            live = jnp.sum(jnp.where(lane == ctx, table, 0.0), axis=1, keepdims=True)
+            start = jnp.sum(jnp.where(lane < ctx, table, 0.0), axis=1, keepdims=True) - everything
+            spot = (place + ctx * rows).astype(F32)
             for h in range(heads):
                 slope = slope_ref[h] * LOG2E
                 bias[h : h + 1, j * slots : (j + 1) * slots] = jnp.where(
-                    slot < owns[back][other], slope * (slot + start), NEG
+                    slot < live, slope * (slot + start), NEG
                 )
                 at = cached + j * rows
-                bias[h : h + 1, at : at + rows] = jnp.where(ys[back] <= y, slope * spot, NEG)
+                bias[h : h + 1, at : at + rows] = jnp.where(yj <= y, slope * spot, NEG)
 
     row = lax.broadcasted_iota(jnp.int32, (2 * rows, 1), 0)
     first = (z + 8 - 2 * tile) % 8
@@ -327,9 +315,8 @@
                 out_ref[2 * p + b, rows:] = tail
 
 
-def attend(slopes, queries, planes, packs, slots):
-    padded, width = queries[0].shape
-    rows = padded // 2 - 16
+def attend(slopes, queries, tables, packs, slots):
+    rows, width = queries[0].shape[0] // 2, queries[0].shape[1]
     nk = len(RING) * (slots + rows)
     whole = lambda a: pl.BlockSpec(a.shape, lambda i: (0,) * a.ndim)
     out = jax.ShapeDtypeStruct((8, rows + 16, width), BF16)
@@ -337,14 +324,14 @@
         functools.partial(attend_kernel, slots),
         grid=(4,),
         in_specs=[pl.BlockSpec(memory_space=SMEM)]
-        + [whole(a) for a in (*queries, *planes, *packs)],
+        + [whole(a) for a in (*queries, *tables, *packs)],
         out_specs=whole(out),
         out_shape=out,
         scratch_shapes=[VMEM((2 * rows, width), BF16), VMEM((8, nk), F32)],
         compiler_params=params(40),
         cost_estimate=cost(32 * rows * nk * width, 4 * nk * width, 16 * rows * nk),
         name="attend",
-    )(slopes, *queries, *planes, *packs)
+    )(slopes, *queries, *tables, *packs)
 
 
 def merge_kernel(heads, parts_ref, out_ref):
@@ -443,7 +430,7 @@
 
 
 def short_project_kernel(
-    sum_ref, term_ref, rim_a, rim_b, w_ref, cols_ref, qkv_ref, normed
+    sum_ref, term_ref, rim_a, rim_b, w_ref, cols_ref, q_ref, kv_ref, normed
 ):
     step = pl.program_id(0)
     rows, d = sum_ref.shape
@@ -474,13 +461,19 @@
 
     out = jnp.dot(normed[...], w_ref[0], preferred_element_type=F32)
 
-    scaled = jnp.where(step == 0, out * SCALE2, out).astype(BF16)
-    for i in range(3):
-
-        @pl.when(step == i)
-        def _(i=i):
-            for c in range(qkv_ref.shape[0]):
-                qkv_ref[c, :, i * width : (i + 1) * width] = scaled
+    @pl.when(step == 0)
+    def _():
+        scaled = (out * SCALE2).astype(BF16)
+        for c in range(q_ref.shape[0]):
+            q_ref[c] = scaled
+
+    @pl.when(step == 1)
+    def _():
+        kv_ref[:, :width] = out.astype(BF16)
+
+    @pl.when(step == 2)
+    def _():
+        kv_ref[:, width:] = out.astype(BF16)
 
 
 def short_project(total, term, rims, weight3, copies):
@@ -488,7 +481,7 @@
     groups = n // GROUP
     width = weight3.shape[2]
     whole = lambda shape: pl.BlockSpec(shape, lambda i: (0,) * len(shape))
-    shapes = [(n, d // 4), (copies, groups, 3 * width)]
+    shapes = [(n, d // 4), (copies, groups, width), (groups, 2 * width)]
     return pl.pallas_call(
         short_project_kernel,
         grid=(3,),
@@ -503,23 +496,8 @@
     )(total, term, *rims, weight3)
 
 
-def keys_kernel(qkv_ref, out_ref):
-    width = out_ref.shape[2]
-    out_ref[...] = qkv_ref[:, :, width // 2 :]
-
-
-def keys_of(qkv):
-    blocks, groups, width = qkv.shape
-    return pl.pallas_call(
-        keys_kernel,
-        out_shape=jax.ShapeDtypeStruct((blocks, groups, width // 3 * 2), BF16),
-        compiler_params=params(8),
-        cost_estimate=cost(0, 4 * qkv.size),
-        name="keys_of",
-    )(qkv)
-
-
-def short_attend_kernel(slope_ref, qkv_ref, kv_ref, out_ref):
+def short_attend_kernel(slope_ref, q_ref, *refs):
+    key_refs, out_ref = refs[:4], refs[4]
     y, z, xl = place_of_device()
     blocks, groups, padded = out_ref.shape
     width = padded - HS
@@ -528,7 +506,9 @@
     row = lax.broadcasted_iota(jnp.int32, (n, 1), 0)
     row_pos = (y * 16 + xl + 2 * (row // groups)) * groups + row % groups
     key = lax.broadcasted_iota(jnp.int32, (1, n), 1)
-    key_pos = ((z // 2) * 16 + z % 2 + 2 * (key // groups)) * groups + key % groups
+    ys = (y + 4 - key // (2 * groups)) % 4
+    side = jnp.where((key // groups) % 2 == 1, 1 - xl, xl)
+    key_pos = (ys * 16 + z * 2 + side) * groups + key % groups
     usable = key_pos <= row_pos
     spot = key_pos.astype(F32)
     lane = lax.broadcasted_iota(jnp.int32, (n, HS), 1)
@@ -536,9 +516,10 @@
     outs = []
     for h in range(heads):
         cols = slice(h * HS, (h + 1) * HS)
-        q = qkv_ref[:, :, cols].reshape(n, HS)
-        k = kv_ref[:, :, cols].reshape(n, HS)
-        v = kv_ref[:, :, width + h * HS : width + (h + 1) * HS].reshape(n, HS)
+        cols_v = slice(width + h * HS, width + (h + 1) * HS)
+        q = q_ref[:, :, cols].reshape(n, HS)
+        k = jnp.concatenate([r[:, cols] for r in key_refs], axis=0)
+        v = jnp.concatenate([r[:, cols_v] for r in key_refs], axis=0)
         s = dot_t(q, k) + (slope_ref[h] * LOG2E) * spot
         s = jnp.where(usable, s, NEG)
         top = jnp.max(s, axis=1, keepdims=True)
@@ -553,21 +534,20 @@
     out_ref[...] = out.reshape(out_ref.shape)
 
 
-def short_attend(slopes, qkv, kv):
-    blocks, groups, width3 = qkv.shape
-    width = width3 // 3
+def short_attend(slopes, queries, keys):
+    blocks, groups, width = queries.shape
     n = blocks * groups
     smem = pl.BlockSpec(memory_space=SMEM)
     vmem = pl.BlockSpec(memory_space=VMEM)
     return pl.pallas_call(
         short_attend_kernel,
-        in_specs=[smem, vmem, vmem],
+        in_specs=[smem] + [vmem] * 5,
         out_specs=vmem,
         out_shape=jax.ShapeDtypeStruct((blocks, groups, width + HS), BF16),
         compiler_params=params(16),
         cost_estimate=cost(4 * n * n * width, 8 * n * width),
         name="short_attend",
-    )(slopes, qkv, kv)
+    )(slopes, queries, *keys)
 
 
 def short_merge_kernel(heads, parts_ref, w_ref, *outs):
@@ -662,17 +642,10 @@
     return moved(x, axis, by), moved(x, axis, -by)
 
 
-def across(block):
-    ny, nz, nx = (lax.axis_size(a) for a in ("y", "z", "xl"))
-    assert ny * nx == nz
-    pairs = []
-    for y in range(ny):
-        for z in range(nz):
-            for x in range(nx):
-                line = y * nx + x
-                to = ((z // nx) * nz + line) * nx + z % nx
-                pairs.append(((y * nz + z) * nx + x, to))
-    return lax.ppermute(block, ("y", "z", "xl"), pairs)
+def counts_along(table, axis, *flips):
+    for flip in flips:
+        table = added(table, swap(table, axis, flip))
+    return table
 
 
 def after(x, *others):
@@ -693,29 +666,31 @@
 ):
     axes = ("y", "z", "xl", "tp")
     slots = cache_keys.shape[0]
-    count = jnp.broadcast_to(cache_count.astype(BF16)[None], (16, cache_keys.shape[1]))
-    other_count = swap(count, "xl")
     q, pack = project(
-        cache_count, tokens, jnp.transpose(project_weight, (1, 0, 2)), cache_keys, cache_values
+        tokens, jnp.transpose(project_weight, (1, 0, 2)), cache_keys, cache_values
     )
-    q, pack, other_count = lax.optimization_barrier((q, pack, other_count))
-    marked = mark(q, count, other_count)
+    table = counts_along(own_count(cache_count), "xl", 1)
+    q, pack, table = lax.optimization_barrier((q, pack, table))
+    table = counts_along(table, "z", 1)
     left, right = both_ways(pack, "y", 1)
-    other, left, right, mate = lax.optimization_barrier(
-        (swap(pack, "xl"), left, right, swap(marked, "z"))
+    other, left, right, mate, table = lax.optimization_barrier(
+        (swap(pack, "xl"), left, right, swap(q, "z"), table)
     )
+    pair = join(q, mate)
     left_other, right_other = both_ways(other, "y", 1)
-    pair = join(marked, mate)
     left_pair, right_pair = both_ways(pair, "z", 2)
+    table = counts_along(table, "z", 2, 4)
+    left_other, right_other, left_pair, right_pair, left, table = lax.optimization_barrier(
+        (left_other, right_other, left_pair, right_pair, left, table)
+    )
+    table = counts_along(table, "y", 1)
+    tables = [table, swap(table, "y", 2)]
+    far, far_other = moved(left, "y", 1), moved(right_other, "y", -1)
     near = halves(left_pair, right_pair)
     queries = [pair, left_pair, right_pair, moved(near[0], "z", 2), moved(near[1], "z", -2)]
-    far, far_other = moved(left, "y", 1), moved(right_other, "y", -1)
-    crossed = swap(after(output_weight, other), "tp", 2)
-    plane = plane_counts(queries)
-    planes = [plane] + [moved(plane, "y", by) for by in (1, 2, 3)]
+    crossed = swap(after(output_weight, far), "tp", 2)
     packs = [pack, other, left, left_other, right, right_other, far, far_other]
-    parts = attend(distance_slope, queries, planes, packs, slots)
-    parts, crossed = lax.optimization_barrier((parts, crossed))
+    parts = attend(distance_slope, queries, tables, packs, slots)
 
     att = merge(exchange(parts, "z"))
     total, term, rim = layer_product(
@@ -727,15 +702,16 @@
         lax.ppermute(rim, axes, ahead),
         lax.ppermute(rim, axes, [(i, j ^ 1) for i, j in ahead]),
     ]
-    layer, qkv = short_project(
+    layer, sq, skv = short_project(
         total,
         swap(term, "tp", 1),
         rims,
         jnp.transpose(short_project_weight, (1, 0, 2)),
         lax.axis_size("z"),
     )
-    qkv = exchange(qkv, "z")
-    sparts = short_attend(short_slope, qkv, across(keys_of(qkv)))
+    pair = join(skv, swap(skv, "xl"))
+    keys = [pair] + [moved(pair, "y", by) for by in (1, 2, 3)]
+    sparts = short_attend(short_slope, exchange(sq, "z"), keys)
     terms = short_merge(exchange(sparts, "z"), short_output)
     terms = [swap(t, "tp", flip) if flip else t for flip, t in enumerate(terms)]
     return final_sum(layer, terms)

time: 194 us -> 166 us (0.86)
  blocking collectives: 74.6 us -> 15.1 us
  starting transfers between devices: 50.4 us -> 71.1 us
  waiting for transfers between devices: 42.6 us -> 47.7 us
  local copies, waits for them, and re-layouts: 1.86 us -> 6.13 us
  Pallas kernels: 22.2 us -> 24.4 us
    all_to_all x3 -> x1, blocking collectives: 74.6 us -> 15.1 us  [exchange(): return lax.all_to_all(blocks, axis, 0, 0)]
    ppermute x13, waiting for transfers between devices: 31.5 us -> 10.3 us  [moved(): return lax.ppermute(x, axis, [(i, (i + by) % n) for i in range(n)])]
    ppermute x9 -> x15, waiting for transfers between devices: 8.73 us -> 24.6 us  [swap(): lax.ppermute(x, axis, [(i, i ^ flip) for i in range(lax.axis_size(axis))])]
    all_to_all x0 -> x2, starting transfers between devices: none -> 14.6 us  [exchange(): return lax.all_to_all(blocks, axis, 0, 0)]
    all_to_all x0 -> x2, waiting for transfers between devices: none -> 10.5 us  [exchange(): return lax.all_to_all(blocks, axis, 0, 0)]
    ppermute x9 -> x15, starting transfers between devices: 26.5 us -> 32.6 us  [swap(): lax.ppermute(x, axis, [(i, i ^ flip) for i in range(lax.axis_size(axis))])]
    unnamed x16 -> x18, local copies, waits for them, and re-layouts: 1.86 us -> 6.13 us
    pallas_call x5 -> x8, Pallas kernels: 4.45 us -> 4.44 us  [the longest x1 3.37 us: project(): pl.pallas_call(project_kernel, in_specs=[hbm] * 4, out_specs=[vmem, vmem]...]
  transfers between devices with their start and end apart: 25 -> 32, of which waited for: 13 -> 17; matrix products, arithmetic and copies ran while one was open for 0% -> 0% of each run, Pallas kernels for 8% -> 3%
where the time goes in v5:
time: 166 us; the launch traced here: 165 us
  starting transfers between devices  71.1 us (43%)
  waiting for transfers between devices  47.7 us (29%)
  Pallas kernels  24.4 us (15%)
  blocking collectives  15.1 us (9%)
  local copies, waits for them, and re-layouts  6.13 us (4%)
    ppermute x15, starting transfers between devices, swap(): lax.ppermute(x, axis, [(i, i ^ flip) for i in range(lax.axis_size(axis))])  32.6 us
    ppermute x15, waiting for transfers between devices, swap(): lax.ppermute(x, axis, [(i, i ^ flip) for i in range(lax.axis_size(axis))])  24.6 us
    ppermute x13, starting transfers between devices, moved(): return lax.ppermute(x, axis, [(i, (i + by) % n) for i in range(n)])  19 us
    all_to_all x1, blocking collectives, exchange(): return lax.all_to_all(blocks, axis, 0, 0)  15.1 us
    all_to_all x2, starting transfers between devices, exchange(): return lax.all_to_all(blocks, axis, 0, 0)  14.6 us
    pallas_call x1, Pallas kernels, attend(): pl.pallas_call(functools.partial(attend_kernel, slots), grid=(4,), in_spe...  12.2 us
    all_to_all x2, waiting for transfers between devices, exchange(): return lax.all_to_all(blocks, axis, 0, 0)  10.5 us
    ppermute x13, waiting for transfers between devices, moved(): return lax.ppermute(x, axis, [(i, (i + by) % n) for i in range(n)])  10.3 us
  transfers between devices with their start and end apart: 32, of which 17 were waited for; matrix products, arithmetic and copies ran while one was open for 0% of the time, Pallas kernels for 3%

profile of v5, /device:TPU:1, one launch (start us, length us, event | category | flops | bytes accessed | tf_op | source)
XLA Modules:
  0.0 165.3 jit_solution(1104423566209368516)
XLA Ops:
  0.7 2.1 %collective-permute-start = (f32[8,128]{1,0:T(8,128)S(1)}, f32[8,128]{1,0:T(8,128)S(1)}, u32[]{:S(2)}, u32[]{:S(2)}) collective-permute-start(f32[8,128]{1,0:T(8,128)S(1)} %own_count.1.a_ref), channel_id=1, source_target_pairs={{0,4},{4,0},{1,5},{5,1},{2,6},{6,2},{3,7},{7,3},{8,12},{12,8},{9,1... | collective-permute-start | bytes 12296 | tf_op jit(solution)/shard_map/ppermute | solution.py:633
  2.8 3.4 %project.1 = (bf16[128,256]{1,0:T(8,128)(2,1)}, bf16[768,256]{1,0:T(8,128)(2,1)}) custom-call(bf16[128,2048]{1,0:T(8,128)(2,1)} %tok_hbm.3, bf16[3,2048,256]{2,1,0:T(8,128)(2,1)} %bitcast.3, bf16[256,256]{1,0:T(8,128)(2,1)} %ck_hbm.1, bf16[256,256]{1,0:T(8,128)(2,1)} %cv_hbm.1), custom_call_target="tpu_custom_call" | custom-call | flops 402653184 | bytes 3670016 | tf_op jit(solution)/shard_map/project/pallas_call | solution.py:83
  6.2 2.8 %collective-permute-start.3 = (bf16[768,256]{1,0:T(8,128)(2,1)}, bf16[768,256]{1,0:T(8,128)(2,1)S(1)}, u32[]{:S(2)}, u32[]{:S(2)}) collective-permute-start(bf16[768,256]{1,0:T(8,128)(2,1)} %get-tuple-element.37.refs_7_), channel_id=1, source_target_pairs={{0,192},{64,0},{128,64},{192,128},{1,193},{65,1},{129,65},{193,129... | collective-permute-start | bytes 1179656 | tf_op jit(solution)/shard_map/ppermute | solution.py:638
  9.3 1.6 collective-permute-start.4
  11.0 2.7 %collective-permute-done.5.b_ref = f32[8,128]{1,0:T(8,128)S(1)} collective-permute-done((f32[8,128]{1,0:T(8,128)S(1)}, f32[8,128]{1,0:T(8,128)S(1)}, u32[]{:S(2)}, u32[]{:S(2)}) %collective-permute-start.5) | collective-permute-done | bytes 4128 | tf_op jit(solution)/shard_map/ppermute | solution.py:633
  13.7 3.1 %collective-permute-done.3.refs_11_ = bf16[768,256]{1,0:T(8,128)(2,1)S(1)} collective-permute-done((bf16[768,256]{1,0:T(8,128)(2,1)}, bf16[768,256]{1,0:T(8,128)(2,1)S(1)}, u32[]{:S(2)}, u32[]{:S(2)}) %collective-permute-start.3) | collective-permute-done | bytes 393248 | tf_op jit(solution)/shard_map/ppermute | solution.py:638
  16.8 3.0 %collective-permute-done.2.refs_9_ = bf16[768,256]{1,0:T(8,128)(2,1)S(1)} collective-permute-done((bf16[768,256]{1,0:T(8,128)(2,1)}, bf16[768,256]{1,0:T(8,128)(2,1)S(1)}, u32[]{:S(2)}, u32[]{:S(2)}) %collective-permute-start.2) | collective-permute-done | bytes 393248 | tf_op jit(solution)/shard_map/ppermute | solution.py:638
  19.8 1.2 collective-permute-start.7
  22.1 6.1 %collective-permute-start.9 = (bf16[256,256]{1,0:T(8,128)(2,1)S(1)}, bf16[256,256]{1,0:T(8,128)(2,1)S(1)}, u32[]{:S(2)}, u32[]{:S(2)}) collective-permute-start(bf16[256,256]{1,0:T(8,128)(2,1)S(1)} %join.2.refs_0_), channel_id=1, source_target_pairs={{0,48},{8,56},{16,0},{24,8},{32,16},{40,24},{48,32},{56,40},{1,49}... | collective-permute-start | bytes 393224 | tf_op jit(solution)/shard_map/ppermute | solution.py:638
  28.2 1.3 collective-permute-start.10
  29.5 2.8 %collective-permute-done.10.b_ref = f32[8,128]{1,0:T(8,128)S(1)} collective-permute-done((f32[8,128]{1,0:T(8,128)S(1)}, f32[8,128]{1,0:T(8,128)S(1)}, u32[]{:S(2)}, u32[]{:S(2)}) %collective-permute-start.10) | collective-permute-done | bytes 4128 | tf_op jit(solution)/shard_map/ppermute | solution.py:633
  32.3 3.3 %collective-permute-start.11 = (f32[8,128]{1,0:T(8,128)S(1)}, f32[8,128]{1,0:T(8,128)S(1)}, u32[]{:S(2)}, u32[]{:S(2)}) collective-permute-start(f32[8,128]{1,0:T(8,128)S(1)} %added.7.a_ref), channel_id=1, source_target_pairs={{0,32},{8,40},{16,48},{24,56},{32,0},{40,8},{48,16},{56,24},{1,33}... | collective-permute-start | bytes 12296 | tf_op jit(solution)/shard_map/ppermute | solution.py:633
  35.6 3.1 %collective-permute-done.11.b_ref = f32[8,128]{1,0:T(8,128)S(1)} collective-permute-done((f32[8,128]{1,0:T(8,128)S(1)}, f32[8,128]{1,0:T(8,128)S(1)}, u32[]{:S(2)}, u32[]{:S(2)}) %collective-permute-start.11) | collective-permute-done | bytes 4128 | tf_op jit(solution)/shard_map/ppermute | solution.py:633
  38.8 2.7 %collective-permute-start.17 = (bf16[768,256]{1,0:T(8,128)(2,1)S(1)}, bf16[768,256]{1,0:T(8,128)(2,1)S(1)}, u32[]{:S(2)}, u32[]{:S(2)}) collective-permute-start(bf16[768,256]{1,0:T(8,128)(2,1)S(1)} %collective-permute-done.7.refs_12_), channel_id=1, source_target_pairs={{0,192},{64,0},{128,64},{192,128},{1,193},{65,1},{129,65},{193,129... | collective-permute-start | bytes 1179656 | tf_op jit(solution)/shard_map/ppermute | solution.py:638
  41.5 1.5 collective-permute-start.12
  43.0 2.2 %collective-permute-start.13 = (bf16[128,256]{1,0:T(8,128)(2,1)S(1)}, bf16[128,256]{1,0:T(8,128)(2,1)S(1)}, u32[]{:S(2)}, u32[]{:S(2)}) collective-permute-start(bf16[128,256]{1,0:T(8,128)(2,1)S(1)} %get-tuple-element.46), channel_id=1, source_target_pairs={{0,48},{8,56},{16,0},{24,8},{32,16},{40,24},{48,32},{56,40},{1,49}... | collective-permute-start | bytes 196616 | tf_op jit(solution)/shard_map/ppermute | solution.py:638
  45.1 2.8 %collective-permute-done.14.b_ref = f32[8,128]{1,0:T(8,128)S(1)} collective-permute-done((f32[8,128]{1,0:T(8,128)S(1)}, f32[8,128]{1,0:T(8,128)S(1)}, u32[]{:S(2)}, u32[]{:S(2)}) %collective-permute-start.14) | collective-permute-done | bytes 4128 | tf_op jit(solution)/shard_map/ppermute | solution.py:633
  48.0 1.1 collective-permute-start.15
  49.0 3.0 %collective-permute-done.15.refs_6_ = f32[8,128]{1,0:T(8,128)S(1)} collective-permute-done((f32[8,128]{1,0:T(8,128)S(1)}, f32[8,128]{1,0:T(8,128)S(1)}, u32[]{:S(2)}, u32[]{:S(2)}) %collective-permute-start.15) | collective-permute-done | bytes 4128 | tf_op jit(solution)/shard_map/ppermute | solution.py:633
  52.1 1.0 copy-done.7
  53.1 12.2 %attend.1 = bf16[8,144,256]{2,1,0:T(8,128)(2,1)S(1)} custom-call(f32[2]{0:T(128)S(1)} %copy-done.8, bf16[256,256]{1,0:T(8,128)(2,1)S(1)} %join.2.refs_0_, bf16[256,256]{1,0:T(8,128)(2,1)S(1)} %collective-permute-done.8.left_ref.refs_1_, bf16[256,256]{1,0:T(8,128)(2,1)S(1)} %collective-permute-done.9.right_ref.refs_2_, ...), custom_call_target="tpu_custom_call" | custom-call | flops 3221225472 | bytes 3145728 | tf_op jit(solution)/shard_map/attend/pallas_call | solution.py:323
  66.1 5.1 %all-to-all-start = ((bf16[8,144,256]{2,1,0:T(8,128)(2,1)}), bf16[8,144,256]{2,1,0:T(8,128)(2,1)}, u32[]{:S(2)}, u32[]{:S(2)}) async-start(bf16[8,144,256]{2,1,0:T(8,128)(2,1)} %copy-done.4), calls=%async_computation | async-start | bytes 1179648 | tf_op jit(solution)/shard_map/all_to_all | solution.py:629
  71.2 2.4 %collective-permute-start.19 = (bf16[256,2048]{1,0:T(8,128)(2,1)}, bf16[256,2048]{1,0:T(8,128)(2,1)}, u32[]{:S(2)}, u32[]{:S(2)}) collective-permute-start(bf16[256,2048]{1,0:T(8,128)(2,1)} %wa_hbm.1), channel_id=1, source_target_pairs={{0,2},{1,3},{2,0},{3,1},{4,6},{5,7},{6,4},{7,5},{8,10},{9,11},{10,... | collective-permute-start | bytes 3145736 | tf_op jit(solution)/shard_map/ppermute | solution.py:633
  73.6 10.5 %all-to-all-done.parts_ref = bf16[8,144,256]{2,1,0:T(8,128)(2,1)} async-done(((bf16[8,144,256]{2,1,0:T(8,128)(2,1)}), bf16[8,144,256]{2,1,0:T(8,128)(2,1)}, u32[]{:S(2)}, u32[]{:S(2)}) %all-to-all-start) | async-done | bytes 589856 | tf_op jit(solution)/shard_map/all_to_all | solution.py:629
  84.2 2.3 %merge.1.a_ref = bf16[128,256]{1,0:T(8,128)(2,1)S(1)} custom-call(bf16[8,144,256]{2,1,0:T(8,128)(2,1)} %all-to-all-done.parts_ref), custom_call_target="tpu_custom_call" | custom-call | flops 1048576 | bytes 589824 | tf_op jit(solution)/shard_map/merge/pallas_call | solution.py:365
  86.5 2.5 %collective-permute-start.18 = (bf16[128,256]{1,0:T(8,128)(2,1)S(1)}, bf16[128,256]{1,0:T(8,128)(2,1)S(1)}, u32[]{:S(2)}, u32[]{:S(2)}) collective-permute-start(bf16[128,256]{1,0:T(8,128)(2,1)S(1)} %merge.1.a_ref), channel_id=1, source_target_pairs={{0,2},{1,3},{2,0},{3,1},{4,6},{5,7},{6,4},{7,5},{8,10},{9,11},{10,... | collective-permute-start | bytes 196616 | tf_op jit(solution)/shard_map/ppermute | solution.py:633
  89.9 2.5 %collective-permute-done.18.b_ref = bf16[128,256]{1,0:T(8,128)(2,1)S(1)} collective-permute-done((bf16[128,256]{1,0:T(8,128)(2,1)S(1)}, bf16[128,256]{1,0:T(8,128)(2,1)S(1)}, u32[]{:S(2)}, u32[]{:S(2)}) %collective-permute-start.18) | collective-permute-done | bytes 65568 | tf_op jit(solution)/shard_map/ppermute | solution.py:633
  92.3 1.0 copy-done.1
  93.4 1.2 copy-done.3
  94.6 2.0 %layer_product.1 = (f32[128,2048]{1,0:T(8,128)S(1)}, bf16[128,2048]{1,0:T(8,128)(2,1)S(1)}, bf16[32,2048]{1,0:T(8,128)(2,1)S(1)}) custom-call(bf16[128,2048]{1,0:T(8,128)(2,1)S(1)} %copy-done.1, bf16[128,256]{1,0:T(8,128)(2,1)S(1)} %merge.1.a_ref, bf16[128,256]{1,0:T(8,128)(2,1)S(1)} %collective-permute-done.18.b_ref, bf16[256,2048]{1,0:T(8,128)(2,1)S(1)} %copy-done.3, ...), custom_call_target="tpu_custom_call" | custom-call | flops 268435456 | bytes 2097152 | tf_op jit(solution)/shard_map/layer_product/pallas_call | solution.py:411
  96.7 9.0 %collective-permute-start.20 = (bf16[128,2048]{1,0:T(8,128)(2,1)S(1)}, bf16[128,2048]{1,0:T(8,128)(2,1)S(1)}, u32[]{:S(2)}, u32[]{:S(2)}) collective-permute-start(bf16[128,2048]{1,0:T(8,128)(2,1)S(1)} %get-tuple-element.54), channel_id=1, source_target_pairs={{0,1},{1,0},{2,3},{3,2},{4,5},{5,4},{6,7},{7,6},{8,9},{9,8},{10,11... | collective-permute-start | bytes 1572872 | tf_op jit(solution)/shard_map/ppermute | solution.py:633
  105.7 2.1 %collective-permute-start.22 = (bf16[32,2048]{1,0:T(8,128)(2,1)S(1)}, bf16[32,2048]{1,0:T(8,128)(2,1)S(1)}, u32[]{:S(2)}, u32[]{:S(2)}) collective-permute-start(bf16[32,2048]{1,0:T(8,128)(2,1)S(1)} %get-tuple-element.55), channel_id=1, source_target_pairs={{0,5},{1,4},{2,7},{3,6},{4,9},{5,8},{6,11},{7,10},{8,13},{9,12},{1... | collective-permute-start | bytes 393224 | tf_op jit(solution)/shard_map/ppermute | solution.py:703
  107.8 2.9 %collective-permute-start.21 = (bf16[32,2048]{1,0:T(8,128)(2,1)S(1)}, bf16[32,2048]{1,0:T(8,128)(2,1)S(1)}, u32[]{:S(2)}, u32[]{:S(2)}) collective-permute-start(bf16[32,2048]{1,0:T(8,128)(2,1)S(1)} %get-tuple-element.55), channel_id=1, source_target_pairs={{0,4},{1,5},{2,6},{3,7},{4,8},{5,9},{6,10},{7,11},{8,12},{9,13},{1... | collective-permute-start | bytes 393224 | tf_op jit(solution)/shard_map/ppermute | solution.py:702
  110.7 2.3 %collective-permute-done.21.rim_a = bf16[32,2048]{1,0:T(8,128)(2,1)S(1)} collective-permute-done((bf16[32,2048]{1,0:T(8,128)(2,1)S(1)}, bf16[32,2048]{1,0:T(8,128)(2,1)S(1)}, u32[]{:S(2)}, u32[]{:S(2)}) %collective-permute-start.21) | collective-permute-done | bytes 131104 | tf_op jit(solution)/shard_map/ppermute | solution.py:702
  113.1 1.9 %short_project.1 = (bf16[128,512]{1,0:T(8,128)(2,1)S(1)}, bf16[8,32,256]{2,1,0:T(8,128)(2,1)}, bf16[32,512]{1,0:T(8,128)(2,1)S(1)}) custom-call(f32[128,2048]{1,0:T(8,128)S(1)} %get-tuple-element.53.sum_ref, bf16[128,2048]{1,0:T(8,128)(2,1)S(1)} %collective-permute-done.20.term_ref, bf16[32,2048]{1,0:T(8,128)(2,1)S(1)} %collective-permute-done.21.rim_a, ...), custom_call_target="tpu_custom_call" | custom-call | flops 100663296 | bytes 3670016 | tf_op jit(solution)/shard_map/short_project/pallas_call | solution.py:485
  115.0 9.5 %all-to-all-start.1 = ((bf16[8,32,256]{2,1,0:T(8,128)(2,1)}), bf16[8,32,256]{2,1,0:T(8,128)(2,1)S(1)}, u32[]{:S(2)}, u32[]{:S(2)}) async-start(bf16[8,32,256]{2,1,0:T(8,128)(2,1)} %get-tuple-element.57), calls=%async_computation.1 | async-start | bytes 262144 | tf_op jit(solution)/shard_map/all_to_all | solution.py:629
  124.5 2.8 %collective-permute-done.23.b_ref = bf16[32,512]{1,0:T(8,128)(2,1)S(1)} collective-permute-done((bf16[32,512]{1,0:T(8,128)(2,1)S(1)}, bf16[32,512]{1,0:T(8,128)(2,1)S(1)}, u32[]{:S(2)}, u32[]{:S(2)}) %collective-permute-start.23) | collective-permute-done | bytes 32800 | tf_op jit(solution)/shard_map/ppermute | solution.py:633
  127.9 1.1 collective-permute-start.25
  129.5 1.2 collective-permute-done.26.refs_3_
  130.7 1.8 %collective-permute-done.25.refs_2_ = bf16[64,512]{1,0:T(8,128)(2,1)S(1)} collective-permute-done((bf16[64,512]{1,0:T(8,128)(2,1)S(1)}, bf16[64,512]{1,0:T(8,128)(2,1)S(1)}, u32[]{:S(2)}, u32[]{:S(2)}) %collective-permute-start.25) | collective-permute-done | bytes 65568 | tf_op jit(solution)/shard_map/ppermute | solution.py:638
  132.5 1.1 collective-permute-done.24.refs_1_
  133.6 1.0 short_attend.1
  134.6 15.1 %all_to_all.15.parts_ref = bf16[8,32,384]{2,1,0:T(8,128)(2,1)S(1)} all-to-all(bf16[8,32,384]{2,1,0:T(8,128)(2,1)S(1)} %short_attend.1), channel_id=1, replica_groups=mesh['y'=4,'z'=8,'xl'=2,'tp'=4] {'z'}, dimensions={0} | all-to-all | bytes 393216 | tf_op jit(solution)/shard_map/all_to_all | solution.py:629
  149.7 1.2 copy-done.2
  151.4 5.7 %collective-permute-start.27 = (bf16[32,512]{1,0:T(8,128)(2,1)S(1)}, bf16[32,512]{1,0:T(8,128)(2,1)S(1)}, u32[]{:S(2)}, u32[]{:S(2)}) collective-permute-start(bf16[32,512]{1,0:T(8,128)(2,1)S(1)} %get-tuple-element.60), channel_id=1, source_target_pairs={{0,1},{1,0},{2,3},{3,2},{4,5},{5,4},{6,7},{7,6},{8,9},{9,8},{10,11... | collective-permute-start | bytes 98312 | tf_op jit(solution)/shard_map/ppermute | solution.py:633
  157.1 2.5 %collective-permute-start.28 = (bf16[32,512]{1,0:T(8,128)(2,1)S(1)}, bf16[32,512]{1,0:T(8,128)(2,1)S(1)}, u32[]{:S(2)}, u32[]{:S(2)}) collective-permute-start(bf16[32,512]{1,0:T(8,128)(2,1)S(1)} %get-tuple-element.61), channel_id=1, source_target_pairs={{0,2},{1,3},{2,0},{3,1},{4,6},{5,7},{6,4},{7,5},{8,10},{9,11},{10,... | collective-permute-start | bytes 98312 | tf_op jit(solution)/shard_map/ppermute | solution.py:633
  160.3 1.0 collective-permute-done.28.refs_2_
  161.4 3.0 %collective-permute-done.29.refs_3_ = bf16[32,512]{1,0:T(8,128)(2,1)S(1)} collective-permute-done((bf16[32,512]{1,0:T(8,128)(2,1)S(1)}, bf16[32,512]{1,0:T(8,128)(2,1)S(1)}, u32[]{:S(2)}, u32[]{:S(2)}) %collective-permute-start.29) | collective-permute-done | bytes 32800 | tf_op jit(solution)/shard_map/ppermute | solution.py:633
  (52 shorter events, 6.6 us)
Async XLA Ops:
  0.0 52.1 %copy-start.8 = (f32[2]{0:T(128)S(1)}, f32[2]{0:T(128)}, u32[]{:S(2)}) copy-start(f32[2]{0:T(128)} %slope_ref.2) | copy-start | bytes 28
  0.7 5.5 %collective-permute-start = (f32[8,128]{1,0:T(8,128)S(1)}, f32[8,128]{1,0:T(8,128)S(1)}, u32[]{:S(2)}, u32[]{:S(2)}) collective-permute-start(f32[8,128]{1,0:T(8,128)S(1)} %own_count.1.a_ref), channel_id=1, source_target_pairs={{0,4},{4,0},{1,5},{5,1},{2,6},{6,2},{3,7},{7,3},{8,12},{12,8},{9,1... | collective-permute-start | bytes 12296 | tf_op jit(solution)/shard_map/ppermute | solution.py:633
  6.2 10.6 %collective-permute-start.3 = (bf16[768,256]{1,0:T(8,128)(2,1)}, bf16[768,256]{1,0:T(8,128)(2,1)S(1)}, u32[]{:S(2)}, u32[]{:S(2)}) collective-permute-start(bf16[768,256]{1,0:T(8,128)(2,1)} %get-tuple-element.37.refs_7_), channel_id=1, source_target_pairs={{0,192},{64,0},{128,64},{192,128},{1,193},{65,1},{129,65},{193,129... | collective-permute-start | bytes 1179656 | tf_op jit(solution)/shard_map/ppermute | solution.py:638
  9.0 10.8 %collective-permute-start.2 = (bf16[768,256]{1,0:T(8,128)(2,1)}, bf16[768,256]{1,0:T(8,128)(2,1)S(1)}, u32[]{:S(2)}, u32[]{:S(2)}) collective-permute-start(bf16[768,256]{1,0:T(8,128)(2,1)} %get-tuple-element.37.refs_7_), channel_id=1, source_target_pairs={{0,64},{64,128},{128,192},{192,0},{1,65},{65,129},{129,193},{193,1... | collective-permute-start | bytes 1179656 | tf_op jit(solution)/shard_map/ppermute | solution.py:638
  9.0 10.8 %collective-permute-start.1 = (bf16[768,256]{1,0:T(8,128)(2,1)}, bf16[768,256]{1,0:T(8,128)(2,1)S(1)}, u32[]{:S(2)}, u32[]{:S(2)}) collective-permute-start(bf16[768,256]{1,0:T(8,128)(2,1)} %get-tuple-element.37.refs_7_), channel_id=1, source_target_pairs={{0,4},{4,0},{1,5},{5,1},{2,6},{6,2},{3,7},{7,3},{8,12},{12,8},{9,1... | collective-permute-start | bytes 1179656 | tf_op jit(solution)/shard_map/ppermute | solution.py:633
  9.3 4.4 %collective-permute-start.4 = (bf16[128,256]{1,0:T(8,128)(2,1)}, bf16[128,256]{1,0:T(8,128)(2,1)S(1)}, u32[]{:S(2)}, u32[]{:S(2)}) collective-permute-start(bf16[128,256]{1,0:T(8,128)(2,1)} %get-tuple-element.36.a_ref), channel_id=1, source_target_pairs={{0,8},{8,0},{16,24},{24,16},{32,40},{40,32},{48,56},{56,48},{1,9},... | collective-permute-start | bytes 196616 | tf_op jit(solution)/shard_map/ppermute | solution.py:633
  10.9 2.8 %collective-permute-start.5 = (f32[8,128]{1,0:T(8,128)S(1)}, f32[8,128]{1,0:T(8,128)S(1)}, u32[]{:S(2)}, u32[]{:S(2)}) collective-permute-start(f32[8,128]{1,0:T(8,128)S(1)} %added.5.a_ref), channel_id=1, source_target_pairs={{0,8},{8,0},{16,24},{24,16},{32,40},{40,32},{48,56},{56,48},{1,9},... | collective-permute-start | bytes 12296 | tf_op jit(solution)/shard_map/ppermute | solution.py:633
  19.8 18.9 %collective-permute-start.7 = (bf16[768,256]{1,0:T(8,128)(2,1)S(1)}, bf16[768,256]{1,0:T(8,128)(2,1)S(1)}, u32[]{:S(2)}, u32[]{:S(2)}) collective-permute-start(bf16[768,256]{1,0:T(8,128)(2,1)S(1)} %collective-permute-done.1.refs_8_), channel_id=1, source_target_pairs={{0,192},{64,0},{128,64},{192,128},{1,193},{65,1},{129,65},{193,129... | collective-permute-start | bytes 1179656 | tf_op jit(solution)/shard_map/ppermute | solution.py:638
  21.0 17.7 %collective-permute-start.6 = (bf16[768,256]{1,0:T(8,128)(2,1)S(1)}, bf16[768,256]{1,0:T(8,128)(2,1)S(1)}, u32[]{:S(2)}, u32[]{:S(2)}) collective-permute-start(bf16[768,256]{1,0:T(8,128)(2,1)S(1)} %collective-permute-done.1.refs_8_), channel_id=1, source_target_pairs={{0,64},{64,128},{128,192},{192,0},{1,65},{65,129},{129,193},{193,1... | collective-permute-start | bytes 1179656 | tf_op jit(solution)/shard_map/ppermute | solution.py:638
  21.3 0.8 copy-start.5
  22.1 16.6 %collective-permute-start.9 = (bf16[256,256]{1,0:T(8,128)(2,1)S(1)}, bf16[256,256]{1,0:T(8,128)(2,1)S(1)}, u32[]{:S(2)}, u32[]{:S(2)}) collective-permute-start(bf16[256,256]{1,0:T(8,128)(2,1)S(1)} %join.2.refs_0_), channel_id=1, source_target_pairs={{0,48},{8,56},{16,0},{24,8},{32,16},{40,24},{48,32},{56,40},{1,49}... | collective-permute-start | bytes 393224 | tf_op jit(solution)/shard_map/ppermute | solution.py:638
  28.2 10.4 %collective-permute-start.8 = (bf16[256,256]{1,0:T(8,128)(2,1)S(1)}, bf16[256,256]{1,0:T(8,128)(2,1)S(1)}, u32[]{:S(2)}, u32[]{:S(2)}) collective-permute-start(bf16[256,256]{1,0:T(8,128)(2,1)S(1)} %join.2.refs_0_), channel_id=1, source_target_pairs={{0,16},{8,24},{16,32},{24,40},{32,48},{40,56},{48,0},{56,8},{1,17}... | collective-permute-start | bytes 393224 | tf_op jit(solution)/shard_map/ppermute | solution.py:638
  28.2 4.1 %collective-permute-start.10 = (f32[8,128]{1,0:T(8,128)S(1)}, f32[8,128]{1,0:T(8,128)S(1)}, u32[]{:S(2)}, u32[]{:S(2)}) collective-permute-start(f32[8,128]{1,0:T(8,128)S(1)} %added.6.a_ref), channel_id=1, source_target_pairs={{0,16},{8,24},{16,0},{24,8},{32,48},{40,56},{48,32},{56,40},{1,17}... | collective-permute-start | bytes 12296 | tf_op jit(solution)/shard_map/ppermute | solution.py:633
  32.3 6.4 %collective-permute-start.11 = (f32[8,128]{1,0:T(8,128)S(1)}, f32[8,128]{1,0:T(8,128)S(1)}, u32[]{:S(2)}, u32[]{:S(2)}) collective-permute-start(f32[8,128]{1,0:T(8,128)S(1)} %added.7.a_ref), channel_id=1, source_target_pairs={{0,32},{8,40},{16,48},{24,56},{32,0},{40,8},{48,16},{56,24},{1,33}... | collective-permute-start | bytes 12296 | tf_op jit(solution)/shard_map/ppermute | solution.py:633
  38.7 13.3 %collective-permute-start.16 = (bf16[768,256]{1,0:T(8,128)(2,1)S(1)}, bf16[768,256]{1,0:T(8,128)(2,1)S(1)}, u32[]{:S(2)}, u32[]{:S(2)}) collective-permute-start(bf16[768,256]{1,0:T(8,128)(2,1)S(1)} %collective-permute-done.2.refs_9_), channel_id=1, source_target_pairs={{0,64},{64,128},{128,192},{192,0},{1,65},{65,129},{129,193},{193,1... | collective-permute-start | bytes 1179656 | tf_op jit(solution)/shard_map/ppermute | solution.py:638
  38.8 13.2 %collective-permute-start.17 = (bf16[768,256]{1,0:T(8,128)(2,1)S(1)}, bf16[768,256]{1,0:T(8,128)(2,1)S(1)}, u32[]{:S(2)}, u32[]{:S(2)}) collective-permute-start(bf16[768,256]{1,0:T(8,128)(2,1)S(1)} %collective-permute-done.7.refs_12_), channel_id=1, source_target_pairs={{0,192},{64,0},{128,64},{192,128},{1,193},{65,1},{129,65},{193,129... | collective-permute-start | bytes 1179656 | tf_op jit(solution)/shard_map/ppermute | solution.py:638
  41.5 10.6 %collective-permute-start.12 = (bf16[128,256]{1,0:T(8,128)(2,1)S(1)}, bf16[128,256]{1,0:T(8,128)(2,1)S(1)}, u32[]{:S(2)}, u32[]{:S(2)}) collective-permute-start(bf16[128,256]{1,0:T(8,128)(2,1)S(1)} %get-tuple-element.45), channel_id=1, source_target_pairs={{0,16},{8,24},{16,32},{24,40},{32,48},{40,56},{48,0},{56,8},{1,17}... | collective-permute-start | bytes 196616 | tf_op jit(solution)/shard_map/ppermute | solution.py:638
  43.0 9.1 %collective-permute-start.13 = (bf16[128,256]{1,0:T(8,128)(2,1)S(1)}, bf16[128,256]{1,0:T(8,128)(2,1)S(1)}, u32[]{:S(2)}, u32[]{:S(2)}) collective-permute-start(bf16[128,256]{1,0:T(8,128)(2,1)S(1)} %get-tuple-element.46), channel_id=1, source_target_pairs={{0,48},{8,56},{16,0},{24,8},{32,16},{40,24},{48,32},{56,40},{1,49}... | collective-permute-start | bytes 196616 | tf_op jit(solution)/shard_map/ppermute | solution.py:638
  45.1 2.8 %collective-permute-start.14 = (f32[8,128]{1,0:T(8,128)S(1)}, f32[8,128]{1,0:T(8,128)S(1)}, u32[]{:S(2)}, u32[]{:S(2)}) collective-permute-start(f32[8,128]{1,0:T(8,128)S(1)} %added.8.a_ref), channel_id=1, source_target_pairs={{0,64},{64,0},{128,192},{192,128},{1,65},{65,1},{129,193},{193,129... | collective-permute-start | bytes 12296 | tf_op jit(solution)/shard_map/ppermute | solution.py:633
  48.0 4.1 %collective-permute-start.15 = (f32[8,128]{1,0:T(8,128)S(1)}, f32[8,128]{1,0:T(8,128)S(1)}, u32[]{:S(2)}, u32[]{:S(2)}) collective-permute-start(f32[8,128]{1,0:T(8,128)S(1)} %added.9.refs_5_), channel_id=1, source_target_pairs={{0,128},{64,192},{128,0},{192,64},{1,129},{65,193},{129,1},{193,65... | collective-permute-start | bytes 12296 | tf_op jit(solution)/shard_map/ppermute | solution.py:633
  52.1 1.0 copy-start.7
  65.3 0.8 copy-start.4
  66.1 46.9 %copy-start = (bf16[2048,3,256]{2,0,1:T(8,128)(2,1)S(1)}, bf16[2048,3,256]{2,0,1:T(8,128)(2,1)}, u32[]{:S(2)}) copy-start(bf16[2048,3,256]{2,0,1:T(8,128)(2,1)} %param.17) | copy-start | bytes 9437188
  66.1 18.0 %all-to-all-start = ((bf16[8,144,256]{2,1,0:T(8,128)(2,1)}), bf16[8,144,256]{2,1,0:T(8,128)(2,1)}, u32[]{:S(2)}, u32[]{:S(2)}) async-start(bf16[8,144,256]{2,1,0:T(8,128)(2,1)} %copy-done.4), calls=%async_computation | async-start | bytes 1179648 | tf_op jit(solution)/shard_map/all_to_all | solution.py:629
  71.2 18.7 %collective-permute-start.19 = (bf16[256,2048]{1,0:T(8,128)(2,1)}, bf16[256,2048]{1,0:T(8,128)(2,1)}, u32[]{:S(2)}, u32[]{:S(2)}) collective-permute-start(bf16[256,2048]{1,0:T(8,128)(2,1)} %wa_hbm.1), channel_id=1, source_target_pairs={{0,2},{1,3},{2,0},{3,1},{4,6},{5,7},{6,4},{7,5},{8,10},{9,11},{10,... | collective-permute-start | bytes 3145736 | tf_op jit(solution)/shard_map/ppermute | solution.py:633
  86.5 5.9 %collective-permute-start.18 = (bf16[128,256]{1,0:T(8,128)(2,1)S(1)}, bf16[128,256]{1,0:T(8,128)(2,1)S(1)}, u32[]{:S(2)}, u32[]{:S(2)}) collective-permute-start(bf16[128,256]{1,0:T(8,128)(2,1)S(1)} %merge.1.a_ref), channel_id=1, source_target_pairs={{0,2},{1,3},{2,0},{3,1},{4,6},{5,7},{6,4},{7,5},{8,10},{9,11},{10,... | collective-permute-start | bytes 196616 | tf_op jit(solution)/shard_map/ppermute | solution.py:633
  92.3 1.0 copy-start.1
  93.4 1.2 copy-start.3
  96.6 36.9 %copy-start.6 = (f32[2]{0:T(128)S(1)}, f32[2]{0:T(128)}, u32[]{:S(2)}) copy-start(f32[2]{0:T(128)} %slope_ref.3) | copy-start | bytes 28
  96.7 16.4 %collective-permute-start.20 = (bf16[128,2048]{1,0:T(8,128)(2,1)S(1)}, bf16[128,2048]{1,0:T(8,128)(2,1)S(1)}, u32[]{:S(2)}, u32[]{:S(2)}) collective-permute-start(bf16[128,2048]{1,0:T(8,128)(2,1)S(1)} %get-tuple-element.54), channel_id=1, source_target_pairs={{0,1},{1,0},{2,3},{3,2},{4,5},{5,4},{6,7},{7,6},{8,9},{9,8},{10,11... | collective-permute-start | bytes 1572872 | tf_op jit(solution)/shard_map/ppermute | solution.py:633
  105.7 5.0 %collective-permute-start.22 = (bf16[32,2048]{1,0:T(8,128)(2,1)S(1)}, bf16[32,2048]{1,0:T(8,128)(2,1)S(1)}, u32[]{:S(2)}, u32[]{:S(2)}) collective-permute-start(bf16[32,2048]{1,0:T(8,128)(2,1)S(1)} %get-tuple-element.55), channel_id=1, source_target_pairs={{0,5},{1,4},{2,7},{3,6},{4,9},{5,8},{6,11},{7,10},{8,13},{9,12},{1... | collective-permute-start | bytes 393224 | tf_op jit(solution)/shard_map/ppermute | solution.py:703
  107.8 5.3 %collective-permute-start.21 = (bf16[32,2048]{1,0:T(8,128)(2,1)S(1)}, bf16[32,2048]{1,0:T(8,128)(2,1)S(1)}, u32[]{:S(2)}, u32[]{:S(2)}) collective-permute-start(bf16[32,2048]{1,0:T(8,128)(2,1)S(1)} %get-tuple-element.55), channel_id=1, source_target_pairs={{0,4},{1,5},{2,6},{3,7},{4,8},{5,9},{6,10},{7,11},{8,12},{9,13},{1... | collective-permute-start | bytes 393224 | tf_op jit(solution)/shard_map/ppermute | solution.py:702
  115.0 18.6 %all-to-all-start.1 = ((bf16[8,32,256]{2,1,0:T(8,128)(2,1)}), bf16[8,32,256]{2,1,0:T(8,128)(2,1)S(1)}, u32[]{:S(2)}, u32[]{:S(2)}) async-start(bf16[8,32,256]{2,1,0:T(8,128)(2,1)} %get-tuple-element.57), calls=%async_computation.1 | async-start | bytes 262144 | tf_op jit(solution)/shard_map/all_to_all | solution.py:629
  124.5 2.8 %collective-permute-start.23 = (bf16[32,512]{1,0:T(8,128)(2,1)S(1)}, bf16[32,512]{1,0:T(8,128)(2,1)S(1)}, u32[]{:S(2)}, u32[]{:S(2)}) collective-permute-start(bf16[32,512]{1,0:T(8,128)(2,1)S(1)} %get-tuple-element.58.a_ref), channel_id=1, source_target_pairs={{0,4},{4,0},{1,5},{5,1},{2,6},{6,2},{3,7},{7,3},{8,12},{12,8},{9,1... | collective-permute-start | bytes 98312 | tf_op jit(solution)/shard_map/ppermute | solution.py:633
  127.3 3.4 %collective-permute-start.26 = (bf16[64,512]{1,0:T(8,128)(2,1)S(1)}, bf16[64,512]{1,0:T(8,128)(2,1)S(1)}, u32[]{:S(2)}, u32[]{:S(2)}) collective-permute-start(bf16[64,512]{1,0:T(8,128)(2,1)S(1)} %join.3.refs_0_), channel_id=1, source_target_pairs={{0,192},{64,0},{128,64},{192,128},{1,193},{65,1},{129,65},{193,129... | collective-permute-start | bytes 196616 | tf_op jit(solution)/shard_map/ppermute | solution.py:638
  127.9 4.6 %collective-permute-start.25 = (bf16[64,512]{1,0:T(8,128)(2,1)S(1)}, bf16[64,512]{1,0:T(8,128)(2,1)S(1)}, u32[]{:S(2)}, u32[]{:S(2)}) collective-permute-start(bf16[64,512]{1,0:T(8,128)(2,1)S(1)} %join.3.refs_0_), channel_id=1, source_target_pairs={{0,128},{64,192},{128,0},{192,64},{1,129},{65,193},{129,1},{193,65... | collective-permute-start | bytes 196616 | tf_op jit(solution)/shard_map/ppermute | solution.py:638
  128.9 4.6 %collective-permute-start.24 = (bf16[64,512]{1,0:T(8,128)(2,1)S(1)}, bf16[64,512]{1,0:T(8,128)(2,1)S(1)}, u32[]{:S(2)}, u32[]{:S(2)}) collective-permute-start(bf16[64,512]{1,0:T(8,128)(2,1)S(1)} %join.3.refs_0_), channel_id=1, source_target_pairs={{0,64},{64,128},{128,192},{192,0},{1,65},{65,129},{129,193},{193,1... | collective-permute-start | bytes 196616 | tf_op jit(solution)/shard_map/ppermute | solution.py:638
  149.7 1.2 copy-start.2
  151.4 8.9 %collective-permute-start.27 = (bf16[32,512]{1,0:T(8,128)(2,1)S(1)}, bf16[32,512]{1,0:T(8,128)(2,1)S(1)}, u32[]{:S(2)}, u32[]{:S(2)}) collective-permute-start(bf16[32,512]{1,0:T(8,128)(2,1)S(1)} %get-tuple-element.60), channel_id=1, source_target_pairs={{0,1},{1,0},{2,3},{3,2},{4,5},{5,4},{6,7},{7,6},{8,9},{9,8},{10,11... | collective-permute-start | bytes 98312 | tf_op jit(solution)/shard_map/ppermute | solution.py:633
  157.1 4.3 %collective-permute-start.28 = (bf16[32,512]{1,0:T(8,128)(2,1)S(1)}, bf16[32,512]{1,0:T(8,128)(2,1)S(1)}, u32[]{:S(2)}, u32[]{:S(2)}) collective-permute-start(bf16[32,512]{1,0:T(8,128)(2,1)S(1)} %get-tuple-element.61), channel_id=1, source_target_pairs={{0,2},{1,3},{2,0},{3,1},{4,6},{5,7},{6,4},{7,5},{8,10},{9,11},{10,... | collective-permute-start | bytes 98312 | tf_op jit(solution)/shard_map/ppermute | solution.py:633
  159.6 4.9 %collective-permute-start.29 = (bf16[32,512]{1,0:T(8,128)(2,1)S(1)}, bf16[32,512]{1,0:T(8,128)(2,1)S(1)}, u32[]{:S(2)}, u32[]{:S(2)}) collective-permute-start(bf16[32,512]{1,0:T(8,128)(2,1)S(1)} %get-tuple-element.62), channel_id=1, source_target_pairs={{0,3},{1,2},{2,1},{3,0},{4,7},{5,6},{6,5},{7,4},{8,11},{9,10},{10,... | collective-permute-start | bytes 98312 | tf_op jit(solution)/shard_map/ppermute | solution.py:633

commit v6 on v5

--- a/solution.py
+++ b/solution.py
@@ -45,58 +45,84 @@
     return hi, mid, lo
 
 
-def project_kernel(
-    tok_hbm, w_hbm, ck_hbm, cv_hbm, q_ref, pack_ref, tok, weight, sems
-):
-    rows = tok.shape[0]
-    slots = ck_hbm.shape[0]
-    copies = [pltpu.make_async_copy(tok_hbm, tok, sems.at[0])]
-    copies += [
-        pltpu.make_async_copy(w_hbm.at[i], weight.at[i], sems.at[1 + i]) for i in range(3)
-    ]
-    copies += [
-        pltpu.make_async_copy(ck_hbm, pack_ref.at[:slots], sems.at[4]),
-        pltpu.make_async_copy(cv_hbm, pack_ref.at[slots : 2 * slots], sems.at[5]),
+def query_kernel(tok_hbm, w_hbm, q_ref, normed_ref, tok, weight, sems):
+    copies = [
+        pltpu.make_async_copy(tok_hbm, tok, sems.at[0]),
+        pltpu.make_async_copy(w_hbm.at[0], weight, sems.at[1]),
     ]
     for copy in copies:
         copy.start()
     copies[0].wait()
     normed = rms_scaled(tok[...].astype(F32))
-    for i in range(3):
+    normed_ref[...] = normed
+    copies[1].wait()
+    out = jnp.dot(normed, weight[...], preferred_element_type=F32)
+    q_ref[...] = (out * SCALE2).astype(BF16)
+
+
+def project_queries(rows, weight3):
+    n, d = rows.shape
+    width = weight3.shape[2]
+    hbm = pl.BlockSpec(memory_space=HBM)
+    vmem = pl.BlockSpec(memory_space=VMEM)
+    return pl.pallas_call(
+        query_kernel,
+        in_specs=[hbm, hbm],
+        out_specs=[vmem, vmem],
+        out_shape=[jax.ShapeDtypeStruct((n, w), BF16) for w in (width, d)],
+        scratch_shapes=[
+            VMEM((n, d), BF16),
+            VMEM((d, width), BF16),
+            pltpu.SemaphoreType.DMA((2,)),
+        ],
+        compiler_params=params(60),
+        cost_estimate=cost(2 * n * d * width, 2 * (n * d + d * width)),
+        name="project_queries",
+    )(rows, weight3)
+
+
+def pack_kernel(normed_hbm, w_hbm, ck_hbm, cv_hbm, pack_ref, normed, weight, sems):
+    rows = normed.shape[0]
+    slots = ck_hbm.shape[0]
+    copies = [pltpu.make_async_copy(normed_hbm, normed, sems.at[0])]
+    copies += [
+        pltpu.make_async_copy(w_hbm.at[1 + i], weight.at[i], sems.at[1 + i]) for i in range(2)
+    ]
+    copies += [
+        pltpu.make_async_copy(ck_hbm, pack_ref.at[:slots], sems.at[3]),
+        pltpu.make_async_copy(cv_hbm, pack_ref.at[slots : 2 * slots], sems.at[4]),
+    ]
+    for copy in copies:
+        copy.start()
+    copies[0].wait()
+    for i in range(2):
         copies[1 + i].wait()
-        out = jnp.dot(normed, weight[i], preferred_element_type=F32)
-        if i == 0:
-            q_ref[...] = (out * SCALE2).astype(BF16)
-        else:
-            at = 2 * slots + (i - 1) * rows
-            pack_ref[at : at + rows] = out.astype(BF16)
+        out = jnp.dot(normed[...], weight[i], preferred_element_type=F32)
+        at = 2 * slots + i * rows
+        pack_ref[at : at + rows] = out.astype(BF16)
+    copies[3].wait()
     copies[4].wait()
-    copies[5].wait()
-
-
-def project(rows, weight3, cache_keys, cache_values):
-    n, d = rows.shape
+
+
+def project_pack(normed, weight3, cache_keys, cache_values):
+    n, d = normed.shape
     width = weight3.shape[2]
     total = 2 * (n + cache_keys.shape[0])
     hbm = pl.BlockSpec(memory_space=HBM)
-    vmem = pl.BlockSpec(memory_space=VMEM)
-    return pl.pallas_call(
-        project_kernel,
+    return pl.pallas_call(
+        pack_kernel,
         in_specs=[hbm] * 4,
-        out_specs=[vmem, vmem],
-        out_shape=[
-            jax.ShapeDtypeStruct((n, width), BF16),
-            jax.ShapeDtypeStruct((total, width), BF16),
-        ],
+        out_specs=pl.BlockSpec(memory_space=VMEM),
+        out_shape=jax.ShapeDtypeStruct((total, width), BF16),
         scratch_shapes=[
             VMEM((n, d), BF16),
-            VMEM(weight3.shape, BF16),
-            pltpu.SemaphoreType.DMA((6,)),
+            VMEM((2, d, width), BF16),
+            pltpu.SemaphoreType.DMA((5,)),
         ],
         compiler_params=params(60),
-        cost_estimate=cost(6 * n * d * width, 2 * (n * d + 3 * d * width)),
-        name="project",
-    )(rows, weight3, cache_keys, cache_values)
+        cost_estimate=cost(4 * n * d * width, 2 * (n * d + 2 * d * width)),
+        name="project_pack",
+    )(normed, weight3, cache_keys, cache_values)
 
 
 def table_kernel(count_ref, out_ref):
@@ -550,7 +576,10 @@
     )(slopes, queries, *keys)
 
 
-def short_merge_kernel(heads, parts_ref, w_ref, *outs):
+def short_merge_kernel(heads, parts_ref, w_hbm, *refs):
+    outs, (w_ref, sem) = refs[:4], refs[4:]
+    load = pltpu.make_async_copy(w_hbm, w_ref, sem)
+    load.start()
     sources, rows, padded = parts_ref.shape
     width = padded - HS
     merged = []
@@ -573,6 +602,7 @@
         merged.append((acc / total).astype(BF16))
     att = jnp.concatenate(merged, axis=1)
     cols = outs[0].shape[1]
+    load.wait()
     terms = [
         jnp.dot(
             att, w_ref[:, t * cols : (t + 1) * cols], preferred_element_type=F32
@@ -594,8 +624,10 @@
     out = jax.ShapeDtypeStruct((rows, cols), BF16)
     return pl.pallas_call(
         functools.partial(short_merge_kernel, width // HS),
+        in_specs=[pl.BlockSpec(memory_space=VMEM), pl.BlockSpec(memory_space=HBM)],
         out_shape=[out] * 4,
-        compiler_params=params(16),
+        scratch_shapes=[VMEM(weight.shape, BF16), pltpu.SemaphoreType.DMA],
+        compiler_params=params(60),
         cost_estimate=cost(8 * rows * width * cols, 8 * width * cols),
         name="short_merge",
     )(parts, weight)
@@ -666,12 +698,14 @@
 ):
     axes = ("y", "z", "xl", "tp")
     slots = cache_keys.shape[0]
-    q, pack = project(
-        tokens, jnp.transpose(project_weight, (1, 0, 2)), cache_keys, cache_values
-    )
+    weight3 = jnp.transpose(project_weight, (1, 0, 2))
     table = counts_along(own_count(cache_count), "xl", 1)
-    q, pack, table = lax.optimization_barrier((q, pack, table))
+    q, normed = project_queries(tokens, weight3)
+    normed, table = lax.optimization_barrier((normed, table))
     table = counts_along(table, "z", 1)
+    pack = project_pack(normed, weight3, cache_keys, cache_values)
+    pack, table = lax.optimization_barrier((pack, table))
+    table = counts_along(table, "z", 2, 4)
     left, right = both_ways(pack, "y", 1)
     other, left, right, mate, table = lax.optimization_barrier(
         (swap(pack, "xl"), left, right, swap(q, "z"), table)
@@ -679,18 +713,18 @@
     pair = join(q, mate)
     left_other, right_other = both_ways(other, "y", 1)
     left_pair, right_pair = both_ways(pair, "z", 2)
-    table = counts_along(table, "z", 2, 4)
+    table = counts_along(table, "y", 1)
     left_other, right_other, left_pair, right_pair, left, table = lax.optimization_barrier(
         (left_other, right_other, left_pair, right_pair, left, table)
     )
-    table = counts_along(table, "y", 1)
     tables = [table, swap(table, "y", 2)]
     far, far_other = moved(left, "y", 1), moved(right_other, "y", -1)
     near = halves(left_pair, right_pair)
     queries = [pair, left_pair, right_pair, moved(near[0], "z", 2), moved(near[1], "z", -2)]
-    crossed = swap(after(output_weight, far), "tp", 2)
+    crossed = swap(after(output_weight, other), "tp", 2)
     packs = [pack, other, left, left_other, right, right_other, far, far_other]
     parts = attend(distance_slope, queries, tables, packs, slots)
+    parts, crossed = lax.optimization_barrier((parts, crossed))
 
     att = merge(exchange(parts, "z"))
     total, term, rim = layer_product(

time: 166 us -> 168 us (1.012)
  blocking collectives: 15.1 us -> 33.3 us
  waiting for transfers between devices: 47.7 us -> 32.6 us
  local copies, waits for them, and re-layouts: 6.13 us -> 1.78 us
  Pallas kernels: 24.4 us -> 27.5 us
    all_to_all x1 -> x2, blocking collectives: 15.1 us -> 33.3 us  [exchange(): return lax.all_to_all(blocks, axis, 0, 0)]
    all_to_all x2 -> x1, waiting for transfers between devices: 10.5 us -> 0.01 us  [exchange(): return lax.all_to_all(blocks, axis, 0, 0)]
    all_to_all x2 -> x1, starting transfers between devices: 14.6 us -> 4.62 us  [exchange(): return lax.all_to_all(blocks, axis, 0, 0)]
    ppermute x15, waiting for transfers between devices: 24.6 us -> 14.7 us  [swap(): lax.ppermute(x, axis, [(i, i ^ flip) for i in range(lax.axis_size(axis))])]
    ppermute x15, starting transfers between devices: 32.6 us -> 41.6 us  [swap(): lax.ppermute(x, axis, [(i, i ^ flip) for i in range(lax.axis_size(axis))])]
    pallas_call x2 -> x3, Pallas kernels: 3.86 us -> 8.58 us  [the longest x1 3.11 us: short_merge(): pl.pallas_call(functools.partial(short_merge_kernel, width // HS), in_spe...]
    ppermute x13, waiting for transfers between devices: 10.3 us -> 14.8 us  [moved(): return lax.ppermute(x, axis, [(i, (i + by) % n) for i in range(n)])]
    unnamed x18 -> x16, local copies, waits for them, and re-layouts: 6.13 us -> 1.78 us
  transfers between devices with their start and end apart: 32 -> 31, of which waited for: 17 -> 16; matrix products, arithmetic and copies ran while one was open for 0% -> 0% of each run, Pallas kernels for 3% -> 11%
where the time goes in v6:
time: 168 us; the launch traced here: 167 us
  starting transfers between devices  71.2 us (42%)
  blocking collectives  33.3 us (20%)
  waiting for transfers between devices  32.6 us (19%)
  Pallas kernels  27.5 us (16%)
  local copies, waits for them, and re-layouts  1.78 us (1%)
    ppermute x15, starting transfers between devices, swap(): lax.ppermute(x, axis, [(i, i ^ flip) for i in range(lax.axis_size(axis))])  41.6 us
    all_to_all x2, blocking collectives, exchange(): return lax.all_to_all(blocks, axis, 0, 0)  33.3 us
    ppermute x13, starting transfers between devices, moved(): return lax.ppermute(x, axis, [(i, (i + by) % n) for i in range(n)])  19.8 us
    ppermute x13, waiting for transfers between devices, moved(): return lax.ppermute(x, axis, [(i, (i + by) % n) for i in range(n)])  14.8 us
    ppermute x15, waiting for transfers between devices, swap(): lax.ppermute(x, axis, [(i, i ^ flip) for i in range(lax.axis_size(axis))])  14.7 us
    pallas_call x1, Pallas kernels, attend(): pl.pallas_call(functools.partial(attend_kernel, slots), grid=(4,), in_spe...  12.5 us
    all_to_all x1, starting transfers between devices, exchange(): return lax.all_to_all(blocks, axis, 0, 0)  4.62 us
  transfers between devices with their start and end apart: 31, of which 16 were waited for; matrix products, arithmetic and copies ran while one was open for 0% of the time, Pallas kernels for 11%

profile of v6, /device:TPU:1, one launch (start us, length us, event | category | flops | bytes accessed | tf_op | source)
XLA Modules:
  0.0 167.2 jit_solution(7219754942865759262)
XLA Ops:
  0.7 2.1 %collective-permute-start = (f32[8,128]{1,0:T(8,128)S(1)}, f32[8,128]{1,0:T(8,128)S(1)}, u32[]{:S(2)}, u32[]{:S(2)}) collective-permute-start(f32[8,128]{1,0:T(8,128)S(1)} %own_count.1.a_ref), channel_id=1, source_target_pairs={{0,4},{4,0},{1,5},{5,1},{2,6},{6,2},{3,7},{7,3},{8,12},{12,8},{9,1... | collective-permute-start | bytes 12296 | tf_op jit(solution)/shard_map/ppermute | solution.py:665
  2.8 2.4 %project_queries.1 = (bf16[128,256]{1,0:T(8,128)(2,1)}, bf16[128,2048]{1,0:T(8,128)(2,1)}) custom-call(bf16[128,2048]{1,0:T(8,128)(2,1)} %tok_hbm.3, bf16[3,2048,256]{2,1,0:T(8,128)(2,1)} %bitcast.3), custom_call_target="tpu_custom_call" | custom-call | flops 134217728 | bytes 1572864 | tf_op jit(solution)/shard_map/project_queries/pallas_call | solution.py:68
  5.3 1.7 %collective-permute-start.1 = (f32[8,128]{1,0:T(8,128)S(1)}, f32[8,128]{1,0:T(8,128)S(1)}, u32[]{:S(2)}, u32[]{:S(2)}) collective-permute-start(f32[8,128]{1,0:T(8,128)S(1)} %added.5.a_ref), channel_id=1, source_target_pairs={{0,8},{8,0},{16,24},{24,16},{32,40},{40,32},{48,56},{56,48},{1,9},... | collective-permute-start | bytes 12296 | tf_op jit(solution)/shard_map/ppermute | solution.py:665
  7.0 3.0 %project_pack.1.refs_7_ = bf16[768,256]{1,0:T(8,128)(2,1)} custom-call(bf16[128,2048]{1,0:T(8,128)(2,1)} %get-tuple-element.39.normed_hbm, bf16[3,2048,256]{2,1,0:T(8,128)(2,1)} %bitcast.4, bf16[256,256]{1,0:T(8,128)(2,1)} %ck_hbm.1, bf16[256,256]{1,0:T(8,128)(2,1)} %cv_hbm.1), custom_call_target="tpu_custom_call" | custom-call | flops 268435456 | bytes 2621440 | tf_op jit(solution)/shard_map/project_pack/pallas_call | solution.py:112
  10.1 2.8 %collective-permute-start.4 = (bf16[768,256]{1,0:T(8,128)(2,1)}, bf16[768,256]{1,0:T(8,128)(2,1)S(1)}, u32[]{:S(2)}, u32[]{:S(2)}) collective-permute-start(bf16[768,256]{1,0:T(8,128)(2,1)} %project_pack.1.refs_7_), channel_id=1, source_target_pairs={{0,192},{64,0},{128,64},{192,128},{1,193},{65,1},{129,65},{193,129... | collective-permute-start | bytes 1179656 | tf_op jit(solution)/shard_map/ppermute | solution.py:670
  13.2 3.0 %collective-permute-start.6 = (f32[8,128]{1,0:T(8,128)S(1)}, f32[8,128]{1,0:T(8,128)S(1)}, u32[]{:S(2)}, u32[]{:S(2)}) collective-permute-start(f32[8,128]{1,0:T(8,128)S(1)} %added.6.a_ref), channel_id=1, source_target_pairs={{0,16},{8,24},{16,0},{24,8},{32,48},{40,56},{48,32},{56,40},{1,17}... | collective-permute-start | bytes 12296 | tf_op jit(solution)/shard_map/ppermute | solution.py:665
  16.2 1.0 collective-permute-done.6.b_ref
  17.2 6.1 %collective-permute-start.7 = (f32[8,128]{1,0:T(8,128)S(1)}, f32[8,128]{1,0:T(8,128)S(1)}, u32[]{:S(2)}, u32[]{:S(2)}) collective-permute-start(f32[8,128]{1,0:T(8,128)S(1)} %added.7.a_ref), channel_id=1, source_target_pairs={{0,32},{8,40},{16,48},{24,56},{32,0},{40,8},{48,16},{56,24},{1,33}... | collective-permute-start | bytes 12296 | tf_op jit(solution)/shard_map/ppermute | solution.py:665
  23.3 1.0 collective-permute-done.7.b_ref
  24.3 3.0 %collective-permute-start.9 = (bf16[768,256]{1,0:T(8,128)(2,1)S(1)}, bf16[768,256]{1,0:T(8,128)(2,1)S(1)}, u32[]{:S(2)}, u32[]{:S(2)}) collective-permute-start(bf16[768,256]{1,0:T(8,128)(2,1)S(1)} %collective-permute-done.2.refs_8_), channel_id=1, source_target_pairs={{0,192},{64,0},{128,64},{192,128},{1,193},{65,1},{129,65},{193,129... | collective-permute-start | bytes 1179656 | tf_op jit(solution)/shard_map/ppermute | solution.py:670
  27.3 2.7 %collective-permute-start.18 = (bf16[256,2048]{1,0:T(8,128)(2,1)S(1)}, bf16[256,2048]{1,0:T(8,128)(2,1)S(1)}, u32[]{:S(2)}, u32[]{:S(2)}) collective-permute-start(bf16[256,2048]{1,0:T(8,128)(2,1)S(1)} %copy-done.2), channel_id=1, source_target_pairs={{0,2},{1,3},{2,0},{3,1},{4,6},{5,7},{6,4},{7,5},{8,10},{9,11},{10,... | collective-permute-start | bytes 3145736 | tf_op jit(solution)/shard_map/ppermute | solution.py:665
  30.1 4.6 %collective-permute-start.11 = (bf16[256,256]{1,0:T(8,128)(2,1)S(1)}, bf16[256,256]{1,0:T(8,128)(2,1)S(1)}, u32[]{:S(2)}, u32[]{:S(2)}) collective-permute-start(bf16[256,256]{1,0:T(8,128)(2,1)S(1)} %join.2.refs_0_), channel_id=1, source_target_pairs={{0,48},{8,56},{16,0},{24,8},{32,16},{40,24},{48,32},{56,40},{1,49}... | collective-permute-start | bytes 393224 | tf_op jit(solution)/shard_map/ppermute | solution.py:670
  34.7 3.3 %collective-permute-done.11.right_ref.refs_2_ = bf16[256,256]{1,0:T(8,128)(2,1)S(1)} collective-permute-done((bf16[256,256]{1,0:T(8,128)(2,1)S(1)}, bf16[256,256]{1,0:T(8,128)(2,1)S(1)}, u32[]{:S(2)}, u32[]{:S(2)}) %collective-permute-start.11) | collective-permute-done | bytes 131104 | tf_op jit(solution)/shard_map/ppermute | solution.py:670
  38.0 3.5 %collective-permute-done.10.left_ref.refs_1_ = bf16[256,256]{1,0:T(8,128)(2,1)S(1)} collective-permute-done((bf16[256,256]{1,0:T(8,128)(2,1)S(1)}, bf16[256,256]{1,0:T(8,128)(2,1)S(1)}, u32[]{:S(2)}, u32[]{:S(2)}) %collective-permute-start.10) | collective-permute-done | bytes 131104 | tf_op jit(solution)/shard_map/ppermute | solution.py:670
  41.4 1.5 collective-permute-start.16
  42.9 1.3 collective-permute-start.17
  44.2 2.9 %collective-permute-start.15 = (f32[8,128]{1,0:T(8,128)S(1)}, f32[8,128]{1,0:T(8,128)S(1)}, u32[]{:S(2)}, u32[]{:S(2)}) collective-permute-start(f32[8,128]{1,0:T(8,128)S(1)} %added.9.refs_5_), channel_id=1, source_target_pairs={{0,128},{64,192},{128,0},{192,64},{1,129},{65,193},{129,1},{193,65... | collective-permute-start | bytes 12296 | tf_op jit(solution)/shard_map/ppermute | solution.py:665
  47.4 3.8 %collective-permute-done.15.refs_6_ = f32[8,128]{1,0:T(8,128)S(1)} collective-permute-done((f32[8,128]{1,0:T(8,128)S(1)}, f32[8,128]{1,0:T(8,128)S(1)}, u32[]{:S(2)}, u32[]{:S(2)}) %collective-permute-start.15) | collective-permute-done | bytes 4128 | tf_op jit(solution)/shard_map/ppermute | solution.py:665
  51.8 1.1 collective-permute-done.13.refs_3_
  52.9 2.6 %collective-permute-done.14.refs_4_ = bf16[128,256]{1,0:T(8,128)(2,1)S(1)} collective-permute-done((bf16[128,256]{1,0:T(8,128)(2,1)S(1)}, bf16[128,256]{1,0:T(8,128)(2,1)S(1)}, u32[]{:S(2)}, u32[]{:S(2)}) %collective-permute-start.14) | collective-permute-done | bytes 65568 | tf_op jit(solution)/shard_map/ppermute | solution.py:670
  55.5 1.0 copy-done.3
  56.5 12.5 %attend.1 = bf16[8,144,256]{2,1,0:T(8,128)(2,1)S(1)} custom-call(f32[2]{0:T(128)S(1)} %copy-done.7, bf16[256,256]{1,0:T(8,128)(2,1)S(1)} %join.2.refs_0_, bf16[256,256]{1,0:T(8,128)(2,1)S(1)} %collective-permute-done.10.left_ref.refs_1_, bf16[256,256]{1,0:T(8,128)(2,1)S(1)} %collective-permute-done.11.right_ref.refs_2_, ...), custom_call_target="tpu_custom_call" | custom-call | flops 3221225472 | bytes 3145728 | tf_op jit(solution)/shard_map/attend/pallas_call | solution.py:349
  69.0 17.9 %all_to_all.15.parts_ref = bf16[8,144,256]{2,1,0:T(8,128)(2,1)S(1)} all-to-all(bf16[8,144,256]{2,1,0:T(8,128)(2,1)S(1)} %attend.1), channel_id=1, replica_groups=mesh['y'=4,'z'=8,'xl'=2,'tp'=4] {'z'}, dimensions={0} | all-to-all | bytes 1179648 | tf_op jit(solution)/shard_map/all_to_all | solution.py:661
  86.9 1.2 merge.1.a_ref
  88.1 1.0 collective-permute-start.19
  89.1 3.8 %collective-permute-done.19.b_ref = bf16[128,256]{1,0:T(8,128)(2,1)S(1)} collective-permute-done((bf16[128,256]{1,0:T(8,128)(2,1)S(1)}, bf16[128,256]{1,0:T(8,128)(2,1)S(1)}, u32[]{:S(2)}, u32[]{:S(2)}) %collective-permute-start.19) | collective-permute-done | bytes 65568 | tf_op jit(solution)/shard_map/ppermute | solution.py:665
  92.9 1.3 layer_product.1
  94.3 11.4 %collective-permute-start.20 = (bf16[128,2048]{1,0:T(8,128)(2,1)S(1)}, bf16[128,2048]{1,0:T(8,128)(2,1)S(1)}, u32[]{:S(2)}, u32[]{:S(2)}) collective-permute-start(bf16[128,2048]{1,0:T(8,128)(2,1)S(1)} %get-tuple-element.60), channel_id=1, source_target_pairs={{0,1},{1,0},{2,3},{3,2},{4,5},{5,4},{6,7},{7,6},{8,9},{9,8},{10,11... | collective-permute-start | bytes 1572872 | tf_op jit(solution)/shard_map/ppermute | solution.py:665
  105.7 2.7 %collective-permute-start.22 = (bf16[32,2048]{1,0:T(8,128)(2,1)S(1)}, bf16[32,2048]{1,0:T(8,128)(2,1)S(1)}, u32[]{:S(2)}, u32[]{:S(2)}) collective-permute-start(bf16[32,2048]{1,0:T(8,128)(2,1)S(1)} %get-tuple-element.61), channel_id=1, source_target_pairs={{0,5},{1,4},{2,7},{3,6},{4,9},{5,8},{6,11},{7,10},{8,13},{9,12},{1... | collective-permute-start | bytes 393224 | tf_op jit(solution)/shard_map/ppermute | solution.py:737
  108.4 2.4 %collective-permute-start.21 = (bf16[32,2048]{1,0:T(8,128)(2,1)S(1)}, bf16[32,2048]{1,0:T(8,128)(2,1)S(1)}, u32[]{:S(2)}, u32[]{:S(2)}) collective-permute-start(bf16[32,2048]{1,0:T(8,128)(2,1)S(1)} %get-tuple-element.61), channel_id=1, source_target_pairs={{0,4},{1,5},{2,6},{3,7},{4,8},{5,9},{6,10},{7,11},{8,12},{9,13},{1... | collective-permute-start | bytes 393224 | tf_op jit(solution)/shard_map/ppermute | solution.py:736
  111.1 2.9 %collective-permute-done.21.rim_a = bf16[32,2048]{1,0:T(8,128)(2,1)S(1)} collective-permute-done((bf16[32,2048]{1,0:T(8,128)(2,1)S(1)}, bf16[32,2048]{1,0:T(8,128)(2,1)S(1)}, u32[]{:S(2)}, u32[]{:S(2)}) %collective-permute-start.21) | collective-permute-done | bytes 131104 | tf_op jit(solution)/shard_map/ppermute | solution.py:736
  114.0 1.9 %short_project.1 = (bf16[128,512]{1,0:T(8,128)(2,1)S(1)}, bf16[8,32,256]{2,1,0:T(8,128)(2,1)}, bf16[32,512]{1,0:T(8,128)(2,1)S(1)}) custom-call(f32[128,2048]{1,0:T(8,128)S(1)} %get-tuple-element.59.sum_ref, bf16[128,2048]{1,0:T(8,128)(2,1)S(1)} %collective-permute-done.20.term_ref, bf16[32,2048]{1,0:T(8,128)(2,1)S(1)} %collective-permute-done.21.rim_a, ...), custom_call_target="tpu_custom_call" | custom-call | flops 100663296 | bytes 3670016 | tf_op jit(solution)/shard_map/short_project/pallas_call | solution.py:511
  115.9 4.6 %all-to-all-start.1 = ((bf16[8,32,256]{2,1,0:T(8,128)(2,1)}), bf16[8,32,256]{2,1,0:T(8,128)(2,1)S(1)}, u32[]{:S(2)}, u32[]{:S(2)}) async-start(bf16[8,32,256]{2,1,0:T(8,128)(2,1)} %get-tuple-element.63), calls=%async_computation.1 | async-start | bytes 262144 | tf_op jit(solution)/shard_map/all_to_all | solution.py:661
  120.5 1.4 collective-permute-start.23
  121.9 1.4 collective-permute-done.23.b_ref
  123.3 4.7 %collective-permute-start.26 = (bf16[64,512]{1,0:T(8,128)(2,1)S(1)}, bf16[64,512]{1,0:T(8,128)(2,1)S(1)}, u32[]{:S(2)}, u32[]{:S(2)}) collective-permute-start(bf16[64,512]{1,0:T(8,128)(2,1)S(1)} %join.3.refs_0_), channel_id=1, source_target_pairs={{0,192},{64,0},{128,64},{192,128},{1,193},{65,1},{129,65},{193,129... | collective-permute-start | bytes 196616 | tf_op jit(solution)/shard_map/ppermute | solution.py:670
  128.0 1.0 collective-permute-start.25
  129.3 3.3 %collective-permute-done.25.refs_2_ = bf16[64,512]{1,0:T(8,128)(2,1)S(1)} collective-permute-done((bf16[64,512]{1,0:T(8,128)(2,1)S(1)}, bf16[64,512]{1,0:T(8,128)(2,1)S(1)}, u32[]{:S(2)}, u32[]{:S(2)}) %collective-permute-start.25) | collective-permute-done | bytes 65568 | tf_op jit(solution)/shard_map/ppermute | solution.py:670
  133.4 1.0 short_attend.1
  134.4 15.3 %all_to_all.16.parts_ref = bf16[8,32,384]{2,1,0:T(8,128)(2,1)} all-to-all(bf16[8,32,384]{2,1,0:T(8,128)(2,1)S(1)} %short_attend.1), channel_id=1, replica_groups=mesh['y'=4,'z'=8,'xl'=2,'tp'=4] {'z'}, dimensions={0} | all-to-all | bytes 393216 | tf_op jit(solution)/shard_map/all_to_all | solution.py:661
  149.7 3.1 %short_merge.1 = (bf16[32,512]{1,0:T(8,128)(2,1)}, bf16[32,512]{1,0:T(8,128)(2,1)}, bf16[32,512]{1,0:T(8,128)(2,1)}, bf16[32,512]{1,0:T(8,128)(2,1)}) custom-call(bf16[8,32,384]{2,1,0:T(8,128)(2,1)} %all_to_all.16.parts_ref, bf16[256,2048]{1,0:T(8,128)(2,1)} %w_hbm.1), custom_call_target="tpu_custom_call" | custom-call | flops 33554432 | bytes 1048576 | tf_op jit(solution)/shard_map/short_merge/pallas_call | solution.py:625
  152.8 5.7 %collective-permute-start.27 = (bf16[32,512]{1,0:T(8,128)(2,1)}, bf16[32,512]{1,0:T(8,128)(2,1)S(1)}, u32[]{:S(2)}, u32[]{:S(2)}) collective-permute-start(bf16[32,512]{1,0:T(8,128)(2,1)} %get-tuple-element.66), channel_id=1, source_target_pairs={{0,1},{1,0},{2,3},{3,2},{4,5},{5,4},{6,7},{7,6},{8,9},{9,8},{10,11... | collective-permute-start | bytes 98312 | tf_op jit(solution)/shard_map/ppermute | solution.py:665
  158.5 1.9 %collective-permute-start.28 = (bf16[32,512]{1,0:T(8,128)(2,1)}, bf16[32,512]{1,0:T(8,128)(2,1)S(1)}, u32[]{:S(2)}, u32[]{:S(2)}) collective-permute-start(bf16[32,512]{1,0:T(8,128)(2,1)} %get-tuple-element.67), channel_id=1, source_target_pairs={{0,2},{1,3},{2,0},{3,1},{4,6},{5,7},{6,4},{7,5},{8,10},{9,11},{10,... | collective-permute-start | bytes 98312 | tf_op jit(solution)/shard_map/ppermute | solution.py:665
  160.5 1.3 collective-permute-start.29
  161.8 1.3 collective-permute-done.28.refs_2_
  163.0 2.5 %collective-permute-done.29.refs_3_ = bf16[32,512]{1,0:T(8,128)(2,1)S(1)} collective-permute-done((bf16[32,512]{1,0:T(8,128)(2,1)}, bf16[32,512]{1,0:T(8,128)(2,1)S(1)}, u32[]{:S(2)}, u32[]{:S(2)}) %collective-permute-start.29) | collective-permute-done | bytes 32800 | tf_op jit(solution)/shard_map/ppermute | solution.py:665
  165.5 0.8 copy-done.5
  166.3 0.9 final_sum.1
  (50 shorter events, 2.6 us)
Async XLA Ops:
  0.7 4.6 %collective-permute-start = (f32[8,128]{1,0:T(8,128)S(1)}, f32[8,128]{1,0:T(8,128)S(1)}, u32[]{:S(2)}, u32[]{:S(2)}) collective-permute-start(f32[8,128]{1,0:T(8,128)S(1)} %own_count.1.a_ref), channel_id=1, source_target_pairs={{0,4},{4,0},{1,5},{5,1},{2,6},{6,2},{3,7},{7,3},{8,12},{12,8},{9,1... | collective-permute-start | bytes 12296 | tf_op jit(solution)/shard_map/ppermute | solution.py:665
  2.8 24.5 %copy-start.2 = (bf16[256,2048]{1,0:T(8,128)(2,1)S(1)}, bf16[256,2048]{1,0:T(8,128)(2,1)}, u32[]{:S(2)}) copy-start(bf16[256,2048]{1,0:T(8,128)(2,1)} %wa_hbm.1) | copy-start | bytes 3145732
  5.2 7.9 %copy-start.4 = (bf16[128,256]{1,0:T(8,128)(2,1)S(1)}, bf16[128,256]{1,0:T(8,128)(2,1)}, u32[]{:S(2)}) copy-start(bf16[128,256]{1,0:T(8,128)(2,1)} %get-tuple-element.37.a_ref) | copy-start | bytes 196612
  5.3 50.2 %copy-start.7 = (f32[2]{0:T(128)S(1)}, f32[2]{0:T(128)}, u32[]{:S(2)}) copy-start(f32[2]{0:T(128)} %slope_ref.2) | copy-start | bytes 28
  5.3 4.8 %collective-permute-start.1 = (f32[8,128]{1,0:T(8,128)S(1)}, f32[8,128]{1,0:T(8,128)S(1)}, u32[]{:S(2)}, u32[]{:S(2)}) collective-permute-start(f32[8,128]{1,0:T(8,128)S(1)} %added.5.a_ref), channel_id=1, source_target_pairs={{0,8},{8,0},{16,24},{24,16},{32,40},{40,32},{48,56},{56,48},{1,9},... | collective-permute-start | bytes 12296 | tf_op jit(solution)/shard_map/ppermute | solution.py:665
  10.1 14.2 %collective-permute-start.4 = (bf16[768,256]{1,0:T(8,128)(2,1)}, bf16[768,256]{1,0:T(8,128)(2,1)S(1)}, u32[]{:S(2)}, u32[]{:S(2)}) collective-permute-start(bf16[768,256]{1,0:T(8,128)(2,1)} %project_pack.1.refs_7_), channel_id=1, source_target_pairs={{0,192},{64,0},{128,64},{192,128},{1,193},{65,1},{129,65},{193,129... | collective-permute-start | bytes 1179656 | tf_op jit(solution)/shard_map/ppermute | solution.py:670
  12.9 11.4 %collective-permute-start.3 = (bf16[768,256]{1,0:T(8,128)(2,1)}, bf16[768,256]{1,0:T(8,128)(2,1)S(1)}, u32[]{:S(2)}, u32[]{:S(2)}) collective-permute-start(bf16[768,256]{1,0:T(8,128)(2,1)} %project_pack.1.refs_7_), channel_id=1, source_target_pairs={{0,64},{64,128},{128,192},{192,0},{1,65},{65,129},{129,193},{193,1... | collective-permute-start | bytes 1179656 | tf_op jit(solution)/shard_map/ppermute | solution.py:670
  12.9 11.4 %collective-permute-start.2 = (bf16[768,256]{1,0:T(8,128)(2,1)}, bf16[768,256]{1,0:T(8,128)(2,1)S(1)}, u32[]{:S(2)}, u32[]{:S(2)}) collective-permute-start(bf16[768,256]{1,0:T(8,128)(2,1)} %project_pack.1.refs_7_), channel_id=1, source_target_pairs={{0,4},{4,0},{1,5},{5,1},{2,6},{6,2},{3,7},{7,3},{8,12},{12,8},{9,1... | collective-permute-start | bytes 1179656 | tf_op jit(solution)/shard_map/ppermute | solution.py:665
  13.2 11.1 %collective-permute-start.5 = (bf16[128,256]{1,0:T(8,128)(2,1)S(1)}, bf16[128,256]{1,0:T(8,128)(2,1)S(1)}, u32[]{:S(2)}, u32[]{:S(2)}) collective-permute-start(bf16[128,256]{1,0:T(8,128)(2,1)S(1)} %copy-done.4), channel_id=1, source_target_pairs={{0,8},{8,0},{16,24},{24,16},{32,40},{40,32},{48,56},{56,48},{1,9},... | collective-permute-start | bytes 196616 | tf_op jit(solution)/shard_map/ppermute | solution.py:665
  13.2 4.0 %collective-permute-start.6 = (f32[8,128]{1,0:T(8,128)S(1)}, f32[8,128]{1,0:T(8,128)S(1)}, u32[]{:S(2)}, u32[]{:S(2)}) collective-permute-start(f32[8,128]{1,0:T(8,128)S(1)} %added.6.a_ref), channel_id=1, source_target_pairs={{0,16},{8,24},{16,0},{24,8},{32,48},{40,56},{48,32},{56,40},{1,17}... | collective-permute-start | bytes 12296 | tf_op jit(solution)/shard_map/ppermute | solution.py:665
  17.2 7.1 %collective-permute-start.7 = (f32[8,128]{1,0:T(8,128)S(1)}, f32[8,128]{1,0:T(8,128)S(1)}, u32[]{:S(2)}, u32[]{:S(2)}) collective-permute-start(f32[8,128]{1,0:T(8,128)S(1)} %added.7.a_ref), channel_id=1, source_target_pairs={{0,32},{8,40},{16,48},{24,56},{32,0},{40,8},{48,16},{56,24},{1,33}... | collective-permute-start | bytes 12296 | tf_op jit(solution)/shard_map/ppermute | solution.py:665
  24.3 17.1 %collective-permute-start.9 = (bf16[768,256]{1,0:T(8,128)(2,1)S(1)}, bf16[768,256]{1,0:T(8,128)(2,1)S(1)}, u32[]{:S(2)}, u32[]{:S(2)}) collective-permute-start(bf16[768,256]{1,0:T(8,128)(2,1)S(1)} %collective-permute-done.2.refs_8_), channel_id=1, source_target_pairs={{0,192},{64,0},{128,64},{192,128},{1,193},{65,1},{129,65},{193,129... | collective-permute-start | bytes 1179656 | tf_op jit(solution)/shard_map/ppermute | solution.py:670
  27.3 14.1 %collective-permute-start.8 = (bf16[768,256]{1,0:T(8,128)(2,1)S(1)}, bf16[768,256]{1,0:T(8,128)(2,1)S(1)}, u32[]{:S(2)}, u32[]{:S(2)}) collective-permute-start(bf16[768,256]{1,0:T(8,128)(2,1)S(1)} %collective-permute-done.2.refs_8_), channel_id=1, source_target_pairs={{0,64},{64,128},{128,192},{192,0},{1,65},{65,129},{129,193},{193,1... | collective-permute-start | bytes 1179656 | tf_op jit(solution)/shard_map/ppermute | solution.py:670
  27.3 41.6 %collective-permute-start.18 = (bf16[256,2048]{1,0:T(8,128)(2,1)S(1)}, bf16[256,2048]{1,0:T(8,128)(2,1)S(1)}, u32[]{:S(2)}, u32[]{:S(2)}) collective-permute-start(bf16[256,2048]{1,0:T(8,128)(2,1)S(1)} %copy-done.2), channel_id=1, source_target_pairs={{0,2},{1,3},{2,0},{3,1},{4,6},{5,7},{6,4},{7,5},{8,10},{9,11},{10,... | collective-permute-start | bytes 3145736 | tf_op jit(solution)/shard_map/ppermute | solution.py:665
  30.1 4.6 %collective-permute-start.12 = (f32[8,128]{1,0:T(8,128)S(1)}, f32[8,128]{1,0:T(8,128)S(1)}, u32[]{:S(2)}, u32[]{:S(2)}) collective-permute-start(f32[8,128]{1,0:T(8,128)S(1)} %added.8.a_ref), channel_id=1, source_target_pairs={{0,64},{64,0},{128,192},{192,128},{1,65},{65,1},{129,193},{193,129... | collective-permute-start | bytes 12296 | tf_op jit(solution)/shard_map/ppermute | solution.py:665
  30.1 7.9 %collective-permute-start.11 = (bf16[256,256]{1,0:T(8,128)(2,1)S(1)}, bf16[256,256]{1,0:T(8,128)(2,1)S(1)}, u32[]{:S(2)}, u32[]{:S(2)}) collective-permute-start(bf16[256,256]{1,0:T(8,128)(2,1)S(1)} %join.2.refs_0_), channel_id=1, source_target_pairs={{0,48},{8,56},{16,0},{24,8},{32,16},{40,24},{48,32},{56,40},{1,49}... | collective-permute-start | bytes 393224 | tf_op jit(solution)/shard_map/ppermute | solution.py:670
  34.7 6.8 %collective-permute-start.10 = (bf16[256,256]{1,0:T(8,128)(2,1)S(1)}, bf16[256,256]{1,0:T(8,128)(2,1)S(1)}, u32[]{:S(2)}, u32[]{:S(2)}) collective-permute-start(bf16[256,256]{1,0:T(8,128)(2,1)S(1)} %join.2.refs_0_), channel_id=1, source_target_pairs={{0,16},{8,24},{16,32},{24,40},{32,48},{40,56},{48,0},{56,8},{1,17}... | collective-permute-start | bytes 393224 | tf_op jit(solution)/shard_map/ppermute | solution.py:670
  41.4 14.0 %collective-permute-start.16 = (bf16[768,256]{1,0:T(8,128)(2,1)S(1)}, bf16[768,256]{1,0:T(8,128)(2,1)S(1)}, u32[]{:S(2)}, u32[]{:S(2)}) collective-permute-start(bf16[768,256]{1,0:T(8,128)(2,1)S(1)} %collective-permute-done.3.refs_9_), channel_id=1, source_target_pairs={{0,64},{64,128},{128,192},{192,0},{1,65},{65,129},{129,193},{193,1... | collective-permute-start | bytes 1179656 | tf_op jit(solution)/shard_map/ppermute | solution.py:670
  42.9 12.6 %collective-permute-start.17 = (bf16[768,256]{1,0:T(8,128)(2,1)S(1)}, bf16[768,256]{1,0:T(8,128)(2,1)S(1)}, u32[]{:S(2)}, u32[]{:S(2)}) collective-permute-start(bf16[768,256]{1,0:T(8,128)(2,1)S(1)} %collective-permute-done.9.refs_12_), channel_id=1, source_target_pairs={{0,192},{64,0},{128,64},{192,128},{1,193},{65,1},{129,65},{193,129... | collective-permute-start | bytes 1179656 | tf_op jit(solution)/shard_map/ppermute | solution.py:670
  44.2 7.0 %collective-permute-start.15 = (f32[8,128]{1,0:T(8,128)S(1)}, f32[8,128]{1,0:T(8,128)S(1)}, u32[]{:S(2)}, u32[]{:S(2)}) collective-permute-start(f32[8,128]{1,0:T(8,128)S(1)} %added.9.refs_5_), channel_id=1, source_target_pairs={{0,128},{64,192},{128,0},{192,64},{1,129},{65,193},{129,1},{193,65... | collective-permute-start | bytes 12296 | tf_op jit(solution)/shard_map/ppermute | solution.py:665
  47.1 5.8 %collective-permute-start.13 = (bf16[128,256]{1,0:T(8,128)(2,1)S(1)}, bf16[128,256]{1,0:T(8,128)(2,1)S(1)}, u32[]{:S(2)}, u32[]{:S(2)}) collective-permute-start(bf16[128,256]{1,0:T(8,128)(2,1)S(1)} %get-tuple-element.49), channel_id=1, source_target_pairs={{0,16},{8,24},{16,32},{24,40},{32,48},{40,56},{48,0},{56,8},{1,17}... | collective-permute-start | bytes 196616 | tf_op jit(solution)/shard_map/ppermute | solution.py:670
  51.2 41.8 %copy-start.1 = (bf16[128,2048]{1,0:T(8,128)(2,1)S(1)}, bf16[128,2048]{1,0:T(8,128)(2,1)}, u32[]{:S(2)}) copy-start(bf16[128,2048]{1,0:T(8,128)(2,1)} %tok_hbm.3) | copy-start | bytes 1572868
  51.2 4.3 %collective-permute-start.14 = (bf16[128,256]{1,0:T(8,128)(2,1)S(1)}, bf16[128,256]{1,0:T(8,128)(2,1)S(1)}, u32[]{:S(2)}, u32[]{:S(2)}) collective-permute-start(bf16[128,256]{1,0:T(8,128)(2,1)S(1)} %get-tuple-element.50), channel_id=1, source_target_pairs={{0,48},{8,56},{16,0},{24,8},{32,16},{40,24},{48,32},{56,40},{1,49}... | collective-permute-start | bytes 196616 | tf_op jit(solution)/shard_map/ppermute | solution.py:670
  55.5 1.0 copy-start.3
  68.9 45.0 %copy-start = (bf16[2048,3,256]{2,0,1:T(8,128)(2,1)S(1)}, bf16[2048,3,256]{2,0,1:T(8,128)(2,1)}, u32[]{:S(2)}) copy-start(bf16[2048,3,256]{2,0,1:T(8,128)(2,1)} %param.17) | copy-start | bytes 9437188
  88.1 4.8 %collective-permute-start.19 = (bf16[128,256]{1,0:T(8,128)(2,1)S(1)}, bf16[128,256]{1,0:T(8,128)(2,1)S(1)}, u32[]{:S(2)}, u32[]{:S(2)}) collective-permute-start(bf16[128,256]{1,0:T(8,128)(2,1)S(1)} %merge.1.a_ref), channel_id=1, source_target_pairs={{0,2},{1,3},{2,0},{3,1},{4,6},{5,7},{6,4},{7,5},{8,10},{9,11},{10,... | collective-permute-start | bytes 196616 | tf_op jit(solution)/shard_map/ppermute | solution.py:665
  94.3 39.1 %copy-start.6 = (f32[2]{0:T(128)S(1)}, f32[2]{0:T(128)}, u32[]{:S(2)}) copy-start(f32[2]{0:T(128)} %slope_ref.3) | copy-start | bytes 28
  94.3 19.7 %collective-permute-start.20 = (bf16[128,2048]{1,0:T(8,128)(2,1)S(1)}, bf16[128,2048]{1,0:T(8,128)(2,1)S(1)}, u32[]{:S(2)}, u32[]{:S(2)}) collective-permute-start(bf16[128,2048]{1,0:T(8,128)(2,1)S(1)} %get-tuple-element.60), channel_id=1, source_target_pairs={{0,1},{1,0},{2,3},{3,2},{4,5},{5,4},{6,7},{7,6},{8,9},{9,8},{10,11... | collective-permute-start | bytes 1572872 | tf_op jit(solution)/shard_map/ppermute | solution.py:665
  105.7 5.4 %collective-permute-start.22 = (bf16[32,2048]{1,0:T(8,128)(2,1)S(1)}, bf16[32,2048]{1,0:T(8,128)(2,1)S(1)}, u32[]{:S(2)}, u32[]{:S(2)}) collective-permute-start(bf16[32,2048]{1,0:T(8,128)(2,1)S(1)} %get-tuple-element.61), channel_id=1, source_target_pairs={{0,5},{1,4},{2,7},{3,6},{4,9},{5,8},{6,11},{7,10},{8,13},{9,12},{1... | collective-permute-start | bytes 393224 | tf_op jit(solution)/shard_map/ppermute | solution.py:737
  108.4 5.5 %collective-permute-start.21 = (bf16[32,2048]{1,0:T(8,128)(2,1)S(1)}, bf16[32,2048]{1,0:T(8,128)(2,1)S(1)}, u32[]{:S(2)}, u32[]{:S(2)}) collective-permute-start(bf16[32,2048]{1,0:T(8,128)(2,1)S(1)} %get-tuple-element.61), channel_id=1, source_target_pairs={{0,4},{1,5},{2,6},{3,7},{4,8},{5,9},{6,10},{7,11},{8,12},{9,13},{1... | collective-permute-start | bytes 393224 | tf_op jit(solution)/shard_map/ppermute | solution.py:736
  115.9 17.5 %all-to-all-start.1 = ((bf16[8,32,256]{2,1,0:T(8,128)(2,1)}), bf16[8,32,256]{2,1,0:T(8,128)(2,1)S(1)}, u32[]{:S(2)}, u32[]{:S(2)}) async-start(bf16[8,32,256]{2,1,0:T(8,128)(2,1)} %get-tuple-element.63), calls=%async_computation.1 | async-start | bytes 262144 | tf_op jit(solution)/shard_map/all_to_all | solution.py:661
  120.5 2.8 %collective-permute-start.23 = (bf16[32,512]{1,0:T(8,128)(2,1)S(1)}, bf16[32,512]{1,0:T(8,128)(2,1)S(1)}, u32[]{:S(2)}, u32[]{:S(2)}) collective-permute-start(bf16[32,512]{1,0:T(8,128)(2,1)S(1)} %get-tuple-element.64.a_ref), channel_id=1, source_target_pairs={{0,4},{4,0},{1,5},{5,1},{2,6},{6,2},{3,7},{7,3},{8,12},{12,8},{9,1... | collective-permute-start | bytes 98312 | tf_op jit(solution)/shard_map/ppermute | solution.py:665
  123.3 6.0 %collective-permute-start.26 = (bf16[64,512]{1,0:T(8,128)(2,1)S(1)}, bf16[64,512]{1,0:T(8,128)(2,1)S(1)}, u32[]{:S(2)}, u32[]{:S(2)}) collective-permute-start(bf16[64,512]{1,0:T(8,128)(2,1)S(1)} %join.3.refs_0_), channel_id=1, source_target_pairs={{0,192},{64,0},{128,64},{192,128},{1,193},{65,1},{129,65},{193,129... | collective-permute-start | bytes 196616 | tf_op jit(solution)/shard_map/ppermute | solution.py:670
  128.0 4.6 %collective-permute-start.25 = (bf16[64,512]{1,0:T(8,128)(2,1)S(1)}, bf16[64,512]{1,0:T(8,128)(2,1)S(1)}, u32[]{:S(2)}, u32[]{:S(2)}) collective-permute-start(bf16[64,512]{1,0:T(8,128)(2,1)S(1)} %join.3.refs_0_), channel_id=1, source_target_pairs={{0,128},{64,192},{128,0},{192,64},{1,129},{65,193},{129,1},{193,65... | collective-permute-start | bytes 196616 | tf_op jit(solution)/shard_map/ppermute | solution.py:670
  129.0 4.3 %collective-permute-start.24 = (bf16[64,512]{1,0:T(8,128)(2,1)S(1)}, bf16[64,512]{1,0:T(8,128)(2,1)S(1)}, u32[]{:S(2)}, u32[]{:S(2)}) collective-permute-start(bf16[64,512]{1,0:T(8,128)(2,1)S(1)} %join.3.refs_0_), channel_id=1, source_target_pairs={{0,64},{64,128},{128,192},{192,0},{1,65},{65,129},{129,193},{193,1... | collective-permute-start | bytes 196616 | tf_op jit(solution)/shard_map/ppermute | solution.py:670
  152.8 8.9 %collective-permute-start.27 = (bf16[32,512]{1,0:T(8,128)(2,1)}, bf16[32,512]{1,0:T(8,128)(2,1)S(1)}, u32[]{:S(2)}, u32[]{:S(2)}) collective-permute-start(bf16[32,512]{1,0:T(8,128)(2,1)} %get-tuple-element.66), channel_id=1, source_target_pairs={{0,1},{1,0},{2,3},{3,2},{4,5},{5,4},{6,7},{7,6},{8,9},{9,8},{10,11... | collective-permute-start | bytes 98312 | tf_op jit(solution)/shard_map/ppermute | solution.py:665
  158.5 4.5 %collective-permute-start.28 = (bf16[32,512]{1,0:T(8,128)(2,1)}, bf16[32,512]{1,0:T(8,128)(2,1)S(1)}, u32[]{:S(2)}, u32[]{:S(2)}) collective-permute-start(bf16[32,512]{1,0:T(8,128)(2,1)} %get-tuple-element.67), channel_id=1, source_target_pairs={{0,2},{1,3},{2,0},{3,1},{4,6},{5,7},{6,4},{7,5},{8,10},{9,11},{10,... | collective-permute-start | bytes 98312 | tf_op jit(solution)/shard_map/ppermute | solution.py:665
  160.5 5.1 %collective-permute-start.29 = (bf16[32,512]{1,0:T(8,128)(2,1)}, bf16[32,512]{1,0:T(8,128)(2,1)S(1)}, u32[]{:S(2)}, u32[]{:S(2)}) collective-permute-start(bf16[32,512]{1,0:T(8,128)(2,1)} %get-tuple-element.68), channel_id=1, source_target_pairs={{0,3},{1,2},{2,1},{3,0},{4,7},{5,6},{6,5},{7,4},{8,11},{9,10},{10,... | collective-permute-start | bytes 98312 | tf_op jit(solution)/shard_map/ppermute | solution.py:665
  165.5 0.8 copy-start.5

commit v7 on v6

--- a/solution.py
+++ b/solution.py
@@ -81,7 +81,9 @@
     )(rows, weight3)
 
 
-def pack_kernel(normed_hbm, w_hbm, ck_hbm, cv_hbm, pack_ref, normed, weight, sems):
+def pack_kernel(
+    normed_hbm, w_hbm, ck_hbm, cv_hbm, table_ref, pack_ref, normed, weight, sems
+):
     rows = normed.shape[0]
     slots = ck_hbm.shape[0]
     copies = [pltpu.make_async_copy(normed_hbm, normed, sems.at[0])]
@@ -94,6 +96,8 @@
     ]
     for copy in copies:
         copy.start()
+    table = jnp.sum(table_ref[...].astype(F32), axis=0)
+    pack_ref[2 * (slots + rows) :] = table.astype(BF16)
     copies[0].wait()
     for i in range(2):
         copies[1 + i].wait()
@@ -104,14 +108,14 @@
     copies[4].wait()
 
 
-def project_pack(normed, weight3, cache_keys, cache_values):
+def project_pack(normed, weight3, cache_keys, cache_values, table):
     n, d = normed.shape
     width = weight3.shape[2]
-    total = 2 * (n + cache_keys.shape[0])
+    total = 2 * (n + cache_keys.shape[0]) + table.shape[1]
     hbm = pl.BlockSpec(memory_space=HBM)
     return pl.pallas_call(
         pack_kernel,
-        in_specs=[hbm] * 4,
+        in_specs=[hbm] * 4 + [pl.BlockSpec(memory_space=VMEM)],
         out_specs=pl.BlockSpec(memory_space=VMEM),
         out_shape=jax.ShapeDtypeStruct((total, width), BF16),
         scratch_shapes=[
@@ -122,38 +126,24 @@
         compiler_params=params(60),
         cost_estimate=cost(4 * n * d * width, 2 * (n * d + 2 * d * width)),
         name="project_pack",
-    )(normed, weight3, cache_keys, cache_values)
+    )(normed, weight3, cache_keys, cache_values, table)
 
 
 def table_kernel(count_ref, out_ref):
     y, z, xl = place_of_device()
-    lane = lax.broadcasted_iota(jnp.int32, out_ref.shape, 1)
-    out_ref[...] = jnp.where(lane == y * 16 + z * 2 + xl, count_ref[0], 0).astype(F32)
-
-
-def own_count(count):
+    lane = lax.broadcasted_iota(jnp.int32, out_ref.shape, 2)
+    out_ref[...] = jnp.where(lane == y * 16 + z * 2 + xl, count_ref[0], 0).astype(F32).astype(BF16)
+
+
+def own_count(count, copies, width):
     return pl.pallas_call(
         table_kernel,
         in_specs=[pl.BlockSpec(memory_space=SMEM)],
-        out_shape=jax.ShapeDtypeStruct((8, HS), F32),
+        out_shape=jax.ShapeDtypeStruct((copies, 16, width), BF16),
         compiler_params=params(8),
-        cost_estimate=cost(0, 4096),
+        cost_estimate=cost(0, 32 * copies * width),
         name="own_count",
     )(count)
-
-
-def add_kernel(a_ref, b_ref, out_ref):
-    out_ref[...] = a_ref[...] + b_ref[...]
-
-
-def added(a, b):
-    return pl.pallas_call(
-        add_kernel,
-        out_shape=jax.ShapeDtypeStruct(a.shape, a.dtype),
-        compiler_params=params(8),
-        cost_estimate=cost(a.size, 12 * a.size),
-        name="added",
-    )(a, b)
 
 
 def join_kernel(a_ref, b_ref, out_ref):
@@ -229,7 +219,9 @@
         both = None
         for j in range(pieces):
             term = jnp.dot(
-                jnp.exp2(pending[j] - top).astype(BF16), value(h, j), preferred_element_type=F32
+                jnp.exp2((pending[j] - top).astype(BF16)),
+                value(h, j),
+                preferred_element_type=F32,
             )
             both = term if both is None else both + term
             if h + 1 < heads:
@@ -244,8 +236,8 @@
 
 
 def attend_kernel(slots, slope_ref, *refs):
-    queries, tables, packs = refs[:5], refs[5:7], refs[7:15]
-    out_ref, q_tile, bias = refs[15:]
+    queries, packs = refs[:5], refs[5:13]
+    out_ref, q_tile, bias = refs[13:]
     tile = pl.program_id(0)
     y, z, xl = place_of_device()
     rows = q_tile.shape[0] // 2
@@ -269,7 +261,9 @@
 
     @pl.when(tile == 0)
     def _():
-        table = (tables[0][...] + tables[1][...])[:1]
+        table = functools.reduce(
+            jnp.add, [pack[2 * (slots + rows) :].astype(F32) for pack in packs]
+        )[:1]
         lane = lax.broadcasted_iota(jnp.int32, table.shape, 1)
         everything = jnp.sum(table, axis=1, keepdims=True)
         slot = lax.broadcasted_iota(jnp.int32, (1, slots), 1).astype(F32)
@@ -341,7 +335,7 @@
                 out_ref[2 * p + b, rows:] = tail
 
 
-def attend(slopes, queries, tables, packs, slots):
+def attend(slopes, queries, packs, slots):
     rows, width = queries[0].shape[0] // 2, queries[0].shape[1]
     nk = len(RING) * (slots + rows)
     whole = lambda a: pl.BlockSpec(a.shape, lambda i: (0,) * a.ndim)
@@ -350,14 +344,14 @@
         functools.partial(attend_kernel, slots),
         grid=(4,),
         in_specs=[pl.BlockSpec(memory_space=SMEM)]
-        + [whole(a) for a in (*queries, *tables, *packs)],
+        + [whole(a) for a in (*queries, *packs)],
         out_specs=whole(out),
         out_shape=out,
         scratch_shapes=[VMEM((2 * rows, width), BF16), VMEM((8, nk), F32)],
         compiler_params=params(40),
         cost_estimate=cost(32 * rows * nk * width, 4 * nk * width, 16 * rows * nk),
         name="attend",
-    )(slopes, *queries, *tables, *packs)
+    )(slopes, *queries, *packs)
 
 
 def merge_kernel(heads, parts_ref, out_ref):
@@ -576,10 +570,7 @@
     )(slopes, queries, *keys)
 
 
-def short_merge_kernel(heads, parts_ref, w_hbm, *refs):
-    outs, (w_ref, sem) = refs[:4], refs[4:]
-    load = pltpu.make_async_copy(w_hbm, w_ref, sem)
-    load.start()
+def short_merge_kernel(heads, parts_ref, w_ref, *outs):
     sources, rows, padded = parts_ref.shape
     width = padded - HS
     merged = []
@@ -602,7 +593,6 @@
         merged.append((acc / total).astype(BF16))
     att = jnp.concatenate(merged, axis=1)
     cols = outs[0].shape[1]
-    load.wait()
     terms = [
         jnp.dot(
             att, w_ref[:, t * cols : (t + 1) * cols], preferred_element_type=F32
@@ -624,10 +614,8 @@
     out = jax.ShapeDtypeStruct((rows, cols), BF16)
     return pl.pallas_call(
         functools.partial(short_merge_kernel, width // HS),
-        in_specs=[pl.BlockSpec(memory_space=VMEM), pl.BlockSpec(memory_space=HBM)],
         out_shape=[out] * 4,
-        scratch_shapes=[VMEM(weight.shape, BF16), pltpu.SemaphoreType.DMA],
-        compiler_params=params(60),
+        compiler_params=params(16),
         cost_estimate=cost(8 * rows * width * cols, 8 * width * cols),
         name="short_merge",
     )(parts, weight)
@@ -672,12 +660,6 @@
 
 def both_ways(x, axis, by):
     return moved(x, axis, by), moved(x, axis, -by)
-
-
-def counts_along(table, axis, *flips):
-    for flip in flips:
-        table = added(table, swap(table, axis, flip))
-    return table
 
 
 def after(x, *others):
@@ -699,31 +681,26 @@
     axes = ("y", "z", "xl", "tp")
     slots = cache_keys.shape[0]
     weight3 = jnp.transpose(project_weight, (1, 0, 2))
-    table = counts_along(own_count(cache_count), "xl", 1)
+    nz = lax.axis_size("z")
+    table = exchange(own_count(cache_count, nz, cache_keys.shape[1]), "z")
     q, normed = project_queries(tokens, weight3)
-    normed, table = lax.optimization_barrier((normed, table))
-    table = counts_along(table, "z", 1)
-    pack = project_pack(normed, weight3, cache_keys, cache_values)
-    pack, table = lax.optimization_barrier((pack, table))
-    table = counts_along(table, "z", 2, 4)
+    pack = project_pack(normed, weight3, cache_keys, cache_values, table)
     left, right = both_ways(pack, "y", 1)
-    other, left, right, mate, table = lax.optimization_barrier(
-        (swap(pack, "xl"), left, right, swap(q, "z"), table)
+    other, left, right, mate = lax.optimization_barrier(
+        (swap(pack, "xl"), left, right, swap(q, "z"))
     )
     pair = join(q, mate)
     left_other, right_other = both_ways(other, "y", 1)
     left_pair, right_pair = both_ways(pair, "z", 2)
-    table = counts_along(table, "y", 1)
-    left_other, right_other, left_pair, right_pair, left, table = lax.optimization_barrier(
-        (left_other, right_other, left_pair, right_pair, left, table)
+    left_other, right_other, left_pair, right_pair, left = lax.optimization_barrier(
+        (left_other, right_other, left_pair, right_pair, left)
     )
-    tables = [table, swap(table, "y", 2)]
     far, far_other = moved(left, "y", 1), moved(right_other, "y", -1)
     near = halves(left_pair, right_pair)
     queries = [pair, left_pair, right_pair, moved(near[0], "z", 2), moved(near[1], "z", -2)]
     crossed = swap(after(output_weight, other), "tp", 2)
     packs = [pack, other, left, left_other, right, right_other, far, far_other]
-    parts = attend(distance_slope, queries, tables, packs, slots)
+    parts = attend(distance_slope, queries, packs, slots)
     parts, crossed = lax.optimization_barrier((parts, crossed))
 
     att = merge(exchange(parts, "z"))
@@ -741,9 +718,11 @@
         swap(term, "tp", 1),
         rims,
         jnp.transpose(short_project_weight, (1, 0, 2)),
-        lax.axis_size("z"),
+        nz,
     )
-    pair = join(skv, swap(skv, "xl"))
+    mate = swap(skv, "xl")
+    sq, mate = lax.optimization_barrier((sq, mate))
+    pair = join(skv, mate)
     keys = [pair] + [moved(pair, "y", by) for by in (1, 2, 3)]
     sparts = short_attend(short_slope, exchange(sq, "z"), keys)
     terms = short_merge(exchange(sparts, "z"), short_output)

time: 168 us -> 160 us (0.952)
  starting transfers between devices: 71.2 us -> 61.6 us
  waiting for transfers between devices: 32.6 us -> 36.8 us
    ppermute x15 -> x9, starting transfers between devices: 41.6 us -> 24 us  [swap(): lax.ppermute(x, axis, [(i, i ^ flip) for i in range(lax.axis_size(axis))])]
    all_to_all x1 -> x2, starting transfers between devices: 4.62 us -> 14 us  [exchange(): return lax.all_to_all(blocks, axis, 0, 0)]
    all_to_all x1 -> x2, waiting for transfers between devices: 0.01 us -> 4.77 us  [exchange(): return lax.all_to_all(blocks, axis, 0, 0)]
    ppermute x13, waiting for transfers between devices: 14.8 us -> 17.6 us  [moved(): return lax.ppermute(x, axis, [(i, (i + by) % n) for i in range(n)])]
    ppermute x15 -> x9, waiting for transfers between devices: 14.7 us -> 12.1 us  [swap(): lax.ppermute(x, axis, [(i, i ^ flip) for i in range(lax.axis_size(axis))])]
    pallas_call x7 -> x2, Pallas kernels: 6.17 us -> 4.37 us  [the longest x1 3.88 us: project_pack(): pl.pallas_call(pack_kernel, in_specs=[hbm] * 4 + [pl.BlockSpec(memory_spa...]
  transfers between devices with their start and end apart: 31 -> 26, of which waited for: 16 -> 16; matrix products, arithmetic and copies ran while one was open for 0% -> 0% of each run, Pallas kernels for 11% -> 9%
where the time goes in v7:
time: 160 us; the launch traced here: 159 us
  starting transfers between devices  61.6 us (38%)
  waiting for transfers between devices  36.8 us (23%)
  blocking collectives  32.2 us (20%)
  Pallas kernels  26.3 us (16%)
  local copies, waits for them, and re-layouts  1.65 us (1%)
    all_to_all x2, blocking collectives, exchange(): return lax.all_to_all(blocks, axis, 0, 0)  32.2 us
    ppermute x9, starting transfers between devices, swap(): lax.ppermute(x, axis, [(i, i ^ flip) for i in range(lax.axis_size(axis))])  24 us
    ppermute x13, starting transfers between devices, moved(): return lax.ppermute(x, axis, [(i, (i + by) % n) for i in range(n)])  18.4 us
    ppermute x13, waiting for transfers between devices, moved(): return lax.ppermute(x, axis, [(i, (i + by) % n) for i in range(n)])  17.6 us
    all_to_all x2, starting transfers between devices, exchange(): return lax.all_to_all(blocks, axis, 0, 0)  14 us
    pallas_call x1, Pallas kernels, attend(): pl.pallas_call(functools.partial(attend_kernel, slots), grid=(4,), in_spe...  12.4 us
    ppermute x9, waiting for transfers between devices, swap(): lax.ppermute(x, axis, [(i, i ^ flip) for i in range(lax.axis_size(axis))])  12.1 us
    all_to_all x2, waiting for transfers between devices, exchange(): return lax.all_to_all(blocks, axis, 0, 0)  4.77 us
  transfers between devices with their start and end apart: 26, of which 16 were waited for; matrix products, arithmetic and copies ran while one was open for 0% of the time, Pallas kernels for 9%

profile of v7, /device:TPU:1, one launch (start us, length us, event | category | flops | bytes accessed | tf_op | source)
XLA Modules:
  0.0 159.4 jit_solution(134855545533635402)
XLA Ops:
  0.7 0.6 own_count.1
  1.3 9.0 %all-to-all-start = ((bf16[8,16,256]{2,1,0:T(8,128)(2,1)}), bf16[8,16,256]{2,1,0:T(8,128)(2,1)S(1)}, u32[]{:S(2)}, u32[]{:S(2)}) async-start(bf16[8,16,256]{2,1,0:T(8,128)(2,1)} %own_count.1), calls=%async_computation | async-start | bytes 131072 | tf_op jit(solution)/shard_map/all_to_all | solution.py:649
  10.3 2.4 %project_queries.1 = (bf16[128,256]{1,0:T(8,128)(2,1)}, bf16[128,2048]{1,0:T(8,128)(2,1)}) custom-call(bf16[128,2048]{1,0:T(8,128)(2,1)} %tok_hbm.3, bf16[3,2048,256]{2,1,0:T(8,128)(2,1)} %bitcast.3), custom_call_target="tpu_custom_call" | custom-call | flops 134217728 | bytes 1572864 | tf_op jit(solution)/shard_map/project_queries/pallas_call | solution.py:68
  12.8 4.8 %all-to-all-done.table_ref = bf16[8,16,256]{2,1,0:T(8,128)(2,1)S(1)} async-done(((bf16[8,16,256]{2,1,0:T(8,128)(2,1)}), bf16[8,16,256]{2,1,0:T(8,128)(2,1)S(1)}, u32[]{:S(2)}, u32[]{:S(2)}) %all-to-all-start) | async-done | bytes 65568 | tf_op jit(solution)/shard_map/all_to_all | solution.py:649
  17.5 0.6 copy-done.8
  18.2 3.9 %project_pack.1.refs_5_ = bf16[784,256]{1,0:T(8,128)(2,1)} custom-call(bf16[128,2048]{1,0:T(8,128)(2,1)} %get-tuple-element.34.normed_hbm, bf16[3,2048,256]{2,1,0:T(8,128)(2,1)} %bitcast.4, bf16[256,256]{1,0:T(8,128)(2,1)} %ck_hbm.1, bf16[256,256]{1,0:T(8,128)(2,1)} %cv_hbm.1, bf16[8,16,256]{2,1,0:T(8,128)(2,1)} %copy-done.8), custom_call_target="tpu_custom_call" | custom-call | flops 268435456 | bytes 2621440 | tf_op jit(solution)/shard_map/project_pack/pallas_call | solution.py:116
  22.1 2.8 %collective-permute-start.2 = (bf16[784,256]{1,0:T(8,128)(2,1)}, bf16[784,256]{1,0:T(8,128)(2,1)S(1)}, u32[]{:S(2)}, u32[]{:S(2)}) collective-permute-start(bf16[784,256]{1,0:T(8,128)(2,1)} %project_pack.1.refs_5_), channel_id=1, source_target_pairs={{0,192},{64,0},{128,64},{192,128},{1,193},{65,1},{129,65},{193,129... | collective-permute-start | bytes 1204232 | tf_op jit(solution)/shard_map/ppermute | solution.py:658
  24.9 1.2 collective-permute-start
  26.4 3.1 %collective-permute-done.3.b_ref = bf16[128,256]{1,0:T(8,128)(2,1)S(1)} collective-permute-done((bf16[128,256]{1,0:T(8,128)(2,1)S(1)}, bf16[128,256]{1,0:T(8,128)(2,1)S(1)}, u32[]{:S(2)}, u32[]{:S(2)}) %collective-permute-start.3) | collective-permute-done | bytes 65568 | tf_op jit(solution)/shard_map/ppermute | solution.py:653
  29.5 2.2 %collective-permute-done.2.refs_9_ = bf16[784,256]{1,0:T(8,128)(2,1)S(1)} collective-permute-done((bf16[784,256]{1,0:T(8,128)(2,1)}, bf16[784,256]{1,0:T(8,128)(2,1)S(1)}, u32[]{:S(2)}, u32[]{:S(2)}) %collective-permute-start.2) | collective-permute-done | bytes 401440 | tf_op jit(solution)/shard_map/ppermute | solution.py:658
  31.7 3.0 %collective-permute-done.1.refs_7_ = bf16[784,256]{1,0:T(8,128)(2,1)S(1)} collective-permute-done((bf16[784,256]{1,0:T(8,128)(2,1)}, bf16[784,256]{1,0:T(8,128)(2,1)S(1)}, u32[]{:S(2)}, u32[]{:S(2)}) %collective-permute-start.1) | collective-permute-done | bytes 401440 | tf_op jit(solution)/shard_map/ppermute | solution.py:658
  34.7 1.2 collective-permute-start.5
  36.2 2.7 %collective-permute-start.12 = (bf16[256,2048]{1,0:T(8,128)(2,1)S(1)}, bf16[256,2048]{1,0:T(8,128)(2,1)S(1)}, u32[]{:S(2)}, u32[]{:S(2)}) collective-permute-start(bf16[256,2048]{1,0:T(8,128)(2,1)S(1)} %copy-done.3), channel_id=1, source_target_pairs={{0,2},{1,3},{2,0},{3,1},{4,6},{5,7},{6,4},{7,5},{8,10},{9,11},{10,... | collective-permute-start | bytes 3145736 | tf_op jit(solution)/shard_map/ppermute | solution.py:653
  39.3 2.1 %collective-permute-start.6 = (bf16[256,256]{1,0:T(8,128)(2,1)S(1)}, bf16[256,256]{1,0:T(8,128)(2,1)S(1)}, u32[]{:S(2)}, u32[]{:S(2)}) collective-permute-start(bf16[256,256]{1,0:T(8,128)(2,1)S(1)} %join.2.refs_0_), channel_id=1, source_target_pairs={{0,16},{8,24},{16,32},{24,40},{32,48},{40,56},{48,0},{56,8},{1,17}... | collective-permute-start | bytes 393224 | tf_op jit(solution)/shard_map/ppermute | solution.py:658
  41.4 4.0 %collective-permute-done.7.right_ref.refs_2_ = bf16[256,256]{1,0:T(8,128)(2,1)S(1)} collective-permute-done((bf16[256,256]{1,0:T(8,128)(2,1)S(1)}, bf16[256,256]{1,0:T(8,128)(2,1)S(1)}, u32[]{:S(2)}, u32[]{:S(2)}) %collective-permute-start.7) | collective-permute-done | bytes 131104 | tf_op jit(solution)/shard_map/ppermute | solution.py:658
  45.9 2.7 %collective-permute-start.11 = (bf16[784,256]{1,0:T(8,128)(2,1)S(1)}, bf16[784,256]{1,0:T(8,128)(2,1)S(1)}, u32[]{:S(2)}, u32[]{:S(2)}) collective-permute-start(bf16[784,256]{1,0:T(8,128)(2,1)S(1)} %collective-permute-done.5.refs_10_), channel_id=1, source_target_pairs={{0,192},{64,0},{128,64},{192,128},{1,193},{65,1},{129,65},{193,129... | collective-permute-start | bytes 1204232 | tf_op jit(solution)/shard_map/ppermute | solution.py:658
  48.5 1.5 collective-permute-start.8
  50.0 2.2 %collective-permute-start.9 = (bf16[128,256]{1,0:T(8,128)(2,1)S(1)}, bf16[128,256]{1,0:T(8,128)(2,1)S(1)}, u32[]{:S(2)}, u32[]{:S(2)}) collective-permute-start(bf16[128,256]{1,0:T(8,128)(2,1)S(1)} %get-tuple-element.41), channel_id=1, source_target_pairs={{0,48},{8,56},{16,0},{24,8},{32,16},{40,24},{48,32},{56,40},{1,49}... | collective-permute-start | bytes 196616 | tf_op jit(solution)/shard_map/ppermute | solution.py:658
  52.2 1.9 %collective-permute-done.8.refs_3_ = bf16[128,256]{1,0:T(8,128)(2,1)S(1)} collective-permute-done((bf16[128,256]{1,0:T(8,128)(2,1)S(1)}, bf16[128,256]{1,0:T(8,128)(2,1)S(1)}, u32[]{:S(2)}, u32[]{:S(2)}) %collective-permute-start.8) | collective-permute-done | bytes 65568 | tf_op jit(solution)/shard_map/ppermute | solution.py:658
  54.1 1.4 collective-permute-done.9.refs_4_
  55.5 1.0 copy-done.4
  56.5 12.4 %attend.1 = bf16[8,144,256]{2,1,0:T(8,128)(2,1)S(1)} custom-call(f32[2]{0:T(128)S(1)} %copy-done.7, bf16[256,256]{1,0:T(8,128)(2,1)S(1)} %join.2.refs_0_, bf16[256,256]{1,0:T(8,128)(2,1)S(1)} %collective-permute-done.6.left_ref.refs_1_, bf16[256,256]{1,0:T(8,128)(2,1)S(1)} %collective-permute-done.7.right_ref.refs_2_, ...), custom_call_target="tpu_custom_call" | custom-call | flops 3221225472 | bytes 3145728 | tf_op jit(solution)/shard_map/attend/pallas_call | solution.py:343
  69.0 17.4 %all_to_all.20.parts_ref = bf16[8,144,256]{2,1,0:T(8,128)(2,1)S(1)} all-to-all(bf16[8,144,256]{2,1,0:T(8,128)(2,1)S(1)} %attend.1), channel_id=1, replica_groups=mesh['y'=4,'z'=8,'xl'=2,'tp'=4] {'z'}, dimensions={0} | all-to-all | bytes 1179648 | tf_op jit(solution)/shard_map/all_to_all | solution.py:649
  86.3 1.2 merge.1.a_ref
  87.7 4.9 %collective-permute-done.13.b_ref = bf16[128,256]{1,0:T(8,128)(2,1)S(1)} collective-permute-done((bf16[128,256]{1,0:T(8,128)(2,1)S(1)}, bf16[128,256]{1,0:T(8,128)(2,1)S(1)}, u32[]{:S(2)}, u32[]{:S(2)}) %collective-permute-start.13) | collective-permute-done | bytes 65568 | tf_op jit(solution)/shard_map/ppermute | solution.py:653
  92.6 1.3 layer_product.1
  93.9 9.0 %collective-permute-start.14 = (bf16[128,2048]{1,0:T(8,128)(2,1)S(1)}, bf16[128,2048]{1,0:T(8,128)(2,1)S(1)}, u32[]{:S(2)}, u32[]{:S(2)}) collective-permute-start(bf16[128,2048]{1,0:T(8,128)(2,1)S(1)} %get-tuple-element.50), channel_id=1, source_target_pairs={{0,1},{1,0},{2,3},{3,2},{4,5},{5,4},{6,7},{7,6},{8,9},{9,8},{10,11... | collective-permute-start | bytes 1572872 | tf_op jit(solution)/shard_map/ppermute | solution.py:653
  103.0 2.1 %collective-permute-start.16 = (bf16[32,2048]{1,0:T(8,128)(2,1)S(1)}, bf16[32,2048]{1,0:T(8,128)(2,1)S(1)}, u32[]{:S(2)}, u32[]{:S(2)}) collective-permute-start(bf16[32,2048]{1,0:T(8,128)(2,1)S(1)} %get-tuple-element.51), channel_id=1, source_target_pairs={{0,5},{1,4},{2,7},{3,6},{4,9},{5,8},{6,11},{7,10},{8,13},{9,12},{1... | collective-permute-start | bytes 393224 | tf_op jit(solution)/shard_map/ppermute | solution.py:714
  105.1 3.1 %collective-permute-start.15 = (bf16[32,2048]{1,0:T(8,128)(2,1)S(1)}, bf16[32,2048]{1,0:T(8,128)(2,1)S(1)}, u32[]{:S(2)}, u32[]{:S(2)}) collective-permute-start(bf16[32,2048]{1,0:T(8,128)(2,1)S(1)} %get-tuple-element.51), channel_id=1, source_target_pairs={{0,4},{1,5},{2,6},{3,7},{4,8},{5,9},{6,10},{7,11},{8,12},{9,13},{1... | collective-permute-start | bytes 393224 | tf_op jit(solution)/shard_map/ppermute | solution.py:713
  108.2 2.3 %collective-permute-done.15.rim_a = bf16[32,2048]{1,0:T(8,128)(2,1)S(1)} collective-permute-done((bf16[32,2048]{1,0:T(8,128)(2,1)S(1)}, bf16[32,2048]{1,0:T(8,128)(2,1)S(1)}, u32[]{:S(2)}, u32[]{:S(2)}) %collective-permute-start.15) | collective-permute-done | bytes 131104 | tf_op jit(solution)/shard_map/ppermute | solution.py:713
  110.5 2.0 %short_project.1 = (bf16[128,512]{1,0:T(8,128)(2,1)S(1)}, bf16[8,32,256]{2,1,0:T(8,128)(2,1)}, bf16[32,512]{1,0:T(8,128)(2,1)S(1)}) custom-call(f32[128,2048]{1,0:T(8,128)S(1)} %get-tuple-element.49.sum_ref, bf16[128,2048]{1,0:T(8,128)(2,1)S(1)} %collective-permute-done.14.term_ref, bf16[32,2048]{1,0:T(8,128)(2,1)S(1)} %collective-permute-done.15.rim_a, ...), custom_call_target="tpu_custom_call" | custom-call | flops 100663296 | bytes 3670016 | tf_op jit(solution)/shard_map/short_project/pallas_call | solution.py:505
  112.5 2.2 %collective-permute-start.17 = (bf16[32,512]{1,0:T(8,128)(2,1)S(1)}, bf16[32,512]{1,0:T(8,128)(2,1)S(1)}, u32[]{:S(2)}, u32[]{:S(2)}) collective-permute-start(bf16[32,512]{1,0:T(8,128)(2,1)S(1)} %get-tuple-element.54.a_ref), channel_id=1, source_target_pairs={{0,4},{4,0},{1,5},{5,1},{2,6},{6,2},{3,7},{7,3},{8,12},{12,8},{9,1... | collective-permute-start | bytes 98312 | tf_op jit(solution)/shard_map/ppermute | solution.py:653
  114.7 1.3 collective-permute-done.17.b_ref
  116.0 5.0 %all-to-all-start.2 = ((bf16[8,32,256]{2,1,0:T(8,128)(2,1)}), bf16[8,32,256]{2,1,0:T(8,128)(2,1)S(1)}, u32[]{:S(2)}, u32[]{:S(2)}) async-start(bf16[8,32,256]{2,1,0:T(8,128)(2,1)} %get-tuple-element.55), calls=%async_computation.2 | async-start | bytes 262144 | tf_op jit(solution)/shard_map/all_to_all | solution.py:649
  121.0 4.5 %collective-permute-start.20 = (bf16[64,512]{1,0:T(8,128)(2,1)S(1)}, bf16[64,512]{1,0:T(8,128)(2,1)S(1)}, u32[]{:S(2)}, u32[]{:S(2)}) collective-permute-start(bf16[64,512]{1,0:T(8,128)(2,1)S(1)} %join.3.refs_0_), channel_id=1, source_target_pairs={{0,192},{64,0},{128,64},{192,128},{1,193},{65,1},{129,65},{193,129... | collective-permute-start | bytes 196616 | tf_op jit(solution)/shard_map/ppermute | solution.py:658
  125.6 0.8 collective-permute-start.18
  126.3 0.5 collective-permute-done.20.refs_3_
  126.8 3.4 %collective-permute-done.19.refs_2_ = bf16[64,512]{1,0:T(8,128)(2,1)S(1)} collective-permute-done((bf16[64,512]{1,0:T(8,128)(2,1)S(1)}, bf16[64,512]{1,0:T(8,128)(2,1)S(1)}, u32[]{:S(2)}, u32[]{:S(2)}) %collective-permute-start.19) | collective-permute-done | bytes 65568 | tf_op jit(solution)/shard_map/ppermute | solution.py:658
  130.2 0.7 collective-permute-done.18.refs_1_
  130.9 1.0 short_attend.1
  131.9 14.8 %all_to_all.21.parts_ref = bf16[8,32,384]{2,1,0:T(8,128)(2,1)S(1)} all-to-all(bf16[8,32,384]{2,1,0:T(8,128)(2,1)S(1)} %short_attend.1), channel_id=1, replica_groups=mesh['y'=4,'z'=8,'xl'=2,'tp'=4] {'z'}, dimensions={0} | all-to-all | bytes 393216 | tf_op jit(solution)/shard_map/all_to_all | solution.py:649
  146.7 0.5 short_merge.1
  147.3 5.2 %collective-permute-start.21 = (bf16[32,512]{1,0:T(8,128)(2,1)S(1)}, bf16[32,512]{1,0:T(8,128)(2,1)S(1)}, u32[]{:S(2)}, u32[]{:S(2)}) collective-permute-start(bf16[32,512]{1,0:T(8,128)(2,1)S(1)} %get-tuple-element.58), channel_id=1, source_target_pairs={{0,1},{1,0},{2,3},{3,2},{4,5},{5,4},{6,7},{7,6},{8,9},{9,8},{10,11... | collective-permute-start | bytes 98312 | tf_op jit(solution)/shard_map/ppermute | solution.py:653
  152.4 1.2 collective-permute-start.22
  153.6 2.1 %collective-permute-start.23 = (bf16[32,512]{1,0:T(8,128)(2,1)S(1)}, bf16[32,512]{1,0:T(8,128)(2,1)S(1)}, u32[]{:S(2)}, u32[]{:S(2)}) collective-permute-start(bf16[32,512]{1,0:T(8,128)(2,1)S(1)} %get-tuple-element.60), channel_id=1, source_target_pairs={{0,3},{1,2},{2,1},{3,0},{4,7},{5,6},{6,5},{7,4},{8,11},{9,10},{10,... | collective-permute-start | bytes 98312 | tf_op jit(solution)/shard_map/ppermute | solution.py:653
  155.7 1.0 collective-permute-done.22.refs_2_
  156.7 1.7 %collective-permute-done.23.refs_3_ = bf16[32,512]{1,0:T(8,128)(2,1)S(1)} collective-permute-done((bf16[32,512]{1,0:T(8,128)(2,1)S(1)}, bf16[32,512]{1,0:T(8,128)(2,1)S(1)}, u32[]{:S(2)}, u32[]{:S(2)}) %collective-permute-start.23) | collective-permute-done | bytes 32800 | tf_op jit(solution)/shard_map/ppermute | solution.py:653
  158.5 0.9 final_sum.1
  (37 shorter events, 1.7 us)
Async XLA Ops:
  1.3 16.3 %all-to-all-start = ((bf16[8,16,256]{2,1,0:T(8,128)(2,1)}), bf16[8,16,256]{2,1,0:T(8,128)(2,1)S(1)}, u32[]{:S(2)}, u32[]{:S(2)}) async-start(bf16[8,16,256]{2,1,0:T(8,128)(2,1)} %own_count.1), calls=%async_computation | async-start | bytes 131072 | tf_op jit(solution)/shard_map/all_to_all | solution.py:649
  10.3 25.9 %copy-start.3 = (bf16[256,2048]{1,0:T(8,128)(2,1)S(1)}, bf16[256,2048]{1,0:T(8,128)(2,1)}, u32[]{:S(2)}) copy-start(bf16[256,2048]{1,0:T(8,128)(2,1)} %wa_hbm.1) | copy-start | bytes 3145732
  12.8 13.3 %copy-start.5 = (bf16[128,256]{1,0:T(8,128)(2,1)S(1)}, bf16[128,256]{1,0:T(8,128)(2,1)}, u32[]{:S(2)}) copy-start(bf16[128,256]{1,0:T(8,128)(2,1)} %get-tuple-element.33.a_ref) | copy-start | bytes 196612
  12.8 42.8 %copy-start.7 = (f32[2]{0:T(128)S(1)}, f32[2]{0:T(128)}, u32[]{:S(2)}) copy-start(f32[2]{0:T(128)} %slope_ref.2) | copy-start | bytes 28
  17.5 0.6 copy-start.8
  22.1 9.6 %collective-permute-start.2 = (bf16[784,256]{1,0:T(8,128)(2,1)}, bf16[784,256]{1,0:T(8,128)(2,1)S(1)}, u32[]{:S(2)}, u32[]{:S(2)}) collective-permute-start(bf16[784,256]{1,0:T(8,128)(2,1)} %project_pack.1.refs_5_), channel_id=1, source_target_pairs={{0,192},{64,0},{128,64},{192,128},{1,193},{65,1},{129,65},{193,129... | collective-permute-start | bytes 1204232 | tf_op jit(solution)/shard_map/ppermute | solution.py:658
  24.9 9.8 %collective-permute-start.1 = (bf16[784,256]{1,0:T(8,128)(2,1)}, bf16[784,256]{1,0:T(8,128)(2,1)S(1)}, u32[]{:S(2)}, u32[]{:S(2)}) collective-permute-start(bf16[784,256]{1,0:T(8,128)(2,1)} %project_pack.1.refs_5_), channel_id=1, source_target_pairs={{0,64},{64,128},{128,192},{192,0},{1,65},{65,129},{129,193},{193,1... | collective-permute-start | bytes 1204232 | tf_op jit(solution)/shard_map/ppermute | solution.py:658
  24.9 9.8 %collective-permute-start = (bf16[784,256]{1,0:T(8,128)(2,1)}, bf16[784,256]{1,0:T(8,128)(2,1)S(1)}, u32[]{:S(2)}, u32[]{:S(2)}) collective-permute-start(bf16[784,256]{1,0:T(8,128)(2,1)} %project_pack.1.refs_5_), channel_id=1, source_target_pairs={{0,4},{4,0},{1,5},{5,1},{2,6},{6,2},{3,7},{7,3},{8,12},{12,8},{9,1... | collective-permute-start | bytes 1204232 | tf_op jit(solution)/shard_map/ppermute | solution.py:653
  26.1 3.4 %collective-permute-start.3 = (bf16[128,256]{1,0:T(8,128)(2,1)S(1)}, bf16[128,256]{1,0:T(8,128)(2,1)S(1)}, u32[]{:S(2)}, u32[]{:S(2)}) collective-permute-start(bf16[128,256]{1,0:T(8,128)(2,1)S(1)} %copy-done.5), channel_id=1, source_target_pairs={{0,8},{8,0},{16,24},{24,16},{32,40},{40,32},{48,56},{56,48},{1,9},... | collective-permute-start | bytes 196616 | tf_op jit(solution)/shard_map/ppermute | solution.py:653
  34.7 11.2 %collective-permute-start.5 = (bf16[784,256]{1,0:T(8,128)(2,1)S(1)}, bf16[784,256]{1,0:T(8,128)(2,1)S(1)}, u32[]{:S(2)}, u32[]{:S(2)}) collective-permute-start(bf16[784,256]{1,0:T(8,128)(2,1)S(1)} %collective-permute-done.refs_6_), channel_id=1, source_target_pairs={{0,192},{64,0},{128,64},{192,128},{1,193},{65,1},{129,65},{193,129... | collective-permute-start | bytes 1204232 | tf_op jit(solution)/shard_map/ppermute | solution.py:658
  35.9 10.0 %collective-permute-start.4 = (bf16[784,256]{1,0:T(8,128)(2,1)S(1)}, bf16[784,256]{1,0:T(8,128)(2,1)S(1)}, u32[]{:S(2)}, u32[]{:S(2)}) collective-permute-start(bf16[784,256]{1,0:T(8,128)(2,1)S(1)} %collective-permute-done.refs_6_), channel_id=1, source_target_pairs={{0,64},{64,128},{128,192},{192,0},{1,65},{65,129},{129,193},{193,1... | collective-permute-start | bytes 1204232 | tf_op jit(solution)/shard_map/ppermute | solution.py:658
  36.2 32.8 %collective-permute-start.12 = (bf16[256,2048]{1,0:T(8,128)(2,1)S(1)}, bf16[256,2048]{1,0:T(8,128)(2,1)S(1)}, u32[]{:S(2)}, u32[]{:S(2)}) collective-permute-start(bf16[256,2048]{1,0:T(8,128)(2,1)S(1)} %copy-done.3), channel_id=1, source_target_pairs={{0,2},{1,3},{2,0},{3,1},{4,6},{5,7},{6,4},{7,5},{8,10},{9,11},{10,... | collective-permute-start | bytes 3145736 | tf_op jit(solution)/shard_map/ppermute | solution.py:653
  38.9 6.5 %collective-permute-start.7 = (bf16[256,256]{1,0:T(8,128)(2,1)S(1)}, bf16[256,256]{1,0:T(8,128)(2,1)S(1)}, u32[]{:S(2)}, u32[]{:S(2)}) collective-permute-start(bf16[256,256]{1,0:T(8,128)(2,1)S(1)} %join.2.refs_0_), channel_id=1, source_target_pairs={{0,48},{8,56},{16,0},{24,8},{32,16},{40,24},{48,32},{56,40},{1,49}... | collective-permute-start | bytes 393224 | tf_op jit(solution)/shard_map/ppermute | solution.py:658
  39.3 6.5 %collective-permute-start.6 = (bf16[256,256]{1,0:T(8,128)(2,1)S(1)}, bf16[256,256]{1,0:T(8,128)(2,1)S(1)}, u32[]{:S(2)}, u32[]{:S(2)}) collective-permute-start(bf16[256,256]{1,0:T(8,128)(2,1)S(1)} %join.2.refs_0_), channel_id=1, source_target_pairs={{0,16},{8,24},{16,32},{24,40},{32,48},{40,56},{48,0},{56,8},{1,17}... | collective-permute-start | bytes 393224 | tf_op jit(solution)/shard_map/ppermute | solution.py:658
  45.9 9.7 %collective-permute-start.10 = (bf16[784,256]{1,0:T(8,128)(2,1)S(1)}, bf16[784,256]{1,0:T(8,128)(2,1)S(1)}, u32[]{:S(2)}, u32[]{:S(2)}) collective-permute-start(bf16[784,256]{1,0:T(8,128)(2,1)S(1)} %collective-permute-done.1.refs_7_), channel_id=1, source_target_pairs={{0,64},{64,128},{128,192},{192,0},{1,65},{65,129},{129,193},{193,1... | collective-permute-start | bytes 1204232 | tf_op jit(solution)/shard_map/ppermute | solution.py:658
  45.9 9.7 %collective-permute-start.11 = (bf16[784,256]{1,0:T(8,128)(2,1)S(1)}, bf16[784,256]{1,0:T(8,128)(2,1)S(1)}, u32[]{:S(2)}, u32[]{:S(2)}) collective-permute-start(bf16[784,256]{1,0:T(8,128)(2,1)S(1)} %collective-permute-done.5.refs_10_), channel_id=1, source_target_pairs={{0,192},{64,0},{128,64},{192,128},{1,193},{65,1},{129,65},{193,129... | collective-permute-start | bytes 1204232 | tf_op jit(solution)/shard_map/ppermute | solution.py:658
  48.5 5.6 %collective-permute-start.8 = (bf16[128,256]{1,0:T(8,128)(2,1)S(1)}, bf16[128,256]{1,0:T(8,128)(2,1)S(1)}, u32[]{:S(2)}, u32[]{:S(2)}) collective-permute-start(bf16[128,256]{1,0:T(8,128)(2,1)S(1)} %get-tuple-element.40), channel_id=1, source_target_pairs={{0,16},{8,24},{16,32},{24,40},{32,48},{40,56},{48,0},{56,8},{1,17}... | collective-permute-start | bytes 196616 | tf_op jit(solution)/shard_map/ppermute | solution.py:658
  50.0 42.6 %copy-start.1 = (bf16[128,2048]{1,0:T(8,128)(2,1)S(1)}, bf16[128,2048]{1,0:T(8,128)(2,1)}, u32[]{:S(2)}) copy-start(bf16[128,2048]{1,0:T(8,128)(2,1)} %tok_hbm.3) | copy-start | bytes 1572868
  50.0 5.5 %collective-permute-start.9 = (bf16[128,256]{1,0:T(8,128)(2,1)S(1)}, bf16[128,256]{1,0:T(8,128)(2,1)S(1)}, u32[]{:S(2)}, u32[]{:S(2)}) collective-permute-start(bf16[128,256]{1,0:T(8,128)(2,1)S(1)} %get-tuple-element.41), channel_id=1, source_target_pairs={{0,48},{8,56},{16,0},{24,8},{32,16},{40,24},{48,32},{56,40},{1,49}... | collective-permute-start | bytes 196616 | tf_op jit(solution)/shard_map/ppermute | solution.py:658
  55.5 1.0 copy-start.4
  68.9 41.6 %copy-start = (bf16[2048,3,256]{2,0,1:T(8,128)(2,1)S(1)}, bf16[2048,3,256]{2,0,1:T(8,128)(2,1)}, u32[]{:S(2)}) copy-start(bf16[2048,3,256]{2,0,1:T(8,128)(2,1)} %param.17) | copy-start | bytes 9437188
  87.6 5.0 %collective-permute-start.13 = (bf16[128,256]{1,0:T(8,128)(2,1)S(1)}, bf16[128,256]{1,0:T(8,128)(2,1)S(1)}, u32[]{:S(2)}, u32[]{:S(2)}) collective-permute-start(bf16[128,256]{1,0:T(8,128)(2,1)S(1)} %merge.1.a_ref), channel_id=1, source_target_pairs={{0,2},{1,3},{2,0},{3,1},{4,6},{5,7},{6,4},{7,5},{8,10},{9,11},{10,... | collective-permute-start | bytes 196616 | tf_op jit(solution)/shard_map/ppermute | solution.py:653
  93.9 37.0 %copy-start.6 = (f32[2]{0:T(128)S(1)}, f32[2]{0:T(128)}, u32[]{:S(2)}) copy-start(f32[2]{0:T(128)} %slope_ref.3) | copy-start | bytes 28
  93.9 16.6 %collective-permute-start.14 = (bf16[128,2048]{1,0:T(8,128)(2,1)S(1)}, bf16[128,2048]{1,0:T(8,128)(2,1)S(1)}, u32[]{:S(2)}, u32[]{:S(2)}) collective-permute-start(bf16[128,2048]{1,0:T(8,128)(2,1)S(1)} %get-tuple-element.50), channel_id=1, source_target_pairs={{0,1},{1,0},{2,3},{3,2},{4,5},{5,4},{6,7},{7,6},{8,9},{9,8},{10,11... | collective-permute-start | bytes 1572872 | tf_op jit(solution)/shard_map/ppermute | solution.py:653
  103.0 5.2 %collective-permute-start.16 = (bf16[32,2048]{1,0:T(8,128)(2,1)S(1)}, bf16[32,2048]{1,0:T(8,128)(2,1)S(1)}, u32[]{:S(2)}, u32[]{:S(2)}) collective-permute-start(bf16[32,2048]{1,0:T(8,128)(2,1)S(1)} %get-tuple-element.51), channel_id=1, source_target_pairs={{0,5},{1,4},{2,7},{3,6},{4,9},{5,8},{6,11},{7,10},{8,13},{9,12},{1... | collective-permute-start | bytes 393224 | tf_op jit(solution)/shard_map/ppermute | solution.py:714
  105.1 5.4 %collective-permute-start.15 = (bf16[32,2048]{1,0:T(8,128)(2,1)S(1)}, bf16[32,2048]{1,0:T(8,128)(2,1)S(1)}, u32[]{:S(2)}, u32[]{:S(2)}) collective-permute-start(bf16[32,2048]{1,0:T(8,128)(2,1)S(1)} %get-tuple-element.51), channel_id=1, source_target_pairs={{0,4},{1,5},{2,6},{3,7},{4,8},{5,9},{6,10},{7,11},{8,12},{9,13},{1... | collective-permute-start | bytes 393224 | tf_op jit(solution)/shard_map/ppermute | solution.py:713
  110.5 36.2 %copy-start.2 = (bf16[256,2048]{1,0:T(8,128)(2,1)S(1)}, bf16[256,2048]{1,0:T(8,128)(2,1)}, u32[]{:S(2)}) copy-start(bf16[256,2048]{1,0:T(8,128)(2,1)} %w_ref.1) | copy-start | bytes 3145732
  112.5 3.5 %collective-permute-start.17 = (bf16[32,512]{1,0:T(8,128)(2,1)S(1)}, bf16[32,512]{1,0:T(8,128)(2,1)S(1)}, u32[]{:S(2)}, u32[]{:S(2)}) collective-permute-start(bf16[32,512]{1,0:T(8,128)(2,1)S(1)} %get-tuple-element.54.a_ref), channel_id=1, source_target_pairs={{0,4},{4,0},{1,5},{5,1},{2,6},{6,2},{3,7},{7,3},{8,12},{12,8},{9,1... | collective-permute-start | bytes 98312 | tf_op jit(solution)/shard_map/ppermute | solution.py:653
  116.0 14.9 %all-to-all-start.2 = ((bf16[8,32,256]{2,1,0:T(8,128)(2,1)}), bf16[8,32,256]{2,1,0:T(8,128)(2,1)S(1)}, u32[]{:S(2)}, u32[]{:S(2)}) async-start(bf16[8,32,256]{2,1,0:T(8,128)(2,1)} %get-tuple-element.55), calls=%async_computation.2 | async-start | bytes 262144 | tf_op jit(solution)/shard_map/all_to_all | solution.py:649
  121.0 5.8 %collective-permute-start.20 = (bf16[64,512]{1,0:T(8,128)(2,1)S(1)}, bf16[64,512]{1,0:T(8,128)(2,1)S(1)}, u32[]{:S(2)}, u32[]{:S(2)}) collective-permute-start(bf16[64,512]{1,0:T(8,128)(2,1)S(1)} %join.3.refs_0_), channel_id=1, source_target_pairs={{0,192},{64,0},{128,64},{192,128},{1,193},{65,1},{129,65},{193,129... | collective-permute-start | bytes 196616 | tf_op jit(solution)/shard_map/ppermute | solution.py:658
  125.5 4.7 %collective-permute-start.19 = (bf16[64,512]{1,0:T(8,128)(2,1)S(1)}, bf16[64,512]{1,0:T(8,128)(2,1)S(1)}, u32[]{:S(2)}, u32[]{:S(2)}) collective-permute-start(bf16[64,512]{1,0:T(8,128)(2,1)S(1)} %join.3.refs_0_), channel_id=1, source_target_pairs={{0,128},{64,192},{128,0},{192,64},{1,129},{65,193},{129,1},{193,65... | collective-permute-start | bytes 196616 | tf_op jit(solution)/shard_map/ppermute | solution.py:658
  125.6 5.3 %collective-permute-start.18 = (bf16[64,512]{1,0:T(8,128)(2,1)S(1)}, bf16[64,512]{1,0:T(8,128)(2,1)S(1)}, u32[]{:S(2)}, u32[]{:S(2)}) collective-permute-start(bf16[64,512]{1,0:T(8,128)(2,1)S(1)} %join.3.refs_0_), channel_id=1, source_target_pairs={{0,64},{64,128},{128,192},{192,0},{1,65},{65,129},{129,193},{193,1... | collective-permute-start | bytes 196616 | tf_op jit(solution)/shard_map/ppermute | solution.py:658
  147.3 8.4 %collective-permute-start.21 = (bf16[32,512]{1,0:T(8,128)(2,1)S(1)}, bf16[32,512]{1,0:T(8,128)(2,1)S(1)}, u32[]{:S(2)}, u32[]{:S(2)}) collective-permute-start(bf16[32,512]{1,0:T(8,128)(2,1)S(1)} %get-tuple-element.58), channel_id=1, source_target_pairs={{0,1},{1,0},{2,3},{3,2},{4,5},{5,4},{6,7},{7,6},{8,9},{9,8},{10,11... | collective-permute-start | bytes 98312 | tf_op jit(solution)/shard_map/ppermute | solution.py:653
  152.4 4.3 %collective-permute-start.22 = (bf16[32,512]{1,0:T(8,128)(2,1)S(1)}, bf16[32,512]{1,0:T(8,128)(2,1)S(1)}, u32[]{:S(2)}, u32[]{:S(2)}) collective-permute-start(bf16[32,512]{1,0:T(8,128)(2,1)S(1)} %get-tuple-element.59), channel_id=1, source_target_pairs={{0,2},{1,3},{2,0},{3,1},{4,6},{5,7},{6,4},{7,5},{8,10},{9,11},{10,... | collective-permute-start | bytes 98312 | tf_op jit(solution)/shard_map/ppermute | solution.py:653
  153.6 4.9 %collective-permute-start.23 = (bf16[32,512]{1,0:T(8,128)(2,1)S(1)}, bf16[32,512]{1,0:T(8,128)(2,1)S(1)}, u32[]{:S(2)}, u32[]{:S(2)}) collective-permute-start(bf16[32,512]{1,0:T(8,128)(2,1)S(1)} %get-tuple-element.60), channel_id=1, source_target_pairs={{0,3},{1,2},{2,1},{3,0},{4,7},{5,6},{6,5},{7,4},{8,11},{9,10},{10,... | collective-permute-start | bytes 98312 | tf_op jit(solution)/shard_map/ppermute | solution.py:653

commit v8 on v7

--- a/solution.py
+++ b/solution.py
@@ -81,69 +81,102 @@
     )(rows, weight3)
 
 
-def pack_kernel(
-    normed_hbm, w_hbm, ck_hbm, cv_hbm, table_ref, pack_ref, normed, weight, sems
-):
+def key_kernel(normed_hbm, w_hbm, kv_ref, normed, weight, sems):
     rows = normed.shape[0]
-    slots = ck_hbm.shape[0]
     copies = [pltpu.make_async_copy(normed_hbm, normed, sems.at[0])]
     copies += [
         pltpu.make_async_copy(w_hbm.at[1 + i], weight.at[i], sems.at[1 + i]) for i in range(2)
     ]
-    copies += [
-        pltpu.make_async_copy(ck_hbm, pack_ref.at[:slots], sems.at[3]),
-        pltpu.make_async_copy(cv_hbm, pack_ref.at[slots : 2 * slots], sems.at[4]),
-    ]
     for copy in copies:
         copy.start()
-    table = jnp.sum(table_ref[...].astype(F32), axis=0)
-    pack_ref[2 * (slots + rows) :] = table.astype(BF16)
     copies[0].wait()
     for i in range(2):
         copies[1 + i].wait()
         out = jnp.dot(normed[...], weight[i], preferred_element_type=F32)
-        at = 2 * slots + i * rows
-        pack_ref[at : at + rows] = out.astype(BF16)
-    copies[3].wait()
-    copies[4].wait()
-
-
-def project_pack(normed, weight3, cache_keys, cache_values, table):
+        kv_ref[i * rows : (i + 1) * rows] = out.astype(BF16)
+
+
+def project_keys(normed, weight3):
     n, d = normed.shape
     width = weight3.shape[2]
-    total = 2 * (n + cache_keys.shape[0]) + table.shape[1]
     hbm = pl.BlockSpec(memory_space=HBM)
     return pl.pallas_call(
-        pack_kernel,
-        in_specs=[hbm] * 4 + [pl.BlockSpec(memory_space=VMEM)],
+        key_kernel,
+        in_specs=[hbm, hbm],
         out_specs=pl.BlockSpec(memory_space=VMEM),
-        out_shape=jax.ShapeDtypeStruct((total, width), BF16),
+        out_shape=jax.ShapeDtypeStruct((2 * n, width), BF16),
         scratch_shapes=[
             VMEM((n, d), BF16),
             VMEM((2, d, width), BF16),
-            pltpu.SemaphoreType.DMA((5,)),
+            pltpu.SemaphoreType.DMA((3,)),
         ],
         compiler_params=params(60),
         cost_estimate=cost(4 * n * d * width, 2 * (n * d + 2 * d * width)),
-        name="project_pack",
-    )(normed, weight3, cache_keys, cache_values, table)
+        name="project_keys",
+    )(normed, weight3)
+
+
+def pack_kernel(ck_hbm, cv_hbm, kv_hbm, near_ref, far_ref, pack_ref, sems):
+    slots, both = ck_hbm.shape[0], kv_hbm.shape[0]
+    copies = [
+        pltpu.make_async_copy(ck_hbm, pack_ref.at[:slots], sems.at[0]),
+        pltpu.make_async_copy(cv_hbm, pack_ref.at[slots : 2 * slots], sems.at[1]),
+        pltpu.make_async_copy(kv_hbm, pack_ref.at[2 * slots : 2 * slots + both], sems.at[2]),
+    ]
+    for copy in copies:
+        copy.start()
+    table = near_ref[...].astype(F32) + far_ref[...].astype(F32)
+    pack_ref[2 * slots + both :] = table.astype(BF16)
+    for copy in copies:
+        copy.wait()
+
+
+def make_pack(cache_keys, cache_values, kv, near, far):
+    total = 2 * cache_keys.shape[0] + kv.shape[0] + near.shape[0]
+    width = kv.shape[1]
+    hbm = pl.BlockSpec(memory_space=HBM)
+    vmem = pl.BlockSpec(memory_space=VMEM)
+    return pl.pallas_call(
+        pack_kernel,
+        in_specs=[hbm] * 3 + [vmem] * 2,
+        out_specs=vmem,
+        out_shape=jax.ShapeDtypeStruct((total, width), BF16),
+        scratch_shapes=[pltpu.SemaphoreType.DMA((3,))],
+        compiler_params=params(60),
+        cost_estimate=cost(0, 4 * total * width),
+        name="make_pack",
+    )(cache_keys, cache_values, kv, near, far)
 
 
 def table_kernel(count_ref, out_ref):
     y, z, xl = place_of_device()
-    lane = lax.broadcasted_iota(jnp.int32, out_ref.shape, 2)
+    lane = lax.broadcasted_iota(jnp.int32, out_ref.shape, 1)
     out_ref[...] = jnp.where(lane == y * 16 + z * 2 + xl, count_ref[0], 0).astype(F32).astype(BF16)
 
 
-def own_count(count, copies, width):
+def own_count(count, width):
     return pl.pallas_call(
         table_kernel,
         in_specs=[pl.BlockSpec(memory_space=SMEM)],
-        out_shape=jax.ShapeDtypeStruct((copies, 16, width), BF16),
+        out_shape=jax.ShapeDtypeStruct((16, width), BF16),
         compiler_params=params(8),
-        cost_estimate=cost(0, 32 * copies * width),
+        cost_estimate=cost(0, 32 * width),
         name="own_count",
     )(count)
+
+
+def add_kernel(a_ref, b_ref, out_ref):
+    out_ref[...] = (a_ref[...].astype(F32) + b_ref[...].astype(F32)).astype(BF16)
+
+
+def added(a, b):
+    return pl.pallas_call(
+        add_kernel,
+        out_shape=jax.ShapeDtypeStruct(a.shape, a.dtype),
+        compiler_params=params(8),
+        cost_estimate=cost(a.size, 6 * a.size),
+        name="added",
+    )(a, b)
 
 
 def join_kernel(a_ref, b_ref, out_ref):
@@ -240,7 +273,8 @@
     out_ref, q_tile, bias = refs[13:]
     tile = pl.program_id(0)
     y, z, xl = place_of_device()
-    rows = q_tile.shape[0] // 2
+    count = q_tile.shape[0]
+    rows = count // 4
     width = q_tile.shape[1]
     heads = width // HS
     owners = len(RING)
@@ -250,14 +284,17 @@
         return 1 - xl if other else xl
 
     own, left, right, far, far_other = queries
-    for t, (a, b, at) in enumerate(
-        ((own, own, rows), (left, left, rows), (far, far_other, 0), (right, right, rows))
+    for t, pieces in enumerate(
+        (
+            ((own, 0), (own, rows), (left, 0), (left, rows)),
+            ((far, 0), (far_other, 0), (right, 0), (right, rows)),
+        )
     ):
 
         @pl.when(tile == t)
-        def _(a=a, b=b, at=at):
-            q_tile[:rows] = a[:rows]
-            q_tile[rows:] = b[at : at + rows]
+        def _(pieces=pieces):
+            for b, (ref, at) in enumerate(pieces):
+                q_tile[b * rows : (b + 1) * rows] = ref[at : at + rows]
 
     @pl.when(tile == 0)
     def _():
@@ -282,10 +319,10 @@
                 at = cached + j * rows
                 bias[h : h + 1, at : at + rows] = jnp.where(yj <= y, slope * spot, NEG)
 
-    row = lax.broadcasted_iota(jnp.int32, (2 * rows, 1), 0)
-    first = (z + 8 - 2 * tile) % 8
-    row_ctx = y * 16 + xl + 2 * jnp.where(row < rows, first, first ^ 1)
-    row_pos = row_ctx * rows + jnp.where(row < rows, row, row - rows)
+    row = lax.broadcasted_iota(jnp.int32, (count, 1), 0)
+    part = row // rows
+    row_z = ((z + 8 - 4 * tile - 2 * (part // 2)) % 8) ^ (part % 2)
+    row_pos = (y * 16 + xl + 2 * row_z) * rows + row % rows
     place = lax.broadcasted_iota(jnp.int32, (1, rows), 1)
 
     def score(h, q, j):
@@ -308,8 +345,8 @@
             return with_ones(packs[j][slots : 2 * slots, cols])
         return with_ones(packs[j - owners][2 * slots + rows : 2 * (slots + rows), cols])
 
-    lane = lax.broadcasted_iota(jnp.int32, (2 * rows, HS), 1)
-    packed = jnp.zeros((2 * rows, HS), F32)
+    lane = lax.broadcasted_iota(jnp.int32, (count, HS), 1)
+    packed = jnp.zeros((count, HS), F32)
     qs = [q_tile[:, h * HS : (h + 1) * HS] for h in range(heads)]
     done = []
     for h, (top, total, acc) in enumerate(attend_heads(qs, 2 * owners, score, value)):
@@ -318,21 +355,24 @@
             packed = jnp.where(lane == 3 * h + k, piece, packed)
     both = jnp.concatenate(done, axis=1)
     odd = z % 2 == 1
-    blocks = []
-    for own, level in (
-        (jnp.where(odd, both[rows:], both[:rows]), jnp.where(odd, packed[rows:], packed[:rows])),
-        (jnp.where(odd, both[:rows], both[rows:]), jnp.where(odd, packed[:rows], packed[rows:])),
-    ):
-        turned = jnp.transpose(level)[:16]
-        tail = jnp.concatenate([turned, jnp.zeros_like(turned)], axis=1).astype(BF16)
-        blocks.append((own, tail))
-    for p in range(4):
-
-        @pl.when((z // 2 + 4 - tile) % 4 == p)
-        def _(p=p):
-            for b, (own, tail) in enumerate(blocks):
-                out_ref[2 * p + b, :rows] = own
-                out_ref[2 * p + b, rows:] = tail
+    for pair in range(2):
+        a, b = 2 * pair * rows, (2 * pair + 1) * rows
+        end = b + rows
+        blocks = []
+        for own, level in (
+            (jnp.where(odd, both[b:end], both[a:b]), jnp.where(odd, packed[b:end], packed[a:b])),
+            (jnp.where(odd, both[a:b], both[b:end]), jnp.where(odd, packed[a:b], packed[b:end])),
+        ):
+            turned = jnp.transpose(level)[:16]
+            tail = jnp.concatenate([turned, jnp.zeros_like(turned)], axis=1).astype(BF16)
+            blocks.append((own, tail))
+        for p in range(4):
+
+            @pl.when((z // 2 + 4 - 2 * tile - pair) % 4 == p)
+            def _(p=p, blocks=blocks):
+                for i, (own, tail) in enumerate(blocks):
+                    out_ref[2 * p + i, :rows] = own
+                    out_ref[2 * p + i, rows:] = tail
 
 
 def attend(slopes, queries, packs, slots):
@@ -342,13 +382,13 @@
     out = jax.ShapeDtypeStruct((8, rows + 16, width), BF16)
     return pl.pallas_call(
         functools.partial(attend_kernel, slots),
-        grid=(4,),
+        grid=(2,),
         in_specs=[pl.BlockSpec(memory_space=SMEM)]
         + [whole(a) for a in (*queries, *packs)],
         out_specs=whole(out),
         out_shape=out,
-        scratch_shapes=[VMEM((2 * rows, width), BF16), VMEM((8, nk), F32)],
-        compiler_params=params(40),
+        scratch_shapes=[VMEM((4 * rows, width), BF16), VMEM((8, nk), F32)],
+        compiler_params=params(44),
         cost_estimate=cost(32 * rows * nk * width, 4 * nk * width, 16 * rows * nk),
         name="attend",
     )(slopes, *queries, *packs)
@@ -662,6 +702,10 @@
     return moved(x, axis, by), moved(x, axis, -by)
 
 
+def counts_along(table, flip):
+    return added(table, swap(table, "z", flip))
+
+
 def after(x, *others):
     return lax.optimization_barrier((x, *others))[0]
 
@@ -682,9 +726,13 @@
     slots = cache_keys.shape[0]
     weight3 = jnp.transpose(project_weight, (1, 0, 2))
     nz = lax.axis_size("z")
-    table = exchange(own_count(cache_count, nz, cache_keys.shape[1]), "z")
+    near = counts_along(own_count(cache_count, cache_keys.shape[1]), 1)
     q, normed = project_queries(tokens, weight3)
-    pack = project_pack(normed, weight3, cache_keys, cache_values, table)
+    normed, near = lax.optimization_barrier((normed, near))
+    near = counts_along(near, 2)
+    kv = project_keys(normed, weight3)
+    kv, near = lax.optimization_barrier((kv, near))
+    pack = make_pack(cache_keys, cache_values, kv, near, swap(near, "z", 4))
     left, right = both_ways(pack, "y", 1)
     other, left, right, mate = lax.optimization_barrier(
         (swap(pack, "xl"), left, right, swap(q, "z"))

time: 160 us -> 161 us (level)
  starting transfers between devices: 61.6 us -> 63.4 us
    ppermute x9 -> x12, starting transfers between devices: 24 us -> 34.5 us  [swap(): lax.ppermute(x, axis, [(i, i ^ flip) for i in range(lax.axis_size(axis))])]
    all_to_all x2 -> x1, starting transfers between devices: 14 us -> 4.98 us  [exchange(): return lax.all_to_all(blocks, axis, 0, 0)]
    all_to_all x2 -> x1, waiting for transfers between devices: 4.77 us -> 0.01 us  [exchange(): return lax.all_to_all(blocks, axis, 0, 0)]
    ppermute x9 -> x12, waiting for transfers between devices: 12.1 us -> 14.6 us  [swap(): lax.ppermute(x, axis, [(i, i ^ flip) for i in range(lax.axis_size(axis))])]
    pallas_call x2 -> x5, Pallas kernels: 16.3 us -> 16.8 us  [the longest x1 11.3 us: attend(): pl.pallas_call(functools.partial(attend_kernel, slots), grid=(2,), in_spe...]
  transfers between devices with their start and end apart: 26 -> 28, of which waited for: 16 -> 15; matrix products, arithmetic and copies ran while one was open for 0% -> 0% of each run, Pallas kernels for 9% -> 10%
where the time goes in v8:
time: 161 us; the launch traced here: 160 us
  starting transfers between devices  63.4 us (39%)
  waiting for transfers between devices  35.2 us (22%)
  blocking collectives  32.9 us (20%)
  Pallas kernels  26.1 us (16%)
  local copies, waits for them, and re-layouts  1.63 us (1%)
    ppermute x12, starting transfers between devices, swap(): lax.ppermute(x, axis, [(i, i ^ flip) for i in range(lax.axis_size(axis))])  34.5 us
    all_to_all x2, blocking collectives, exchange(): return lax.all_to_all(blocks, axis, 0, 0)  32.9 us
    ppermute x13, starting transfers between devices, moved(): return lax.ppermute(x, axis, [(i, (i + by) % n) for i in range(n)])  18.7 us
    ppermute x13, waiting for transfers between devices, moved(): return lax.ppermute(x, axis, [(i, (i + by) % n) for i in range(n)])  18.3 us
    ppermute x12, waiting for transfers between devices, swap(): lax.ppermute(x, axis, [(i, i ^ flip) for i in range(lax.axis_size(axis))])  14.6 us
    pallas_call x1, Pallas kernels, attend(): pl.pallas_call(functools.partial(attend_kernel, slots), grid=(2,), in_spe...  11.3 us
    all_to_all x1, starting transfers between devices, exchange(): return lax.all_to_all(blocks, axis, 0, 0)  4.98 us
  transfers between devices with their start and end apart: 28, of which 15 were waited for; matrix products, arithmetic and copies ran while one was open for 0% of the time, Pallas kernels for 10%

profile of v8, /device:TPU:1, one launch (start us, length us, event | category | flops | bytes accessed | tf_op | source)
XLA Modules:
  0.0 160.1 jit_solution(3952134714647508967)
XLA Ops:
  0.7 2.6 %collective-permute-start = (bf16[16,256]{1,0:T(8,128)(2,1)S(1)}, bf16[16,256]{1,0:T(8,128)(2,1)S(1)}, u32[]{:S(2)}, u32[]{:S(2)}) collective-permute-start(bf16[16,256]{1,0:T(8,128)(2,1)S(1)} %own_count.1.a_ref), channel_id=1, source_target_pairs={{0,8},{8,0},{16,24},{24,16},{32,40},{40,32},{48,56},{56,48},{1,9},... | collective-permute-start | bytes 24584 | tf_op jit(solution)/shard_map/ppermute | solution.py:693
  3.2 2.3 %project_queries.1 = (bf16[128,256]{1,0:T(8,128)(2,1)}, bf16[128,2048]{1,0:T(8,128)(2,1)}) custom-call(bf16[128,2048]{1,0:T(8,128)(2,1)} %tok_hbm.3, bf16[3,2048,256]{2,1,0:T(8,128)(2,1)} %bitcast.3), custom_call_target="tpu_custom_call" | custom-call | flops 134217728 | bytes 1572864 | tf_op jit(solution)/shard_map/project_queries/pallas_call | solution.py:68
  5.6 3.1 %collective-permute-start.1 = (bf16[16,256]{1,0:T(8,128)(2,1)S(1)}, bf16[16,256]{1,0:T(8,128)(2,1)S(1)}, u32[]{:S(2)}, u32[]{:S(2)}) collective-permute-start(bf16[16,256]{1,0:T(8,128)(2,1)S(1)} %added.2.a_ref), channel_id=1, source_target_pairs={{0,16},{8,24},{16,0},{24,8},{32,48},{40,56},{48,32},{56,40},{1,17}... | collective-permute-start | bytes 24584 | tf_op jit(solution)/shard_map/ppermute | solution.py:693
  8.7 2.9 %project_keys.1.kv_hbm = bf16[256,256]{1,0:T(8,128)(2,1)} custom-call(bf16[128,2048]{1,0:T(8,128)(2,1)} %get-tuple-element.39.normed_hbm, bf16[3,2048,256]{2,1,0:T(8,128)(2,1)} %bitcast.4), custom_call_target="tpu_custom_call" | custom-call | flops 268435456 | bytes 2621440 | tf_op jit(solution)/shard_map/project_keys/pallas_call | solution.py:103
  11.7 4.3 %collective-permute-start.2 = (bf16[16,256]{1,0:T(8,128)(2,1)S(1)}, bf16[16,256]{1,0:T(8,128)(2,1)S(1)}, u32[]{:S(2)}, u32[]{:S(2)}) collective-permute-start(bf16[16,256]{1,0:T(8,128)(2,1)S(1)} %added.3.near_ref), channel_id=1, source_target_pairs={{0,32},{8,40},{16,48},{24,56},{32,0},{40,8},{48,16},{56,24},{1,33}... | collective-permute-start | bytes 24584 | tf_op jit(solution)/shard_map/ppermute | solution.py:693
  16.0 2.2 %collective-permute-done.2.far_ref = bf16[16,256]{1,0:T(8,128)(2,1)S(1)} collective-permute-done((bf16[16,256]{1,0:T(8,128)(2,1)S(1)}, bf16[16,256]{1,0:T(8,128)(2,1)S(1)}, u32[]{:S(2)}, u32[]{:S(2)}) %collective-permute-start.2) | collective-permute-done | bytes 8224 | tf_op jit(solution)/shard_map/ppermute | solution.py:693
  18.2 0.6 copy-done.9
  18.7 2.5 %make_pack.1.refs_5_ = bf16[784,256]{1,0:T(8,128)(2,1)} custom-call(bf16[256,256]{1,0:T(8,128)(2,1)} %ck_hbm.1, bf16[256,256]{1,0:T(8,128)(2,1)} %cv_hbm.1, bf16[256,256]{1,0:T(8,128)(2,1)} %project_keys.1.kv_hbm, bf16[16,256]{1,0:T(8,128)(2,1)} %copy-done.6, bf16[16,256]{1,0:T(8,128)(2,1)} %copy-done.9), custom_call_target="tpu_custom_call" | custom-call | bytes 802816 | tf_op jit(solution)/shard_map/make_pack/pallas_call | solution.py:139
  21.3 2.8 %collective-permute-start.5 = (bf16[784,256]{1,0:T(8,128)(2,1)}, bf16[784,256]{1,0:T(8,128)(2,1)S(1)}, u32[]{:S(2)}, u32[]{:S(2)}) collective-permute-start(bf16[784,256]{1,0:T(8,128)(2,1)} %make_pack.1.refs_5_), channel_id=1, source_target_pairs={{0,192},{64,0},{128,64},{192,128},{1,193},{65,1},{129,65},{193,129... | collective-permute-start | bytes 1204232 | tf_op jit(solution)/shard_map/ppermute | solution.py:698
  24.1 1.2 collective-permute-start.3
  25.3 3.4 %collective-permute-done.6.b_ref = bf16[128,256]{1,0:T(8,128)(2,1)S(1)} collective-permute-done((bf16[128,256]{1,0:T(8,128)(2,1)S(1)}, bf16[128,256]{1,0:T(8,128)(2,1)S(1)}, u32[]{:S(2)}, u32[]{:S(2)}) %collective-permute-start.6) | collective-permute-done | bytes 65568 | tf_op jit(solution)/shard_map/ppermute | solution.py:693
  28.7 1.9 %collective-permute-done.5.refs_9_ = bf16[784,256]{1,0:T(8,128)(2,1)S(1)} collective-permute-done((bf16[784,256]{1,0:T(8,128)(2,1)}, bf16[784,256]{1,0:T(8,128)(2,1)S(1)}, u32[]{:S(2)}, u32[]{:S(2)}) %collective-permute-start.5) | collective-permute-done | bytes 401440 | tf_op jit(solution)/shard_map/ppermute | solution.py:698
  30.6 3.0 %collective-permute-done.4.refs_7_ = bf16[784,256]{1,0:T(8,128)(2,1)S(1)} collective-permute-done((bf16[784,256]{1,0:T(8,128)(2,1)}, bf16[784,256]{1,0:T(8,128)(2,1)S(1)}, u32[]{:S(2)}, u32[]{:S(2)}) %collective-permute-start.4) | collective-permute-done | bytes 401440 | tf_op jit(solution)/shard_map/ppermute | solution.py:698
  33.6 1.2 collective-permute-start.8
  35.1 2.8 %collective-permute-start.15 = (bf16[256,2048]{1,0:T(8,128)(2,1)S(1)}, bf16[256,2048]{1,0:T(8,128)(2,1)S(1)}, u32[]{:S(2)}, u32[]{:S(2)}) collective-permute-start(bf16[256,2048]{1,0:T(8,128)(2,1)S(1)} %copy-done.3), channel_id=1, source_target_pairs={{0,2},{1,3},{2,0},{3,1},{4,6},{5,7},{6,4},{7,5},{8,10},{9,11},{10,... | collective-permute-start | bytes 3145736 | tf_op jit(solution)/shard_map/ppermute | solution.py:693
  37.9 3.2 %collective-permute-start.10 = (bf16[256,256]{1,0:T(8,128)(2,1)S(1)}, bf16[256,256]{1,0:T(8,128)(2,1)S(1)}, u32[]{:S(2)}, u32[]{:S(2)}) collective-permute-start(bf16[256,256]{1,0:T(8,128)(2,1)S(1)} %join.2.refs_0_), channel_id=1, source_target_pairs={{0,48},{8,56},{16,0},{24,8},{32,16},{40,24},{48,32},{56,40},{1,49}... | collective-permute-start | bytes 393224 | tf_op jit(solution)/shard_map/ppermute | solution.py:698
  41.0 3.3 %collective-permute-done.10.right_ref.refs_2_ = bf16[256,256]{1,0:T(8,128)(2,1)S(1)} collective-permute-done((bf16[256,256]{1,0:T(8,128)(2,1)S(1)}, bf16[256,256]{1,0:T(8,128)(2,1)S(1)}, u32[]{:S(2)}, u32[]{:S(2)}) %collective-permute-start.10) | collective-permute-done | bytes 131104 | tf_op jit(solution)/shard_map/ppermute | solution.py:698
  44.3 3.7 %collective-permute-done.9.left_ref.refs_1_ = bf16[256,256]{1,0:T(8,128)(2,1)S(1)} collective-permute-done((bf16[256,256]{1,0:T(8,128)(2,1)S(1)}, bf16[256,256]{1,0:T(8,128)(2,1)S(1)}, u32[]{:S(2)}, u32[]{:S(2)}) %collective-permute-start.9) | collective-permute-done | bytes 131104 | tf_op jit(solution)/shard_map/ppermute | solution.py:698
  48.1 2.7 %collective-permute-start.14 = (bf16[784,256]{1,0:T(8,128)(2,1)S(1)}, bf16[784,256]{1,0:T(8,128)(2,1)S(1)}, u32[]{:S(2)}, u32[]{:S(2)}) collective-permute-start(bf16[784,256]{1,0:T(8,128)(2,1)S(1)} %collective-permute-done.8.refs_10_), channel_id=1, source_target_pairs={{0,192},{64,0},{128,64},{192,128},{1,193},{65,1},{129,65},{193,129... | collective-permute-start | bytes 1204232 | tf_op jit(solution)/shard_map/ppermute | solution.py:698
  50.9 3.6 %collective-permute-start.12 = (bf16[128,256]{1,0:T(8,128)(2,1)S(1)}, bf16[128,256]{1,0:T(8,128)(2,1)S(1)}, u32[]{:S(2)}, u32[]{:S(2)}) collective-permute-start(bf16[128,256]{1,0:T(8,128)(2,1)S(1)} %get-tuple-element.49), channel_id=1, source_target_pairs={{0,48},{8,56},{16,0},{24,8},{32,16},{40,24},{48,32},{56,40},{1,49}... | collective-permute-start | bytes 196616 | tf_op jit(solution)/shard_map/ppermute | solution.py:698
  54.4 1.9 %collective-permute-done.11.refs_3_ = bf16[128,256]{1,0:T(8,128)(2,1)S(1)} collective-permute-done((bf16[128,256]{1,0:T(8,128)(2,1)S(1)}, bf16[128,256]{1,0:T(8,128)(2,1)S(1)}, u32[]{:S(2)}, u32[]{:S(2)}) %collective-permute-start.11) | collective-permute-done | bytes 65568 | tf_op jit(solution)/shard_map/ppermute | solution.py:698
  56.4 1.0 copy-done.4
  57.4 11.3 %attend.1 = bf16[8,144,256]{2,1,0:T(8,128)(2,1)S(1)} custom-call(f32[2]{0:T(128)S(1)} %copy-done.8, bf16[256,256]{1,0:T(8,128)(2,1)S(1)} %join.2.refs_0_, bf16[256,256]{1,0:T(8,128)(2,1)S(1)} %collective-permute-done.9.left_ref.refs_1_, bf16[256,256]{1,0:T(8,128)(2,1)S(1)} %collective-permute-done.10.right_ref.refs_2_, ...), custom_call_target="tpu_custom_call" | custom-call | flops 3221225472 | bytes 3145728 | tf_op jit(solution)/shard_map/attend/pallas_call | solution.py:383
  68.8 17.8 %all_to_all.15.parts_ref = bf16[8,144,256]{2,1,0:T(8,128)(2,1)S(1)} all-to-all(bf16[8,144,256]{2,1,0:T(8,128)(2,1)S(1)} %attend.1), channel_id=1, replica_groups=mesh['y'=4,'z'=8,'xl'=2,'tp'=4] {'z'}, dimensions={0} | all-to-all | bytes 1179648 | tf_op jit(solution)/shard_map/all_to_all | solution.py:689
  86.6 1.2 merge.1.a_ref
  87.9 4.9 %collective-permute-done.16.b_ref = bf16[128,256]{1,0:T(8,128)(2,1)S(1)} collective-permute-done((bf16[128,256]{1,0:T(8,128)(2,1)S(1)}, bf16[128,256]{1,0:T(8,128)(2,1)S(1)}, u32[]{:S(2)}, u32[]{:S(2)}) %collective-permute-start.16) | collective-permute-done | bytes 65568 | tf_op jit(solution)/shard_map/ppermute | solution.py:693
  92.8 1.3 layer_product.1
  94.1 9.9 %collective-permute-start.17 = (bf16[128,2048]{1,0:T(8,128)(2,1)S(1)}, bf16[128,2048]{1,0:T(8,128)(2,1)S(1)}, u32[]{:S(2)}, u32[]{:S(2)}) collective-permute-start(bf16[128,2048]{1,0:T(8,128)(2,1)S(1)} %get-tuple-element.58), channel_id=1, source_target_pairs={{0,1},{1,0},{2,3},{3,2},{4,5},{5,4},{6,7},{7,6},{8,9},{9,8},{10,11... | collective-permute-start | bytes 1572872 | tf_op jit(solution)/shard_map/ppermute | solution.py:693
  104.0 2.1 %collective-permute-start.19 = (bf16[32,2048]{1,0:T(8,128)(2,1)S(1)}, bf16[32,2048]{1,0:T(8,128)(2,1)S(1)}, u32[]{:S(2)}, u32[]{:S(2)}) collective-permute-start(bf16[32,2048]{1,0:T(8,128)(2,1)S(1)} %get-tuple-element.59), channel_id=1, source_target_pairs={{0,5},{1,4},{2,7},{3,6},{4,9},{5,8},{6,11},{7,10},{8,13},{9,12},{1... | collective-permute-start | bytes 393224 | tf_op jit(solution)/shard_map/ppermute | solution.py:762
  106.1 3.1 %collective-permute-start.18 = (bf16[32,2048]{1,0:T(8,128)(2,1)S(1)}, bf16[32,2048]{1,0:T(8,128)(2,1)S(1)}, u32[]{:S(2)}, u32[]{:S(2)}) collective-permute-start(bf16[32,2048]{1,0:T(8,128)(2,1)S(1)} %get-tuple-element.59), channel_id=1, source_target_pairs={{0,4},{1,5},{2,6},{3,7},{4,8},{5,9},{6,10},{7,11},{8,12},{9,13},{1... | collective-permute-start | bytes 393224 | tf_op jit(solution)/shard_map/ppermute | solution.py:761
  109.2 2.3 %collective-permute-done.18.rim_a = bf16[32,2048]{1,0:T(8,128)(2,1)S(1)} collective-permute-done((bf16[32,2048]{1,0:T(8,128)(2,1)S(1)}, bf16[32,2048]{1,0:T(8,128)(2,1)S(1)}, u32[]{:S(2)}, u32[]{:S(2)}) %collective-permute-start.18) | collective-permute-done | bytes 131104 | tf_op jit(solution)/shard_map/ppermute | solution.py:761
  111.6 2.0 %short_project.1 = (bf16[128,512]{1,0:T(8,128)(2,1)S(1)}, bf16[8,32,256]{2,1,0:T(8,128)(2,1)}, bf16[32,512]{1,0:T(8,128)(2,1)S(1)}) custom-call(f32[128,2048]{1,0:T(8,128)S(1)} %get-tuple-element.57.sum_ref, bf16[128,2048]{1,0:T(8,128)(2,1)S(1)} %collective-permute-done.17.term_ref, bf16[32,2048]{1,0:T(8,128)(2,1)S(1)} %collective-permute-done.18.rim_a, ...), custom_call_target="tpu_custom_call" | custom-call | flops 100663296 | bytes 3670016 | tf_op jit(solution)/shard_map/short_project/pallas_call | solution.py:545
  113.5 2.2 %collective-permute-start.20 = (bf16[32,512]{1,0:T(8,128)(2,1)S(1)}, bf16[32,512]{1,0:T(8,128)(2,1)S(1)}, u32[]{:S(2)}, u32[]{:S(2)}) collective-permute-start(bf16[32,512]{1,0:T(8,128)(2,1)S(1)} %get-tuple-element.62.a_ref), channel_id=1, source_target_pairs={{0,4},{4,0},{1,5},{5,1},{2,6},{6,2},{3,7},{7,3},{8,12},{12,8},{9,1... | collective-permute-start | bytes 98312 | tf_op jit(solution)/shard_map/ppermute | solution.py:693
  115.7 1.3 collective-permute-done.20.b_ref
  117.0 5.0 %all-to-all-start.1 = ((bf16[8,32,256]{2,1,0:T(8,128)(2,1)}), bf16[8,32,256]{2,1,0:T(8,128)(2,1)S(1)}, u32[]{:S(2)}, u32[]{:S(2)}) async-start(bf16[8,32,256]{2,1,0:T(8,128)(2,1)} %get-tuple-element.63), calls=%async_computation.1 | async-start | bytes 262144 | tf_op jit(solution)/shard_map/all_to_all | solution.py:689
  122.0 4.3 %collective-permute-start.23 = (bf16[64,512]{1,0:T(8,128)(2,1)S(1)}, bf16[64,512]{1,0:T(8,128)(2,1)S(1)}, u32[]{:S(2)}, u32[]{:S(2)}) collective-permute-start(bf16[64,512]{1,0:T(8,128)(2,1)S(1)} %join.3.refs_0_), channel_id=1, source_target_pairs={{0,192},{64,0},{128,64},{192,128},{1,193},{65,1},{129,65},{193,129... | collective-permute-start | bytes 196616 | tf_op jit(solution)/shard_map/ppermute | solution.py:698
  126.3 0.7 collective-permute-start.21
  127.0 0.7 collective-permute-done.23.refs_3_
  127.6 3.4 %collective-permute-done.22.refs_2_ = bf16[64,512]{1,0:T(8,128)(2,1)S(1)} collective-permute-done((bf16[64,512]{1,0:T(8,128)(2,1)S(1)}, bf16[64,512]{1,0:T(8,128)(2,1)S(1)}, u32[]{:S(2)}, u32[]{:S(2)}) %collective-permute-start.22) | collective-permute-done | bytes 65568 | tf_op jit(solution)/shard_map/ppermute | solution.py:698
  131.3 1.0 short_attend.1
  132.4 15.1 %all_to_all.16.parts_ref = bf16[8,32,384]{2,1,0:T(8,128)(2,1)S(1)} all-to-all(bf16[8,32,384]{2,1,0:T(8,128)(2,1)S(1)} %short_attend.1), channel_id=1, replica_groups=mesh['y'=4,'z'=8,'xl'=2,'tp'=4] {'z'}, dimensions={0} | all-to-all | bytes 393216 | tf_op jit(solution)/shard_map/all_to_all | solution.py:689
  147.5 0.5 short_merge.1
  148.0 5.2 %collective-permute-start.24 = (bf16[32,512]{1,0:T(8,128)(2,1)S(1)}, bf16[32,512]{1,0:T(8,128)(2,1)S(1)}, u32[]{:S(2)}, u32[]{:S(2)}) collective-permute-start(bf16[32,512]{1,0:T(8,128)(2,1)S(1)} %get-tuple-element.66), channel_id=1, source_target_pairs={{0,1},{1,0},{2,3},{3,2},{4,5},{5,4},{6,7},{7,6},{8,9},{9,8},{10,11... | collective-permute-start | bytes 98312 | tf_op jit(solution)/shard_map/ppermute | solution.py:693
  153.2 1.2 collective-permute-start.25
  154.3 2.1 %collective-permute-start.26 = (bf16[32,512]{1,0:T(8,128)(2,1)S(1)}, bf16[32,512]{1,0:T(8,128)(2,1)S(1)}, u32[]{:S(2)}, u32[]{:S(2)}) collective-permute-start(bf16[32,512]{1,0:T(8,128)(2,1)S(1)} %get-tuple-element.68), channel_id=1, source_target_pairs={{0,3},{1,2},{2,1},{3,0},{4,7},{5,6},{6,5},{7,4},{8,11},{9,10},{10,... | collective-permute-start | bytes 98312 | tf_op jit(solution)/shard_map/ppermute | solution.py:693
  156.4 1.0 collective-permute-done.25.refs_2_
  157.4 1.7 %collective-permute-done.26.refs_3_ = bf16[32,512]{1,0:T(8,128)(2,1)S(1)} collective-permute-done((bf16[32,512]{1,0:T(8,128)(2,1)S(1)}, bf16[32,512]{1,0:T(8,128)(2,1)S(1)}, u32[]{:S(2)}, u32[]{:S(2)}) %collective-permute-start.26) | collective-permute-done | bytes 32800 | tf_op jit(solution)/shard_map/ppermute | solution.py:693
  159.2 0.9 final_sum.1
  (46 shorter events, 0.9 us)
Async XLA Ops:
  0.7 4.9 %collective-permute-start = (bf16[16,256]{1,0:T(8,128)(2,1)S(1)}, bf16[16,256]{1,0:T(8,128)(2,1)S(1)}, u32[]{:S(2)}, u32[]{:S(2)}) collective-permute-start(bf16[16,256]{1,0:T(8,128)(2,1)S(1)} %own_count.1.a_ref), channel_id=1, source_target_pairs={{0,8},{8,0},{16,24},{24,16},{32,40},{40,32},{48,56},{56,48},{1,9},... | collective-permute-start | bytes 24584 | tf_op jit(solution)/shard_map/ppermute | solution.py:693
  5.6 19.7 %copy-start.5 = (bf16[128,256]{1,0:T(8,128)(2,1)S(1)}, bf16[128,256]{1,0:T(8,128)(2,1)}, u32[]{:S(2)}) copy-start(bf16[128,256]{1,0:T(8,128)(2,1)} %get-tuple-element.37.a_ref) | copy-start | bytes 196612
  5.6 29.5 %copy-start.3 = (bf16[256,2048]{1,0:T(8,128)(2,1)S(1)}, bf16[256,2048]{1,0:T(8,128)(2,1)}, u32[]{:S(2)}) copy-start(bf16[256,2048]{1,0:T(8,128)(2,1)} %wa_hbm.1) | copy-start | bytes 3145732
  5.6 50.8 %copy-start.8 = (f32[2]{0:T(128)S(1)}, f32[2]{0:T(128)}, u32[]{:S(2)}) copy-start(f32[2]{0:T(128)} %slope_ref.2) | copy-start | bytes 28
  5.6 6.0 %collective-permute-start.1 = (bf16[16,256]{1,0:T(8,128)(2,1)S(1)}, bf16[16,256]{1,0:T(8,128)(2,1)S(1)}, u32[]{:S(2)}, u32[]{:S(2)}) collective-permute-start(bf16[16,256]{1,0:T(8,128)(2,1)S(1)} %added.2.a_ref), channel_id=1, source_target_pairs={{0,16},{8,24},{16,0},{24,8},{32,48},{40,56},{48,32},{56,40},{1,17}... | collective-permute-start | bytes 24584 | tf_op jit(solution)/shard_map/ppermute | solution.py:693
  11.6 6.5 %copy-start.6 = (bf16[16,256]{1,0:T(8,128)(2,1)}, bf16[16,256]{1,0:T(8,128)(2,1)S(1)}, u32[]{:S(2)}) copy-start(bf16[16,256]{1,0:T(8,128)(2,1)S(1)} %added.3.near_ref) | copy-start | bytes 24580
  11.7 6.5 %collective-permute-start.2 = (bf16[16,256]{1,0:T(8,128)(2,1)S(1)}, bf16[16,256]{1,0:T(8,128)(2,1)S(1)}, u32[]{:S(2)}, u32[]{:S(2)}) collective-permute-start(bf16[16,256]{1,0:T(8,128)(2,1)S(1)} %added.3.near_ref), channel_id=1, source_target_pairs={{0,32},{8,40},{16,48},{24,56},{32,0},{40,8},{48,16},{56,24},{1,33}... | collective-permute-start | bytes 24584 | tf_op jit(solution)/shard_map/ppermute | solution.py:693
  18.2 0.6 copy-start.9
  21.3 9.3 %collective-permute-start.5 = (bf16[784,256]{1,0:T(8,128)(2,1)}, bf16[784,256]{1,0:T(8,128)(2,1)S(1)}, u32[]{:S(2)}, u32[]{:S(2)}) collective-permute-start(bf16[784,256]{1,0:T(8,128)(2,1)} %make_pack.1.refs_5_), channel_id=1, source_target_pairs={{0,192},{64,0},{128,64},{192,128},{1,193},{65,1},{129,65},{193,129... | collective-permute-start | bytes 1204232 | tf_op jit(solution)/shard_map/ppermute | solution.py:698
  24.1 9.5 %collective-permute-start.4 = (bf16[784,256]{1,0:T(8,128)(2,1)}, bf16[784,256]{1,0:T(8,128)(2,1)S(1)}, u32[]{:S(2)}, u32[]{:S(2)}) collective-permute-start(bf16[784,256]{1,0:T(8,128)(2,1)} %make_pack.1.refs_5_), channel_id=1, source_target_pairs={{0,64},{64,128},{128,192},{192,0},{1,65},{65,129},{129,193},{193,1... | collective-permute-start | bytes 1204232 | tf_op jit(solution)/shard_map/ppermute | solution.py:698
  24.1 9.5 %collective-permute-start.3 = (bf16[784,256]{1,0:T(8,128)(2,1)}, bf16[784,256]{1,0:T(8,128)(2,1)S(1)}, u32[]{:S(2)}, u32[]{:S(2)}) collective-permute-start(bf16[784,256]{1,0:T(8,128)(2,1)} %make_pack.1.refs_5_), channel_id=1, source_target_pairs={{0,4},{4,0},{1,5},{5,1},{2,6},{6,2},{3,7},{7,3},{8,12},{12,8},{9,1... | collective-permute-start | bytes 1204232 | tf_op jit(solution)/shard_map/ppermute | solution.py:693
  25.3 3.4 %collective-permute-start.6 = (bf16[128,256]{1,0:T(8,128)(2,1)S(1)}, bf16[128,256]{1,0:T(8,128)(2,1)S(1)}, u32[]{:S(2)}, u32[]{:S(2)}) collective-permute-start(bf16[128,256]{1,0:T(8,128)(2,1)S(1)} %copy-done.5), channel_id=1, source_target_pairs={{0,8},{8,0},{16,24},{24,16},{32,40},{40,32},{48,56},{56,48},{1,9},... | collective-permute-start | bytes 196616 | tf_op jit(solution)/shard_map/ppermute | solution.py:693
  33.6 14.5 %collective-permute-start.8 = (bf16[784,256]{1,0:T(8,128)(2,1)S(1)}, bf16[784,256]{1,0:T(8,128)(2,1)S(1)}, u32[]{:S(2)}, u32[]{:S(2)}) collective-permute-start(bf16[784,256]{1,0:T(8,128)(2,1)S(1)} %collective-permute-done.3.refs_6_), channel_id=1, source_target_pairs={{0,192},{64,0},{128,64},{192,128},{1,193},{65,1},{129,65},{193,129... | collective-permute-start | bytes 1204232 | tf_op jit(solution)/shard_map/ppermute | solution.py:698
  34.8 13.3 %collective-permute-start.7 = (bf16[784,256]{1,0:T(8,128)(2,1)S(1)}, bf16[784,256]{1,0:T(8,128)(2,1)S(1)}, u32[]{:S(2)}, u32[]{:S(2)}) collective-permute-start(bf16[784,256]{1,0:T(8,128)(2,1)S(1)} %collective-permute-done.3.refs_6_), channel_id=1, source_target_pairs={{0,64},{64,128},{128,192},{192,0},{1,65},{65,129},{129,193},{193,1... | collective-permute-start | bytes 1204232 | tf_op jit(solution)/shard_map/ppermute | solution.py:698
  35.1 33.7 %collective-permute-start.15 = (bf16[256,2048]{1,0:T(8,128)(2,1)S(1)}, bf16[256,2048]{1,0:T(8,128)(2,1)S(1)}, u32[]{:S(2)}, u32[]{:S(2)}) collective-permute-start(bf16[256,2048]{1,0:T(8,128)(2,1)S(1)} %copy-done.3), channel_id=1, source_target_pairs={{0,2},{1,3},{2,0},{3,1},{4,6},{5,7},{6,4},{7,5},{8,10},{9,11},{10,... | collective-permute-start | bytes 3145736 | tf_op jit(solution)/shard_map/ppermute | solution.py:693
  37.9 6.5 %collective-permute-start.10 = (bf16[256,256]{1,0:T(8,128)(2,1)S(1)}, bf16[256,256]{1,0:T(8,128)(2,1)S(1)}, u32[]{:S(2)}, u32[]{:S(2)}) collective-permute-start(bf16[256,256]{1,0:T(8,128)(2,1)S(1)} %join.2.refs_0_), channel_id=1, source_target_pairs={{0,48},{8,56},{16,0},{24,8},{32,16},{40,24},{48,32},{56,40},{1,49}... | collective-permute-start | bytes 393224 | tf_op jit(solution)/shard_map/ppermute | solution.py:698
  41.0 7.1 %collective-permute-start.9 = (bf16[256,256]{1,0:T(8,128)(2,1)S(1)}, bf16[256,256]{1,0:T(8,128)(2,1)S(1)}, u32[]{:S(2)}, u32[]{:S(2)}) collective-permute-start(bf16[256,256]{1,0:T(8,128)(2,1)S(1)} %join.2.refs_0_), channel_id=1, source_target_pairs={{0,16},{8,24},{16,32},{24,40},{32,48},{40,56},{48,0},{56,8},{1,17}... | collective-permute-start | bytes 393224 | tf_op jit(solution)/shard_map/ppermute | solution.py:698
  48.1 8.3 %collective-permute-start.13 = (bf16[784,256]{1,0:T(8,128)(2,1)S(1)}, bf16[784,256]{1,0:T(8,128)(2,1)S(1)}, u32[]{:S(2)}, u32[]{:S(2)}) collective-permute-start(bf16[784,256]{1,0:T(8,128)(2,1)S(1)} %collective-permute-done.4.refs_7_), channel_id=1, source_target_pairs={{0,64},{64,128},{128,192},{192,0},{1,65},{65,129},{129,193},{193,1... | collective-permute-start | bytes 1204232 | tf_op jit(solution)/shard_map/ppermute | solution.py:698
  48.1 8.3 %collective-permute-start.14 = (bf16[784,256]{1,0:T(8,128)(2,1)S(1)}, bf16[784,256]{1,0:T(8,128)(2,1)S(1)}, u32[]{:S(2)}, u32[]{:S(2)}) collective-permute-start(bf16[784,256]{1,0:T(8,128)(2,1)S(1)} %collective-permute-done.8.refs_10_), channel_id=1, source_target_pairs={{0,192},{64,0},{128,64},{192,128},{1,193},{65,1},{129,65},{193,129... | collective-permute-start | bytes 1204232 | tf_op jit(solution)/shard_map/ppermute | solution.py:698
  50.8 5.6 %collective-permute-start.11 = (bf16[128,256]{1,0:T(8,128)(2,1)S(1)}, bf16[128,256]{1,0:T(8,128)(2,1)S(1)}, u32[]{:S(2)}, u32[]{:S(2)}) collective-permute-start(bf16[128,256]{1,0:T(8,128)(2,1)S(1)} %get-tuple-element.48), channel_id=1, source_target_pairs={{0,16},{8,24},{16,32},{24,40},{32,48},{40,56},{48,0},{56,8},{1,17}... | collective-permute-start | bytes 196616 | tf_op jit(solution)/shard_map/ppermute | solution.py:698
  50.9 41.9 %copy-start.1 = (bf16[128,2048]{1,0:T(8,128)(2,1)S(1)}, bf16[128,2048]{1,0:T(8,128)(2,1)}, u32[]{:S(2)}) copy-start(bf16[128,2048]{1,0:T(8,128)(2,1)} %tok_hbm.3) | copy-start | bytes 1572868
  50.9 5.5 %collective-permute-start.12 = (bf16[128,256]{1,0:T(8,128)(2,1)S(1)}, bf16[128,256]{1,0:T(8,128)(2,1)S(1)}, u32[]{:S(2)}, u32[]{:S(2)}) collective-permute-start(bf16[128,256]{1,0:T(8,128)(2,1)S(1)} %get-tuple-element.49), channel_id=1, source_target_pairs={{0,48},{8,56},{16,0},{24,8},{32,16},{40,24},{48,32},{56,40},{1,49}... | collective-permute-start | bytes 196616 | tf_op jit(solution)/shard_map/ppermute | solution.py:698
  56.4 1.0 copy-start.4
  68.7 42.8 %copy-start = (bf16[2048,3,256]{2,0,1:T(8,128)(2,1)S(1)}, bf16[2048,3,256]{2,0,1:T(8,128)(2,1)}, u32[]{:S(2)}) copy-start(bf16[2048,3,256]{2,0,1:T(8,128)(2,1)} %param.17) | copy-start | bytes 9437188
  87.8 5.0 %collective-permute-start.16 = (bf16[128,256]{1,0:T(8,128)(2,1)S(1)}, bf16[128,256]{1,0:T(8,128)(2,1)S(1)}, u32[]{:S(2)}, u32[]{:S(2)}) collective-permute-start(bf16[128,256]{1,0:T(8,128)(2,1)S(1)} %merge.1.a_ref), channel_id=1, source_target_pairs={{0,2},{1,3},{2,0},{3,1},{4,6},{5,7},{6,4},{7,5},{8,10},{9,11},{10,... | collective-permute-start | bytes 196616 | tf_op jit(solution)/shard_map/ppermute | solution.py:693
  94.1 37.2 %copy-start.7 = (f32[2]{0:T(128)S(1)}, f32[2]{0:T(128)}, u32[]{:S(2)}) copy-start(f32[2]{0:T(128)} %slope_ref.3) | copy-start | bytes 28
  94.1 17.4 %collective-permute-start.17 = (bf16[128,2048]{1,0:T(8,128)(2,1)S(1)}, bf16[128,2048]{1,0:T(8,128)(2,1)S(1)}, u32[]{:S(2)}, u32[]{:S(2)}) collective-permute-start(bf16[128,2048]{1,0:T(8,128)(2,1)S(1)} %get-tuple-element.58), channel_id=1, source_target_pairs={{0,1},{1,0},{2,3},{3,2},{4,5},{5,4},{6,7},{7,6},{8,9},{9,8},{10,11... | collective-permute-start | bytes 1572872 | tf_op jit(solution)/shard_map/ppermute | solution.py:693
  104.0 5.2 %collective-permute-start.19 = (bf16[32,2048]{1,0:T(8,128)(2,1)S(1)}, bf16[32,2048]{1,0:T(8,128)(2,1)S(1)}, u32[]{:S(2)}, u32[]{:S(2)}) collective-permute-start(bf16[32,2048]{1,0:T(8,128)(2,1)S(1)} %get-tuple-element.59), channel_id=1, source_target_pairs={{0,5},{1,4},{2,7},{3,6},{4,9},{5,8},{6,11},{7,10},{8,13},{9,12},{1... | collective-permute-start | bytes 393224 | tf_op jit(solution)/shard_map/ppermute | solution.py:762
  106.1 5.4 %collective-permute-start.18 = (bf16[32,2048]{1,0:T(8,128)(2,1)S(1)}, bf16[32,2048]{1,0:T(8,128)(2,1)S(1)}, u32[]{:S(2)}, u32[]{:S(2)}) collective-permute-start(bf16[32,2048]{1,0:T(8,128)(2,1)S(1)} %get-tuple-element.59), channel_id=1, source_target_pairs={{0,4},{1,5},{2,6},{3,7},{4,8},{5,9},{6,10},{7,11},{8,12},{9,13},{1... | collective-permute-start | bytes 393224 | tf_op jit(solution)/shard_map/ppermute | solution.py:761
  111.6 35.9 %copy-start.2 = (bf16[256,2048]{1,0:T(8,128)(2,1)S(1)}, bf16[256,2048]{1,0:T(8,128)(2,1)}, u32[]{:S(2)}) copy-start(bf16[256,2048]{1,0:T(8,128)(2,1)} %w_ref.1) | copy-start | bytes 3145732
  113.5 3.5 %collective-permute-start.20 = (bf16[32,512]{1,0:T(8,128)(2,1)S(1)}, bf16[32,512]{1,0:T(8,128)(2,1)S(1)}, u32[]{:S(2)}, u32[]{:S(2)}) collective-permute-start(bf16[32,512]{1,0:T(8,128)(2,1)S(1)} %get-tuple-element.62.a_ref), channel_id=1, source_target_pairs={{0,4},{4,0},{1,5},{5,1},{2,6},{6,2},{3,7},{7,3},{8,12},{12,8},{9,1... | collective-permute-start | bytes 98312 | tf_op jit(solution)/shard_map/ppermute | solution.py:693
  117.0 14.3 %all-to-all-start.1 = ((bf16[8,32,256]{2,1,0:T(8,128)(2,1)}), bf16[8,32,256]{2,1,0:T(8,128)(2,1)S(1)}, u32[]{:S(2)}, u32[]{:S(2)}) async-start(bf16[8,32,256]{2,1,0:T(8,128)(2,1)} %get-tuple-element.63), calls=%async_computation.1 | async-start | bytes 262144 | tf_op jit(solution)/shard_map/all_to_all | solution.py:689
  122.0 5.6 %collective-permute-start.23 = (bf16[64,512]{1,0:T(8,128)(2,1)S(1)}, bf16[64,512]{1,0:T(8,128)(2,1)S(1)}, u32[]{:S(2)}, u32[]{:S(2)}) collective-permute-start(bf16[64,512]{1,0:T(8,128)(2,1)S(1)} %join.3.refs_0_), channel_id=1, source_target_pairs={{0,192},{64,0},{128,64},{192,128},{1,193},{65,1},{129,65},{193,129... | collective-permute-start | bytes 196616 | tf_op jit(solution)/shard_map/ppermute | solution.py:698
  126.3 4.7 %collective-permute-start.22 = (bf16[64,512]{1,0:T(8,128)(2,1)S(1)}, bf16[64,512]{1,0:T(8,128)(2,1)S(1)}, u32[]{:S(2)}, u32[]{:S(2)}) collective-permute-start(bf16[64,512]{1,0:T(8,128)(2,1)S(1)} %join.3.refs_0_), channel_id=1, source_target_pairs={{0,128},{64,192},{128,0},{192,64},{1,129},{65,193},{129,1},{193,65... | collective-permute-start | bytes 196616 | tf_op jit(solution)/shard_map/ppermute | solution.py:698
  126.3 5.0 %collective-permute-start.21 = (bf16[64,512]{1,0:T(8,128)(2,1)S(1)}, bf16[64,512]{1,0:T(8,128)(2,1)S(1)}, u32[]{:S(2)}, u32[]{:S(2)}) collective-permute-start(bf16[64,512]{1,0:T(8,128)(2,1)S(1)} %join.3.refs_0_), channel_id=1, source_target_pairs={{0,64},{64,128},{128,192},{192,0},{1,65},{65,129},{129,193},{193,1... | collective-permute-start | bytes 196616 | tf_op jit(solution)/shard_map/ppermute | solution.py:698
  148.0 8.4 %collective-permute-start.24 = (bf16[32,512]{1,0:T(8,128)(2,1)S(1)}, bf16[32,512]{1,0:T(8,128)(2,1)S(1)}, u32[]{:S(2)}, u32[]{:S(2)}) collective-permute-start(bf16[32,512]{1,0:T(8,128)(2,1)S(1)} %get-tuple-element.66), channel_id=1, source_target_pairs={{0,1},{1,0},{2,3},{3,2},{4,5},{5,4},{6,7},{7,6},{8,9},{9,8},{10,11... | collective-permute-start | bytes 98312 | tf_op jit(solution)/shard_map/ppermute | solution.py:693
  153.2 4.3 %collective-permute-start.25 = (bf16[32,512]{1,0:T(8,128)(2,1)S(1)}, bf16[32,512]{1,0:T(8,128)(2,1)S(1)}, u32[]{:S(2)}, u32[]{:S(2)}) collective-permute-start(bf16[32,512]{1,0:T(8,128)(2,1)S(1)} %get-tuple-element.67), channel_id=1, source_target_pairs={{0,2},{1,3},{2,0},{3,1},{4,6},{5,7},{6,4},{7,5},{8,10},{9,11},{10,... | collective-permute-start | bytes 98312 | tf_op jit(solution)/shard_map/ppermute | solution.py:693
  154.3 4.9 %collective-permute-start.26 = (bf16[32,512]{1,0:T(8,128)(2,1)S(1)}, bf16[32,512]{1,0:T(8,128)(2,1)S(1)}, u32[]{:S(2)}, u32[]{:S(2)}) collective-permute-start(bf16[32,512]{1,0:T(8,128)(2,1)S(1)} %get-tuple-element.68), channel_id=1, source_target_pairs={{0,3},{1,2},{2,1},{3,0},{4,7},{5,6},{6,5},{7,4},{8,11},{9,10},{10,... | collective-permute-start | bytes 98312 | tf_op jit(solution)/shard_map/ppermute | solution.py:693

commit v9 on v5

--- a/solution.py
+++ b/solution.py
@@ -102,22 +102,22 @@
 def table_kernel(count_ref, out_ref):
     y, z, xl = place_of_device()
     lane = lax.broadcasted_iota(jnp.int32, out_ref.shape, 1)
-    out_ref[...] = jnp.where(lane == y * 16 + z * 2 + xl, count_ref[0], 0).astype(F32)
-
-
-def own_count(count):
+    out_ref[...] = jnp.where(lane == y * 16 + z * 2 + xl, count_ref[0], 0).astype(F32).astype(BF16)
+
+
+def own_count(count, width):
     return pl.pallas_call(
         table_kernel,
         in_specs=[pl.BlockSpec(memory_space=SMEM)],
-        out_shape=jax.ShapeDtypeStruct((8, HS), F32),
+        out_shape=jax.ShapeDtypeStruct((16, width), BF16),
         compiler_params=params(8),
-        cost_estimate=cost(0, 4096),
+        cost_estimate=cost(0, 32 * width),
         name="own_count",
     )(count)
 
 
 def add_kernel(a_ref, b_ref, out_ref):
-    out_ref[...] = a_ref[...] + b_ref[...]
+    out_ref[...] = (a_ref[...].astype(F32) + b_ref[...].astype(F32)).astype(BF16)
 
 
 def added(a, b):
@@ -125,9 +125,45 @@
         add_kernel,
         out_shape=jax.ShapeDtypeStruct(a.shape, a.dtype),
         compiler_params=params(8),
-        cost_estimate=cost(a.size, 12 * a.size),
+        cost_estimate=cost(a.size, 6 * a.size),
         name="added",
     )(a, b)
+
+
+def mark_kernel(q_ref, a_ref, b_ref, out_ref):
+    rows = q_ref.shape[0]
+    out_ref[:rows] = q_ref[...]
+    out_ref[rows:] = (a_ref[...].astype(F32) + b_ref[...].astype(F32)).astype(BF16)
+
+
+def mark(q, a, b):
+    n, width = q.shape
+    return pl.pallas_call(
+        mark_kernel,
+        out_shape=jax.ShapeDtypeStruct((n + a.shape[0], width), BF16),
+        compiler_params=params(8),
+        cost_estimate=cost(0, 4 * n * width),
+        name="mark",
+    )(q, a, b)
+
+
+def plane_kernel(own, left, right, far, far_other, out_ref):
+    half, rows = far.shape[0], out_ref.shape[0]
+    total = far[half - rows :].astype(F32) + far_other[half - rows :].astype(F32)
+    for ref in (own, left, right):
+        for end in (half, 2 * half):
+            total = total + ref[end - rows : end].astype(F32)
+    out_ref[...] = total.astype(BF16)
+
+
+def plane_counts(queries):
+    return pl.pallas_call(
+        plane_kernel,
+        out_shape=jax.ShapeDtypeStruct((16, queries[0].shape[1]), BF16),
+        compiler_params=params(8),
+        cost_estimate=cost(0, 4096),
+        name="plane_counts",
+    )(*queries)
 
 
 def join_kernel(a_ref, b_ref, out_ref):
@@ -193,17 +229,21 @@
     return [s[:, at : at + HS] for s in pieces for at in range(0, s.shape[1], HS)]
 
 
-def attend_heads(qs, pieces, score, value):
+def attend_heads(qs, pieces, prior, score, value):
     heads = len(qs)
     pending = [score(0, qs[0], j) for j in range(pieces)]
     results = []
     for h in range(heads):
         top = jnp.max(functools.reduce(jnp.maximum, columns_of(pending)), axis=1, keepdims=True)
+        if prior is not None:
+            top = jnp.maximum(top, prior[h])
         following = []
         both = None
         for j in range(pieces):
             term = jnp.dot(
-                jnp.exp2(pending[j] - top).astype(BF16), value(h, j), preferred_element_type=F32
+                jnp.exp2((pending[j] - top).astype(BF16)),
+                value(h, j),
+                preferred_element_type=F32,
             )
             both = term if both is None else both + term
             if h + 1 < heads:
@@ -217,121 +257,179 @@
     return jnp.concatenate([v, jnp.ones_like(v)], axis=1)
 
 
-def attend_kernel(slots, slope_ref, *refs):
-    queries, tables, packs = refs[:5], refs[5:7], refs[7:15]
-    out_ref, q_tile, bias = refs[15:]
+def owner_of(back, other):
+    y, z, xl = place_of_device()
+    return (y + 4 - back) % 4, z, (1 - xl if other else xl)
+
+
+TILES = (((0, 0), (0, 1), (1, 0), (1, 1)), ((3, 0), (4, 0), (2, 0), (2, 1)))
+
+
+def fill_tile(q_tile, queries, tile):
+    rows = q_tile.shape[0] // 4
+    for b, (ref, half) in enumerate(TILES[tile]):
+        at = half * (queries[ref].shape[0] // 2)
+        q_tile[b * rows : (b + 1) * rows] = queries[ref][at : at + rows]
+
+
+def span_kernel(tile, slots, slope_ref, *refs):
+    queries, packs = refs[:5], refs[5:13]
+    acc_ref, stat_ref, q_tile, bias = refs[13:]
+    y, z, xl = place_of_device()
+    count, width = q_tile.shape
+    rows, heads = count // 4, width // HS
+    fill_tile(q_tile, queries, tile)
+    place = lax.broadcasted_iota(jnp.int32, (1, rows), 1)
+    for j, (back, other) in enumerate(RING):
+        yj, zj, side = owner_of(back, other)
+        spot = (place + (yj * 16 + zj * 2 + side) * rows).astype(F32)
+        for h in range(heads):
+            bias[h : h + 1, j * rows : (j + 1) * rows] = jnp.where(
+                yj <= y, slope_ref[h] * LOG2E * spot, NEG
+            )
+    row = lax.broadcasted_iota(jnp.int32, (count, 1), 0)
+    part = row // rows
+    row_z = ((z + 8 - 4 * tile - 2 * (part // 2)) % 8) ^ (part % 2)
+    row_pos = (y * 16 + xl + 2 * row_z) * rows + row % rows
+
+    def score(h, q, j):
+        cols = slice(h * HS, (h + 1) * HS)
+        s = dot_t(q, packs[j][2 * slots : 2 * slots + rows, cols])
+        s = s + bias[h : h + 1, j * rows : (j + 1) * rows]
+        back, other = RING[j]
+        if back == 0:
+            yj, zj, side = owner_of(back, other)
+            s = jnp.where(place + (yj * 16 + zj * 2 + side) * rows <= row_pos, s, NEG)
+        return s
+
+    def value(h, j):
+        return with_ones(packs[j][2 * slots + rows :, h * HS : (h + 1) * HS])
+
+    lane = lax.broadcasted_iota(jnp.int32, (count, HS), 1)
+    packed = jnp.zeros((count, HS), F32)
+    qs = [q_tile[:, h * HS : (h + 1) * HS] for h in range(heads)]
+    for h, (top, total, acc) in enumerate(attend_heads(qs, len(RING), None, score, value)):
+        acc_ref[:, h * HS : (h + 1) * HS] = acc
+        packed = jnp.where(lane == h, top, packed)
+        packed = jnp.where(lane == heads + h, total, packed)
+    stat_ref[...] = packed
+
+
+def span_attend(tile, slopes, queries, packs, slots):
+    width = queries[0].shape[1]
+    rows = packs[0].shape[0] // 2 - slots
+    count, nk = 4 * rows, len(RING) * rows
+    vmem = pl.BlockSpec(memory_space=VMEM)
+    return pl.pallas_call(
+        functools.partial(span_kernel, tile, slots),
+        in_specs=[pl.BlockSpec(memory_space=SMEM)] + [vmem] * 13,
+        out_specs=[vmem, vmem],
+        out_shape=[
+            jax.ShapeDtypeStruct((count, width), F32),
+            jax.ShapeDtypeStruct((count, HS), F32),
+        ],
+        scratch_shapes=[VMEM((count, width), BF16), VMEM((8, nk), F32)],
+        compiler_params=params(32),
+        cost_estimate=cost(4 * count * nk * width, 4 * nk * width, 2 * count * nk),
+        name="span_attend",
+    )(slopes, *queries, *packs)
+
+
+def cache_kernel(slots, slope_ref, *refs):
+    queries, packs, tables, states = refs[:5], refs[5:13], refs[13:15], refs[15:19]
+    out_ref, q_tile, acc_tile, stat_tile, bias = refs[19:]
     tile = pl.program_id(0)
     y, z, xl = place_of_device()
-    rows = q_tile.shape[0] // 2
-    width = q_tile.shape[1]
-    heads = width // HS
-    owners = len(RING)
-    cached = owners * slots
-
-    def side_of(other):
-        return 1 - xl if other else xl
-
-    own, left, right, far, far_other = queries
-    for t, (a, b, at) in enumerate(
-        ((own, own, rows), (left, left, rows), (far, far_other, 0), (right, right, rows))
-    ):
+    count, width = q_tile.shape
+    rows, heads = count // 4, width // HS
+    for t in range(2):
 
         @pl.when(tile == t)
-        def _(a=a, b=b, at=at):
-            q_tile[:rows] = a[:rows]
-            q_tile[rows:] = b[at : at + rows]
+        def _(t=t):
+            fill_tile(q_tile, queries, t)
+            acc_tile[...] = states[2 * t][...]
+            stat_tile[...] = states[2 * t + 1][...]
 
     @pl.when(tile == 0)
     def _():
-        table = (tables[0][...] + tables[1][...])[:1]
+        table = (tables[0][...].astype(F32) + tables[1][...].astype(F32))[:1]
         lane = lax.broadcasted_iota(jnp.int32, table.shape, 1)
         everything = jnp.sum(table, axis=1, keepdims=True)
         slot = lax.broadcasted_iota(jnp.int32, (1, slots), 1).astype(F32)
-        place = lax.broadcasted_iota(jnp.int32, (1, rows), 1)
         for j, (back, other) in enumerate(RING):
-            yj = (y + 4 - back) % 4
-            ctx = yj * 16 + z * 2 + side_of(other)
+            yj, zj, side = owner_of(back, other)
+            ctx = yj * 16 + zj * 2 + side
             live = jnp.sum(jnp.where(lane == ctx, table, 0.0), axis=1, keepdims=True)
             start = jnp.sum(jnp.where(lane < ctx, table, 0.0), axis=1, keepdims=True) - everything
-            spot = (place + ctx * rows).astype(F32)
             for h in range(heads):
-                slope = slope_ref[h] * LOG2E
                 bias[h : h + 1, j * slots : (j + 1) * slots] = jnp.where(
-                    slot < live, slope * (slot + start), NEG
+                    slot < live, slope_ref[h] * LOG2E * (slot + start), NEG
                 )
-                at = cached + j * rows
-                bias[h : h + 1, at : at + rows] = jnp.where(yj <= y, slope * spot, NEG)
-
-    row = lax.broadcasted_iota(jnp.int32, (2 * rows, 1), 0)
-    first = (z + 8 - 2 * tile) % 8
-    row_ctx = y * 16 + xl + 2 * jnp.where(row < rows, first, first ^ 1)
-    row_pos = row_ctx * rows + jnp.where(row < rows, row, row - rows)
-    place = lax.broadcasted_iota(jnp.int32, (1, rows), 1)
 
     def score(h, q, j):
-        cols = slice(h * HS, (h + 1) * HS)
-        if j < owners:
-            s = dot_t(q, packs[j][:slots, cols])
-            return s + bias[h : h + 1, j * slots : (j + 1) * slots]
-        back, other = RING[j - owners]
-        at = cached + (j - owners) * rows
-        s = dot_t(q, packs[j - owners][2 * slots : 2 * slots + rows, cols])
-        s = s + bias[h : h + 1, at : at + rows]
-        if back == 0:
-            first_key = (y * 16 + z * 2 + side_of(other)) * rows
-            s = jnp.where(place + first_key <= row_pos, s, NEG)
-        return s
+        s = dot_t(q, packs[j][:slots, h * HS : (h + 1) * HS])
+        return s + bias[h : h + 1, j * slots : (j + 1) * slots]
 
     def value(h, j):
-        cols = slice(h * HS, (h + 1) * HS)
-        if j < owners:
-            return with_ones(packs[j][slots : 2 * slots, cols])
-        return with_ones(packs[j - owners][2 * slots + rows : 2 * (slots + rows), cols])
-
-    lane = lax.broadcasted_iota(jnp.int32, (2 * rows, HS), 1)
-    packed = jnp.zeros((2 * rows, HS), F32)
+        return with_ones(packs[j][slots : 2 * slots, h * HS : (h + 1) * HS])
+
+    lane = lax.broadcasted_iota(jnp.int32, (count, HS), 1)
+    packed = jnp.zeros((count, HS), F32)
     qs = [q_tile[:, h * HS : (h + 1) * HS] for h in range(heads)]
+    prior = [stat_tile[:, h : h + 1] for h in range(heads)]
     done = []
-    for h, (top, total, acc) in enumerate(attend_heads(qs, 2 * owners, score, value)):
+    for h, (top, total, acc) in enumerate(attend_heads(qs, len(RING), prior, score, value)):
+        fade = jnp.exp2(prior[h] - top)
+        total = total + fade * stat_tile[:, heads + h : heads + h + 1]
+        acc = acc + fade * acc_tile[:, h * HS : (h + 1) * HS]
         done.append((acc / total).astype(BF16))
         for k, piece in enumerate(three_parts(top + jnp.log2(total))):
             packed = jnp.where(lane == 3 * h + k, piece, packed)
     both = jnp.concatenate(done, axis=1)
     odd = z % 2 == 1
-    blocks = []
-    for own, level in (
-        (jnp.where(odd, both[rows:], both[:rows]), jnp.where(odd, packed[rows:], packed[:rows])),
-        (jnp.where(odd, both[:rows], both[rows:]), jnp.where(odd, packed[:rows], packed[rows:])),
-    ):
-        turned = jnp.transpose(level)[:16]
-        tail = jnp.concatenate([turned, jnp.zeros_like(turned)], axis=1).astype(BF16)
-        blocks.append((own, tail))
-    for p in range(4):
-
-        @pl.when((z // 2 + 4 - tile) % 4 == p)
-        def _(p=p):
-            for b, (own, tail) in enumerate(blocks):
-                out_ref[2 * p + b, :rows] = own
-                out_ref[2 * p + b, rows:] = tail
-
-
-def attend(slopes, queries, tables, packs, slots):
-    rows, width = queries[0].shape[0] // 2, queries[0].shape[1]
-    nk = len(RING) * (slots + rows)
+    for pair in range(2):
+        a, b = 2 * pair * rows, (2 * pair + 1) * rows
+        end = b + rows
+        blocks = []
+        for own, level in (
+            (jnp.where(odd, both[b:end], both[a:b]), jnp.where(odd, packed[b:end], packed[a:b])),
+            (jnp.where(odd, both[a:b], both[b:end]), jnp.where(odd, packed[a:b], packed[b:end])),
+        ):
+            turned = jnp.transpose(level)[:16]
+            tail = jnp.concatenate([turned, jnp.zeros_like(turned)], axis=1).astype(BF16)
+            blocks.append((own, tail))
+        for p in range(4):
+
+            @pl.when((z // 2 + 4 - 2 * tile - pair) % 4 == p)
+            def _(p=p, blocks=blocks):
+                for i, (own, tail) in enumerate(blocks):
+                    out_ref[2 * p + i, :rows] = own
+                    out_ref[2 * p + i, rows:] = tail
+
+
+def cache_attend(slopes, queries, packs, tables, states, slots):
+    width = queries[0].shape[1]
+    rows = packs[0].shape[0] // 2 - slots
+    count, nk = 4 * rows, len(RING) * slots
     whole = lambda a: pl.BlockSpec(a.shape, lambda i: (0,) * a.ndim)
+    operands = (*queries, *packs, *tables, *states)
     out = jax.ShapeDtypeStruct((8, rows + 16, width), BF16)
     return pl.pallas_call(
-        functools.partial(attend_kernel, slots),
-        grid=(4,),
-        in_specs=[pl.BlockSpec(memory_space=SMEM)]
-        + [whole(a) for a in (*queries, *tables, *packs)],
+        functools.partial(cache_kernel, slots),
+        grid=(2,),
+        in_specs=[pl.BlockSpec(memory_space=SMEM)] + [whole(a) for a in operands],
         out_specs=whole(out),
         out_shape=out,
-        scratch_shapes=[VMEM((2 * rows, width), BF16), VMEM((8, nk), F32)],
-        compiler_params=params(40),
-        cost_estimate=cost(32 * rows * nk * width, 4 * nk * width, 16 * rows * nk),
-        name="attend",
-    )(slopes, *queries, *tables, *packs)
+        scratch_shapes=[
+            VMEM((count, width), BF16),
+            VMEM((count, width), F32),
+            VMEM((count, HS), F32),
+            VMEM((8, nk), F32),
+        ],
+        compiler_params=params(44),
+        cost_estimate=cost(8 * count * nk * width, 4 * nk * width, 4 * count * nk),
+        name="cache_attend",
+    )(slopes, *operands)
 
 
 def merge_kernel(heads, parts_ref, out_ref):
@@ -642,12 +740,6 @@
     return moved(x, axis, by), moved(x, axis, -by)
 
 
-def counts_along(table, axis, *flips):
-    for flip in flips:
-        table = added(table, swap(table, axis, flip))
-    return table
-
-
 def after(x, *others):
     return lax.optimization_barrier((x, *others))[0]
 
@@ -666,31 +758,41 @@
 ):
     axes = ("y", "z", "xl", "tp")
     slots = cache_keys.shape[0]
+    nz = lax.axis_size("z")
+    count = own_count(cache_count, cache_keys.shape[1])
+    other_count = swap(count, "xl")
     q, pack = project(
         tokens, jnp.transpose(project_weight, (1, 0, 2)), cache_keys, cache_values
     )
-    table = counts_along(own_count(cache_count), "xl", 1)
-    q, pack, table = lax.optimization_barrier((q, pack, table))
-    table = counts_along(table, "z", 1)
+    q, pack, other_count = lax.optimization_barrier((q, pack, other_count))
+    marked = mark(q, count, other_count)
     left, right = both_ways(pack, "y", 1)
-    other, left, right, mate, table = lax.optimization_barrier(
-        (swap(pack, "xl"), left, right, swap(q, "z"), table)
+    other, left, right, mate = lax.optimization_barrier(
+        (swap(pack, "xl"), left, right, swap(marked, "z"))
     )
-    pair = join(q, mate)
+    pair = join(marked, mate)
     left_other, right_other = both_ways(other, "y", 1)
     left_pair, right_pair = both_ways(pair, "z", 2)
-    table = counts_along(table, "z", 2, 4)
-    left_other, right_other, left_pair, right_pair, left, table = lax.optimization_barrier(
-        (left_other, right_other, left_pair, right_pair, left, table)
+    left_other, right_other, left_pair, right_pair, left = lax.optimization_barrier(
+        (left_other, right_other, left_pair, right_pair, left)
     )
-    table = counts_along(table, "y", 1)
-    tables = [table, swap(table, "y", 2)]
     far, far_other = moved(left, "y", 1), moved(right_other, "y", -1)
     near = halves(left_pair, right_pair)
     queries = [pair, left_pair, right_pair, moved(near[0], "z", 2), moved(near[1], "z", -2)]
-    crossed = swap(after(output_weight, far), "tp", 2)
+    crossed = swap(after(output_weight, other), "tp", 2)
     packs = [pack, other, left, left_other, right, right_other, far, far_other]
-    parts = attend(distance_slope, queries, tables, packs, slots)
+    plane = plane_counts(queries)
+    beside = swap(plane, "y")
+    first = span_attend(0, distance_slope, queries, packs, slots)
+    plane, beside, first = lax.optimization_barrier((plane, beside, first))
+    line = added(plane, beside)
+    beyond = swap(line, "y", 2)
+    second = span_attend(1, distance_slope, queries, packs, slots)
+    second, beyond = lax.optimization_barrier((second, beyond))
+    parts = cache_attend(
+        distance_slope, queries, packs, (line, beyond), (*first, *second), slots
+    )
+    parts, crossed = lax.optimization_barrier((parts, crossed))
 
     att = merge(exchange(parts, "z"))
     total, term, rim = layer_product(
@@ -707,9 +809,11 @@
         swap(term, "tp", 1),
         rims,
         jnp.transpose(short_project_weight, (1, 0, 2)),
-        lax.axis_size("z"),
+        nz,
     )
-    pair = join(skv, swap(skv, "xl"))
+    mate = swap(skv, "xl")
+    sq, mate = lax.optimization_barrier((sq, mate))
+    pair = join(skv, mate)
     keys = [pair] + [moved(pair, "y", by) for by in (1, 2, 3)]
     sparts = short_attend(short_slope, exchange(sq, "z"), keys)
     terms = short_merge(exchange(sparts, "z"), short_output)

time: 166 us -> 155 us (0.934)
  blocking collectives: 15.1 us -> 32.6 us
  waiting for transfers between devices: 47.7 us -> 32.6 us
  starting transfers between devices: 71.1 us -> 62 us
  local copies, waits for them, and re-layouts: 6.13 us -> 1.86 us
    all_to_all x1 -> x2, blocking collectives: 15.1 us -> 32.6 us  [exchange(): return lax.all_to_all(blocks, axis, 0, 0)]
    ppermute x15 -> x12, waiting for transfers between devices: 24.6 us -> 10.6 us  [swap(): lax.ppermute(x, axis, [(i, i ^ flip) for i in range(lax.axis_size(axis))])]
    all_to_all x2 -> x1, waiting for transfers between devices: 10.5 us -> 0.01 us  [exchange(): return lax.all_to_all(blocks, axis, 0, 0)]
    all_to_all x2 -> x1, starting transfers between devices: 14.6 us -> 4.88 us  [exchange(): return lax.all_to_all(blocks, axis, 0, 0)]
    ppermute x13, waiting for transfers between devices: 10.3 us -> 19.9 us  [moved(): return lax.ppermute(x, axis, [(i, (i + by) % n) for i in range(n)])]
    unnamed x18, local copies, waits for them, and re-layouts: 6.13 us -> 1.86 us
    ppermute x13, starting transfers between devices: 19 us -> 22.4 us  [moved(): return lax.ppermute(x, axis, [(i, (i + by) % n) for i in range(n)])]
    ppermute x15 -> x12, starting transfers between devices: 32.6 us -> 29.3 us  [swap(): lax.ppermute(x, axis, [(i, i ^ flip) for i in range(lax.axis_size(axis))])]
  transfers between devices with their start and end apart: 32 -> 28, of which waited for: 17 -> 13; matrix products, arithmetic and copies ran while one was open for 0% -> 0% of each run, Pallas kernels for 3% -> 12%
where the time goes in v9:
time: 155 us
  starting transfers between devices  62 us (40%)
  waiting for transfers between devices  32.6 us (21%)
  blocking collectives  32.6 us (21%)
  Pallas kernels  24.9 us (16%)
  local copies, waits for them, and re-layouts  1.86 us (1%)
    all_to_all x2, blocking collectives, exchange(): return lax.all_to_all(blocks, axis, 0, 0)  32.6 us
    ppermute x12, starting transfers between devices, swap(): lax.ppermute(x, axis, [(i, i ^ flip) for i in range(lax.axis_size(axis))])  29.3 us
    ppermute x13, starting transfers between devices, moved(): return lax.ppermute(x, axis, [(i, (i + by) % n) for i in range(n)])  22.4 us
    ppermute x13, waiting for transfers between devices, moved(): return lax.ppermute(x, axis, [(i, (i + by) % n) for i in range(n)])  19.9 us
    ppermute x12, waiting for transfers between devices, swap(): lax.ppermute(x, axis, [(i, i ^ flip) for i in range(lax.axis_size(axis))])  10.6 us
    pallas_call x1, Pallas kernels, cache_attend(): pl.pallas_call(functools.partial(cache_kernel, slots), grid=(2,), in_spec...  9 us
    pallas_call x2, Pallas kernels, span_attend(): pl.pallas_call(functools.partial(span_kernel, tile, slots), in_specs=[pl....  5.48 us
    all_to_all x1, starting transfers between devices, exchange(): return lax.all_to_all(blocks, axis, 0, 0)  4.88 us
  transfers between devices with their start and end apart: 28, of which 13 were waited for; matrix products, arithmetic and copies ran while one was open for 0% of the time, Pallas kernels for 12%

profile of v9, /device:TPU:1, one launch (start us, length us, event | category | flops | bytes accessed | tf_op | source)
XLA Modules:
  0.0 155.0 jit_solution(17758007416935550224)
XLA Ops:
  0.8 2.1 %collective-permute-start = (bf16[16,256]{1,0:T(8,128)(2,1)S(1)}, bf16[16,256]{1,0:T(8,128)(2,1)S(1)}, u32[]{:S(2)}, u32[]{:S(2)}) collective-permute-start(bf16[16,256]{1,0:T(8,128)(2,1)S(1)} %own_count.1.a_ref), channel_id=1, source_target_pairs={{0,4},{4,0},{1,5},{5,1},{2,6},{6,2},{3,7},{7,3},{8,12},{12,8},{9,1... | collective-permute-start | bytes 24584 | tf_op jit(solution)/shard_map/ppermute | solution.py:731
  2.9 3.4 %project.1 = (bf16[128,256]{1,0:T(8,128)(2,1)}, bf16[768,256]{1,0:T(8,128)(2,1)}) custom-call(bf16[128,2048]{1,0:T(8,128)(2,1)} %tok_hbm.3, bf16[3,2048,256]{2,1,0:T(8,128)(2,1)} %bitcast.3, bf16[256,256]{1,0:T(8,128)(2,1)} %ck_hbm.1, bf16[256,256]{1,0:T(8,128)(2,1)} %cv_hbm.1), custom_call_target="tpu_custom_call" | custom-call | flops 402653184 | bytes 3670016 | tf_op jit(solution)/shard_map/project/pallas_call | solution.py:83
  6.3 2.8 %collective-permute-start.3 = (bf16[768,256]{1,0:T(8,128)(2,1)}, bf16[768,256]{1,0:T(8,128)(2,1)S(1)}, u32[]{:S(2)}, u32[]{:S(2)}) collective-permute-start(bf16[768,256]{1,0:T(8,128)(2,1)} %get-tuple-element.51.refs_5_), channel_id=1, source_target_pairs={{0,192},{64,0},{128,64},{192,128},{1,193},{65,1},{129,65},{193,129... | collective-permute-start | bytes 1179656 | tf_op jit(solution)/shard_map/ppermute | solution.py:736
  9.4 0.8 copy-done.6
  10.2 1.7 %collective-permute-start.4 = (bf16[144,256]{1,0:T(8,128)(2,1)S(1)}, bf16[144,256]{1,0:T(8,128)(2,1)S(1)}, u32[]{:S(2)}, u32[]{:S(2)}) collective-permute-start(bf16[144,256]{1,0:T(8,128)(2,1)S(1)} %mark.1.a_ref), channel_id=1, source_target_pairs={{0,8},{8,0},{16,24},{24,16},{32,40},{40,32},{48,56},{56,48},{1,9},... | collective-permute-start | bytes 221192 | tf_op jit(solution)/shard_map/ppermute | solution.py:731
  11.9 2.0 %collective-permute-done.4.b_ref = bf16[144,256]{1,0:T(8,128)(2,1)S(1)} collective-permute-done((bf16[144,256]{1,0:T(8,128)(2,1)S(1)}, bf16[144,256]{1,0:T(8,128)(2,1)S(1)}, u32[]{:S(2)}, u32[]{:S(2)}) %collective-permute-start.4) | collective-permute-done | bytes 73760 | tf_op jit(solution)/shard_map/ppermute | solution.py:731
  14.0 2.9 %collective-permute-done.3.refs_9_ = bf16[768,256]{1,0:T(8,128)(2,1)S(1)} collective-permute-done((bf16[768,256]{1,0:T(8,128)(2,1)}, bf16[768,256]{1,0:T(8,128)(2,1)S(1)}, u32[]{:S(2)}, u32[]{:S(2)}) %collective-permute-start.3) | collective-permute-done | bytes 393248 | tf_op jit(solution)/shard_map/ppermute | solution.py:736
  16.9 3.0 %collective-permute-done.2.refs_7_ = bf16[768,256]{1,0:T(8,128)(2,1)S(1)} collective-permute-done((bf16[768,256]{1,0:T(8,128)(2,1)}, bf16[768,256]{1,0:T(8,128)(2,1)S(1)}, u32[]{:S(2)}, u32[]{:S(2)}) %collective-permute-start.2) | collective-permute-done | bytes 393248 | tf_op jit(solution)/shard_map/ppermute | solution.py:736
  19.9 1.2 collective-permute-start.6
  21.1 0.3 collective-permute-start.5
  21.4 2.5 %collective-permute-start.15 = (bf16[256,2048]{1,0:T(8,128)(2,1)S(1)}, bf16[256,2048]{1,0:T(8,128)(2,1)S(1)}, u32[]{:S(2)}, u32[]{:S(2)}) collective-permute-start(bf16[256,2048]{1,0:T(8,128)(2,1)S(1)} %copy-done.5), channel_id=1, source_target_pairs={{0,2},{1,3},{2,0},{3,1},{4,6},{5,7},{6,4},{7,5},{8,10},{9,11},{10,... | collective-permute-start | bytes 3145736 | tf_op jit(solution)/shard_map/ppermute | solution.py:731
  23.8 6.1 %collective-permute-start.8 = (bf16[288,256]{1,0:T(8,128)(2,1)S(1)}, bf16[288,256]{1,0:T(8,128)(2,1)S(1)}, u32[]{:S(2)}, u32[]{:S(2)}) collective-permute-start(bf16[288,256]{1,0:T(8,128)(2,1)S(1)} %join.2.own.refs_0_), channel_id=1, source_target_pairs={{0,48},{8,56},{16,0},{24,8},{32,16},{40,24},{48,32},{56,40},{1,49}... | collective-permute-start | bytes 442376 | tf_op jit(solution)/shard_map/ppermute | solution.py:736
  29.9 2.2 %collective-permute-done.8.right_ref.right.refs_2_ = bf16[288,256]{1,0:T(8,128)(2,1)S(1)} collective-permute-done((bf16[288,256]{1,0:T(8,128)(2,1)S(1)}, bf16[288,256]{1,0:T(8,128)(2,1)S(1)}, u32[]{:S(2)}, u32[]{:S(2)}) %collective-permute-start.8) | collective-permute-done | bytes 147488 | tf_op jit(solution)/shard_map/ppermute | solution.py:736
  32.1 5.2 %collective-permute-done.7.left_ref.left.refs_1_ = bf16[288,256]{1,0:T(8,128)(2,1)S(1)} collective-permute-done((bf16[288,256]{1,0:T(8,128)(2,1)S(1)}, bf16[288,256]{1,0:T(8,128)(2,1)S(1)}, u32[]{:S(2)}, u32[]{:S(2)}) %collective-permute-start.7) | collective-permute-done | bytes 147488 | tf_op jit(solution)/shard_map/ppermute | solution.py:736
  37.4 2.7 %collective-permute-start.12 = (bf16[768,256]{1,0:T(8,128)(2,1)S(1)}, bf16[768,256]{1,0:T(8,128)(2,1)S(1)}, u32[]{:S(2)}, u32[]{:S(2)}) collective-permute-start(bf16[768,256]{1,0:T(8,128)(2,1)S(1)} %collective-permute-done.6.refs_10_), channel_id=1, source_target_pairs={{0,192},{64,0},{128,64},{192,128},{1,193},{65,1},{129,65},{193,129... | collective-permute-start | bytes 1179656 | tf_op jit(solution)/shard_map/ppermute | solution.py:736
  40.1 3.6 %collective-permute-start.10 = (bf16[144,256]{1,0:T(8,128)(2,1)S(1)}, bf16[144,256]{1,0:T(8,128)(2,1)S(1)}, u32[]{:S(2)}, u32[]{:S(2)}) collective-permute-start(bf16[144,256]{1,0:T(8,128)(2,1)S(1)} %get-tuple-element.58), channel_id=1, source_target_pairs={{0,48},{8,56},{16,0},{24,8},{32,16},{40,24},{48,32},{56,40},{1,49}... | collective-permute-start | bytes 221192 | tf_op jit(solution)/shard_map/ppermute | solution.py:736
  43.7 2.2 %collective-permute-done.9.far.refs_3_ = bf16[144,256]{1,0:T(8,128)(2,1)S(1)} collective-permute-done((bf16[144,256]{1,0:T(8,128)(2,1)S(1)}, bf16[144,256]{1,0:T(8,128)(2,1)S(1)}, u32[]{:S(2)}, u32[]{:S(2)}) %collective-permute-start.9) | collective-permute-done | bytes 73760 | tf_op jit(solution)/shard_map/ppermute | solution.py:736
  45.9 0.3 collective-permute-start.13
  46.2 1.0 copy-done.2
  47.2 2.7 %span_attend.2 = (f32[512,256]{1,0:T(8,128)S(1)}, f32[512,128]{1,0:T(8,128)S(1)}) custom-call(f32[2]{0:T(128)S(1)} %copy-done.7, bf16[288,256]{1,0:T(8,128)(2,1)S(1)} %join.2.own.refs_0_, bf16[288,256]{1,0:T(8,128)(2,1)S(1)} %collective-permute-done.7.left_ref.left.refs_1_, bf16[288,256]{1,0:T(8,128)(2,1)S(1)} %collective-permute-done.8.right_ref.right.refs_2_, ...), custom_call_target="tpu_custom_call" | custom-call | flops 536870912 | bytes 1048576 | tf_op jit(solution)/shard_map/span_attend/pallas_call | solution.py:323
  50.0 2.3 %collective-permute-start.14 = (bf16[16,256]{1,0:T(8,128)(2,1)S(1)}, bf16[16,256]{1,0:T(8,128)(2,1)S(1)}, u32[]{:S(2)}, u32[]{:S(2)}) collective-permute-start(bf16[16,256]{1,0:T(8,128)(2,1)S(1)} %added.1.refs_13_), channel_id=1, source_target_pairs={{0,128},{64,192},{128,0},{192,64},{1,129},{65,193},{129,1},{193,65... | collective-permute-start | bytes 24584 | tf_op jit(solution)/shard_map/ppermute | solution.py:731
  52.3 2.7 %span_attend.3 = (f32[512,256]{1,0:T(8,128)S(1)}, f32[512,128]{1,0:T(8,128)S(1)}) custom-call(f32[2]{0:T(128)S(1)} %copy-done.7, bf16[288,256]{1,0:T(8,128)(2,1)S(1)} %join.2.own.refs_0_, bf16[288,256]{1,0:T(8,128)(2,1)S(1)} %collective-permute-done.7.left_ref.left.refs_1_, bf16[288,256]{1,0:T(8,128)(2,1)S(1)} %collective-permute-done.8.right_ref.right.refs_2_, ...), custom_call_target="tpu_custom_call" | custom-call | flops 536870912 | bytes 1048576 | tf_op jit(solution)/shard_map/span_attend/pallas_call | solution.py:323
  55.0 9.0 %cache_attend.1 = bf16[8,144,256]{2,1,0:T(8,128)(2,1)S(1)} custom-call(f32[2]{0:T(128)S(1)} %copy-done.7, bf16[288,256]{1,0:T(8,128)(2,1)S(1)} %join.2.own.refs_0_, bf16[288,256]{1,0:T(8,128)(2,1)S(1)} %collective-permute-done.7.left_ref.left.refs_1_, bf16[288,256]{1,0:T(8,128)(2,1)S(1)} %collective-permute-done.8.right_ref.right.refs_2_, ...), custom_call_target="tpu_custom_call" | custom-call | flops 2147483648 | bytes 2097152 | tf_op jit(solution)/shard_map/cache_attend/pallas_call | solution.py:417
  64.1 17.9 %all_to_all.15.parts_ref = bf16[8,144,256]{2,1,0:T(8,128)(2,1)S(1)} all-to-all(bf16[8,144,256]{2,1,0:T(8,128)(2,1)S(1)} %cache_attend.1), channel_id=1, replica_groups=mesh['y'=4,'z'=8,'xl'=2,'tp'=4] {'z'}, dimensions={0} | all-to-all | bytes 1179648 | tf_op jit(solution)/shard_map/all_to_all | solution.py:727
  82.0 1.2 merge.1.a_ref
  83.3 4.9 %collective-permute-done.16.b_ref = bf16[128,256]{1,0:T(8,128)(2,1)S(1)} collective-permute-done((bf16[128,256]{1,0:T(8,128)(2,1)S(1)}, bf16[128,256]{1,0:T(8,128)(2,1)S(1)}, u32[]{:S(2)}, u32[]{:S(2)}) %collective-permute-start.16) | collective-permute-done | bytes 65568 | tf_op jit(solution)/shard_map/ppermute | solution.py:731
  88.2 1.3 layer_product.1
  89.6 8.9 %collective-permute-start.17 = (bf16[128,2048]{1,0:T(8,128)(2,1)S(1)}, bf16[128,2048]{1,0:T(8,128)(2,1)S(1)}, u32[]{:S(2)}, u32[]{:S(2)}) collective-permute-start(bf16[128,2048]{1,0:T(8,128)(2,1)S(1)} %get-tuple-element.78), channel_id=1, source_target_pairs={{0,1},{1,0},{2,3},{3,2},{4,5},{5,4},{6,7},{7,6},{8,9},{9,8},{10,11... | collective-permute-start | bytes 1572872 | tf_op jit(solution)/shard_map/ppermute | solution.py:731
  98.5 1.8 %collective-permute-start.19 = (bf16[32,2048]{1,0:T(8,128)(2,1)S(1)}, bf16[32,2048]{1,0:T(8,128)(2,1)S(1)}, u32[]{:S(2)}, u32[]{:S(2)}) collective-permute-start(bf16[32,2048]{1,0:T(8,128)(2,1)S(1)} %get-tuple-element.79), channel_id=1, source_target_pairs={{0,5},{1,4},{2,7},{3,6},{4,9},{5,8},{6,11},{7,10},{8,13},{9,12},{1... | collective-permute-start | bytes 393224 | tf_op jit(solution)/shard_map/ppermute | solution.py:805
  100.2 3.7 %collective-permute-start.18 = (bf16[32,2048]{1,0:T(8,128)(2,1)S(1)}, bf16[32,2048]{1,0:T(8,128)(2,1)S(1)}, u32[]{:S(2)}, u32[]{:S(2)}) collective-permute-start(bf16[32,2048]{1,0:T(8,128)(2,1)S(1)} %get-tuple-element.79), channel_id=1, source_target_pairs={{0,4},{1,5},{2,6},{3,7},{4,8},{5,9},{6,10},{7,11},{8,12},{9,13},{1... | collective-permute-start | bytes 393224 | tf_op jit(solution)/shard_map/ppermute | solution.py:804
  103.9 2.1 %collective-permute-done.18.rim_a = bf16[32,2048]{1,0:T(8,128)(2,1)S(1)} collective-permute-done((bf16[32,2048]{1,0:T(8,128)(2,1)S(1)}, bf16[32,2048]{1,0:T(8,128)(2,1)S(1)}, u32[]{:S(2)}, u32[]{:S(2)}) %collective-permute-start.18) | collective-permute-done | bytes 131104 | tf_op jit(solution)/shard_map/ppermute | solution.py:804
  106.0 2.0 %short_project.1 = (bf16[128,512]{1,0:T(8,128)(2,1)S(1)}, bf16[8,32,256]{2,1,0:T(8,128)(2,1)}, bf16[32,512]{1,0:T(8,128)(2,1)S(1)}) custom-call(f32[128,2048]{1,0:T(8,128)S(1)} %get-tuple-element.77.sum_ref, bf16[128,2048]{1,0:T(8,128)(2,1)S(1)} %collective-permute-done.17.term_ref, bf16[32,2048]{1,0:T(8,128)(2,1)S(1)} %collective-permute-done.18.rim_a, ...), custom_call_target="tpu_custom_call" | custom-call | flops 100663296 | bytes 3670016 | tf_op jit(solution)/shard_map/short_project/pallas_call | solution.py:583
  108.0 2.2 %collective-permute-start.20 = (bf16[32,512]{1,0:T(8,128)(2,1)S(1)}, bf16[32,512]{1,0:T(8,128)(2,1)S(1)}, u32[]{:S(2)}, u32[]{:S(2)}) collective-permute-start(bf16[32,512]{1,0:T(8,128)(2,1)S(1)} %get-tuple-element.82.a_ref), channel_id=1, source_target_pairs={{0,4},{4,0},{1,5},{5,1},{2,6},{6,2},{3,7},{7,3},{8,12},{12,8},{9,1... | collective-permute-start | bytes 98312 | tf_op jit(solution)/shard_map/ppermute | solution.py:731
  110.2 1.3 collective-permute-done.20.b_ref
  111.5 4.9 %all-to-all-start.1 = ((bf16[8,32,256]{2,1,0:T(8,128)(2,1)}), bf16[8,32,256]{2,1,0:T(8,128)(2,1)S(1)}, u32[]{:S(2)}, u32[]{:S(2)}) async-start(bf16[8,32,256]{2,1,0:T(8,128)(2,1)} %get-tuple-element.83), calls=%async_computation.1 | async-start | bytes 262144 | tf_op jit(solution)/shard_map/all_to_all | solution.py:727
  116.4 4.0 %collective-permute-start.23 = (bf16[64,512]{1,0:T(8,128)(2,1)S(1)}, bf16[64,512]{1,0:T(8,128)(2,1)S(1)}, u32[]{:S(2)}, u32[]{:S(2)}) collective-permute-start(bf16[64,512]{1,0:T(8,128)(2,1)S(1)} %join.3.refs_0_), channel_id=1, source_target_pairs={{0,192},{64,0},{128,64},{192,128},{1,193},{65,1},{129,65},{193,129... | collective-permute-start | bytes 196616 | tf_op jit(solution)/shard_map/ppermute | solution.py:736
  120.4 1.5 collective-permute-start.22
  122.1 3.2 %collective-permute-done.22.refs_2_ = bf16[64,512]{1,0:T(8,128)(2,1)S(1)} collective-permute-done((bf16[64,512]{1,0:T(8,128)(2,1)S(1)}, bf16[64,512]{1,0:T(8,128)(2,1)S(1)}, u32[]{:S(2)}, u32[]{:S(2)}) %collective-permute-start.22) | collective-permute-done | bytes 65568 | tf_op jit(solution)/shard_map/ppermute | solution.py:736
  125.3 1.2 collective-permute-done.21.refs_1_
  126.5 1.0 short_attend.1
  127.6 14.7 %all_to_all.16.parts_ref = bf16[8,32,384]{2,1,0:T(8,128)(2,1)S(1)} all-to-all(bf16[8,32,384]{2,1,0:T(8,128)(2,1)S(1)} %short_attend.1), channel_id=1, replica_groups=mesh['y'=4,'z'=8,'xl'=2,'tp'=4] {'z'}, dimensions={0} | all-to-all | bytes 393216 | tf_op jit(solution)/shard_map/all_to_all | solution.py:727
  142.3 0.5 short_merge.1
  142.8 5.7 %collective-permute-start.24 = (bf16[32,512]{1,0:T(8,128)(2,1)S(1)}, bf16[32,512]{1,0:T(8,128)(2,1)S(1)}, u32[]{:S(2)}, u32[]{:S(2)}) collective-permute-start(bf16[32,512]{1,0:T(8,128)(2,1)S(1)} %get-tuple-element.86), channel_id=1, source_target_pairs={{0,1},{1,0},{2,3},{3,2},{4,5},{5,4},{6,7},{7,6},{8,9},{9,8},{10,11... | collective-permute-start | bytes 98312 | tf_op jit(solution)/shard_map/ppermute | solution.py:731
  148.4 0.5 collective-permute-start.25
  149.0 2.7 %collective-permute-start.26 = (bf16[32,512]{1,0:T(8,128)(2,1)S(1)}, bf16[32,512]{1,0:T(8,128)(2,1)S(1)}, u32[]{:S(2)}, u32[]{:S(2)}) collective-permute-start(bf16[32,512]{1,0:T(8,128)(2,1)S(1)} %get-tuple-element.88), channel_id=1, source_target_pairs={{0,3},{1,2},{2,1},{3,0},{4,7},{5,6},{6,5},{7,4},{8,11},{9,10},{10,... | collective-permute-start | bytes 98312 | tf_op jit(solution)/shard_map/ppermute | solution.py:731
  151.7 1.0 collective-permute-done.25.refs_2_
  152.7 1.3 collective-permute-done.26.refs_3_
  154.1 0.9 final_sum.1
  (45 shorter events, 0.8 us)
Async XLA Ops:
  0.0 21.4 %copy-start.5 = (bf16[256,2048]{1,0:T(8,128)(2,1)S(1)}, bf16[256,2048]{1,0:T(8,128)(2,1)}, u32[]{:S(2)}) copy-start(bf16[256,2048]{1,0:T(8,128)(2,1)} %wa_hbm.1) | copy-start | bytes 3145732
  0.0 46.2 %copy-start.7 = (f32[2]{0:T(128)S(1)}, f32[2]{0:T(128)}, u32[]{:S(2)}) copy-start(f32[2]{0:T(128)} %slope_ref.6) | copy-start | bytes 28
  0.8 5.5 %collective-permute-start = (bf16[16,256]{1,0:T(8,128)(2,1)S(1)}, bf16[16,256]{1,0:T(8,128)(2,1)S(1)}, u32[]{:S(2)}, u32[]{:S(2)}) collective-permute-start(bf16[16,256]{1,0:T(8,128)(2,1)S(1)} %own_count.1.a_ref), channel_id=1, source_target_pairs={{0,4},{4,0},{1,5},{5,1},{2,6},{6,2},{3,7},{7,3},{8,12},{12,8},{9,1... | collective-permute-start | bytes 24584 | tf_op jit(solution)/shard_map/ppermute | solution.py:731
  6.3 10.6 %collective-permute-start.3 = (bf16[768,256]{1,0:T(8,128)(2,1)}, bf16[768,256]{1,0:T(8,128)(2,1)S(1)}, u32[]{:S(2)}, u32[]{:S(2)}) collective-permute-start(bf16[768,256]{1,0:T(8,128)(2,1)} %get-tuple-element.51.refs_5_), channel_id=1, source_target_pairs={{0,192},{64,0},{128,64},{192,128},{1,193},{65,1},{129,65},{193,129... | collective-permute-start | bytes 1179656 | tf_op jit(solution)/shard_map/ppermute | solution.py:736
  9.1 10.8 %collective-permute-start.2 = (bf16[768,256]{1,0:T(8,128)(2,1)}, bf16[768,256]{1,0:T(8,128)(2,1)S(1)}, u32[]{:S(2)}, u32[]{:S(2)}) collective-permute-start(bf16[768,256]{1,0:T(8,128)(2,1)} %get-tuple-element.51.refs_5_), channel_id=1, source_target_pairs={{0,64},{64,128},{128,192},{192,0},{1,65},{65,129},{129,193},{193,1... | collective-permute-start | bytes 1179656 | tf_op jit(solution)/shard_map/ppermute | solution.py:736
  9.1 10.8 %collective-permute-start.1 = (bf16[768,256]{1,0:T(8,128)(2,1)}, bf16[768,256]{1,0:T(8,128)(2,1)S(1)}, u32[]{:S(2)}, u32[]{:S(2)}) collective-permute-start(bf16[768,256]{1,0:T(8,128)(2,1)} %get-tuple-element.51.refs_5_), channel_id=1, source_target_pairs={{0,4},{4,0},{1,5},{5,1},{2,6},{6,2},{3,7},{7,3},{8,12},{12,8},{9,1... | collective-permute-start | bytes 1179656 | tf_op jit(solution)/shard_map/ppermute | solution.py:731
  9.3 0.8 copy-start.6
  10.2 3.8 %collective-permute-start.4 = (bf16[144,256]{1,0:T(8,128)(2,1)S(1)}, bf16[144,256]{1,0:T(8,128)(2,1)S(1)}, u32[]{:S(2)}, u32[]{:S(2)}) collective-permute-start(bf16[144,256]{1,0:T(8,128)(2,1)S(1)} %mark.1.a_ref), channel_id=1, source_target_pairs={{0,8},{8,0},{16,24},{24,16},{32,40},{40,32},{48,56},{56,48},{1,9},... | collective-permute-start | bytes 221192 | tf_op jit(solution)/shard_map/ppermute | solution.py:731
  19.9 17.5 %collective-permute-start.6 = (bf16[768,256]{1,0:T(8,128)(2,1)S(1)}, bf16[768,256]{1,0:T(8,128)(2,1)S(1)}, u32[]{:S(2)}, u32[]{:S(2)}) collective-permute-start(bf16[768,256]{1,0:T(8,128)(2,1)S(1)} %collective-permute-done.1.refs_6_), channel_id=1, source_target_pairs={{0,192},{64,0},{128,64},{192,128},{1,193},{65,1},{129,65},{193,129... | collective-permute-start | bytes 1179656 | tf_op jit(solution)/shard_map/ppermute | solution.py:736
  21.1 16.3 %collective-permute-start.5 = (bf16[768,256]{1,0:T(8,128)(2,1)S(1)}, bf16[768,256]{1,0:T(8,128)(2,1)S(1)}, u32[]{:S(2)}, u32[]{:S(2)}) collective-permute-start(bf16[768,256]{1,0:T(8,128)(2,1)S(1)} %collective-permute-done.1.refs_6_), channel_id=1, source_target_pairs={{0,64},{64,128},{128,192},{192,0},{1,65},{65,129},{129,193},{193,1... | collective-permute-start | bytes 1179656 | tf_op jit(solution)/shard_map/ppermute | solution.py:736
  21.4 42.7 %collective-permute-start.15 = (bf16[256,2048]{1,0:T(8,128)(2,1)S(1)}, bf16[256,2048]{1,0:T(8,128)(2,1)S(1)}, u32[]{:S(2)}, u32[]{:S(2)}) collective-permute-start(bf16[256,2048]{1,0:T(8,128)(2,1)S(1)} %copy-done.5), channel_id=1, source_target_pairs={{0,2},{1,3},{2,0},{3,1},{4,6},{5,7},{6,4},{7,5},{8,10},{9,11},{10,... | collective-permute-start | bytes 3145736 | tf_op jit(solution)/shard_map/ppermute | solution.py:731
  23.8 8.3 %collective-permute-start.8 = (bf16[288,256]{1,0:T(8,128)(2,1)S(1)}, bf16[288,256]{1,0:T(8,128)(2,1)S(1)}, u32[]{:S(2)}, u32[]{:S(2)}) collective-permute-start(bf16[288,256]{1,0:T(8,128)(2,1)S(1)} %join.2.own.refs_0_), channel_id=1, source_target_pairs={{0,48},{8,56},{16,0},{24,8},{32,16},{40,24},{48,32},{56,40},{1,49}... | collective-permute-start | bytes 442376 | tf_op jit(solution)/shard_map/ppermute | solution.py:736
  29.9 7.4 %collective-permute-start.7 = (bf16[288,256]{1,0:T(8,128)(2,1)S(1)}, bf16[288,256]{1,0:T(8,128)(2,1)S(1)}, u32[]{:S(2)}, u32[]{:S(2)}) collective-permute-start(bf16[288,256]{1,0:T(8,128)(2,1)S(1)} %join.2.own.refs_0_), channel_id=1, source_target_pairs={{0,16},{8,24},{16,32},{24,40},{32,48},{40,56},{48,0},{56,8},{1,17}... | collective-permute-start | bytes 442376 | tf_op jit(solution)/shard_map/ppermute | solution.py:736
  37.4 8.8 %collective-permute-start.11 = (bf16[768,256]{1,0:T(8,128)(2,1)S(1)}, bf16[768,256]{1,0:T(8,128)(2,1)S(1)}, u32[]{:S(2)}, u32[]{:S(2)}) collective-permute-start(bf16[768,256]{1,0:T(8,128)(2,1)S(1)} %collective-permute-done.2.refs_7_), channel_id=1, source_target_pairs={{0,64},{64,128},{128,192},{192,0},{1,65},{65,129},{129,193},{193,1... | collective-permute-start | bytes 1179656 | tf_op jit(solution)/shard_map/ppermute | solution.py:736
  37.4 8.8 %collective-permute-start.12 = (bf16[768,256]{1,0:T(8,128)(2,1)S(1)}, bf16[768,256]{1,0:T(8,128)(2,1)S(1)}, u32[]{:S(2)}, u32[]{:S(2)}) collective-permute-start(bf16[768,256]{1,0:T(8,128)(2,1)S(1)} %collective-permute-done.6.refs_10_), channel_id=1, source_target_pairs={{0,192},{64,0},{128,64},{192,128},{1,193},{65,1},{129,65},{193,129... | collective-permute-start | bytes 1179656 | tf_op jit(solution)/shard_map/ppermute | solution.py:736
  40.1 5.8 %collective-permute-start.9 = (bf16[144,256]{1,0:T(8,128)(2,1)S(1)}, bf16[144,256]{1,0:T(8,128)(2,1)S(1)}, u32[]{:S(2)}, u32[]{:S(2)}) collective-permute-start(bf16[144,256]{1,0:T(8,128)(2,1)S(1)} %get-tuple-element.57), channel_id=1, source_target_pairs={{0,16},{8,24},{16,32},{24,40},{32,48},{40,56},{48,0},{56,8},{1,17}... | collective-permute-start | bytes 221192 | tf_op jit(solution)/shard_map/ppermute | solution.py:736
  40.1 5.7 %collective-permute-start.10 = (bf16[144,256]{1,0:T(8,128)(2,1)S(1)}, bf16[144,256]{1,0:T(8,128)(2,1)S(1)}, u32[]{:S(2)}, u32[]{:S(2)}) collective-permute-start(bf16[144,256]{1,0:T(8,128)(2,1)S(1)} %get-tuple-element.58), channel_id=1, source_target_pairs={{0,48},{8,56},{16,0},{24,8},{32,16},{40,24},{48,32},{56,40},{1,49}... | collective-permute-start | bytes 221192 | tf_op jit(solution)/shard_map/ppermute | solution.py:736
  45.9 9.2 %copy-start.3 = (bf16[768,256]{1,0:T(8,128)(2,1)S(1)}, bf16[768,256]{1,0:T(8,128)(2,1)}, u32[]{:S(2)}) copy-start(bf16[768,256]{1,0:T(8,128)(2,1)} %get-tuple-element.51.refs_5_) | copy-start | bytes 1179652
  45.9 4.1 %collective-permute-start.13 = (bf16[16,256]{1,0:T(8,128)(2,1)S(1)}, bf16[16,256]{1,0:T(8,128)(2,1)S(1)}, u32[]{:S(2)}, u32[]{:S(2)}) collective-permute-start(bf16[16,256]{1,0:T(8,128)(2,1)S(1)} %plane_counts.1.a_ref), channel_id=1, source_target_pairs={{0,64},{64,0},{128,192},{192,128},{1,65},{65,1},{129,193},{193,129... | collective-permute-start | bytes 24584 | tf_op jit(solution)/shard_map/ppermute | solution.py:731
  46.2 1.0 copy-start.2
  50.0 5.0 %collective-permute-start.14 = (bf16[16,256]{1,0:T(8,128)(2,1)S(1)}, bf16[16,256]{1,0:T(8,128)(2,1)S(1)}, u32[]{:S(2)}, u32[]{:S(2)}) collective-permute-start(bf16[16,256]{1,0:T(8,128)(2,1)S(1)} %added.1.refs_13_), channel_id=1, source_target_pairs={{0,128},{64,192},{128,0},{192,64},{1,129},{65,193},{129,1},{193,65... | collective-permute-start | bytes 24584 | tf_op jit(solution)/shard_map/ppermute | solution.py:731
  55.0 33.2 %copy-start.1 = (bf16[128,2048]{1,0:T(8,128)(2,1)S(1)}, bf16[128,2048]{1,0:T(8,128)(2,1)}, u32[]{:S(2)}) copy-start(bf16[128,2048]{1,0:T(8,128)(2,1)} %tok_hbm.3) | copy-start | bytes 1572868
  64.1 42.0 %copy-start = (bf16[2048,3,256]{2,0,1:T(8,128)(2,1)S(1)}, bf16[2048,3,256]{2,0,1:T(8,128)(2,1)}, u32[]{:S(2)}) copy-start(bf16[2048,3,256]{2,0,1:T(8,128)(2,1)} %param.17) | copy-start | bytes 9437188
  83.2 5.0 %collective-permute-start.16 = (bf16[128,256]{1,0:T(8,128)(2,1)S(1)}, bf16[128,256]{1,0:T(8,128)(2,1)S(1)}, u32[]{:S(2)}, u32[]{:S(2)}) collective-permute-start(bf16[128,256]{1,0:T(8,128)(2,1)S(1)} %merge.1.a_ref), channel_id=1, source_target_pairs={{0,2},{1,3},{2,0},{3,1},{4,6},{5,7},{6,4},{7,5},{8,10},{9,11},{10,... | collective-permute-start | bytes 196616 | tf_op jit(solution)/shard_map/ppermute | solution.py:731
  89.5 37.0 %copy-start.8 = (f32[2]{0:T(128)S(1)}, f32[2]{0:T(128)}, u32[]{:S(2)}) copy-start(f32[2]{0:T(128)} %slope_ref.7) | copy-start | bytes 28
  89.6 16.5 %collective-permute-start.17 = (bf16[128,2048]{1,0:T(8,128)(2,1)S(1)}, bf16[128,2048]{1,0:T(8,128)(2,1)S(1)}, u32[]{:S(2)}, u32[]{:S(2)}) collective-permute-start(bf16[128,2048]{1,0:T(8,128)(2,1)S(1)} %get-tuple-element.78), channel_id=1, source_target_pairs={{0,1},{1,0},{2,3},{3,2},{4,5},{5,4},{6,7},{7,6},{8,9},{9,8},{10,11... | collective-permute-start | bytes 1572872 | tf_op jit(solution)/shard_map/ppermute | solution.py:731
  98.5 5.4 %collective-permute-start.19 = (bf16[32,2048]{1,0:T(8,128)(2,1)S(1)}, bf16[32,2048]{1,0:T(8,128)(2,1)S(1)}, u32[]{:S(2)}, u32[]{:S(2)}) collective-permute-start(bf16[32,2048]{1,0:T(8,128)(2,1)S(1)} %get-tuple-element.79), channel_id=1, source_target_pairs={{0,5},{1,4},{2,7},{3,6},{4,9},{5,8},{6,11},{7,10},{8,13},{9,12},{1... | collective-permute-start | bytes 393224 | tf_op jit(solution)/shard_map/ppermute | solution.py:805
  100.2 5.8 %collective-permute-start.18 = (bf16[32,2048]{1,0:T(8,128)(2,1)S(1)}, bf16[32,2048]{1,0:T(8,128)(2,1)S(1)}, u32[]{:S(2)}, u32[]{:S(2)}) collective-permute-start(bf16[32,2048]{1,0:T(8,128)(2,1)S(1)} %get-tuple-element.79), channel_id=1, source_target_pairs={{0,4},{1,5},{2,6},{3,7},{4,8},{5,9},{6,10},{7,11},{8,12},{9,13},{1... | collective-permute-start | bytes 393224 | tf_op jit(solution)/shard_map/ppermute | solution.py:804
  106.0 36.2 %copy-start.4 = (bf16[256,2048]{1,0:T(8,128)(2,1)S(1)}, bf16[256,2048]{1,0:T(8,128)(2,1)}, u32[]{:S(2)}) copy-start(bf16[256,2048]{1,0:T(8,128)(2,1)} %w_ref.1) | copy-start | bytes 3145732
  108.0 3.5 %collective-permute-start.20 = (bf16[32,512]{1,0:T(8,128)(2,1)S(1)}, bf16[32,512]{1,0:T(8,128)(2,1)S(1)}, u32[]{:S(2)}, u32[]{:S(2)}) collective-permute-start(bf16[32,512]{1,0:T(8,128)(2,1)S(1)} %get-tuple-element.82.a_ref), channel_id=1, source_target_pairs={{0,4},{4,0},{1,5},{5,1},{2,6},{6,2},{3,7},{7,3},{8,12},{12,8},{9,1... | collective-permute-start | bytes 98312 | tf_op jit(solution)/shard_map/ppermute | solution.py:731
  111.5 15.0 %all-to-all-start.1 = ((bf16[8,32,256]{2,1,0:T(8,128)(2,1)}), bf16[8,32,256]{2,1,0:T(8,128)(2,1)S(1)}, u32[]{:S(2)}, u32[]{:S(2)}) async-start(bf16[8,32,256]{2,1,0:T(8,128)(2,1)} %get-tuple-element.83), calls=%async_computation.1 | async-start | bytes 262144 | tf_op jit(solution)/shard_map/all_to_all | solution.py:727
  116.4 5.8 %collective-permute-start.23 = (bf16[64,512]{1,0:T(8,128)(2,1)S(1)}, bf16[64,512]{1,0:T(8,128)(2,1)S(1)}, u32[]{:S(2)}, u32[]{:S(2)}) collective-permute-start(bf16[64,512]{1,0:T(8,128)(2,1)S(1)} %join.3.refs_0_), channel_id=1, source_target_pairs={{0,192},{64,0},{128,64},{192,128},{1,193},{65,1},{129,65},{193,129... | collective-permute-start | bytes 196616 | tf_op jit(solution)/shard_map/ppermute | solution.py:736
  120.4 4.9 %collective-permute-start.22 = (bf16[64,512]{1,0:T(8,128)(2,1)S(1)}, bf16[64,512]{1,0:T(8,128)(2,1)S(1)}, u32[]{:S(2)}, u32[]{:S(2)}) collective-permute-start(bf16[64,512]{1,0:T(8,128)(2,1)S(1)} %join.3.refs_0_), channel_id=1, source_target_pairs={{0,128},{64,192},{128,0},{192,64},{1,129},{65,193},{129,1},{193,65... | collective-permute-start | bytes 196616 | tf_op jit(solution)/shard_map/ppermute | solution.py:736
  121.9 4.6 %collective-permute-start.21 = (bf16[64,512]{1,0:T(8,128)(2,1)S(1)}, bf16[64,512]{1,0:T(8,128)(2,1)S(1)}, u32[]{:S(2)}, u32[]{:S(2)}) collective-permute-start(bf16[64,512]{1,0:T(8,128)(2,1)S(1)} %join.3.refs_0_), channel_id=1, source_target_pairs={{0,64},{64,128},{128,192},{192,0},{1,65},{65,129},{129,193},{193,1... | collective-permute-start | bytes 196616 | tf_op jit(solution)/shard_map/ppermute | solution.py:736
  142.8 8.9 %collective-permute-start.24 = (bf16[32,512]{1,0:T(8,128)(2,1)S(1)}, bf16[32,512]{1,0:T(8,128)(2,1)S(1)}, u32[]{:S(2)}, u32[]{:S(2)}) collective-permute-start(bf16[32,512]{1,0:T(8,128)(2,1)S(1)} %get-tuple-element.86), channel_id=1, source_target_pairs={{0,1},{1,0},{2,3},{3,2},{4,5},{5,4},{6,7},{7,6},{8,9},{9,8},{10,11... | collective-permute-start | bytes 98312 | tf_op jit(solution)/shard_map/ppermute | solution.py:731
  148.4 4.3 %collective-permute-start.25 = (bf16[32,512]{1,0:T(8,128)(2,1)S(1)}, bf16[32,512]{1,0:T(8,128)(2,1)S(1)}, u32[]{:S(2)}, u32[]{:S(2)}) collective-permute-start(bf16[32,512]{1,0:T(8,128)(2,1)S(1)} %get-tuple-element.87), channel_id=1, source_target_pairs={{0,2},{1,3},{2,0},{3,1},{4,6},{5,7},{6,4},{7,5},{8,10},{9,11},{10,... | collective-permute-start | bytes 98312 | tf_op jit(solution)/shard_map/ppermute | solution.py:731
  149.0 5.1 %collective-permute-start.26 = (bf16[32,512]{1,0:T(8,128)(2,1)S(1)}, bf16[32,512]{1,0:T(8,128)(2,1)S(1)}, u32[]{:S(2)}, u32[]{:S(2)}) collective-permute-start(bf16[32,512]{1,0:T(8,128)(2,1)S(1)} %get-tuple-element.88), channel_id=1, source_target_pairs={{0,3},{1,2},{2,1},{3,0},{4,7},{5,6},{6,5},{7,4},{8,11},{9,10},{10,... | collective-permute-start | bytes 98312 | tf_op jit(solution)/shard_map/ppermute | solution.py:731

commit v10 on v9

--- a/solution.py
+++ b/solution.py
@@ -10,6 +10,7 @@
 
 HS = 128
 GROUP = 4
+HALO = 16
 NEG = -1e30
 LOG2E = math.log2(math.e)
 SCALE2 = HS ** -0.5 * LOG2E
@@ -130,21 +131,50 @@
     )(a, b)
 
 
-def mark_kernel(q_ref, a_ref, b_ref, out_ref):
-    rows = q_ref.shape[0]
-    out_ref[:rows] = q_ref[...]
-    out_ref[rows:] = (a_ref[...].astype(F32) + b_ref[...].astype(F32)).astype(BF16)
-
-
-def mark(q, a, b):
+def mark_kernel(halo_hbm, w_hbm, q_hbm, a_hbm, b_hbm, out_ref, halo, weight, a, b, sems):
+    rows = q_hbm.shape[0]
+    copies = [
+        pltpu.make_async_copy(src, dst, sems.at[i])
+        for i, (src, dst) in enumerate(
+            (
+                (halo_hbm, halo),
+                (w_hbm.at[0], weight),
+                (q_hbm, out_ref.at[:rows]),
+                (a_hbm, a),
+                (b_hbm, b),
+            )
+        )
+    ]
+    for copy in copies:
+        copy.start()
+    for copy in copies:
+        copy.wait()
+    normed = rms_scaled(halo[...].astype(F32))
+    out = jnp.dot(normed, weight[...], preferred_element_type=F32)
+    out_ref[rows : rows + HALO] = (out * SCALE2).astype(BF16)
+    out_ref[rows + HALO :] = (a[...].astype(F32) + b[...].astype(F32)).astype(BF16)
+
+
+def mark(halo, weight3, q, a, b):
     n, width = q.shape
+    d = halo.shape[1]
+    hbm = pl.BlockSpec(memory_space=HBM)
     return pl.pallas_call(
         mark_kernel,
-        out_shape=jax.ShapeDtypeStruct((n + a.shape[0], width), BF16),
-        compiler_params=params(8),
-        cost_estimate=cost(0, 4 * n * width),
+        in_specs=[hbm] * 5,
+        out_specs=pl.BlockSpec(memory_space=VMEM),
+        out_shape=jax.ShapeDtypeStruct((n + HALO + a.shape[0], width), BF16),
+        scratch_shapes=[
+            VMEM(halo.shape, BF16),
+            VMEM((d, width), BF16),
+            VMEM(a.shape, BF16),
+            VMEM(b.shape, BF16),
+            pltpu.SemaphoreType.DMA((5,)),
+        ],
+        compiler_params=params(60),
+        cost_estimate=cost(2 * HALO * d * width, 2 * d * width),
         name="mark",
-    )(q, a, b)
+    )(halo, weight3, q, a, b)
 
 
 def plane_kernel(own, left, right, far, far_other, out_ref):
@@ -241,9 +271,7 @@
         both = None
         for j in range(pieces):
             term = jnp.dot(
-                jnp.exp2((pending[j] - top).astype(BF16)),
-                value(h, j),
-                preferred_element_type=F32,
+                jnp.exp2(pending[j] - top).astype(BF16), value(h, j), preferred_element_type=F32
             )
             both = term if both is None else both + term
             if h + 1 < heads:
@@ -268,7 +296,7 @@
 def fill_tile(q_tile, queries, tile):
     rows = q_tile.shape[0] // 4
     for b, (ref, half) in enumerate(TILES[tile]):
-        at = half * (queries[ref].shape[0] // 2)
+        at = half * (rows + 16)
         q_tile[b * rows : (b + 1) * rows] = queries[ref][at : at + rows]
 
 
@@ -277,7 +305,8 @@
     acc_ref, stat_ref, q_tile, bias = refs[13:]
     y, z, xl = place_of_device()
     count, width = q_tile.shape
-    rows, heads = count // 4, width // HS
+    block, heads = count // 4, width // HS
+    rows = block - HALO
     fill_tile(q_tile, queries, tile)
     place = lax.broadcasted_iota(jnp.int32, (1, rows), 1)
     for j, (back, other) in enumerate(RING):
@@ -288,16 +317,20 @@
                 yj <= y, slope_ref[h] * LOG2E * spot, NEG
             )
     row = lax.broadcasted_iota(jnp.int32, (count, 1), 0)
-    part = row // rows
-    row_z = ((z + 8 - 4 * tile - 2 * (part // 2)) % 8) ^ (part % 2)
-    row_pos = (y * 16 + xl + 2 * row_z) * rows + row % rows
+    row_pos = jnp.zeros((count, 1), jnp.int32)
+    for part in range(4):
+        row_z = ((z + 8 - 4 * tile - 2 * (part // 2)) % 8) ^ (part % 2)
+        first = (y * 16 + xl + 2 * row_z) * rows
+        at = row - part * block
+        at = jnp.where(at < rows, at, at - block)
+        row_pos = jnp.where(row >= part * block, first + at, row_pos)
 
     def score(h, q, j):
         cols = slice(h * HS, (h + 1) * HS)
         s = dot_t(q, packs[j][2 * slots : 2 * slots + rows, cols])
         s = s + bias[h : h + 1, j * rows : (j + 1) * rows]
         back, other = RING[j]
-        if back == 0:
+        if back <= 1:
             yj, zj, side = owner_of(back, other)
             s = jnp.where(place + (yj * 16 + zj * 2 + side) * rows <= row_pos, s, NEG)
         return s
@@ -318,7 +351,7 @@
 def span_attend(tile, slopes, queries, packs, slots):
     width = queries[0].shape[1]
     rows = packs[0].shape[0] // 2 - slots
-    count, nk = 4 * rows, len(RING) * rows
+    count, nk = 4 * (rows + HALO), len(RING) * rows
     vmem = pl.BlockSpec(memory_space=VMEM)
     return pl.pallas_call(
         functools.partial(span_kernel, tile, slots),
@@ -341,7 +374,8 @@
     tile = pl.program_id(0)
     y, z, xl = place_of_device()
     count, width = q_tile.shape
-    rows, heads = count // 4, width // HS
+    block, heads = count // 4, width // HS
+    rows = block - HALO
     for t in range(2):
 
         @pl.when(tile == t)
@@ -388,28 +422,30 @@
     both = jnp.concatenate(done, axis=1)
     odd = z % 2 == 1
     for pair in range(2):
-        a, b = 2 * pair * rows, (2 * pair + 1) * rows
-        end = b + rows
+        a, b = 2 * pair * block, (2 * pair + 1) * block
+        end = b + block
         blocks = []
         for own, level in (
             (jnp.where(odd, both[b:end], both[a:b]), jnp.where(odd, packed[b:end], packed[a:b])),
             (jnp.where(odd, both[a:b], both[b:end]), jnp.where(odd, packed[a:b], packed[b:end])),
         ):
-            turned = jnp.transpose(level)[:16]
-            tail = jnp.concatenate([turned, jnp.zeros_like(turned)], axis=1).astype(BF16)
-            blocks.append((own, tail))
+            ahead = jnp.concatenate(
+                [level[rows:], jnp.zeros((HS - HALO, HS), F32)], axis=0
+            )
+            tail = [jnp.transpose(level[:rows])[:16], jnp.transpose(ahead)[:16]]
+            blocks.append((own, jnp.concatenate(tail, axis=1).astype(BF16)))
         for p in range(4):
 
             @pl.when((z // 2 + 4 - 2 * tile - pair) % 4 == p)
             def _(p=p, blocks=blocks):
                 for i, (own, tail) in enumerate(blocks):
-                    out_ref[2 * p + i, :rows] = own
-                    out_ref[2 * p + i, rows:] = tail
+                    out_ref[2 * p + i, :block] = own
+                    out_ref[2 * p + i, block:] = tail
 
 
 def cache_attend(slopes, queries, packs, tables, states, slots):
     width = queries[0].shape[1]
-    rows = packs[0].shape[0] // 2 - slots
+    rows = packs[0].shape[0] // 2 - slots + HALO
     count, nk = 4 * rows, len(RING) * slots
     whole = lambda a: pl.BlockSpec(a.shape, lambda i: (0,) * a.ndim)
     operands = (*queries, *packs, *tables, *states)
@@ -435,10 +471,15 @@
 def merge_kernel(heads, parts_ref, out_ref):
     sources, padded, width = parts_ref.shape
     rows = padded - 16
-    levels = jnp.concatenate(
-        [parts_ref[s, rows:, :HS].astype(F32) for s in range(sources)], axis=0
+    levels = [
+        jnp.concatenate(
+            [parts_ref[s, rows:, cols].astype(F32) for s in range(sources)], axis=0
+        )
+        for cols in (slice(0, HS), slice(HS, 2 * HS))
+    ]
+    turned = jnp.concatenate(
+        [jnp.transpose(levels[0]), jnp.transpose(levels[1])[: rows - HS]], axis=0
     )
-    turned = jnp.transpose(levels)
     for h in range(heads):
         cols = slice(h * HS, (h + 1) * HS)
         level = []
@@ -470,7 +511,7 @@
 
 
 def product_kernel(
-    tok_hbm, a_ref, b_ref, wa_hbm, wb_hbm, sum_ref, term_ref, rim_ref, tok, wa, wb, sems
+    tok_hbm, halo_hbm, a_ref, b_ref, wa_hbm, wb_hbm, sum_ref, term_ref, tok, wa, wb, sems
 ):
     chunks = wa.shape[0]
     cols = wa.shape[2]
@@ -480,9 +521,16 @@
         copies.append(
             [
                 pltpu.make_async_copy(src.at[:, at], dst.at[c], sems.at[i, c])
-                for i, (src, dst) in enumerate(((wa_hbm, wa), (wb_hbm, wb), (tok_hbm, tok)))
+                for i, (src, dst) in enumerate(((wa_hbm, wa), (wb_hbm, wb)))
             ]
         )
+        rows = tok_hbm.shape[0]
+        for i, (src, to) in enumerate(
+            ((tok_hbm, pl.ds(0, rows)), (halo_hbm, pl.ds(rows, HALO)))
+        ):
+            copies[-1].append(
+                pltpu.make_async_copy(src.at[:, at], tok.at[c, to], sems.at[2 + i, c])
+            )
     for group in copies:
         for copy in group:
             copy.start()
@@ -496,61 +544,59 @@
         total = tok[c].astype(F32) + term
         sum_ref[:, at] = total
         term_ref[:, at] = term.astype(BF16)
-        rim_ref[:16, at] = total[-16:].astype(BF16)
-        rim_ref[16:, at] = term[-16:].astype(BF16)
-
-
-def layer_product(tokens, atts, weights):
-    rows, d = tokens.shape
+
+
+def layer_product(tokens, halo, atts, weights):
+    rows, d = tokens.shape[0] + HALO, tokens.shape[1]
     chunks = 4
     inner = weights[0].shape[0]
     hbm = pl.BlockSpec(memory_space=HBM)
     vmem = pl.BlockSpec(memory_space=VMEM)
     return pl.pallas_call(
         product_kernel,
-        in_specs=[hbm, vmem, vmem, hbm, hbm],
-        out_specs=[vmem] * 3,
+        in_specs=[hbm, hbm, vmem, vmem, hbm, hbm],
+        out_specs=[vmem] * 2,
         out_shape=[
             jax.ShapeDtypeStruct((rows, d), F32),
             jax.ShapeDtypeStruct((rows, d), BF16),
-            jax.ShapeDtypeStruct((32, d), BF16),
         ],
         scratch_shapes=[
             VMEM((chunks, rows, d // chunks), BF16),
             VMEM((chunks, inner, d // chunks), BF16),
             VMEM((chunks, inner, d // chunks), BF16),
-            pltpu.SemaphoreType.DMA((3, chunks)),
+            pltpu.SemaphoreType.DMA((4, chunks)),
         ],
         compiler_params=params(16),
         cost_estimate=cost(4 * rows * d * inner, 4 * inner * d),
         name="layer_product",
-    )(tokens, *atts, *weights)
+    )(tokens, halo, *atts, *weights)
 
 
 def short_project_kernel(
-    sum_ref, term_ref, rim_a, rim_b, w_ref, cols_ref, q_ref, kv_ref, normed
+    sum_ref, term_ref, w_ref, cols_ref, q_ref, kv_ref, normed
 ):
     step = pl.program_id(0)
-    rows, d = sum_ref.shape
+    rows, d = sum_ref.shape[0] - HALO, sum_ref.shape[1]
     groups = rows // GROUP
-    rim_rows = 16
     width = w_ref.shape[2]
 
     @pl.when(step == 0)
     def _():
         layer = (sum_ref[...] + term_ref[...].astype(F32)).astype(BF16)
+        y, z, xl = place_of_device()
+        rim = jnp.where(y * 16 + z * 2 + xl > 0, layer[rows:], jnp.zeros((HALO, d), BF16))
+        layer = layer[:rows]
         part = d // 4
         tp = lax.axis_index("tp")
         mine = layer[:, :part]
         for t in range(1, 4):
             mine = jnp.where(tp == t, layer[:, t * part : (t + 1) * part], mine)
         cols_ref[...] = mine
-        rim = (rim_a[:rim_rows].astype(F32) + rim_b[rim_rows:].astype(F32)).astype(BF16)
         g = lax.broadcasted_iota(jnp.int32, (groups, rows), 0) * GROUP
         t = lax.broadcasted_iota(jnp.int32, (groups, rows), 1)
         own = jnp.where((t <= g) & (t > g - GROUP), 1.0 / GROUP, 0.0).astype(BF16)
-        g = lax.broadcasted_iota(jnp.int32, (groups, rim_rows), 0) * GROUP
-        t = lax.broadcasted_iota(jnp.int32, (groups, rim_rows), 1) - rim_rows
+        g = lax.broadcasted_iota(jnp.int32, (groups, HALO), 0) * GROUP
+        t = lax.broadcasted_iota(jnp.int32, (groups, HALO), 1) - HALO
         before = jnp.where(t > g - GROUP, 1.0 / GROUP, 0.0).astype(BF16)
         pooled = jnp.dot(own, layer, preferred_element_type=F32) + jnp.dot(
             before, rim, preferred_element_type=F32
@@ -574,8 +620,8 @@
         kv_ref[:, width:] = out.astype(BF16)
 
 
-def short_project(total, term, rims, weight3, copies):
-    n, d = total.shape
+def short_project(total, term, weight3, copies):
+    n, d = total.shape[0] - HALO, total.shape[1]
     groups = n // GROUP
     width = weight3.shape[2]
     whole = lambda shape: pl.BlockSpec(shape, lambda i: (0,) * len(shape))
@@ -583,7 +629,7 @@
     return pl.pallas_call(
         short_project_kernel,
         grid=(3,),
-        in_specs=[whole((n, d)), whole((n, d)), whole((32, d)), whole((32, d))]
+        in_specs=[whole(total.shape), whole(term.shape)]
         + [pl.BlockSpec((1, d, width), lambda i: (i, 0, 0))],
         out_specs=[whole(s) for s in shapes],
         out_shape=[jax.ShapeDtypeStruct(s, BF16) for s in shapes],
@@ -591,7 +637,7 @@
         compiler_params=params(16),
         cost_estimate=cost(6 * groups * d * width, 2 * (n * d + 3 * d * width)),
         name="short_project",
-    )(total, term, *rims, weight3)
+    )(total, term, weight3)
 
 
 def short_attend_kernel(slope_ref, q_ref, *refs):
@@ -761,11 +807,13 @@
     nz = lax.axis_size("z")
     count = own_count(cache_count, cache_keys.shape[1])
     other_count = swap(count, "xl")
-    q, pack = project(
-        tokens, jnp.transpose(project_weight, (1, 0, 2)), cache_keys, cache_values
-    )
-    q, pack, other_count = lax.optimization_barrier((q, pack, other_count))
-    marked = mark(q, count, other_count)
+    n, tp = lax.axis_size(axes), lax.axis_size("tp")
+    halo = lax.ppermute(tokens[-HALO:], axes, [(i, i + tp) for i in range(n - tp)])
+    weight3 = jnp.transpose(project_weight, (1, 0, 2))
+    q, pack = project(tokens, weight3, cache_keys, cache_values)
+    q, pack, other_count, halo = lax.optimization_barrier((q, pack, other_count, halo))
+    marked = mark(halo, weight3, q, count, other_count)
+    marked, pack = lax.optimization_barrier((marked, pack))
     left, right = both_ways(pack, "y", 1)
     other, left, right, mate = lax.optimization_barrier(
         (swap(pack, "xl"), left, right, swap(marked, "z"))
@@ -795,19 +843,12 @@
     parts, crossed = lax.optimization_barrier((parts, crossed))
 
     att = merge(exchange(parts, "z"))
-    total, term, rim = layer_product(
-        tokens, (att, swap(att, "tp", 2)), (output_weight, crossed)
+    total, term = layer_product(
+        tokens, halo, (att, swap(att, "tp", 2)), (output_weight, crossed)
     )
-    n, tp = lax.axis_size(axes), lax.axis_size("tp")
-    ahead = [(i, i + tp) for i in range(n - tp)]
-    rims = [
-        lax.ppermute(rim, axes, ahead),
-        lax.ppermute(rim, axes, [(i, j ^ 1) for i, j in ahead]),
-    ]
     layer, sq, skv = short_project(
         total,
         swap(term, "tp", 1),
-        rims,
         jnp.transpose(short_project_weight, (1, 0, 2)),
         nz,
     )

time: 155 us -> 153 us (0.987)
  starting transfers between devices: 62 us -> 49.9 us
  waiting for transfers between devices: 32.6 us -> 36.9 us
  Pallas kernels: 24.9 us -> 29.1 us
    ppermute x12, starting transfers between devices: 29.3 us -> 23.9 us  [swap(): lax.ppermute(x, axis, [(i, i ^ flip) for i in range(lax.axis_size(axis))])]
    ppermute x12, waiting for transfers between devices: 10.6 us -> 14.8 us  [swap(): lax.ppermute(x, axis, [(i, i ^ flip) for i in range(lax.axis_size(axis))])]
    ppermute x13, starting transfers between devices: 22.4 us -> 18.7 us  [moved(): return lax.ppermute(x, axis, [(i, (i + by) % n) for i in range(n)])]
    pallas_call x3, Pallas kernels: 3.28 us -> 5.61 us  [the longest x1 2.27 us: mark(): pl.pallas_call(mark_kernel, in_specs=[hbm] * 5, out_specs=pl.BlockSpec(me...]
    ppermute x2 -> x1, waiting for transfers between devices: 2.13 us -> 0.01 us  [on_device(): lax.ppermute(tokens[-HALO:], axes, [(i, i + tp) for i in range(n - tp)])]
    ppermute x2 -> x1, starting transfers between devices: 5.41 us -> 3.94 us  [on_device(): lax.ppermute(tokens[-HALO:], axes, [(i, i + tp) for i in range(n - tp)])]
  transfers between devices with their start and end apart: 28 -> 27, of which waited for: 13 -> 15; matrix products, arithmetic and copies ran while one was open for 0% -> 0% of each run, Pallas kernels for 12% -> 13%
where the time goes in v10:
time: 153 us
  starting transfers between devices  49.9 us (33%)
  waiting for transfers between devices  36.9 us (24%)
  blocking collectives  33.3 us (22%)
  Pallas kernels  29.1 us (19%)
  local copies, waits for them, and re-layouts  2.38 us (2%)
    all_to_all x2, blocking collectives, exchange(): return lax.all_to_all(blocks, axis, 0, 0)  33.3 us
    ppermute x12, starting transfers between devices, swap(): lax.ppermute(x, axis, [(i, i ^ flip) for i in range(lax.axis_size(axis))])  23.9 us
    ppermute x13, waiting for transfers between devices, moved(): return lax.ppermute(x, axis, [(i, (i + by) % n) for i in range(n)])  21.4 us
    ppermute x13, starting transfers between devices, moved(): return lax.ppermute(x, axis, [(i, (i + by) % n) for i in range(n)])  18.7 us
    ppermute x12, waiting for transfers between devices, swap(): lax.ppermute(x, axis, [(i, i ^ flip) for i in range(lax.axis_size(axis))])  14.8 us
    pallas_call x1, Pallas kernels, cache_attend(): pl.pallas_call(functools.partial(cache_kernel, slots), grid=(2,), in_spec...  9.79 us
    pallas_call x2, Pallas kernels, span_attend(): pl.pallas_call(functools.partial(span_kernel, tile, slots), in_specs=[pl....  6.32 us
    ppermute x1, starting transfers between devices, on_device(): lax.ppermute(tokens[-HALO:], axes, [(i, i + tp) for i in range(n - tp)])  3.94 us
  transfers between devices with their start and end apart: 27, of which 15 were waited for; matrix products, arithmetic and copies ran while one was open for 0% of the time, Pallas kernels for 13%

profile of v10, /device:TPU:1, one launch (start us, length us, event | category | flops | bytes accessed | tf_op | source)
XLA Modules:
  0.0 152.6 jit_solution(4250496138375940864)
XLA Ops:
  0.0 0.8 slice.3
  0.8 3.9 %collective-permute-start.1 = (bf16[16,2048]{1,0:T(8,128)(2,1)S(1)}, bf16[16,2048]{1,0:T(8,128)(2,1)S(1)}, u32[]{:S(2)}, u32[]{:S(2)}) collective-permute-start(bf16[16,2048]{1,0:T(8,128)(2,1)S(1)} %slice.3), channel_id=1, source_target_pairs={{0,4},{1,5},{2,6},{3,7},{4,8},{5,9},{6,10},{7,11},{8,12},{9,13},{1... | collective-permute-start | bytes 196616 | tf_op jit(solution)/shard_map/ppermute | solution.py:811
  5.5 1.7 %collective-permute-start = (bf16[16,256]{1,0:T(8,128)(2,1)S(1)}, bf16[16,256]{1,0:T(8,128)(2,1)S(1)}, u32[]{:S(2)}, u32[]{:S(2)}) collective-permute-start(bf16[16,256]{1,0:T(8,128)(2,1)S(1)} %own_count.1.a_hbm), channel_id=1, source_target_pairs={{0,4},{4,0},{1,5},{5,1},{2,6},{6,2},{3,7},{7,3},{8,12},{12,8},{9,1... | collective-permute-start | bytes 24584 | tf_op jit(solution)/shard_map/ppermute | solution.py:777
  7.2 3.5 %project.1 = (bf16[128,256]{1,0:T(8,128)(2,1)}, bf16[768,256]{1,0:T(8,128)(2,1)}) custom-call(bf16[128,2048]{1,0:T(8,128)(2,1)} %tok_hbm.3, bf16[3,2048,256]{2,1,0:T(8,128)(2,1)} %bitcast.3, bf16[256,256]{1,0:T(8,128)(2,1)} %ck_hbm.1, bf16[256,256]{1,0:T(8,128)(2,1)} %cv_hbm.1), custom_call_target="tpu_custom_call" | custom-call | flops 402653184 | bytes 3670016 | tf_op jit(solution)/shard_map/project/pallas_call | solution.py:84
  10.7 0.6 copy-done.11
  11.3 2.3 %mark.1.a_ref = bf16[160,256]{1,0:T(8,128)(2,1)} custom-call(bf16[16,2048]{1,0:T(8,128)(2,1)} %copy-done.6, bf16[3,2048,256]{2,1,0:T(8,128)(2,1)} %bitcast.4, bf16[128,256]{1,0:T(8,128)(2,1)} %get-tuple-element.52.q_hbm, bf16[16,256]{1,0:T(8,128)(2,1)} %copy-done.8, bf16[16,256]{1,0:T(8,128)(2,1)} %copy-done.11), custom_call_target="tpu_custom_call" | custom-call | flops 16777216 | bytes 1048576 | tf_op jit(solution)/shard_map/mark/pallas_call | solution.py:162
  13.6 4.0 %collective-permute-start.4 = (bf16[768,256]{1,0:T(8,128)(2,1)S(1)}, bf16[768,256]{1,0:T(8,128)(2,1)S(1)}, u32[]{:S(2)}, u32[]{:S(2)}) collective-permute-start(bf16[768,256]{1,0:T(8,128)(2,1)S(1)} %copy-done.2), channel_id=1, source_target_pairs={{0,192},{64,0},{128,64},{192,128},{1,193},{65,1},{129,65},{193,129... | collective-permute-start | bytes 1179656 | tf_op jit(solution)/shard_map/ppermute | solution.py:782
  17.6 0.4 collective-permute-start.5
  18.1 3.3 %collective-permute-done.5.b_ref = bf16[160,256]{1,0:T(8,128)(2,1)S(1)} collective-permute-done((bf16[160,256]{1,0:T(8,128)(2,1)}, bf16[160,256]{1,0:T(8,128)(2,1)S(1)}, u32[]{:S(2)}, u32[]{:S(2)}) %collective-permute-start.5) | collective-permute-done | bytes 81952 | tf_op jit(solution)/shard_map/ppermute | solution.py:777
  21.4 3.1 %collective-permute-done.4.refs_9_ = bf16[768,256]{1,0:T(8,128)(2,1)S(1)} collective-permute-done((bf16[768,256]{1,0:T(8,128)(2,1)S(1)}, bf16[768,256]{1,0:T(8,128)(2,1)S(1)}, u32[]{:S(2)}, u32[]{:S(2)}) %collective-permute-start.4) | collective-permute-done | bytes 393248 | tf_op jit(solution)/shard_map/ppermute | solution.py:782
  24.5 3.1 %collective-permute-done.3.refs_7_ = bf16[768,256]{1,0:T(8,128)(2,1)S(1)} collective-permute-done((bf16[768,256]{1,0:T(8,128)(2,1)S(1)}, bf16[768,256]{1,0:T(8,128)(2,1)S(1)}, u32[]{:S(2)}, u32[]{:S(2)}) %collective-permute-start.3) | collective-permute-done | bytes 393248 | tf_op jit(solution)/shard_map/ppermute | solution.py:782
  27.6 1.2 collective-permute-start.7
  29.1 2.5 %collective-permute-start.16 = (bf16[256,2048]{1,0:T(8,128)(2,1)S(1)}, bf16[256,2048]{1,0:T(8,128)(2,1)S(1)}, u32[]{:S(2)}, u32[]{:S(2)}) collective-permute-start(bf16[256,2048]{1,0:T(8,128)(2,1)S(1)} %copy-done.4), channel_id=1, source_target_pairs={{0,2},{1,3},{2,0},{3,1},{4,6},{5,7},{6,4},{7,5},{8,10},{9,11},{10,... | collective-permute-start | bytes 3145736 | tf_op jit(solution)/shard_map/ppermute | solution.py:777
  31.5 0.9 copy-done.5
  32.4 4.6 %collective-permute-start.9 = (bf16[320,256]{1,0:T(8,128)(2,1)S(1)}, bf16[320,256]{1,0:T(8,128)(2,1)S(1)}, u32[]{:S(2)}, u32[]{:S(2)}) collective-permute-start(bf16[320,256]{1,0:T(8,128)(2,1)S(1)} %join.2.own.refs_0_), channel_id=1, source_target_pairs={{0,48},{8,56},{16,0},{24,8},{32,16},{40,24},{48,32},{56,40},{1,49}... | collective-permute-start | bytes 491528 | tf_op jit(solution)/shard_map/ppermute | solution.py:782
  37.0 3.7 %collective-permute-done.9.right_ref.right.refs_2_ = bf16[320,256]{1,0:T(8,128)(2,1)S(1)} collective-permute-done((bf16[320,256]{1,0:T(8,128)(2,1)S(1)}, bf16[320,256]{1,0:T(8,128)(2,1)S(1)}, u32[]{:S(2)}, u32[]{:S(2)}) %collective-permute-start.9) | collective-permute-done | bytes 163872 | tf_op jit(solution)/shard_map/ppermute | solution.py:782
  40.7 4.2 %collective-permute-done.8.left_ref.left.refs_1_ = bf16[320,256]{1,0:T(8,128)(2,1)S(1)} collective-permute-done((bf16[320,256]{1,0:T(8,128)(2,1)S(1)}, bf16[320,256]{1,0:T(8,128)(2,1)S(1)}, u32[]{:S(2)}, u32[]{:S(2)}) %collective-permute-start.8) | collective-permute-done | bytes 163872 | tf_op jit(solution)/shard_map/ppermute | solution.py:782
  44.9 0.9 collective-permute-start.12
  45.8 1.8 %collective-permute-start.13 = (bf16[768,256]{1,0:T(8,128)(2,1)S(1)}, bf16[768,256]{1,0:T(8,128)(2,1)S(1)}, u32[]{:S(2)}, u32[]{:S(2)}) collective-permute-start(bf16[768,256]{1,0:T(8,128)(2,1)S(1)} %collective-permute-done.7.refs_10_), channel_id=1, source_target_pairs={{0,192},{64,0},{128,64},{192,128},{1,193},{65,1},{129,65},{193,129... | collective-permute-start | bytes 1179656 | tf_op jit(solution)/shard_map/ppermute | solution.py:782
  47.7 3.6 %collective-permute-start.11 = (bf16[160,256]{1,0:T(8,128)(2,1)S(1)}, bf16[160,256]{1,0:T(8,128)(2,1)S(1)}, u32[]{:S(2)}, u32[]{:S(2)}) collective-permute-start(bf16[160,256]{1,0:T(8,128)(2,1)S(1)} %get-tuple-element.63), channel_id=1, source_target_pairs={{0,48},{8,56},{16,0},{24,8},{32,16},{40,24},{48,32},{56,40},{1,49}... | collective-permute-start | bytes 245768 | tf_op jit(solution)/shard_map/ppermute | solution.py:782
  51.2 2.4 %collective-permute-done.10.far.refs_3_ = bf16[160,256]{1,0:T(8,128)(2,1)S(1)} collective-permute-done((bf16[160,256]{1,0:T(8,128)(2,1)S(1)}, bf16[160,256]{1,0:T(8,128)(2,1)S(1)}, u32[]{:S(2)}, u32[]{:S(2)}) %collective-permute-start.10) | collective-permute-done | bytes 81952 | tf_op jit(solution)/shard_map/ppermute | solution.py:782
  54.0 3.2 %span_attend.2 = (f32[576,256]{1,0:T(8,128)S(1)}, f32[576,128]{1,0:T(8,128)S(1)}) custom-call(f32[2]{0:T(128)S(1)} %copy-done.9, bf16[320,256]{1,0:T(8,128)(2,1)S(1)} %join.2.own.refs_0_, bf16[320,256]{1,0:T(8,128)(2,1)S(1)} %collective-permute-done.8.left_ref.left.refs_1_, bf16[320,256]{1,0:T(8,128)(2,1)S(1)} %collective-permute-done.9.right_ref.right.refs_2_, ...), custom_call_target="tpu_custom_call" | custom-call | flops 603979776 | bytes 1048576 | tf_op jit(solution)/shard_map/span_attend/pallas_call | solution.py:356
  57.2 2.2 %collective-permute-start.15 = (bf16[16,256]{1,0:T(8,128)(2,1)S(1)}, bf16[16,256]{1,0:T(8,128)(2,1)S(1)}, u32[]{:S(2)}, u32[]{:S(2)}) collective-permute-start(bf16[16,256]{1,0:T(8,128)(2,1)S(1)} %added.1.refs_13_), channel_id=1, source_target_pairs={{0,128},{64,192},{128,0},{192,64},{1,129},{65,193},{129,1},{193,65... | collective-permute-start | bytes 24584 | tf_op jit(solution)/shard_map/ppermute | solution.py:777
  59.4 3.2 %span_attend.3 = (f32[576,256]{1,0:T(8,128)S(1)}, f32[576,128]{1,0:T(8,128)S(1)}) custom-call(f32[2]{0:T(128)S(1)} %copy-done.9, bf16[320,256]{1,0:T(8,128)(2,1)S(1)} %join.2.own.refs_0_, bf16[320,256]{1,0:T(8,128)(2,1)S(1)} %collective-permute-done.8.left_ref.left.refs_1_, bf16[320,256]{1,0:T(8,128)(2,1)S(1)} %collective-permute-done.9.right_ref.right.refs_2_, ...), custom_call_target="tpu_custom_call" | custom-call | flops 603979776 | bytes 1048576 | tf_op jit(solution)/shard_map/span_attend/pallas_call | solution.py:356
  62.6 9.8 %cache_attend.1 = bf16[8,160,256]{2,1,0:T(8,128)(2,1)S(1)} custom-call(f32[2]{0:T(128)S(1)} %copy-done.9, bf16[320,256]{1,0:T(8,128)(2,1)S(1)} %join.2.own.refs_0_, bf16[320,256]{1,0:T(8,128)(2,1)S(1)} %collective-permute-done.8.left_ref.left.refs_1_, bf16[320,256]{1,0:T(8,128)(2,1)S(1)} %collective-permute-done.9.right_ref.right.refs_2_, ...), custom_call_target="tpu_custom_call" | custom-call | flops 2415919104 | bytes 2097152 | tf_op jit(solution)/shard_map/cache_attend/pallas_call | solution.py:453
  72.4 19.2 %all_to_all.15.parts_ref = bf16[8,160,256]{2,1,0:T(8,128)(2,1)S(1)} all-to-all(bf16[8,160,256]{2,1,0:T(8,128)(2,1)S(1)} %cache_attend.1), channel_id=1, replica_groups=mesh['y'=4,'z'=8,'xl'=2,'tp'=4] {'z'}, dimensions={0} | all-to-all | bytes 1310720 | tf_op jit(solution)/shard_map/all_to_all | solution.py:773
  91.6 1.4 merge.1.a_ref
  93.4 5.0 %collective-permute-done.17.b_ref = bf16[144,256]{1,0:T(8,128)(2,1)S(1)} collective-permute-done((bf16[144,256]{1,0:T(8,128)(2,1)S(1)}, bf16[144,256]{1,0:T(8,128)(2,1)S(1)}, u32[]{:S(2)}, u32[]{:S(2)}) %collective-permute-start.17) | collective-permute-done | bytes 73760 | tf_op jit(solution)/shard_map/ppermute | solution.py:777
  98.4 1.4 layer_product.1
  99.8 8.6 %collective-permute-start.18 = (bf16[144,2048]{1,0:T(8,128)(2,1)S(1)}, bf16[144,2048]{1,0:T(8,128)(2,1)S(1)}, u32[]{:S(2)}, u32[]{:S(2)}) collective-permute-start(bf16[144,2048]{1,0:T(8,128)(2,1)S(1)} %get-tuple-element.83), channel_id=1, source_target_pairs={{0,1},{1,0},{2,3},{3,2},{4,5},{5,4},{6,7},{7,6},{8,9},{9,8},{10,11... | collective-permute-start | bytes 1769480 | tf_op jit(solution)/shard_map/ppermute | solution.py:777
  108.4 1.6 %collective-permute-done.18.term_ref = bf16[144,2048]{1,0:T(8,128)(2,1)S(1)} collective-permute-done((bf16[144,2048]{1,0:T(8,128)(2,1)S(1)}, bf16[144,2048]{1,0:T(8,128)(2,1)S(1)}, u32[]{:S(2)}, u32[]{:S(2)}) %collective-permute-start.18) | collective-permute-done | bytes 589856 | tf_op jit(solution)/shard_map/ppermute | solution.py:777
  110.0 1.9 %short_project.1 = (bf16[128,512]{1,0:T(8,128)(2,1)S(1)}, bf16[8,32,256]{2,1,0:T(8,128)(2,1)}, bf16[32,512]{1,0:T(8,128)(2,1)S(1)}) custom-call(f32[144,2048]{1,0:T(8,128)S(1)} %get-tuple-element.82.sum_ref, bf16[144,2048]{1,0:T(8,128)(2,1)S(1)} %collective-permute-done.18.term_ref, bf16[3,2048,256]{2,1,0:T(8,128)(2,1)S(1)} %bitcast.2), custom_call_target="tpu_custom_call" | custom-call | flops 100663296 | bytes 3670016 | tf_op jit(solution)/shard_map/short_project/pallas_call | solution.py:629
  112.0 2.8 %collective-permute-done.19.b_ref = bf16[32,512]{1,0:T(8,128)(2,1)S(1)} collective-permute-done((bf16[32,512]{1,0:T(8,128)(2,1)S(1)}, bf16[32,512]{1,0:T(8,128)(2,1)S(1)}, u32[]{:S(2)}, u32[]{:S(2)}) %collective-permute-start.19) | collective-permute-done | bytes 32800 | tf_op jit(solution)/shard_map/ppermute | solution.py:777
  114.7 3.4 %all-to-all-start.1 = ((bf16[8,32,256]{2,1,0:T(8,128)(2,1)}), bf16[8,32,256]{2,1,0:T(8,128)(2,1)S(1)}, u32[]{:S(2)}, u32[]{:S(2)}) async-start(bf16[8,32,256]{2,1,0:T(8,128)(2,1)} %get-tuple-element.87), calls=%async_computation.1 | async-start | bytes 262144 | tf_op jit(solution)/shard_map/all_to_all | solution.py:773
  118.1 1.6 %collective-permute-start.22 = (bf16[64,512]{1,0:T(8,128)(2,1)S(1)}, bf16[64,512]{1,0:T(8,128)(2,1)S(1)}, u32[]{:S(2)}, u32[]{:S(2)}) collective-permute-start(bf16[64,512]{1,0:T(8,128)(2,1)S(1)} %join.3.refs_0_), channel_id=1, source_target_pairs={{0,192},{64,0},{128,64},{192,128},{1,193},{65,1},{129,65},{193,129... | collective-permute-start | bytes 196616 | tf_op jit(solution)/shard_map/ppermute | solution.py:782
  119.7 0.4 collective-permute-start.21
  120.4 0.9 collective-permute-done.22.refs_3_
  121.3 3.1 %collective-permute-done.21.refs_2_ = bf16[64,512]{1,0:T(8,128)(2,1)S(1)} collective-permute-done((bf16[64,512]{1,0:T(8,128)(2,1)S(1)}, bf16[64,512]{1,0:T(8,128)(2,1)S(1)}, u32[]{:S(2)}, u32[]{:S(2)}) %collective-permute-start.21) | collective-permute-done | bytes 65568 | tf_op jit(solution)/shard_map/ppermute | solution.py:782
  124.4 0.9 collective-permute-done.20.refs_1_
  125.3 0.7 all-to-all-done.1.q_ref
  126.0 1.0 short_attend.1
  127.0 14.2 %all_to_all.16.parts_ref = bf16[8,32,384]{2,1,0:T(8,128)(2,1)S(1)} all-to-all(bf16[8,32,384]{2,1,0:T(8,128)(2,1)S(1)} %short_attend.1), channel_id=1, replica_groups=mesh['y'=4,'z'=8,'xl'=2,'tp'=4] {'z'}, dimensions={0} | all-to-all | bytes 393216 | tf_op jit(solution)/shard_map/all_to_all | solution.py:773
  141.2 0.5 short_merge.1
  141.7 4.6 %collective-permute-start.23 = (bf16[32,512]{1,0:T(8,128)(2,1)S(1)}, bf16[32,512]{1,0:T(8,128)(2,1)S(1)}, u32[]{:S(2)}, u32[]{:S(2)}) collective-permute-start(bf16[32,512]{1,0:T(8,128)(2,1)S(1)} %get-tuple-element.90), channel_id=1, source_target_pairs={{0,1},{1,0},{2,3},{3,2},{4,5},{5,4},{6,7},{7,6},{8,9},{9,8},{10,11... | collective-permute-start | bytes 98312 | tf_op jit(solution)/shard_map/ppermute | solution.py:777
  146.3 3.2 %collective-permute-start.25 = (bf16[32,512]{1,0:T(8,128)(2,1)S(1)}, bf16[32,512]{1,0:T(8,128)(2,1)S(1)}, u32[]{:S(2)}, u32[]{:S(2)}) collective-permute-start(bf16[32,512]{1,0:T(8,128)(2,1)S(1)} %get-tuple-element.92), channel_id=1, source_target_pairs={{0,3},{1,2},{2,1},{3,0},{4,7},{5,6},{6,5},{7,4},{8,11},{9,10},{10,... | collective-permute-start | bytes 98312 | tf_op jit(solution)/shard_map/ppermute | solution.py:777
  149.6 1.0 collective-permute-done.24.refs_2_
  150.6 1.1 collective-permute-done.25.refs_3_
  151.7 0.9 final_sum.1
  (50 shorter events, 1.5 us)
Async XLA Ops:
  0.8 9.8 %collective-permute-start.1 = (bf16[16,2048]{1,0:T(8,128)(2,1)S(1)}, bf16[16,2048]{1,0:T(8,128)(2,1)S(1)}, u32[]{:S(2)}, u32[]{:S(2)}) collective-permute-start(bf16[16,2048]{1,0:T(8,128)(2,1)S(1)} %slice.3), channel_id=1, source_target_pairs={{0,4},{1,5},{2,6},{3,7},{4,8},{5,9},{6,10},{7,11},{8,12},{9,13},{1... | collective-permute-start | bytes 196616 | tf_op jit(solution)/shard_map/ppermute | solution.py:811
  5.5 5.2 %copy-start.8 = (bf16[16,256]{1,0:T(8,128)(2,1)}, bf16[16,256]{1,0:T(8,128)(2,1)S(1)}, u32[]{:S(2)}) copy-start(bf16[16,256]{1,0:T(8,128)(2,1)S(1)} %own_count.1.a_hbm) | copy-start | bytes 24580
  5.5 5.2 %collective-permute-start = (bf16[16,256]{1,0:T(8,128)(2,1)S(1)}, bf16[16,256]{1,0:T(8,128)(2,1)S(1)}, u32[]{:S(2)}, u32[]{:S(2)}) collective-permute-start(bf16[16,256]{1,0:T(8,128)(2,1)S(1)} %own_count.1.a_hbm), channel_id=1, source_target_pairs={{0,4},{4,0},{1,5},{5,1},{2,6},{6,2},{3,7},{7,3},{8,12},{12,8},{9,1... | collective-permute-start | bytes 24584 | tf_op jit(solution)/shard_map/ppermute | solution.py:777
  7.2 21.9 %copy-start.4 = (bf16[256,2048]{1,0:T(8,128)(2,1)S(1)}, bf16[256,2048]{1,0:T(8,128)(2,1)}, u32[]{:S(2)}) copy-start(bf16[256,2048]{1,0:T(8,128)(2,1)} %wa_hbm.1) | copy-start | bytes 3145732
  10.6 3.0 %copy-start.2 = (bf16[768,256]{1,0:T(8,128)(2,1)S(1)}, bf16[768,256]{1,0:T(8,128)(2,1)}, u32[]{:S(2)}) copy-start(bf16[768,256]{1,0:T(8,128)(2,1)} %get-tuple-element.56.refs_5_) | copy-start | bytes 1179652
  10.7 43.4 %copy-start.9 = (f32[2]{0:T(128)S(1)}, f32[2]{0:T(128)}, u32[]{:S(2)}) copy-start(f32[2]{0:T(128)} %slope_ref.6) | copy-start | bytes 28
  10.7 0.6 copy-start.11
  10.7 0.6 copy-start.6
  13.6 10.9 %collective-permute-start.4 = (bf16[768,256]{1,0:T(8,128)(2,1)S(1)}, bf16[768,256]{1,0:T(8,128)(2,1)S(1)}, u32[]{:S(2)}, u32[]{:S(2)}) collective-permute-start(bf16[768,256]{1,0:T(8,128)(2,1)S(1)} %copy-done.2), channel_id=1, source_target_pairs={{0,192},{64,0},{128,64},{192,128},{1,193},{65,1},{129,65},{193,129... | collective-permute-start | bytes 1179656 | tf_op jit(solution)/shard_map/ppermute | solution.py:782
  17.6 10.0 %collective-permute-start.3 = (bf16[768,256]{1,0:T(8,128)(2,1)S(1)}, bf16[768,256]{1,0:T(8,128)(2,1)S(1)}, u32[]{:S(2)}, u32[]{:S(2)}) collective-permute-start(bf16[768,256]{1,0:T(8,128)(2,1)S(1)} %copy-done.2), channel_id=1, source_target_pairs={{0,64},{64,128},{128,192},{192,0},{1,65},{65,129},{129,193},{193,1... | collective-permute-start | bytes 1179656 | tf_op jit(solution)/shard_map/ppermute | solution.py:782
  17.6 10.0 %collective-permute-start.2 = (bf16[768,256]{1,0:T(8,128)(2,1)S(1)}, bf16[768,256]{1,0:T(8,128)(2,1)S(1)}, u32[]{:S(2)}, u32[]{:S(2)}) collective-permute-start(bf16[768,256]{1,0:T(8,128)(2,1)S(1)} %copy-done.2), channel_id=1, source_target_pairs={{0,4},{4,0},{1,5},{5,1},{2,6},{6,2},{3,7},{7,3},{8,12},{12,8},{9,1... | collective-permute-start | bytes 1179656 | tf_op jit(solution)/shard_map/ppermute | solution.py:777
  17.6 3.8 %collective-permute-start.5 = (bf16[160,256]{1,0:T(8,128)(2,1)}, bf16[160,256]{1,0:T(8,128)(2,1)S(1)}, u32[]{:S(2)}, u32[]{:S(2)}) collective-permute-start(bf16[160,256]{1,0:T(8,128)(2,1)} %mark.1.a_ref), channel_id=1, source_target_pairs={{0,8},{8,0},{16,24},{24,16},{32,40},{40,32},{48,56},{56,48},{1,9},... | collective-permute-start | bytes 245768 | tf_op jit(solution)/shard_map/ppermute | solution.py:777
  27.6 17.3 %collective-permute-start.7 = (bf16[768,256]{1,0:T(8,128)(2,1)S(1)}, bf16[768,256]{1,0:T(8,128)(2,1)S(1)}, u32[]{:S(2)}, u32[]{:S(2)}) collective-permute-start(bf16[768,256]{1,0:T(8,128)(2,1)S(1)} %collective-permute-done.2.refs_6_), channel_id=1, source_target_pairs={{0,192},{64,0},{128,64},{192,128},{1,193},{65,1},{129,65},{193,129... | collective-permute-start | bytes 1179656 | tf_op jit(solution)/shard_map/ppermute | solution.py:782
  28.8 16.1 %collective-permute-start.6 = (bf16[768,256]{1,0:T(8,128)(2,1)S(1)}, bf16[768,256]{1,0:T(8,128)(2,1)S(1)}, u32[]{:S(2)}, u32[]{:S(2)}) collective-permute-start(bf16[768,256]{1,0:T(8,128)(2,1)S(1)} %collective-permute-done.2.refs_6_), channel_id=1, source_target_pairs={{0,64},{64,128},{128,192},{192,0},{1,65},{65,129},{129,193},{193,1... | collective-permute-start | bytes 1179656 | tf_op jit(solution)/shard_map/ppermute | solution.py:782
  29.1 43.3 %collective-permute-start.16 = (bf16[256,2048]{1,0:T(8,128)(2,1)S(1)}, bf16[256,2048]{1,0:T(8,128)(2,1)S(1)}, u32[]{:S(2)}, u32[]{:S(2)}) collective-permute-start(bf16[256,2048]{1,0:T(8,128)(2,1)S(1)} %copy-done.4), channel_id=1, source_target_pairs={{0,2},{1,3},{2,0},{3,1},{4,6},{5,7},{6,4},{7,5},{8,10},{9,11},{10,... | collective-permute-start | bytes 3145736 | tf_op jit(solution)/shard_map/ppermute | solution.py:777
  31.5 0.9 copy-start.5
  32.4 8.3 %collective-permute-start.9 = (bf16[320,256]{1,0:T(8,128)(2,1)S(1)}, bf16[320,256]{1,0:T(8,128)(2,1)S(1)}, u32[]{:S(2)}, u32[]{:S(2)}) collective-permute-start(bf16[320,256]{1,0:T(8,128)(2,1)S(1)} %join.2.own.refs_0_), channel_id=1, source_target_pairs={{0,48},{8,56},{16,0},{24,8},{32,16},{40,24},{48,32},{56,40},{1,49}... | collective-permute-start | bytes 491528 | tf_op jit(solution)/shard_map/ppermute | solution.py:782
  37.0 7.8 %collective-permute-start.8 = (bf16[320,256]{1,0:T(8,128)(2,1)S(1)}, bf16[320,256]{1,0:T(8,128)(2,1)S(1)}, u32[]{:S(2)}, u32[]{:S(2)}) collective-permute-start(bf16[320,256]{1,0:T(8,128)(2,1)S(1)} %join.2.own.refs_0_), channel_id=1, source_target_pairs={{0,16},{8,24},{16,32},{24,40},{32,48},{40,56},{48,0},{56,8},{1,17}... | collective-permute-start | bytes 491528 | tf_op jit(solution)/shard_map/ppermute | solution.py:782
  44.9 9.1 %collective-permute-start.12 = (bf16[768,256]{1,0:T(8,128)(2,1)S(1)}, bf16[768,256]{1,0:T(8,128)(2,1)S(1)}, u32[]{:S(2)}, u32[]{:S(2)}) collective-permute-start(bf16[768,256]{1,0:T(8,128)(2,1)S(1)} %collective-permute-done.3.refs_7_), channel_id=1, source_target_pairs={{0,64},{64,128},{128,192},{192,0},{1,65},{65,129},{129,193},{193,1... | collective-permute-start | bytes 1179656 | tf_op jit(solution)/shard_map/ppermute | solution.py:782
  45.8 8.2 %collective-permute-start.13 = (bf16[768,256]{1,0:T(8,128)(2,1)S(1)}, bf16[768,256]{1,0:T(8,128)(2,1)S(1)}, u32[]{:S(2)}, u32[]{:S(2)}) collective-permute-start(bf16[768,256]{1,0:T(8,128)(2,1)S(1)} %collective-permute-done.7.refs_10_), channel_id=1, source_target_pairs={{0,192},{64,0},{128,64},{192,128},{1,193},{65,1},{129,65},{193,129... | collective-permute-start | bytes 1179656 | tf_op jit(solution)/shard_map/ppermute | solution.py:782
  47.6 6.1 %collective-permute-start.10 = (bf16[160,256]{1,0:T(8,128)(2,1)S(1)}, bf16[160,256]{1,0:T(8,128)(2,1)S(1)}, u32[]{:S(2)}, u32[]{:S(2)}) collective-permute-start(bf16[160,256]{1,0:T(8,128)(2,1)S(1)} %get-tuple-element.62), channel_id=1, source_target_pairs={{0,16},{8,24},{16,32},{24,40},{32,48},{40,56},{48,0},{56,8},{1,17}... | collective-permute-start | bytes 245768 | tf_op jit(solution)/shard_map/ppermute | solution.py:782
  47.7 6.0 %collective-permute-start.11 = (bf16[160,256]{1,0:T(8,128)(2,1)S(1)}, bf16[160,256]{1,0:T(8,128)(2,1)S(1)}, u32[]{:S(2)}, u32[]{:S(2)}) collective-permute-start(bf16[160,256]{1,0:T(8,128)(2,1)S(1)} %get-tuple-element.63), channel_id=1, source_target_pairs={{0,48},{8,56},{16,0},{24,8},{32,16},{40,24},{48,32},{56,40},{1,49}... | collective-permute-start | bytes 245768 | tf_op jit(solution)/shard_map/ppermute | solution.py:782
  53.7 3.5 %collective-permute-start.14 = (bf16[16,256]{1,0:T(8,128)(2,1)S(1)}, bf16[16,256]{1,0:T(8,128)(2,1)S(1)}, u32[]{:S(2)}, u32[]{:S(2)}) collective-permute-start(bf16[16,256]{1,0:T(8,128)(2,1)S(1)} %plane_counts.1.a_ref), channel_id=1, source_target_pairs={{0,64},{64,0},{128,192},{192,128},{1,65},{65,1},{129,193},{193,129... | collective-permute-start | bytes 24584 | tf_op jit(solution)/shard_map/ppermute | solution.py:777
  57.2 5.4 %collective-permute-start.15 = (bf16[16,256]{1,0:T(8,128)(2,1)S(1)}, bf16[16,256]{1,0:T(8,128)(2,1)S(1)}, u32[]{:S(2)}, u32[]{:S(2)}) collective-permute-start(bf16[16,256]{1,0:T(8,128)(2,1)S(1)} %added.1.refs_13_), channel_id=1, source_target_pairs={{0,128},{64,192},{128,0},{192,64},{1,129},{65,193},{129,1},{193,65... | collective-permute-start | bytes 24584 | tf_op jit(solution)/shard_map/ppermute | solution.py:777
  62.6 35.8 %copy-start.1 = (bf16[128,2048]{1,0:T(8,128)(2,1)S(1)}, bf16[128,2048]{1,0:T(8,128)(2,1)}, u32[]{:S(2)}) copy-start(bf16[128,2048]{1,0:T(8,128)(2,1)} %tok_hbm.3) | copy-start | bytes 1572868
  62.6 35.8 %copy-start.7 = (bf16[16,2048]{1,0:T(8,128)(2,1)S(1)}, bf16[16,2048]{1,0:T(8,128)(2,1)}, u32[]{:S(2)}) copy-start(bf16[16,2048]{1,0:T(8,128)(2,1)} %copy-done.6) | copy-start | bytes 196612
  72.4 37.6 %copy-start = (bf16[2048,3,256]{2,0,1:T(8,128)(2,1)S(1)}, bf16[2048,3,256]{2,0,1:T(8,128)(2,1)}, u32[]{:S(2)}) copy-start(bf16[2048,3,256]{2,0,1:T(8,128)(2,1)} %param.17) | copy-start | bytes 9437188
  93.0 5.3 %collective-permute-start.17 = (bf16[144,256]{1,0:T(8,128)(2,1)S(1)}, bf16[144,256]{1,0:T(8,128)(2,1)S(1)}, u32[]{:S(2)}, u32[]{:S(2)}) collective-permute-start(bf16[144,256]{1,0:T(8,128)(2,1)S(1)} %merge.1.a_ref), channel_id=1, source_target_pairs={{0,2},{1,3},{2,0},{3,1},{4,6},{5,7},{6,4},{7,5},{8,10},{9,11},{10,... | collective-permute-start | bytes 221192 | tf_op jit(solution)/shard_map/ppermute | solution.py:777
  99.8 26.2 %copy-start.10 = (f32[2]{0:T(128)S(1)}, f32[2]{0:T(128)}, u32[]{:S(2)}) copy-start(f32[2]{0:T(128)} %slope_ref.7) | copy-start | bytes 28
  99.8 10.3 %collective-permute-start.18 = (bf16[144,2048]{1,0:T(8,128)(2,1)S(1)}, bf16[144,2048]{1,0:T(8,128)(2,1)S(1)}, u32[]{:S(2)}, u32[]{:S(2)}) collective-permute-start(bf16[144,2048]{1,0:T(8,128)(2,1)S(1)} %get-tuple-element.83), channel_id=1, source_target_pairs={{0,1},{1,0},{2,3},{3,2},{4,5},{5,4},{6,7},{7,6},{8,9},{9,8},{10,11... | collective-permute-start | bytes 1769480 | tf_op jit(solution)/shard_map/ppermute | solution.py:777
  110.0 31.1 %copy-start.3 = (bf16[256,2048]{1,0:T(8,128)(2,1)S(1)}, bf16[256,2048]{1,0:T(8,128)(2,1)}, u32[]{:S(2)}) copy-start(bf16[256,2048]{1,0:T(8,128)(2,1)} %w_ref.1) | copy-start | bytes 3145732
  112.0 2.8 %collective-permute-start.19 = (bf16[32,512]{1,0:T(8,128)(2,1)S(1)}, bf16[32,512]{1,0:T(8,128)(2,1)S(1)}, u32[]{:S(2)}, u32[]{:S(2)}) collective-permute-start(bf16[32,512]{1,0:T(8,128)(2,1)S(1)} %get-tuple-element.86.a_ref), channel_id=1, source_target_pairs={{0,4},{4,0},{1,5},{5,1},{2,6},{6,2},{3,7},{7,3},{8,12},{12,8},{9,1... | collective-permute-start | bytes 98312 | tf_op jit(solution)/shard_map/ppermute | solution.py:777
  114.7 11.2 %all-to-all-start.1 = ((bf16[8,32,256]{2,1,0:T(8,128)(2,1)}), bf16[8,32,256]{2,1,0:T(8,128)(2,1)S(1)}, u32[]{:S(2)}, u32[]{:S(2)}) async-start(bf16[8,32,256]{2,1,0:T(8,128)(2,1)} %get-tuple-element.87), calls=%async_computation.1 | async-start | bytes 262144 | tf_op jit(solution)/shard_map/all_to_all | solution.py:773
  118.1 3.2 %collective-permute-start.22 = (bf16[64,512]{1,0:T(8,128)(2,1)S(1)}, bf16[64,512]{1,0:T(8,128)(2,1)S(1)}, u32[]{:S(2)}, u32[]{:S(2)}) collective-permute-start(bf16[64,512]{1,0:T(8,128)(2,1)S(1)} %join.3.refs_0_), channel_id=1, source_target_pairs={{0,192},{64,0},{128,64},{192,128},{1,193},{65,1},{129,65},{193,129... | collective-permute-start | bytes 196616 | tf_op jit(solution)/shard_map/ppermute | solution.py:782
  119.7 4.7 %collective-permute-start.21 = (bf16[64,512]{1,0:T(8,128)(2,1)S(1)}, bf16[64,512]{1,0:T(8,128)(2,1)S(1)}, u32[]{:S(2)}, u32[]{:S(2)}) collective-permute-start(bf16[64,512]{1,0:T(8,128)(2,1)S(1)} %join.3.refs_0_), channel_id=1, source_target_pairs={{0,128},{64,192},{128,0},{192,64},{1,129},{65,193},{129,1},{193,65... | collective-permute-start | bytes 196616 | tf_op jit(solution)/shard_map/ppermute | solution.py:782
  120.1 5.2 %collective-permute-start.20 = (bf16[64,512]{1,0:T(8,128)(2,1)S(1)}, bf16[64,512]{1,0:T(8,128)(2,1)S(1)}, u32[]{:S(2)}, u32[]{:S(2)}) collective-permute-start(bf16[64,512]{1,0:T(8,128)(2,1)S(1)} %join.3.refs_0_), channel_id=1, source_target_pairs={{0,64},{64,128},{128,192},{192,0},{1,65},{65,129},{129,193},{193,1... | collective-permute-start | bytes 196616 | tf_op jit(solution)/shard_map/ppermute | solution.py:782
  141.7 7.9 %collective-permute-start.23 = (bf16[32,512]{1,0:T(8,128)(2,1)S(1)}, bf16[32,512]{1,0:T(8,128)(2,1)S(1)}, u32[]{:S(2)}, u32[]{:S(2)}) collective-permute-start(bf16[32,512]{1,0:T(8,128)(2,1)S(1)} %get-tuple-element.90), channel_id=1, source_target_pairs={{0,1},{1,0},{2,3},{3,2},{4,5},{5,4},{6,7},{7,6},{8,9},{9,8},{10,11... | collective-permute-start | bytes 98312 | tf_op jit(solution)/shard_map/ppermute | solution.py:777
  146.3 4.3 %collective-permute-start.24 = (bf16[32,512]{1,0:T(8,128)(2,1)S(1)}, bf16[32,512]{1,0:T(8,128)(2,1)S(1)}, u32[]{:S(2)}, u32[]{:S(2)}) collective-permute-start(bf16[32,512]{1,0:T(8,128)(2,1)S(1)} %get-tuple-element.91), channel_id=1, source_target_pairs={{0,2},{1,3},{2,0},{3,1},{4,6},{5,7},{6,4},{7,5},{8,10},{9,11},{10,... | collective-permute-start | bytes 98312 | tf_op jit(solution)/shard_map/ppermute | solution.py:777
  146.3 5.3 %collective-permute-start.25 = (bf16[32,512]{1,0:T(8,128)(2,1)S(1)}, bf16[32,512]{1,0:T(8,128)(2,1)S(1)}, u32[]{:S(2)}, u32[]{:S(2)}) collective-permute-start(bf16[32,512]{1,0:T(8,128)(2,1)S(1)} %get-tuple-element.92), channel_id=1, source_target_pairs={{0,3},{1,2},{2,1},{3,0},{4,7},{5,6},{6,5},{7,4},{8,11},{9,10},{10,... | collective-permute-start | bytes 98312 | tf_op jit(solution)/shard_map/ppermute | solution.py:777

commit v11 on v10

--- a/solution.py
+++ b/solution.py
@@ -607,9 +607,7 @@
 
     @pl.when(step == 0)
     def _():
-        scaled = (out * SCALE2).astype(BF16)
-        for c in range(q_ref.shape[0]):
-            q_ref[c] = scaled
+        q_ref[...] = (out * SCALE2).astype(BF16)
 
     @pl.when(step == 1)
     def _():
@@ -620,12 +618,12 @@
         kv_ref[:, width:] = out.astype(BF16)
 
 
-def short_project(total, term, weight3, copies):
+def short_project(total, term, weight3):
     n, d = total.shape[0] - HALO, total.shape[1]
     groups = n // GROUP
     width = weight3.shape[2]
     whole = lambda shape: pl.BlockSpec(shape, lambda i: (0,) * len(shape))
-    shapes = [(n, d // 4), (copies, groups, width), (groups, 2 * width)]
+    shapes = [(n, d // 4), (groups, width), (groups, 2 * width)]
     return pl.pallas_call(
         short_project_kernel,
         grid=(3,),
@@ -640,15 +638,21 @@
     )(total, term, weight3)
 
 
-def short_attend_kernel(slope_ref, q_ref, *refs):
-    key_refs, out_ref = refs[:4], refs[4]
+def short_attend_kernel(slope_ref, *refs):
+    queries, key_refs, out_ref = refs[:4], refs[4:8], refs[8]
     y, z, xl = place_of_device()
     blocks, groups, padded = out_ref.shape
     width = padded - HS
     heads = width // HS
     n = blocks * groups
     row = lax.broadcasted_iota(jnp.int32, (n, 1), 0)
-    row_pos = (y * 16 + xl + 2 * (row // groups)) * groups + row % groups
+    zs = row // groups
+    row_pos = (y * 16 + xl + 2 * zs) * groups + row % groups
+    back = (z // 2 + 4 - zs // 2) % 4
+    came = (2 * back + (zs ^ z) % 2) * groups + row % groups
+    order = jnp.where(lax.broadcasted_iota(jnp.int32, (n, n), 1) == came, 1.0, 0.0).astype(BF16)
+    lined = jnp.concatenate([r[...] for r in queries], axis=0)
+    lined = jnp.dot(order, lined, preferred_element_type=F32).astype(BF16)
     key = lax.broadcasted_iota(jnp.int32, (1, n), 1)
     ys = (y + 4 - key // (2 * groups)) % 4
     side = jnp.where((key // groups) % 2 == 1, 1 - xl, xl)
@@ -661,7 +665,7 @@
     for h in range(heads):
         cols = slice(h * HS, (h + 1) * HS)
         cols_v = slice(width + h * HS, width + (h + 1) * HS)
-        q = q_ref[:, :, cols].reshape(n, HS)
+        q = lined[:, cols]
         k = jnp.concatenate([r[:, cols] for r in key_refs], axis=0)
         v = jnp.concatenate([r[:, cols_v] for r in key_refs], axis=0)
         s = dot_t(q, k) + (slope_ref[h] * LOG2E) * spot
@@ -679,19 +683,19 @@
 
 
 def short_attend(slopes, queries, keys):
-    blocks, groups, width = queries.shape
+    blocks, groups, width = 8, queries[0].shape[0] // 2, queries[0].shape[1]
     n = blocks * groups
     smem = pl.BlockSpec(memory_space=SMEM)
     vmem = pl.BlockSpec(memory_space=VMEM)
     return pl.pallas_call(
         short_attend_kernel,
-        in_specs=[smem] + [vmem] * 5,
+        in_specs=[smem] + [vmem] * 8,
         out_specs=vmem,
         out_shape=jax.ShapeDtypeStruct((blocks, groups, width + HS), BF16),
         compiler_params=params(16),
         cost_estimate=cost(4 * n * n * width, 8 * n * width),
         name="short_attend",
-    )(slopes, queries, *keys)
+    )(slopes, *queries, *keys)
 
 
 def short_merge_kernel(heads, parts_ref, w_ref, *outs):
@@ -804,7 +808,6 @@
 ):
     axes = ("y", "z", "xl", "tp")
     slots = cache_keys.shape[0]
-    nz = lax.axis_size("z")
     count = own_count(cache_count, cache_keys.shape[1])
     other_count = swap(count, "xl")
     n, tp = lax.axis_size(axes), lax.axis_size("tp")
@@ -827,7 +830,7 @@
     far, far_other = moved(left, "y", 1), moved(right_other, "y", -1)
     near = halves(left_pair, right_pair)
     queries = [pair, left_pair, right_pair, moved(near[0], "z", 2), moved(near[1], "z", -2)]
-    crossed = swap(after(output_weight, other), "tp", 2)
+    crossed = swap(after(output_weight, left), "tp", 2)
     packs = [pack, other, left, left_other, right, right_other, far, far_other]
     plane = plane_counts(queries)
     beside = swap(plane, "y")
@@ -850,13 +853,12 @@
         total,
         swap(term, "tp", 1),
         jnp.transpose(short_project_weight, (1, 0, 2)),
-        nz,
     )
-    mate = swap(skv, "xl")
-    sq, mate = lax.optimization_barrier((sq, mate))
-    pair = join(skv, mate)
+    pair = join(sq, swap(sq, "z"))
+    queries = [pair] + [moved(pair, "z", by) for by in (2, 4, 6)]
+    pair = join(skv, swap(skv, "xl"))
     keys = [pair] + [moved(pair, "y", by) for by in (1, 2, 3)]
-    sparts = short_attend(short_slope, exchange(sq, "z"), keys)
+    sparts = short_attend(short_slope, queries, keys)
     terms = short_merge(exchange(sparts, "z"), short_output)
     terms = [swap(t, "tp", flip) if flip else t for flip, t in enumerate(terms)]
     return final_sum(layer, terms)

time: 153 us -> 153 us (level)
  blocking collectives: 33.3 us -> 30.8 us
  waiting for transfers between devices: 36.9 us -> 39.1 us
    all_to_all x1 -> x0, starting transfers between devices: 3.37 us -> none  [exchange(): return lax.all_to_all(blocks, axis, 0, 0)]
    all_to_all x2, blocking collectives: 33.3 us -> 30.8 us  [exchange(): return lax.all_to_all(blocks, axis, 0, 0)]
    ppermute x12 -> x13, starting transfers between devices: 23.9 us -> 26.4 us  [swap(): lax.ppermute(x, axis, [(i, i ^ flip) for i in range(lax.axis_size(axis))])]
    ppermute x13 -> x16, starting transfers between devices: 18.7 us -> 20.5 us  [moved(): return lax.ppermute(x, axis, [(i, (i + by) % n) for i in range(n)])]
    ppermute x13 -> x16, waiting for transfers between devices: 21.4 us -> 23.1 us  [moved(): return lax.ppermute(x, axis, [(i, (i + by) % n) for i in range(n)])]
    ppermute x12 -> x13, waiting for transfers between devices: 14.8 us -> 16 us  [swap(): lax.ppermute(x, axis, [(i, i ^ flip) for i in range(lax.axis_size(axis))])]
  transfers between devices with their start and end apart: 27 -> 30, of which waited for: 15 -> 15; matrix products, arithmetic and copies ran while one was open for 0% -> 0% of each run, Pallas kernels for 13% -> 13%
where the time goes in v11:
time: 153 us
  starting transfers between devices  50.9 us (33%)
  waiting for transfers between devices  39.1 us (26%)
  blocking collectives  30.8 us (20%)
  Pallas kernels  28.6 us (19%)
  local copies, waits for them, and re-layouts  2.39 us (2%)
    all_to_all x2, blocking collectives, exchange(): return lax.all_to_all(blocks, axis, 0, 0)  30.8 us
    ppermute x13, starting transfers between devices, swap(): lax.ppermute(x, axis, [(i, i ^ flip) for i in range(lax.axis_size(axis))])  26.4 us
    ppermute x16, waiting for transfers between devices, moved(): return lax.ppermute(x, axis, [(i, (i + by) % n) for i in range(n)])  23.1 us
    ppermute x16, starting transfers between devices, moved(): return lax.ppermute(x, axis, [(i, (i + by) % n) for i in range(n)])  20.5 us
    ppermute x13, waiting for transfers between devices, swap(): lax.ppermute(x, axis, [(i, i ^ flip) for i in range(lax.axis_size(axis))])  16 us
    pallas_call x1, Pallas kernels, cache_attend(): pl.pallas_call(functools.partial(cache_kernel, slots), grid=(2,), in_spec...  9.77 us
    pallas_call x2, Pallas kernels, span_attend(): pl.pallas_call(functools.partial(span_kernel, tile, slots), in_specs=[pl....  6.31 us
    ppermute x1, starting transfers between devices, on_device(): lax.ppermute(tokens[-HALO:], axes, [(i, i + tp) for i in range(n - tp)])  3.94 us
  transfers between devices with their start and end apart: 30, of which 15 were waited for; matrix products, arithmetic and copies ran while one was open for 0% of the time, Pallas kernels for 13%

profile of v11, /device:TPU:1, one launch (start us, length us, event | category | flops | bytes accessed | tf_op | source)
XLA Modules:
  0.0 152.7 jit_solution(10193572630891705902)
XLA Ops:
  0.0 0.8 slice.3
  0.8 3.9 %collective-permute-start.1 = (bf16[16,2048]{1,0:T(8,128)(2,1)S(1)}, bf16[16,2048]{1,0:T(8,128)(2,1)S(1)}, u32[]{:S(2)}, u32[]{:S(2)}) collective-permute-start(bf16[16,2048]{1,0:T(8,128)(2,1)S(1)} %slice.3), channel_id=1, source_target_pairs={{0,4},{1,5},{2,6},{3,7},{4,8},{5,9},{6,10},{7,11},{8,12},{9,13},{1... | collective-permute-start | bytes 196616 | tf_op jit(solution)/shard_map/ppermute | solution.py:814
  5.5 1.7 %collective-permute-start = (bf16[16,256]{1,0:T(8,128)(2,1)S(1)}, bf16[16,256]{1,0:T(8,128)(2,1)S(1)}, u32[]{:S(2)}, u32[]{:S(2)}) collective-permute-start(bf16[16,256]{1,0:T(8,128)(2,1)S(1)} %own_count.1.a_hbm), channel_id=1, source_target_pairs={{0,4},{4,0},{1,5},{5,1},{2,6},{6,2},{3,7},{7,3},{8,12},{12,8},{9,1... | collective-permute-start | bytes 24584 | tf_op jit(solution)/shard_map/ppermute | solution.py:781
  7.2 3.4 %project.1 = (bf16[128,256]{1,0:T(8,128)(2,1)}, bf16[768,256]{1,0:T(8,128)(2,1)}) custom-call(bf16[128,2048]{1,0:T(8,128)(2,1)} %tok_hbm.3, bf16[3,2048,256]{2,1,0:T(8,128)(2,1)} %bitcast.3, bf16[256,256]{1,0:T(8,128)(2,1)} %ck_hbm.1, bf16[256,256]{1,0:T(8,128)(2,1)} %cv_hbm.1), custom_call_target="tpu_custom_call" | custom-call | flops 402653184 | bytes 3670016 | tf_op jit(solution)/shard_map/project/pallas_call | solution.py:84
  10.7 0.6 copy-done.11
  11.3 2.3 %mark.1.a_ref = bf16[160,256]{1,0:T(8,128)(2,1)} custom-call(bf16[16,2048]{1,0:T(8,128)(2,1)} %copy-done.6, bf16[3,2048,256]{2,1,0:T(8,128)(2,1)} %bitcast.4, bf16[128,256]{1,0:T(8,128)(2,1)} %get-tuple-element.50.q_hbm, bf16[16,256]{1,0:T(8,128)(2,1)} %copy-done.8, bf16[16,256]{1,0:T(8,128)(2,1)} %copy-done.11), custom_call_target="tpu_custom_call" | custom-call | flops 16777216 | bytes 1048576 | tf_op jit(solution)/shard_map/mark/pallas_call | solution.py:162
  13.6 4.0 %collective-permute-start.4 = (bf16[768,256]{1,0:T(8,128)(2,1)S(1)}, bf16[768,256]{1,0:T(8,128)(2,1)S(1)}, u32[]{:S(2)}, u32[]{:S(2)}) collective-permute-start(bf16[768,256]{1,0:T(8,128)(2,1)S(1)} %copy-done.2), channel_id=1, source_target_pairs={{0,192},{64,0},{128,64},{192,128},{1,193},{65,1},{129,65},{193,129... | collective-permute-start | bytes 1179656 | tf_op jit(solution)/shard_map/ppermute | solution.py:786
  18.1 3.4 %collective-permute-done.5.b_ref = bf16[160,256]{1,0:T(8,128)(2,1)S(1)} collective-permute-done((bf16[160,256]{1,0:T(8,128)(2,1)}, bf16[160,256]{1,0:T(8,128)(2,1)S(1)}, u32[]{:S(2)}, u32[]{:S(2)}) %collective-permute-start.5) | collective-permute-done | bytes 81952 | tf_op jit(solution)/shard_map/ppermute | solution.py:781
  21.4 3.1 %collective-permute-done.4.refs_9_ = bf16[768,256]{1,0:T(8,128)(2,1)S(1)} collective-permute-done((bf16[768,256]{1,0:T(8,128)(2,1)S(1)}, bf16[768,256]{1,0:T(8,128)(2,1)S(1)}, u32[]{:S(2)}, u32[]{:S(2)}) %collective-permute-start.4) | collective-permute-done | bytes 393248 | tf_op jit(solution)/shard_map/ppermute | solution.py:786
  24.5 3.1 %collective-permute-done.3.refs_7_ = bf16[768,256]{1,0:T(8,128)(2,1)S(1)} collective-permute-done((bf16[768,256]{1,0:T(8,128)(2,1)S(1)}, bf16[768,256]{1,0:T(8,128)(2,1)S(1)}, u32[]{:S(2)}, u32[]{:S(2)}) %collective-permute-start.3) | collective-permute-done | bytes 393248 | tf_op jit(solution)/shard_map/ppermute | solution.py:786
  27.6 1.2 collective-permute-start.7
  29.1 0.9 copy-done.5
  30.0 4.3 %collective-permute-start.9 = (bf16[320,256]{1,0:T(8,128)(2,1)S(1)}, bf16[320,256]{1,0:T(8,128)(2,1)S(1)}, u32[]{:S(2)}, u32[]{:S(2)}) collective-permute-start(bf16[320,256]{1,0:T(8,128)(2,1)S(1)} %join.3.own.refs_0_), channel_id=1, source_target_pairs={{0,48},{8,56},{16,0},{24,8},{32,16},{40,24},{48,32},{56,40},{1,49}... | collective-permute-start | bytes 491528 | tf_op jit(solution)/shard_map/ppermute | solution.py:786
  34.3 3.9 %collective-permute-done.9.right_ref.right.refs_2_ = bf16[320,256]{1,0:T(8,128)(2,1)S(1)} collective-permute-done((bf16[320,256]{1,0:T(8,128)(2,1)S(1)}, bf16[320,256]{1,0:T(8,128)(2,1)S(1)}, u32[]{:S(2)}, u32[]{:S(2)}) %collective-permute-start.9) | collective-permute-done | bytes 163872 | tf_op jit(solution)/shard_map/ppermute | solution.py:786
  38.2 4.5 %collective-permute-done.8.left_ref.left.refs_1_ = bf16[320,256]{1,0:T(8,128)(2,1)S(1)} collective-permute-done((bf16[320,256]{1,0:T(8,128)(2,1)S(1)}, bf16[320,256]{1,0:T(8,128)(2,1)S(1)}, u32[]{:S(2)}, u32[]{:S(2)}) %collective-permute-start.8) | collective-permute-done | bytes 163872 | tf_op jit(solution)/shard_map/ppermute | solution.py:786
  42.7 2.8 %collective-permute-start.16 = (bf16[256,2048]{1,0:T(8,128)(2,1)S(1)}, bf16[256,2048]{1,0:T(8,128)(2,1)S(1)}, u32[]{:S(2)}, u32[]{:S(2)}) collective-permute-start(bf16[256,2048]{1,0:T(8,128)(2,1)S(1)} %copy-done.4), channel_id=1, source_target_pairs={{0,2},{1,3},{2,0},{3,1},{4,6},{5,7},{6,4},{7,5},{8,10},{9,11},{10,... | collective-permute-start | bytes 3145736 | tf_op jit(solution)/shard_map/ppermute | solution.py:781
  45.6 1.6 %collective-permute-start.13 = (bf16[768,256]{1,0:T(8,128)(2,1)S(1)}, bf16[768,256]{1,0:T(8,128)(2,1)S(1)}, u32[]{:S(2)}, u32[]{:S(2)}) collective-permute-start(bf16[768,256]{1,0:T(8,128)(2,1)S(1)} %collective-permute-done.7.refs_10_), channel_id=1, source_target_pairs={{0,192},{64,0},{128,64},{192,128},{1,193},{65,1},{129,65},{193,129... | collective-permute-start | bytes 1179656 | tf_op jit(solution)/shard_map/ppermute | solution.py:786
  47.3 3.6 %collective-permute-start.11 = (bf16[160,256]{1,0:T(8,128)(2,1)S(1)}, bf16[160,256]{1,0:T(8,128)(2,1)S(1)}, u32[]{:S(2)}, u32[]{:S(2)}) collective-permute-start(bf16[160,256]{1,0:T(8,128)(2,1)S(1)} %get-tuple-element.61), channel_id=1, source_target_pairs={{0,48},{8,56},{16,0},{24,8},{32,16},{40,24},{48,32},{56,40},{1,49}... | collective-permute-start | bytes 245768 | tf_op jit(solution)/shard_map/ppermute | solution.py:786
  50.8 2.1 %collective-permute-done.10.far.refs_3_ = bf16[160,256]{1,0:T(8,128)(2,1)S(1)} collective-permute-done((bf16[160,256]{1,0:T(8,128)(2,1)S(1)}, bf16[160,256]{1,0:T(8,128)(2,1)S(1)}, u32[]{:S(2)}, u32[]{:S(2)}) %collective-permute-start.10) | collective-permute-done | bytes 81952 | tf_op jit(solution)/shard_map/ppermute | solution.py:786
  53.1 1.2 collective-permute-start.14
  54.3 1.0 collective-permute-done.12.refs_11_
  55.3 3.2 %span_attend.2 = (f32[576,256]{1,0:T(8,128)S(1)}, f32[576,128]{1,0:T(8,128)S(1)}) custom-call(f32[2]{0:T(128)S(1)} %copy-done.9, bf16[320,256]{1,0:T(8,128)(2,1)S(1)} %join.3.own.refs_0_, bf16[320,256]{1,0:T(8,128)(2,1)S(1)} %collective-permute-done.8.left_ref.left.refs_1_, bf16[320,256]{1,0:T(8,128)(2,1)S(1)} %collective-permute-done.9.right_ref.right.refs_2_, ...), custom_call_target="tpu_custom_call" | custom-call | flops 603979776 | bytes 1048576 | tf_op jit(solution)/shard_map/span_attend/pallas_call | solution.py:356
  58.5 2.3 %collective-permute-start.15 = (bf16[16,256]{1,0:T(8,128)(2,1)S(1)}, bf16[16,256]{1,0:T(8,128)(2,1)S(1)}, u32[]{:S(2)}, u32[]{:S(2)}) collective-permute-start(bf16[16,256]{1,0:T(8,128)(2,1)S(1)} %added.1.refs_13_), channel_id=1, source_target_pairs={{0,128},{64,192},{128,0},{192,64},{1,129},{65,193},{129,1},{193,65... | collective-permute-start | bytes 24584 | tf_op jit(solution)/shard_map/ppermute | solution.py:781
  60.8 3.2 %span_attend.3 = (f32[576,256]{1,0:T(8,128)S(1)}, f32[576,128]{1,0:T(8,128)S(1)}) custom-call(f32[2]{0:T(128)S(1)} %copy-done.9, bf16[320,256]{1,0:T(8,128)(2,1)S(1)} %join.3.own.refs_0_, bf16[320,256]{1,0:T(8,128)(2,1)S(1)} %collective-permute-done.8.left_ref.left.refs_1_, bf16[320,256]{1,0:T(8,128)(2,1)S(1)} %collective-permute-done.9.right_ref.right.refs_2_, ...), custom_call_target="tpu_custom_call" | custom-call | flops 603979776 | bytes 1048576 | tf_op jit(solution)/shard_map/span_attend/pallas_call | solution.py:356
  64.0 9.8 %cache_attend.1 = bf16[8,160,256]{2,1,0:T(8,128)(2,1)S(1)} custom-call(f32[2]{0:T(128)S(1)} %copy-done.9, bf16[320,256]{1,0:T(8,128)(2,1)S(1)} %join.3.own.refs_0_, bf16[320,256]{1,0:T(8,128)(2,1)S(1)} %collective-permute-done.8.left_ref.left.refs_1_, bf16[320,256]{1,0:T(8,128)(2,1)S(1)} %collective-permute-done.9.right_ref.right.refs_2_, ...), custom_call_target="tpu_custom_call" | custom-call | flops 2415919104 | bytes 2097152 | tf_op jit(solution)/shard_map/cache_attend/pallas_call | solution.py:453
  73.8 18.8 %all_to_all.10.parts_ref = bf16[8,160,256]{2,1,0:T(8,128)(2,1)S(1)} all-to-all(bf16[8,160,256]{2,1,0:T(8,128)(2,1)S(1)} %cache_attend.1), channel_id=1, replica_groups=mesh['y'=4,'z'=8,'xl'=2,'tp'=4] {'z'}, dimensions={0} | all-to-all | bytes 1310720 | tf_op jit(solution)/shard_map/all_to_all | solution.py:777
  92.5 1.4 merge.1.a_ref
  94.3 5.0 %collective-permute-done.17.b_ref = bf16[144,256]{1,0:T(8,128)(2,1)S(1)} collective-permute-done((bf16[144,256]{1,0:T(8,128)(2,1)S(1)}, bf16[144,256]{1,0:T(8,128)(2,1)S(1)}, u32[]{:S(2)}, u32[]{:S(2)}) %collective-permute-start.17) | collective-permute-done | bytes 73760 | tf_op jit(solution)/shard_map/ppermute | solution.py:781
  99.3 1.4 layer_product.1
  100.7 8.8 %collective-permute-start.18 = (bf16[144,2048]{1,0:T(8,128)(2,1)S(1)}, bf16[144,2048]{1,0:T(8,128)(2,1)S(1)}, u32[]{:S(2)}, u32[]{:S(2)}) collective-permute-start(bf16[144,2048]{1,0:T(8,128)(2,1)S(1)} %get-tuple-element.81), channel_id=1, source_target_pairs={{0,1},{1,0},{2,3},{3,2},{4,5},{5,4},{6,7},{7,6},{8,9},{9,8},{10,11... | collective-permute-start | bytes 1769480 | tf_op jit(solution)/shard_map/ppermute | solution.py:781
  109.5 1.6 %collective-permute-done.18.term_ref = bf16[144,2048]{1,0:T(8,128)(2,1)S(1)} collective-permute-done((bf16[144,2048]{1,0:T(8,128)(2,1)S(1)}, bf16[144,2048]{1,0:T(8,128)(2,1)S(1)}, u32[]{:S(2)}, u32[]{:S(2)}) %collective-permute-start.18) | collective-permute-done | bytes 589856 | tf_op jit(solution)/shard_map/ppermute | solution.py:781
  111.1 1.2 short_project.1
  112.6 2.5 %collective-permute-done.19.b_ref = bf16[32,256]{1,0:T(8,128)(2,1)S(1)} collective-permute-done((bf16[32,256]{1,0:T(8,128)(2,1)S(1)}, bf16[32,256]{1,0:T(8,128)(2,1)S(1)}, u32[]{:S(2)}, u32[]{:S(2)}) %collective-permute-start.19) | collective-permute-done | bytes 16416 | tf_op jit(solution)/shard_map/ppermute | solution.py:781
  115.2 0.4 collective-permute-start.26
  115.6 1.2 collective-permute-start.25
  116.8 0.8 collective-permute-start.24
  117.6 3.1 %collective-permute-start.21 = (bf16[64,256]{1,0:T(8,128)(2,1)S(1)}, bf16[64,256]{1,0:T(8,128)(2,1)S(1)}, u32[]{:S(2)}, u32[]{:S(2)}) collective-permute-start(bf16[64,256]{1,0:T(8,128)(2,1)S(1)} %join.4.refs_0_), channel_id=1, source_target_pairs={{0,32},{8,40},{16,48},{24,56},{32,0},{40,8},{48,16},{56,24},{1,33}... | collective-permute-start | bytes 98312 | tf_op jit(solution)/shard_map/ppermute | solution.py:786
  120.6 3.7 %collective-permute-done.21.refs_2_ = bf16[64,256]{1,0:T(8,128)(2,1)S(1)} collective-permute-done((bf16[64,256]{1,0:T(8,128)(2,1)S(1)}, bf16[64,256]{1,0:T(8,128)(2,1)S(1)}, u32[]{:S(2)}, u32[]{:S(2)}) %collective-permute-start.21) | collective-permute-done | bytes 32800 | tf_op jit(solution)/shard_map/ppermute | solution.py:786
  124.3 1.5 collective-permute-done.20.refs_1_
  125.9 1.2 short_attend.1
  127.1 12.0 %all_to_all.11.parts_ref = bf16[8,32,384]{2,1,0:T(8,128)(2,1)S(1)} all-to-all(bf16[8,32,384]{2,1,0:T(8,128)(2,1)S(1)} %short_attend.1), channel_id=1, replica_groups=mesh['y'=4,'z'=8,'xl'=2,'tp'=4] {'z'}, dimensions={0} | all-to-all | bytes 393216 | tf_op jit(solution)/shard_map/all_to_all | solution.py:777
  139.2 0.5 short_merge.1
  139.7 5.4 %collective-permute-start.27 = (bf16[32,512]{1,0:T(8,128)(2,1)S(1)}, bf16[32,512]{1,0:T(8,128)(2,1)S(1)}, u32[]{:S(2)}, u32[]{:S(2)}) collective-permute-start(bf16[32,512]{1,0:T(8,128)(2,1)S(1)} %get-tuple-element.86), channel_id=1, source_target_pairs={{0,1},{1,0},{2,3},{3,2},{4,5},{5,4},{6,7},{7,6},{8,9},{9,8},{10,11... | collective-permute-start | bytes 98312 | tf_op jit(solution)/shard_map/ppermute | solution.py:781
  145.0 1.9 %collective-permute-start.28 = (bf16[32,512]{1,0:T(8,128)(2,1)S(1)}, bf16[32,512]{1,0:T(8,128)(2,1)S(1)}, u32[]{:S(2)}, u32[]{:S(2)}) collective-permute-start(bf16[32,512]{1,0:T(8,128)(2,1)S(1)} %get-tuple-element.87), channel_id=1, source_target_pairs={{0,2},{1,3},{2,0},{3,1},{4,6},{5,7},{6,4},{7,5},{8,10},{9,11},{10,... | collective-permute-start | bytes 98312 | tf_op jit(solution)/shard_map/ppermute | solution.py:781
  146.9 1.4 collective-permute-start.29
  148.3 1.0 collective-permute-done.28.refs_2_
  149.3 2.4 %collective-permute-done.29.refs_3_ = bf16[32,512]{1,0:T(8,128)(2,1)S(1)} collective-permute-done((bf16[32,512]{1,0:T(8,128)(2,1)S(1)}, bf16[32,512]{1,0:T(8,128)(2,1)S(1)}, u32[]{:S(2)}, u32[]{:S(2)}) %collective-permute-start.29) | collective-permute-done | bytes 32800 | tf_op jit(solution)/shard_map/ppermute | solution.py:781
  151.8 0.9 final_sum.1
  (57 shorter events, 1.8 us)
Async XLA Ops:
  0.8 9.8 %collective-permute-start.1 = (bf16[16,2048]{1,0:T(8,128)(2,1)S(1)}, bf16[16,2048]{1,0:T(8,128)(2,1)S(1)}, u32[]{:S(2)}, u32[]{:S(2)}) collective-permute-start(bf16[16,2048]{1,0:T(8,128)(2,1)S(1)} %slice.3), channel_id=1, source_target_pairs={{0,4},{1,5},{2,6},{3,7},{4,8},{5,9},{6,10},{7,11},{8,12},{9,13},{1... | collective-permute-start | bytes 196616 | tf_op jit(solution)/shard_map/ppermute | solution.py:814
  5.5 5.2 %copy-start.8 = (bf16[16,256]{1,0:T(8,128)(2,1)}, bf16[16,256]{1,0:T(8,128)(2,1)S(1)}, u32[]{:S(2)}) copy-start(bf16[16,256]{1,0:T(8,128)(2,1)S(1)} %own_count.1.a_hbm) | copy-start | bytes 24580
  5.5 5.2 %collective-permute-start = (bf16[16,256]{1,0:T(8,128)(2,1)S(1)}, bf16[16,256]{1,0:T(8,128)(2,1)S(1)}, u32[]{:S(2)}, u32[]{:S(2)}) collective-permute-start(bf16[16,256]{1,0:T(8,128)(2,1)S(1)} %own_count.1.a_hbm), channel_id=1, source_target_pairs={{0,4},{4,0},{1,5},{5,1},{2,6},{6,2},{3,7},{7,3},{8,12},{12,8},{9,1... | collective-permute-start | bytes 24584 | tf_op jit(solution)/shard_map/ppermute | solution.py:781
  7.2 35.6 %copy-start.4 = (bf16[256,2048]{1,0:T(8,128)(2,1)S(1)}, bf16[256,2048]{1,0:T(8,128)(2,1)}, u32[]{:S(2)}) copy-start(bf16[256,2048]{1,0:T(8,128)(2,1)} %wa_hbm.1) | copy-start | bytes 3145732
  10.6 3.0 %copy-start.2 = (bf16[768,256]{1,0:T(8,128)(2,1)S(1)}, bf16[768,256]{1,0:T(8,128)(2,1)}, u32[]{:S(2)}) copy-start(bf16[768,256]{1,0:T(8,128)(2,1)} %get-tuple-element.54.refs_5_) | copy-start | bytes 1179652
  10.6 44.7 %copy-start.9 = (f32[2]{0:T(128)S(1)}, f32[2]{0:T(128)}, u32[]{:S(2)}) copy-start(f32[2]{0:T(128)} %slope_ref.6) | copy-start | bytes 28
  10.7 0.6 copy-start.11
  10.7 0.6 copy-start.6
  13.6 10.9 %collective-permute-start.4 = (bf16[768,256]{1,0:T(8,128)(2,1)S(1)}, bf16[768,256]{1,0:T(8,128)(2,1)S(1)}, u32[]{:S(2)}, u32[]{:S(2)}) collective-permute-start(bf16[768,256]{1,0:T(8,128)(2,1)S(1)} %copy-done.2), channel_id=1, source_target_pairs={{0,192},{64,0},{128,64},{192,128},{1,193},{65,1},{129,65},{193,129... | collective-permute-start | bytes 1179656 | tf_op jit(solution)/shard_map/ppermute | solution.py:786
  17.6 10.0 %collective-permute-start.3 = (bf16[768,256]{1,0:T(8,128)(2,1)S(1)}, bf16[768,256]{1,0:T(8,128)(2,1)S(1)}, u32[]{:S(2)}, u32[]{:S(2)}) collective-permute-start(bf16[768,256]{1,0:T(8,128)(2,1)S(1)} %copy-done.2), channel_id=1, source_target_pairs={{0,64},{64,128},{128,192},{192,0},{1,65},{65,129},{129,193},{193,1... | collective-permute-start | bytes 1179656 | tf_op jit(solution)/shard_map/ppermute | solution.py:786
  17.6 10.0 %collective-permute-start.2 = (bf16[768,256]{1,0:T(8,128)(2,1)S(1)}, bf16[768,256]{1,0:T(8,128)(2,1)S(1)}, u32[]{:S(2)}, u32[]{:S(2)}) collective-permute-start(bf16[768,256]{1,0:T(8,128)(2,1)S(1)} %copy-done.2), channel_id=1, source_target_pairs={{0,4},{4,0},{1,5},{5,1},{2,6},{6,2},{3,7},{7,3},{8,12},{12,8},{9,1... | collective-permute-start | bytes 1179656 | tf_op jit(solution)/shard_map/ppermute | solution.py:781
  17.6 3.8 %collective-permute-start.5 = (bf16[160,256]{1,0:T(8,128)(2,1)}, bf16[160,256]{1,0:T(8,128)(2,1)S(1)}, u32[]{:S(2)}, u32[]{:S(2)}) collective-permute-start(bf16[160,256]{1,0:T(8,128)(2,1)} %mark.1.a_ref), channel_id=1, source_target_pairs={{0,8},{8,0},{16,24},{24,16},{32,40},{40,32},{48,56},{56,48},{1,9},... | collective-permute-start | bytes 245768 | tf_op jit(solution)/shard_map/ppermute | solution.py:781
  27.6 15.1 %collective-permute-start.7 = (bf16[768,256]{1,0:T(8,128)(2,1)S(1)}, bf16[768,256]{1,0:T(8,128)(2,1)S(1)}, u32[]{:S(2)}, u32[]{:S(2)}) collective-permute-start(bf16[768,256]{1,0:T(8,128)(2,1)S(1)} %collective-permute-done.2.refs_6_), channel_id=1, source_target_pairs={{0,192},{64,0},{128,64},{192,128},{1,193},{65,1},{129,65},{193,129... | collective-permute-start | bytes 1179656 | tf_op jit(solution)/shard_map/ppermute | solution.py:786
  28.8 13.9 %collective-permute-start.6 = (bf16[768,256]{1,0:T(8,128)(2,1)S(1)}, bf16[768,256]{1,0:T(8,128)(2,1)S(1)}, u32[]{:S(2)}, u32[]{:S(2)}) collective-permute-start(bf16[768,256]{1,0:T(8,128)(2,1)S(1)} %collective-permute-done.2.refs_6_), channel_id=1, source_target_pairs={{0,64},{64,128},{128,192},{192,0},{1,65},{65,129},{129,193},{193,1... | collective-permute-start | bytes 1179656 | tf_op jit(solution)/shard_map/ppermute | solution.py:786
  29.1 0.9 copy-start.5
  30.0 8.2 %collective-permute-start.9 = (bf16[320,256]{1,0:T(8,128)(2,1)S(1)}, bf16[320,256]{1,0:T(8,128)(2,1)S(1)}, u32[]{:S(2)}, u32[]{:S(2)}) collective-permute-start(bf16[320,256]{1,0:T(8,128)(2,1)S(1)} %join.3.own.refs_0_), channel_id=1, source_target_pairs={{0,48},{8,56},{16,0},{24,8},{32,16},{40,24},{48,32},{56,40},{1,49}... | collective-permute-start | bytes 491528 | tf_op jit(solution)/shard_map/ppermute | solution.py:786
  34.3 8.5 %collective-permute-start.8 = (bf16[320,256]{1,0:T(8,128)(2,1)S(1)}, bf16[320,256]{1,0:T(8,128)(2,1)S(1)}, u32[]{:S(2)}, u32[]{:S(2)}) collective-permute-start(bf16[320,256]{1,0:T(8,128)(2,1)S(1)} %join.3.own.refs_0_), channel_id=1, source_target_pairs={{0,16},{8,24},{16,32},{24,40},{32,48},{40,56},{48,0},{56,8},{1,17}... | collective-permute-start | bytes 491528 | tf_op jit(solution)/shard_map/ppermute | solution.py:786
  42.7 31.0 %collective-permute-start.16 = (bf16[256,2048]{1,0:T(8,128)(2,1)S(1)}, bf16[256,2048]{1,0:T(8,128)(2,1)S(1)}, u32[]{:S(2)}, u32[]{:S(2)}) collective-permute-start(bf16[256,2048]{1,0:T(8,128)(2,1)S(1)} %copy-done.4), channel_id=1, source_target_pairs={{0,2},{1,3},{2,0},{3,1},{4,6},{5,7},{6,4},{7,5},{8,10},{9,11},{10,... | collective-permute-start | bytes 3145736 | tf_op jit(solution)/shard_map/ppermute | solution.py:781
  45.6 8.7 %collective-permute-start.13 = (bf16[768,256]{1,0:T(8,128)(2,1)S(1)}, bf16[768,256]{1,0:T(8,128)(2,1)S(1)}, u32[]{:S(2)}, u32[]{:S(2)}) collective-permute-start(bf16[768,256]{1,0:T(8,128)(2,1)S(1)} %collective-permute-done.7.refs_10_), channel_id=1, source_target_pairs={{0,192},{64,0},{128,64},{192,128},{1,193},{65,1},{129,65},{193,129... | collective-permute-start | bytes 1179656 | tf_op jit(solution)/shard_map/ppermute | solution.py:786
  47.2 8.1 %collective-permute-start.12 = (bf16[768,256]{1,0:T(8,128)(2,1)S(1)}, bf16[768,256]{1,0:T(8,128)(2,1)S(1)}, u32[]{:S(2)}, u32[]{:S(2)}) collective-permute-start(bf16[768,256]{1,0:T(8,128)(2,1)S(1)} %collective-permute-done.3.refs_7_), channel_id=1, source_target_pairs={{0,64},{64,128},{128,192},{192,0},{1,65},{65,129},{129,193},{193,1... | collective-permute-start | bytes 1179656 | tf_op jit(solution)/shard_map/ppermute | solution.py:786
  47.2 5.8 %collective-permute-start.10 = (bf16[160,256]{1,0:T(8,128)(2,1)S(1)}, bf16[160,256]{1,0:T(8,128)(2,1)S(1)}, u32[]{:S(2)}, u32[]{:S(2)}) collective-permute-start(bf16[160,256]{1,0:T(8,128)(2,1)S(1)} %get-tuple-element.60), channel_id=1, source_target_pairs={{0,16},{8,24},{16,32},{24,40},{32,48},{40,56},{48,0},{56,8},{1,17}... | collective-permute-start | bytes 245768 | tf_op jit(solution)/shard_map/ppermute | solution.py:786
  47.3 5.8 %collective-permute-start.11 = (bf16[160,256]{1,0:T(8,128)(2,1)S(1)}, bf16[160,256]{1,0:T(8,128)(2,1)S(1)}, u32[]{:S(2)}, u32[]{:S(2)}) collective-permute-start(bf16[160,256]{1,0:T(8,128)(2,1)S(1)} %get-tuple-element.61), channel_id=1, source_target_pairs={{0,48},{8,56},{16,0},{24,8},{32,16},{40,24},{48,32},{56,40},{1,49}... | collective-permute-start | bytes 245768 | tf_op jit(solution)/shard_map/ppermute | solution.py:786
  53.1 5.4 %collective-permute-start.14 = (bf16[16,256]{1,0:T(8,128)(2,1)S(1)}, bf16[16,256]{1,0:T(8,128)(2,1)S(1)}, u32[]{:S(2)}, u32[]{:S(2)}) collective-permute-start(bf16[16,256]{1,0:T(8,128)(2,1)S(1)} %plane_counts.1.a_ref), channel_id=1, source_target_pairs={{0,64},{64,0},{128,192},{192,128},{1,65},{65,1},{129,193},{193,129... | collective-permute-start | bytes 24584 | tf_op jit(solution)/shard_map/ppermute | solution.py:781
  58.5 5.5 %collective-permute-start.15 = (bf16[16,256]{1,0:T(8,128)(2,1)S(1)}, bf16[16,256]{1,0:T(8,128)(2,1)S(1)}, u32[]{:S(2)}, u32[]{:S(2)}) collective-permute-start(bf16[16,256]{1,0:T(8,128)(2,1)S(1)} %added.1.refs_13_), channel_id=1, source_target_pairs={{0,128},{64,192},{128,0},{192,64},{1,129},{65,193},{129,1},{193,65... | collective-permute-start | bytes 24584 | tf_op jit(solution)/shard_map/ppermute | solution.py:781
  63.9 35.3 %copy-start.1 = (bf16[128,2048]{1,0:T(8,128)(2,1)S(1)}, bf16[128,2048]{1,0:T(8,128)(2,1)}, u32[]{:S(2)}) copy-start(bf16[128,2048]{1,0:T(8,128)(2,1)} %tok_hbm.3) | copy-start | bytes 1572868
  64.0 35.3 %copy-start.7 = (bf16[16,2048]{1,0:T(8,128)(2,1)S(1)}, bf16[16,2048]{1,0:T(8,128)(2,1)}, u32[]{:S(2)}) copy-start(bf16[16,2048]{1,0:T(8,128)(2,1)} %copy-done.6) | copy-start | bytes 196612
  73.7 37.4 %copy-start = (bf16[2048,3,256]{2,0,1:T(8,128)(2,1)S(1)}, bf16[2048,3,256]{2,0,1:T(8,128)(2,1)}, u32[]{:S(2)}) copy-start(bf16[2048,3,256]{2,0,1:T(8,128)(2,1)} %param.17) | copy-start | bytes 9437188
  94.0 5.3 %collective-permute-start.17 = (bf16[144,256]{1,0:T(8,128)(2,1)S(1)}, bf16[144,256]{1,0:T(8,128)(2,1)S(1)}, u32[]{:S(2)}, u32[]{:S(2)}) collective-permute-start(bf16[144,256]{1,0:T(8,128)(2,1)S(1)} %merge.1.a_ref), channel_id=1, source_target_pairs={{0,2},{1,3},{2,0},{3,1},{4,6},{5,7},{6,4},{7,5},{8,10},{9,11},{10,... | collective-permute-start | bytes 221192 | tf_op jit(solution)/shard_map/ppermute | solution.py:781
  100.7 25.2 %copy-start.10 = (f32[2]{0:T(128)S(1)}, f32[2]{0:T(128)}, u32[]{:S(2)}) copy-start(f32[2]{0:T(128)} %slope_ref.7) | copy-start | bytes 28
  100.7 38.5 %copy-start.3 = (bf16[256,2048]{1,0:T(8,128)(2,1)S(1)}, bf16[256,2048]{1,0:T(8,128)(2,1)}, u32[]{:S(2)}) copy-start(bf16[256,2048]{1,0:T(8,128)(2,1)} %w_ref.1) | copy-start | bytes 3145732
  100.7 10.4 %collective-permute-start.18 = (bf16[144,2048]{1,0:T(8,128)(2,1)S(1)}, bf16[144,2048]{1,0:T(8,128)(2,1)S(1)}, u32[]{:S(2)}, u32[]{:S(2)}) collective-permute-start(bf16[144,2048]{1,0:T(8,128)(2,1)S(1)} %get-tuple-element.81), channel_id=1, source_target_pairs={{0,1},{1,0},{2,3},{3,2},{4,5},{5,4},{6,7},{7,6},{8,9},{9,8},{10,11... | collective-permute-start | bytes 1769480 | tf_op jit(solution)/shard_map/ppermute | solution.py:781
  112.4 2.8 %collective-permute-start.23 = (bf16[32,512]{1,0:T(8,128)(2,1)S(1)}, bf16[32,512]{1,0:T(8,128)(2,1)S(1)}, u32[]{:S(2)}, u32[]{:S(2)}) collective-permute-start(bf16[32,512]{1,0:T(8,128)(2,1)S(1)} %get-tuple-element.84.a_ref), channel_id=1, source_target_pairs={{0,4},{4,0},{1,5},{5,1},{2,6},{6,2},{3,7},{7,3},{8,12},{12,8},{9,1... | collective-permute-start | bytes 98312 | tf_op jit(solution)/shard_map/ppermute | solution.py:781
  112.4 2.7 %collective-permute-start.19 = (bf16[32,256]{1,0:T(8,128)(2,1)S(1)}, bf16[32,256]{1,0:T(8,128)(2,1)S(1)}, u32[]{:S(2)}, u32[]{:S(2)}) collective-permute-start(bf16[32,256]{1,0:T(8,128)(2,1)S(1)} %get-tuple-element.83.a_ref), channel_id=1, source_target_pairs={{0,8},{8,0},{16,24},{24,16},{32,40},{40,32},{48,56},{56,48},{1,9},... | collective-permute-start | bytes 49160 | tf_op jit(solution)/shard_map/ppermute | solution.py:781
  115.1 5.6 %collective-permute-start.22 = (bf16[64,256]{1,0:T(8,128)(2,1)S(1)}, bf16[64,256]{1,0:T(8,128)(2,1)S(1)}, u32[]{:S(2)}, u32[]{:S(2)}) collective-permute-start(bf16[64,256]{1,0:T(8,128)(2,1)S(1)} %join.4.refs_0_), channel_id=1, source_target_pairs={{0,48},{8,56},{16,0},{24,8},{32,16},{40,24},{48,32},{56,40},{1,49}... | collective-permute-start | bytes 98312 | tf_op jit(solution)/shard_map/ppermute | solution.py:786
  115.2 10.7 %collective-permute-start.26 = (bf16[64,512]{1,0:T(8,128)(2,1)S(1)}, bf16[64,512]{1,0:T(8,128)(2,1)S(1)}, u32[]{:S(2)}, u32[]{:S(2)}) collective-permute-start(bf16[64,512]{1,0:T(8,128)(2,1)S(1)} %join.5.refs_4_), channel_id=1, source_target_pairs={{0,192},{64,0},{128,64},{192,128},{1,193},{65,1},{129,65},{193,129... | collective-permute-start | bytes 196616 | tf_op jit(solution)/shard_map/ppermute | solution.py:786
  115.6 10.3 %collective-permute-start.25 = (bf16[64,512]{1,0:T(8,128)(2,1)S(1)}, bf16[64,512]{1,0:T(8,128)(2,1)S(1)}, u32[]{:S(2)}, u32[]{:S(2)}) collective-permute-start(bf16[64,512]{1,0:T(8,128)(2,1)S(1)} %join.5.refs_4_), channel_id=1, source_target_pairs={{0,128},{64,192},{128,0},{192,64},{1,129},{65,193},{129,1},{193,65... | collective-permute-start | bytes 196616 | tf_op jit(solution)/shard_map/ppermute | solution.py:786
  116.8 9.1 %collective-permute-start.24 = (bf16[64,512]{1,0:T(8,128)(2,1)S(1)}, bf16[64,512]{1,0:T(8,128)(2,1)S(1)}, u32[]{:S(2)}, u32[]{:S(2)}) collective-permute-start(bf16[64,512]{1,0:T(8,128)(2,1)S(1)} %join.5.refs_4_), channel_id=1, source_target_pairs={{0,64},{64,128},{128,192},{192,0},{1,65},{65,129},{129,193},{193,1... | collective-permute-start | bytes 196616 | tf_op jit(solution)/shard_map/ppermute | solution.py:786
  117.6 6.8 %collective-permute-start.21 = (bf16[64,256]{1,0:T(8,128)(2,1)S(1)}, bf16[64,256]{1,0:T(8,128)(2,1)S(1)}, u32[]{:S(2)}, u32[]{:S(2)}) collective-permute-start(bf16[64,256]{1,0:T(8,128)(2,1)S(1)} %join.4.refs_0_), channel_id=1, source_target_pairs={{0,32},{8,40},{16,48},{24,56},{32,0},{40,8},{48,16},{56,24},{1,33}... | collective-permute-start | bytes 98312 | tf_op jit(solution)/shard_map/ppermute | solution.py:786
  120.6 5.2 %collective-permute-start.20 = (bf16[64,256]{1,0:T(8,128)(2,1)S(1)}, bf16[64,256]{1,0:T(8,128)(2,1)S(1)}, u32[]{:S(2)}, u32[]{:S(2)}) collective-permute-start(bf16[64,256]{1,0:T(8,128)(2,1)S(1)} %join.4.refs_0_), channel_id=1, source_target_pairs={{0,16},{8,24},{16,32},{24,40},{32,48},{40,56},{48,0},{56,8},{1,17}... | collective-permute-start | bytes 98312 | tf_op jit(solution)/shard_map/ppermute | solution.py:786
  139.7 8.6 %collective-permute-start.27 = (bf16[32,512]{1,0:T(8,128)(2,1)S(1)}, bf16[32,512]{1,0:T(8,128)(2,1)S(1)}, u32[]{:S(2)}, u32[]{:S(2)}) collective-permute-start(bf16[32,512]{1,0:T(8,128)(2,1)S(1)} %get-tuple-element.86), channel_id=1, source_target_pairs={{0,1},{1,0},{2,3},{3,2},{4,5},{5,4},{6,7},{7,6},{8,9},{9,8},{10,11... | collective-permute-start | bytes 98312 | tf_op jit(solution)/shard_map/ppermute | solution.py:781
  145.0 4.3 %collective-permute-start.28 = (bf16[32,512]{1,0:T(8,128)(2,1)S(1)}, bf16[32,512]{1,0:T(8,128)(2,1)S(1)}, u32[]{:S(2)}, u32[]{:S(2)}) collective-permute-start(bf16[32,512]{1,0:T(8,128)(2,1)S(1)} %get-tuple-element.87), channel_id=1, source_target_pairs={{0,2},{1,3},{2,0},{3,1},{4,6},{5,7},{6,4},{7,5},{8,10},{9,11},{10,... | collective-permute-start | bytes 98312 | tf_op jit(solution)/shard_map/ppermute | solution.py:781
  146.9 4.9 %collective-permute-start.29 = (bf16[32,512]{1,0:T(8,128)(2,1)S(1)}, bf16[32,512]{1,0:T(8,128)(2,1)S(1)}, u32[]{:S(2)}, u32[]{:S(2)}) collective-permute-start(bf16[32,512]{1,0:T(8,128)(2,1)S(1)} %get-tuple-element.88), channel_id=1, source_target_pairs={{0,3},{1,2},{2,1},{3,0},{4,7},{5,6},{6,5},{7,4},{8,11},{9,10},{10,... | collective-permute-start | bytes 98312 | tf_op jit(solution)/shard_map/ppermute | solution.py:781

commit v12 on v11

--- a/solution.py
+++ b/solution.py
@@ -171,7 +171,7 @@
             VMEM(b.shape, BF16),
             pltpu.SemaphoreType.DMA((5,)),
         ],
-        compiler_params=params(60),
+        compiler_params=params(16),
         cost_estimate=cost(2 * HALO * d * width, 2 * d * width),
         name="mark",
     )(halo, weight3, q, a, b)
@@ -816,7 +816,6 @@
     q, pack = project(tokens, weight3, cache_keys, cache_values)
     q, pack, other_count, halo = lax.optimization_barrier((q, pack, other_count, halo))
     marked = mark(halo, weight3, q, count, other_count)
-    marked, pack = lax.optimization_barrier((marked, pack))
     left, right = both_ways(pack, "y", 1)
     other, left, right, mate = lax.optimization_barrier(
         (swap(pack, "xl"), left, right, swap(marked, "z"))

time: 153 us -> 149 us (0.974)
  Pallas kernels: 28.6 us -> 26.9 us
    pallas_call x1, Pallas kernels: 2.27 us -> 0.6 us  [mark(): pl.pallas_call(mark_kernel, in_specs=[hbm] * 5, out_specs=pl.BlockSpec(me...]
  transfers between devices with their start and end apart: 30 -> 30, of which waited for: 15 -> 15; matrix products, arithmetic and copies ran while one was open for 0% -> 0% of each run, Pallas kernels for 13% -> 14%
where the time goes in v12:
time: 149 us
  starting transfers between devices  50.8 us (34%)
  waiting for transfers between devices  37.9 us (25%)
  blocking collectives  30.8 us (21%)
  Pallas kernels  26.9 us (18%)
  local copies, waits for them, and re-layouts  1.87 us (1%)
    all_to_all x2, blocking collectives, exchange(): return lax.all_to_all(blocks, axis, 0, 0)  30.8 us
    ppermute x13, starting transfers between devices, swap(): lax.ppermute(x, axis, [(i, i ^ flip) for i in range(lax.axis_size(axis))])  26.3 us
    ppermute x16, waiting for transfers between devices, moved(): return lax.ppermute(x, axis, [(i, (i + by) % n) for i in range(n)])  22.1 us
    ppermute x16, starting transfers between devices, moved(): return lax.ppermute(x, axis, [(i, (i + by) % n) for i in range(n)])  20.6 us
    ppermute x13, waiting for transfers between devices, swap(): lax.ppermute(x, axis, [(i, i ^ flip) for i in range(lax.axis_size(axis))])  15.8 us
    pallas_call x1, Pallas kernels, cache_attend(): pl.pallas_call(functools.partial(cache_kernel, slots), grid=(2,), in_spec...  9.79 us
    pallas_call x2, Pallas kernels, span_attend(): pl.pallas_call(functools.partial(span_kernel, tile, slots), in_specs=[pl....  6.32 us
    ppermute x1, starting transfers between devices, on_device(): lax.ppermute(tokens[-HALO:], axes, [(i, i + tp) for i in range(n - tp)])  3.94 us
  transfers between devices with their start and end apart: 30, of which 15 were waited for; matrix products, arithmetic and copies ran while one was open for 0% of the time, Pallas kernels for 14%

profile of v12, /device:TPU:1, one launch (start us, length us, event | category | flops | bytes accessed | tf_op | source)
XLA Modules:
  0.0 149.2 jit_solution(9057856108195518451)
XLA Ops:
  0.0 1.0 slice.3
  1.0 3.9 %collective-permute-start.1 = (bf16[16,2048]{1,0:T(8,128)(2,1)S(1)}, bf16[16,2048]{1,0:T(8,128)(2,1)S(1)}, u32[]{:S(2)}, u32[]{:S(2)}) collective-permute-start(bf16[16,2048]{1,0:T(8,128)(2,1)S(1)} %slice.3), channel_id=1, source_target_pairs={{0,4},{1,5},{2,6},{3,7},{4,8},{5,9},{6,10},{7,11},{8,12},{9,13},{1... | collective-permute-start | bytes 196616 | tf_op jit(solution)/shard_map/ppermute | solution.py:814
  5.6 1.7 %collective-permute-start = (bf16[16,256]{1,0:T(8,128)(2,1)S(1)}, bf16[16,256]{1,0:T(8,128)(2,1)S(1)}, u32[]{:S(2)}, u32[]{:S(2)}) collective-permute-start(bf16[16,256]{1,0:T(8,128)(2,1)S(1)} %own_count.1.a_hbm), channel_id=1, source_target_pairs={{0,4},{4,0},{1,5},{5,1},{2,6},{6,2},{3,7},{7,3},{8,12},{12,8},{9,1... | collective-permute-start | bytes 24584 | tf_op jit(solution)/shard_map/ppermute | solution.py:781
  7.3 3.4 %project.1 = (bf16[128,256]{1,0:T(8,128)(2,1)}, bf16[768,256]{1,0:T(8,128)(2,1)}) custom-call(bf16[128,2048]{1,0:T(8,128)(2,1)} %tok_hbm.3, bf16[3,2048,256]{2,1,0:T(8,128)(2,1)} %bitcast.2, bf16[256,256]{1,0:T(8,128)(2,1)} %ck_hbm.1, bf16[256,256]{1,0:T(8,128)(2,1)} %cv_hbm.1), custom_call_target="tpu_custom_call" | custom-call | flops 402653184 | bytes 3670016 | tf_op jit(solution)/shard_map/project/pallas_call | solution.py:84
  10.7 4.1 %collective-permute-start.4 = (bf16[768,256]{1,0:T(8,128)(2,1)}, bf16[768,256]{1,0:T(8,128)(2,1)S(1)}, u32[]{:S(2)}, u32[]{:S(2)}) collective-permute-start(bf16[768,256]{1,0:T(8,128)(2,1)} %get-tuple-element.50.refs_5_), channel_id=1, source_target_pairs={{0,192},{64,0},{128,64},{192,128},{1,193},{65,1},{129,65},{193,129... | collective-permute-start | bytes 1179656 | tf_op jit(solution)/shard_map/ppermute | solution.py:786
  14.8 0.8 copy-done.6
  15.6 0.6 mark.1.a_ref
  16.3 0.5 collective-permute-start.5
  16.8 3.2 %collective-permute-done.5.b_ref = bf16[160,256]{1,0:T(8,128)(2,1)S(1)} collective-permute-done((bf16[160,256]{1,0:T(8,128)(2,1)S(1)}, bf16[160,256]{1,0:T(8,128)(2,1)S(1)}, u32[]{:S(2)}, u32[]{:S(2)}) %collective-permute-start.5) | collective-permute-done | bytes 81952 | tf_op jit(solution)/shard_map/ppermute | solution.py:781
  19.9 2.0 %collective-permute-done.4.refs_9_ = bf16[768,256]{1,0:T(8,128)(2,1)S(1)} collective-permute-done((bf16[768,256]{1,0:T(8,128)(2,1)}, bf16[768,256]{1,0:T(8,128)(2,1)S(1)}, u32[]{:S(2)}, u32[]{:S(2)}) %collective-permute-start.4) | collective-permute-done | bytes 393248 | tf_op jit(solution)/shard_map/ppermute | solution.py:786
  22.0 3.0 %collective-permute-done.3.refs_7_ = bf16[768,256]{1,0:T(8,128)(2,1)S(1)} collective-permute-done((bf16[768,256]{1,0:T(8,128)(2,1)}, bf16[768,256]{1,0:T(8,128)(2,1)S(1)}, u32[]{:S(2)}, u32[]{:S(2)}) %collective-permute-start.3) | collective-permute-done | bytes 393248 | tf_op jit(solution)/shard_map/ppermute | solution.py:786
  25.0 1.2 collective-permute-start.7
  26.5 4.3 %collective-permute-start.9 = (bf16[320,256]{1,0:T(8,128)(2,1)S(1)}, bf16[320,256]{1,0:T(8,128)(2,1)S(1)}, u32[]{:S(2)}, u32[]{:S(2)}) collective-permute-start(bf16[320,256]{1,0:T(8,128)(2,1)S(1)} %join.3.own.refs_0_), channel_id=1, source_target_pairs={{0,48},{8,56},{16,0},{24,8},{32,16},{40,24},{48,32},{56,40},{1,49}... | collective-permute-start | bytes 491528 | tf_op jit(solution)/shard_map/ppermute | solution.py:786
  30.8 3.9 %collective-permute-done.9.right_ref.right.refs_2_ = bf16[320,256]{1,0:T(8,128)(2,1)S(1)} collective-permute-done((bf16[320,256]{1,0:T(8,128)(2,1)S(1)}, bf16[320,256]{1,0:T(8,128)(2,1)S(1)}, u32[]{:S(2)}, u32[]{:S(2)}) %collective-permute-start.9) | collective-permute-done | bytes 163872 | tf_op jit(solution)/shard_map/ppermute | solution.py:786
  34.7 4.6 %collective-permute-done.8.left_ref.left.refs_1_ = bf16[320,256]{1,0:T(8,128)(2,1)S(1)} collective-permute-done((bf16[320,256]{1,0:T(8,128)(2,1)S(1)}, bf16[320,256]{1,0:T(8,128)(2,1)S(1)}, u32[]{:S(2)}, u32[]{:S(2)}) %collective-permute-start.8) | collective-permute-done | bytes 163872 | tf_op jit(solution)/shard_map/ppermute | solution.py:786
  39.3 2.7 %collective-permute-start.16 = (bf16[256,2048]{1,0:T(8,128)(2,1)S(1)}, bf16[256,2048]{1,0:T(8,128)(2,1)S(1)}, u32[]{:S(2)}, u32[]{:S(2)}) collective-permute-start(bf16[256,2048]{1,0:T(8,128)(2,1)S(1)} %copy-done.5), channel_id=1, source_target_pairs={{0,2},{1,3},{2,0},{3,1},{4,6},{5,7},{6,4},{7,5},{8,10},{9,11},{10,... | collective-permute-start | bytes 3145736 | tf_op jit(solution)/shard_map/ppermute | solution.py:781
  42.0 1.6 %collective-permute-start.13 = (bf16[768,256]{1,0:T(8,128)(2,1)S(1)}, bf16[768,256]{1,0:T(8,128)(2,1)S(1)}, u32[]{:S(2)}, u32[]{:S(2)}) collective-permute-start(bf16[768,256]{1,0:T(8,128)(2,1)S(1)} %collective-permute-done.7.refs_10_), channel_id=1, source_target_pairs={{0,192},{64,0},{128,64},{192,128},{1,193},{65,1},{129,65},{193,129... | collective-permute-start | bytes 1179656 | tf_op jit(solution)/shard_map/ppermute | solution.py:786
  43.7 3.6 %collective-permute-start.11 = (bf16[160,256]{1,0:T(8,128)(2,1)S(1)}, bf16[160,256]{1,0:T(8,128)(2,1)S(1)}, u32[]{:S(2)}, u32[]{:S(2)}) collective-permute-start(bf16[160,256]{1,0:T(8,128)(2,1)S(1)} %get-tuple-element.57), channel_id=1, source_target_pairs={{0,48},{8,56},{16,0},{24,8},{32,16},{40,24},{48,32},{56,40},{1,49}... | collective-permute-start | bytes 245768 | tf_op jit(solution)/shard_map/ppermute | solution.py:786
  47.3 2.1 %collective-permute-done.10.far.refs_3_ = bf16[160,256]{1,0:T(8,128)(2,1)S(1)} collective-permute-done((bf16[160,256]{1,0:T(8,128)(2,1)S(1)}, bf16[160,256]{1,0:T(8,128)(2,1)S(1)}, u32[]{:S(2)}, u32[]{:S(2)}) %collective-permute-start.10) | collective-permute-done | bytes 81952 | tf_op jit(solution)/shard_map/ppermute | solution.py:786
  49.6 1.2 collective-permute-start.14
  50.8 1.0 collective-permute-done.12.refs_11_
  51.8 3.2 %span_attend.2 = (f32[576,256]{1,0:T(8,128)S(1)}, f32[576,128]{1,0:T(8,128)S(1)}) custom-call(f32[2]{0:T(128)S(1)} %copy-done.7, bf16[320,256]{1,0:T(8,128)(2,1)S(1)} %join.3.own.refs_0_, bf16[320,256]{1,0:T(8,128)(2,1)S(1)} %collective-permute-done.8.left_ref.left.refs_1_, bf16[320,256]{1,0:T(8,128)(2,1)S(1)} %collective-permute-done.9.right_ref.right.refs_2_, ...), custom_call_target="tpu_custom_call" | custom-call | flops 603979776 | bytes 1048576 | tf_op jit(solution)/shard_map/span_attend/pallas_call | solution.py:356
  55.0 2.3 %collective-permute-start.15 = (bf16[16,256]{1,0:T(8,128)(2,1)S(1)}, bf16[16,256]{1,0:T(8,128)(2,1)S(1)}, u32[]{:S(2)}, u32[]{:S(2)}) collective-permute-start(bf16[16,256]{1,0:T(8,128)(2,1)S(1)} %added.1.refs_13_), channel_id=1, source_target_pairs={{0,128},{64,192},{128,0},{192,64},{1,129},{65,193},{129,1},{193,65... | collective-permute-start | bytes 24584 | tf_op jit(solution)/shard_map/ppermute | solution.py:781
  57.3 3.2 %span_attend.3 = (f32[576,256]{1,0:T(8,128)S(1)}, f32[576,128]{1,0:T(8,128)S(1)}) custom-call(f32[2]{0:T(128)S(1)} %copy-done.7, bf16[320,256]{1,0:T(8,128)(2,1)S(1)} %join.3.own.refs_0_, bf16[320,256]{1,0:T(8,128)(2,1)S(1)} %collective-permute-done.8.left_ref.left.refs_1_, bf16[320,256]{1,0:T(8,128)(2,1)S(1)} %collective-permute-done.9.right_ref.right.refs_2_, ...), custom_call_target="tpu_custom_call" | custom-call | flops 603979776 | bytes 1048576 | tf_op jit(solution)/shard_map/span_attend/pallas_call | solution.py:356
  60.5 9.8 %cache_attend.1 = bf16[8,160,256]{2,1,0:T(8,128)(2,1)S(1)} custom-call(f32[2]{0:T(128)S(1)} %copy-done.7, bf16[320,256]{1,0:T(8,128)(2,1)S(1)} %join.3.own.refs_0_, bf16[320,256]{1,0:T(8,128)(2,1)S(1)} %collective-permute-done.8.left_ref.left.refs_1_, bf16[320,256]{1,0:T(8,128)(2,1)S(1)} %collective-permute-done.9.right_ref.right.refs_2_, ...), custom_call_target="tpu_custom_call" | custom-call | flops 2415919104 | bytes 2097152 | tf_op jit(solution)/shard_map/cache_attend/pallas_call | solution.py:453
  70.3 18.7 %all_to_all.10.parts_ref = bf16[8,160,256]{2,1,0:T(8,128)(2,1)S(1)} all-to-all(bf16[8,160,256]{2,1,0:T(8,128)(2,1)S(1)} %cache_attend.1), channel_id=1, replica_groups=mesh['y'=4,'z'=8,'xl'=2,'tp'=4] {'z'}, dimensions={0} | all-to-all | bytes 1310720 | tf_op jit(solution)/shard_map/all_to_all | solution.py:777
  89.0 1.4 merge.1.a_ref
  90.8 5.0 %collective-permute-done.17.b_ref = bf16[144,256]{1,0:T(8,128)(2,1)S(1)} collective-permute-done((bf16[144,256]{1,0:T(8,128)(2,1)S(1)}, bf16[144,256]{1,0:T(8,128)(2,1)S(1)}, u32[]{:S(2)}, u32[]{:S(2)}) %collective-permute-start.17) | collective-permute-done | bytes 73760 | tf_op jit(solution)/shard_map/ppermute | solution.py:781
  95.8 1.4 layer_product.1
  97.2 8.8 %collective-permute-start.18 = (bf16[144,2048]{1,0:T(8,128)(2,1)S(1)}, bf16[144,2048]{1,0:T(8,128)(2,1)S(1)}, u32[]{:S(2)}, u32[]{:S(2)}) collective-permute-start(bf16[144,2048]{1,0:T(8,128)(2,1)S(1)} %get-tuple-element.77), channel_id=1, source_target_pairs={{0,1},{1,0},{2,3},{3,2},{4,5},{5,4},{6,7},{7,6},{8,9},{9,8},{10,11... | collective-permute-start | bytes 1769480 | tf_op jit(solution)/shard_map/ppermute | solution.py:781
  106.0 1.6 %collective-permute-done.18.term_ref = bf16[144,2048]{1,0:T(8,128)(2,1)S(1)} collective-permute-done((bf16[144,2048]{1,0:T(8,128)(2,1)S(1)}, bf16[144,2048]{1,0:T(8,128)(2,1)S(1)}, u32[]{:S(2)}, u32[]{:S(2)}) %collective-permute-start.18) | collective-permute-done | bytes 589856 | tf_op jit(solution)/shard_map/ppermute | solution.py:781
  107.6 1.2 short_project.1
  109.1 2.5 %collective-permute-done.19.b_ref = bf16[32,256]{1,0:T(8,128)(2,1)S(1)} collective-permute-done((bf16[32,256]{1,0:T(8,128)(2,1)S(1)}, bf16[32,256]{1,0:T(8,128)(2,1)S(1)}, u32[]{:S(2)}, u32[]{:S(2)}) %collective-permute-start.19) | collective-permute-done | bytes 16416 | tf_op jit(solution)/shard_map/ppermute | solution.py:781
  111.7 0.4 collective-permute-start.26
  112.1 1.2 collective-permute-start.25
  113.3 0.8 collective-permute-start.24
  114.0 3.1 %collective-permute-start.21 = (bf16[64,256]{1,0:T(8,128)(2,1)S(1)}, bf16[64,256]{1,0:T(8,128)(2,1)S(1)}, u32[]{:S(2)}, u32[]{:S(2)}) collective-permute-start(bf16[64,256]{1,0:T(8,128)(2,1)S(1)} %join.4.refs_0_), channel_id=1, source_target_pairs={{0,32},{8,40},{16,48},{24,56},{32,0},{40,8},{48,16},{56,24},{1,33}... | collective-permute-start | bytes 98312 | tf_op jit(solution)/shard_map/ppermute | solution.py:786
  117.1 3.7 %collective-permute-done.21.refs_2_ = bf16[64,256]{1,0:T(8,128)(2,1)S(1)} collective-permute-done((bf16[64,256]{1,0:T(8,128)(2,1)S(1)}, bf16[64,256]{1,0:T(8,128)(2,1)S(1)}, u32[]{:S(2)}, u32[]{:S(2)}) %collective-permute-start.21) | collective-permute-done | bytes 32800 | tf_op jit(solution)/shard_map/ppermute | solution.py:786
  120.8 1.5 %collective-permute-done.20.refs_1_ = bf16[64,256]{1,0:T(8,128)(2,1)S(1)} collective-permute-done((bf16[64,256]{1,0:T(8,128)(2,1)S(1)}, bf16[64,256]{1,0:T(8,128)(2,1)S(1)}, u32[]{:S(2)}, u32[]{:S(2)}) %collective-permute-start.20) | collective-permute-done | bytes 32800 | tf_op jit(solution)/shard_map/ppermute | solution.py:786
  122.4 1.2 short_attend.1
  123.6 12.1 %all_to_all.11.parts_ref = bf16[8,32,384]{2,1,0:T(8,128)(2,1)S(1)} all-to-all(bf16[8,32,384]{2,1,0:T(8,128)(2,1)S(1)} %short_attend.1), channel_id=1, replica_groups=mesh['y'=4,'z'=8,'xl'=2,'tp'=4] {'z'}, dimensions={0} | all-to-all | bytes 393216 | tf_op jit(solution)/shard_map/all_to_all | solution.py:777
  135.7 0.5 short_merge.1
  136.2 5.4 %collective-permute-start.27 = (bf16[32,512]{1,0:T(8,128)(2,1)S(1)}, bf16[32,512]{1,0:T(8,128)(2,1)S(1)}, u32[]{:S(2)}, u32[]{:S(2)}) collective-permute-start(bf16[32,512]{1,0:T(8,128)(2,1)S(1)} %get-tuple-element.82), channel_id=1, source_target_pairs={{0,1},{1,0},{2,3},{3,2},{4,5},{5,4},{6,7},{7,6},{8,9},{9,8},{10,11... | collective-permute-start | bytes 98312 | tf_op jit(solution)/shard_map/ppermute | solution.py:781
  141.5 1.8 %collective-permute-start.28 = (bf16[32,512]{1,0:T(8,128)(2,1)S(1)}, bf16[32,512]{1,0:T(8,128)(2,1)S(1)}, u32[]{:S(2)}, u32[]{:S(2)}) collective-permute-start(bf16[32,512]{1,0:T(8,128)(2,1)S(1)} %get-tuple-element.83), channel_id=1, source_target_pairs={{0,2},{1,3},{2,0},{3,1},{4,6},{5,7},{6,4},{7,5},{8,10},{9,11},{10,... | collective-permute-start | bytes 98312 | tf_op jit(solution)/shard_map/ppermute | solution.py:781
  143.4 1.4 collective-permute-start.29
  144.8 1.0 collective-permute-done.28.refs_2_
  145.8 2.4 %collective-permute-done.29.refs_3_ = bf16[32,512]{1,0:T(8,128)(2,1)S(1)} collective-permute-done((bf16[32,512]{1,0:T(8,128)(2,1)S(1)}, bf16[32,512]{1,0:T(8,128)(2,1)S(1)}, u32[]{:S(2)}, u32[]{:S(2)}) %collective-permute-start.29) | collective-permute-done | bytes 32800 | tf_op jit(solution)/shard_map/ppermute | solution.py:781
  148.2 0.9 final_sum.1
  (51 shorter events, 1.3 us)
Async XLA Ops:
  0.0 14.8 %copy-start = (bf16[2048,3,256]{2,0,1:T(8,128)(2,1)S(1)}, bf16[2048,3,256]{2,0,1:T(8,128)(2,1)}, u32[]{:S(2)}) copy-start(bf16[2048,3,256]{2,0,1:T(8,128)(2,1)} %param.11) | copy-start | bytes 9437188
  1.0 9.7 %collective-permute-start.1 = (bf16[16,2048]{1,0:T(8,128)(2,1)S(1)}, bf16[16,2048]{1,0:T(8,128)(2,1)S(1)}, u32[]{:S(2)}, u32[]{:S(2)}) collective-permute-start(bf16[16,2048]{1,0:T(8,128)(2,1)S(1)} %slice.3), channel_id=1, source_target_pairs={{0,4},{1,5},{2,6},{3,7},{4,8},{5,9},{6,10},{7,11},{8,12},{9,13},{1... | collective-permute-start | bytes 196616 | tf_op jit(solution)/shard_map/ppermute | solution.py:814
  5.6 5.1 %collective-permute-start = (bf16[16,256]{1,0:T(8,128)(2,1)S(1)}, bf16[16,256]{1,0:T(8,128)(2,1)S(1)}, u32[]{:S(2)}, u32[]{:S(2)}) collective-permute-start(bf16[16,256]{1,0:T(8,128)(2,1)S(1)} %own_count.1.a_hbm), channel_id=1, source_target_pairs={{0,4},{4,0},{1,5},{5,1},{2,6},{6,2},{3,7},{7,3},{8,12},{12,8},{9,1... | collective-permute-start | bytes 24584 | tf_op jit(solution)/shard_map/ppermute | solution.py:781
  7.3 44.4 %copy-start.7 = (f32[2]{0:T(128)S(1)}, f32[2]{0:T(128)}, u32[]{:S(2)}) copy-start(f32[2]{0:T(128)} %slope_ref.6) | copy-start | bytes 28
  10.7 28.6 %copy-start.5 = (bf16[256,2048]{1,0:T(8,128)(2,1)S(1)}, bf16[256,2048]{1,0:T(8,128)(2,1)}, u32[]{:S(2)}) copy-start(bf16[256,2048]{1,0:T(8,128)(2,1)} %wa_hbm.1) | copy-start | bytes 3145732
  10.7 41.1 %copy-start.3 = (bf16[768,256]{1,0:T(8,128)(2,1)S(1)}, bf16[768,256]{1,0:T(8,128)(2,1)}, u32[]{:S(2)}) copy-start(bf16[768,256]{1,0:T(8,128)(2,1)} %get-tuple-element.50.refs_5_) | copy-start | bytes 1179652
  10.7 11.2 %collective-permute-start.4 = (bf16[768,256]{1,0:T(8,128)(2,1)}, bf16[768,256]{1,0:T(8,128)(2,1)S(1)}, u32[]{:S(2)}, u32[]{:S(2)}) collective-permute-start(bf16[768,256]{1,0:T(8,128)(2,1)} %get-tuple-element.50.refs_5_), channel_id=1, source_target_pairs={{0,192},{64,0},{128,64},{192,128},{1,193},{65,1},{129,65},{193,129... | collective-permute-start | bytes 1179656 | tf_op jit(solution)/shard_map/ppermute | solution.py:786
  14.8 10.2 %collective-permute-start.3 = (bf16[768,256]{1,0:T(8,128)(2,1)}, bf16[768,256]{1,0:T(8,128)(2,1)S(1)}, u32[]{:S(2)}, u32[]{:S(2)}) collective-permute-start(bf16[768,256]{1,0:T(8,128)(2,1)} %get-tuple-element.50.refs_5_), channel_id=1, source_target_pairs={{0,64},{64,128},{128,192},{192,0},{1,65},{65,129},{129,193},{193,1... | collective-permute-start | bytes 1179656 | tf_op jit(solution)/shard_map/ppermute | solution.py:786
  14.8 10.2 %collective-permute-start.2 = (bf16[768,256]{1,0:T(8,128)(2,1)}, bf16[768,256]{1,0:T(8,128)(2,1)S(1)}, u32[]{:S(2)}, u32[]{:S(2)}) collective-permute-start(bf16[768,256]{1,0:T(8,128)(2,1)} %get-tuple-element.50.refs_5_), channel_id=1, source_target_pairs={{0,4},{4,0},{1,5},{5,1},{2,6},{6,2},{3,7},{7,3},{8,12},{12,8},{9,1... | collective-permute-start | bytes 1179656 | tf_op jit(solution)/shard_map/ppermute | solution.py:781
  14.8 0.8 copy-start.6
  16.3 3.7 %collective-permute-start.5 = (bf16[160,256]{1,0:T(8,128)(2,1)S(1)}, bf16[160,256]{1,0:T(8,128)(2,1)S(1)}, u32[]{:S(2)}, u32[]{:S(2)}) collective-permute-start(bf16[160,256]{1,0:T(8,128)(2,1)S(1)} %mark.1.a_ref), channel_id=1, source_target_pairs={{0,8},{8,0},{16,24},{24,16},{32,40},{40,32},{48,56},{56,48},{1,9},... | collective-permute-start | bytes 245768 | tf_op jit(solution)/shard_map/ppermute | solution.py:781
  25.0 14.3 %collective-permute-start.7 = (bf16[768,256]{1,0:T(8,128)(2,1)S(1)}, bf16[768,256]{1,0:T(8,128)(2,1)S(1)}, u32[]{:S(2)}, u32[]{:S(2)}) collective-permute-start(bf16[768,256]{1,0:T(8,128)(2,1)S(1)} %collective-permute-done.2.refs_6_), channel_id=1, source_target_pairs={{0,192},{64,0},{128,64},{192,128},{1,193},{65,1},{129,65},{193,129... | collective-permute-start | bytes 1179656 | tf_op jit(solution)/shard_map/ppermute | solution.py:786
  26.2 13.1 %collective-permute-start.6 = (bf16[768,256]{1,0:T(8,128)(2,1)S(1)}, bf16[768,256]{1,0:T(8,128)(2,1)S(1)}, u32[]{:S(2)}, u32[]{:S(2)}) collective-permute-start(bf16[768,256]{1,0:T(8,128)(2,1)S(1)} %collective-permute-done.2.refs_6_), channel_id=1, source_target_pairs={{0,64},{64,128},{128,192},{192,0},{1,65},{65,129},{129,193},{193,1... | collective-permute-start | bytes 1179656 | tf_op jit(solution)/shard_map/ppermute | solution.py:786
  26.5 8.2 %collective-permute-start.9 = (bf16[320,256]{1,0:T(8,128)(2,1)S(1)}, bf16[320,256]{1,0:T(8,128)(2,1)S(1)}, u32[]{:S(2)}, u32[]{:S(2)}) collective-permute-start(bf16[320,256]{1,0:T(8,128)(2,1)S(1)} %join.3.own.refs_0_), channel_id=1, source_target_pairs={{0,48},{8,56},{16,0},{24,8},{32,16},{40,24},{48,32},{56,40},{1,49}... | collective-permute-start | bytes 491528 | tf_op jit(solution)/shard_map/ppermute | solution.py:786
  30.7 8.6 %collective-permute-start.8 = (bf16[320,256]{1,0:T(8,128)(2,1)S(1)}, bf16[320,256]{1,0:T(8,128)(2,1)S(1)}, u32[]{:S(2)}, u32[]{:S(2)}) collective-permute-start(bf16[320,256]{1,0:T(8,128)(2,1)S(1)} %join.3.own.refs_0_), channel_id=1, source_target_pairs={{0,16},{8,24},{16,32},{24,40},{32,48},{40,56},{48,0},{56,8},{1,17}... | collective-permute-start | bytes 491528 | tf_op jit(solution)/shard_map/ppermute | solution.py:786
  39.3 31.0 %collective-permute-start.16 = (bf16[256,2048]{1,0:T(8,128)(2,1)S(1)}, bf16[256,2048]{1,0:T(8,128)(2,1)S(1)}, u32[]{:S(2)}, u32[]{:S(2)}) collective-permute-start(bf16[256,2048]{1,0:T(8,128)(2,1)S(1)} %copy-done.5), channel_id=1, source_target_pairs={{0,2},{1,3},{2,0},{3,1},{4,6},{5,7},{6,4},{7,5},{8,10},{9,11},{10,... | collective-permute-start | bytes 3145736 | tf_op jit(solution)/shard_map/ppermute | solution.py:781
  42.0 8.8 %collective-permute-start.13 = (bf16[768,256]{1,0:T(8,128)(2,1)S(1)}, bf16[768,256]{1,0:T(8,128)(2,1)S(1)}, u32[]{:S(2)}, u32[]{:S(2)}) collective-permute-start(bf16[768,256]{1,0:T(8,128)(2,1)S(1)} %collective-permute-done.7.refs_10_), channel_id=1, source_target_pairs={{0,192},{64,0},{128,64},{192,128},{1,193},{65,1},{129,65},{193,129... | collective-permute-start | bytes 1179656 | tf_op jit(solution)/shard_map/ppermute | solution.py:786
  43.6 8.1 %collective-permute-start.12 = (bf16[768,256]{1,0:T(8,128)(2,1)S(1)}, bf16[768,256]{1,0:T(8,128)(2,1)S(1)}, u32[]{:S(2)}, u32[]{:S(2)}) collective-permute-start(bf16[768,256]{1,0:T(8,128)(2,1)S(1)} %collective-permute-done.3.refs_7_), channel_id=1, source_target_pairs={{0,64},{64,128},{128,192},{192,0},{1,65},{65,129},{129,193},{193,1... | collective-permute-start | bytes 1179656 | tf_op jit(solution)/shard_map/ppermute | solution.py:786
  43.6 5.8 %collective-permute-start.10 = (bf16[160,256]{1,0:T(8,128)(2,1)S(1)}, bf16[160,256]{1,0:T(8,128)(2,1)S(1)}, u32[]{:S(2)}, u32[]{:S(2)}) collective-permute-start(bf16[160,256]{1,0:T(8,128)(2,1)S(1)} %get-tuple-element.56), channel_id=1, source_target_pairs={{0,16},{8,24},{16,32},{24,40},{32,48},{40,56},{48,0},{56,8},{1,17}... | collective-permute-start | bytes 245768 | tf_op jit(solution)/shard_map/ppermute | solution.py:786
  43.7 5.8 %collective-permute-start.11 = (bf16[160,256]{1,0:T(8,128)(2,1)S(1)}, bf16[160,256]{1,0:T(8,128)(2,1)S(1)}, u32[]{:S(2)}, u32[]{:S(2)}) collective-permute-start(bf16[160,256]{1,0:T(8,128)(2,1)S(1)} %get-tuple-element.57), channel_id=1, source_target_pairs={{0,48},{8,56},{16,0},{24,8},{32,16},{40,24},{48,32},{56,40},{1,49}... | collective-permute-start | bytes 245768 | tf_op jit(solution)/shard_map/ppermute | solution.py:786
  49.6 5.4 %collective-permute-start.14 = (bf16[16,256]{1,0:T(8,128)(2,1)S(1)}, bf16[16,256]{1,0:T(8,128)(2,1)S(1)}, u32[]{:S(2)}, u32[]{:S(2)}) collective-permute-start(bf16[16,256]{1,0:T(8,128)(2,1)S(1)} %plane_counts.1.a_ref), channel_id=1, source_target_pairs={{0,64},{64,0},{128,192},{192,128},{1,65},{65,1},{129,193},{193,129... | collective-permute-start | bytes 24584 | tf_op jit(solution)/shard_map/ppermute | solution.py:781
  55.0 5.5 %collective-permute-start.15 = (bf16[16,256]{1,0:T(8,128)(2,1)S(1)}, bf16[16,256]{1,0:T(8,128)(2,1)S(1)}, u32[]{:S(2)}, u32[]{:S(2)}) collective-permute-start(bf16[16,256]{1,0:T(8,128)(2,1)S(1)} %added.1.refs_13_), channel_id=1, source_target_pairs={{0,128},{64,192},{128,0},{192,64},{1,129},{65,193},{129,1},{193,65... | collective-permute-start | bytes 24584 | tf_op jit(solution)/shard_map/ppermute | solution.py:781
  60.5 35.3 %copy-start.2 = (bf16[128,2048]{1,0:T(8,128)(2,1)S(1)}, bf16[128,2048]{1,0:T(8,128)(2,1)}, u32[]{:S(2)}) copy-start(bf16[128,2048]{1,0:T(8,128)(2,1)} %tok_hbm.3) | copy-start | bytes 1572868
  70.3 37.4 %copy-start.1 = (bf16[2048,3,256]{2,0,1:T(8,128)(2,1)S(1)}, bf16[2048,3,256]{2,0,1:T(8,128)(2,1)}, u32[]{:S(2)}) copy-start(bf16[2048,3,256]{2,0,1:T(8,128)(2,1)} %param.17) | copy-start | bytes 9437188
  90.5 5.3 %collective-permute-start.17 = (bf16[144,256]{1,0:T(8,128)(2,1)S(1)}, bf16[144,256]{1,0:T(8,128)(2,1)S(1)}, u32[]{:S(2)}, u32[]{:S(2)}) collective-permute-start(bf16[144,256]{1,0:T(8,128)(2,1)S(1)} %merge.1.a_ref), channel_id=1, source_target_pairs={{0,2},{1,3},{2,0},{3,1},{4,6},{5,7},{6,4},{7,5},{8,10},{9,11},{10,... | collective-permute-start | bytes 221192 | tf_op jit(solution)/shard_map/ppermute | solution.py:781
  97.2 25.2 %copy-start.8 = (f32[2]{0:T(128)S(1)}, f32[2]{0:T(128)}, u32[]{:S(2)}) copy-start(f32[2]{0:T(128)} %slope_ref.7) | copy-start | bytes 28
  97.2 38.5 %copy-start.4 = (bf16[256,2048]{1,0:T(8,128)(2,1)S(1)}, bf16[256,2048]{1,0:T(8,128)(2,1)}, u32[]{:S(2)}) copy-start(bf16[256,2048]{1,0:T(8,128)(2,1)} %w_ref.1) | copy-start | bytes 3145732
  97.2 10.4 %collective-permute-start.18 = (bf16[144,2048]{1,0:T(8,128)(2,1)S(1)}, bf16[144,2048]{1,0:T(8,128)(2,1)S(1)}, u32[]{:S(2)}, u32[]{:S(2)}) collective-permute-start(bf16[144,2048]{1,0:T(8,128)(2,1)S(1)} %get-tuple-element.77), channel_id=1, source_target_pairs={{0,1},{1,0},{2,3},{3,2},{4,5},{5,4},{6,7},{7,6},{8,9},{9,8},{10,11... | collective-permute-start | bytes 1769480 | tf_op jit(solution)/shard_map/ppermute | solution.py:781
  108.9 2.8 %collective-permute-start.23 = (bf16[32,512]{1,0:T(8,128)(2,1)S(1)}, bf16[32,512]{1,0:T(8,128)(2,1)S(1)}, u32[]{:S(2)}, u32[]{:S(2)}) collective-permute-start(bf16[32,512]{1,0:T(8,128)(2,1)S(1)} %get-tuple-element.80.a_ref), channel_id=1, source_target_pairs={{0,4},{4,0},{1,5},{5,1},{2,6},{6,2},{3,7},{7,3},{8,12},{12,8},{9,1... | collective-permute-start | bytes 98312 | tf_op jit(solution)/shard_map/ppermute | solution.py:781
  108.9 2.7 %collective-permute-start.19 = (bf16[32,256]{1,0:T(8,128)(2,1)S(1)}, bf16[32,256]{1,0:T(8,128)(2,1)S(1)}, u32[]{:S(2)}, u32[]{:S(2)}) collective-permute-start(bf16[32,256]{1,0:T(8,128)(2,1)S(1)} %get-tuple-element.79.a_ref), channel_id=1, source_target_pairs={{0,8},{8,0},{16,24},{24,16},{32,40},{40,32},{48,56},{56,48},{1,9},... | collective-permute-start | bytes 49160 | tf_op jit(solution)/shard_map/ppermute | solution.py:781
  111.6 5.5 %collective-permute-start.22 = (bf16[64,256]{1,0:T(8,128)(2,1)S(1)}, bf16[64,256]{1,0:T(8,128)(2,1)S(1)}, u32[]{:S(2)}, u32[]{:S(2)}) collective-permute-start(bf16[64,256]{1,0:T(8,128)(2,1)S(1)} %join.4.refs_0_), channel_id=1, source_target_pairs={{0,48},{8,56},{16,0},{24,8},{32,16},{40,24},{48,32},{56,40},{1,49}... | collective-permute-start | bytes 98312 | tf_op jit(solution)/shard_map/ppermute | solution.py:786
  111.7 10.7 %collective-permute-start.26 = (bf16[64,512]{1,0:T(8,128)(2,1)S(1)}, bf16[64,512]{1,0:T(8,128)(2,1)S(1)}, u32[]{:S(2)}, u32[]{:S(2)}) collective-permute-start(bf16[64,512]{1,0:T(8,128)(2,1)S(1)} %join.5.refs_4_), channel_id=1, source_target_pairs={{0,192},{64,0},{128,64},{192,128},{1,193},{65,1},{129,65},{193,129... | collective-permute-start | bytes 196616 | tf_op jit(solution)/shard_map/ppermute | solution.py:786
  112.1 10.3 %collective-permute-start.25 = (bf16[64,512]{1,0:T(8,128)(2,1)S(1)}, bf16[64,512]{1,0:T(8,128)(2,1)S(1)}, u32[]{:S(2)}, u32[]{:S(2)}) collective-permute-start(bf16[64,512]{1,0:T(8,128)(2,1)S(1)} %join.5.refs_4_), channel_id=1, source_target_pairs={{0,128},{64,192},{128,0},{192,64},{1,129},{65,193},{129,1},{193,65... | collective-permute-start | bytes 196616 | tf_op jit(solution)/shard_map/ppermute | solution.py:786
  113.3 9.1 %collective-permute-start.24 = (bf16[64,512]{1,0:T(8,128)(2,1)S(1)}, bf16[64,512]{1,0:T(8,128)(2,1)S(1)}, u32[]{:S(2)}, u32[]{:S(2)}) collective-permute-start(bf16[64,512]{1,0:T(8,128)(2,1)S(1)} %join.5.refs_4_), channel_id=1, source_target_pairs={{0,64},{64,128},{128,192},{192,0},{1,65},{65,129},{129,193},{193,1... | collective-permute-start | bytes 196616 | tf_op jit(solution)/shard_map/ppermute | solution.py:786
  114.0 6.8 %collective-permute-start.21 = (bf16[64,256]{1,0:T(8,128)(2,1)S(1)}, bf16[64,256]{1,0:T(8,128)(2,1)S(1)}, u32[]{:S(2)}, u32[]{:S(2)}) collective-permute-start(bf16[64,256]{1,0:T(8,128)(2,1)S(1)} %join.4.refs_0_), channel_id=1, source_target_pairs={{0,32},{8,40},{16,48},{24,56},{32,0},{40,8},{48,16},{56,24},{1,33}... | collective-permute-start | bytes 98312 | tf_op jit(solution)/shard_map/ppermute | solution.py:786
  117.1 5.2 %collective-permute-start.20 = (bf16[64,256]{1,0:T(8,128)(2,1)S(1)}, bf16[64,256]{1,0:T(8,128)(2,1)S(1)}, u32[]{:S(2)}, u32[]{:S(2)}) collective-permute-start(bf16[64,256]{1,0:T(8,128)(2,1)S(1)} %join.4.refs_0_), channel_id=1, source_target_pairs={{0,16},{8,24},{16,32},{24,40},{32,48},{40,56},{48,0},{56,8},{1,17}... | collective-permute-start | bytes 98312 | tf_op jit(solution)/shard_map/ppermute | solution.py:786
  136.2 8.6 %collective-permute-start.27 = (bf16[32,512]{1,0:T(8,128)(2,1)S(1)}, bf16[32,512]{1,0:T(8,128)(2,1)S(1)}, u32[]{:S(2)}, u32[]{:S(2)}) collective-permute-start(bf16[32,512]{1,0:T(8,128)(2,1)S(1)} %get-tuple-element.82), channel_id=1, source_target_pairs={{0,1},{1,0},{2,3},{3,2},{4,5},{5,4},{6,7},{7,6},{8,9},{9,8},{10,11... | collective-permute-start | bytes 98312 | tf_op jit(solution)/shard_map/ppermute | solution.py:781
  141.5 4.3 %collective-permute-start.28 = (bf16[32,512]{1,0:T(8,128)(2,1)S(1)}, bf16[32,512]{1,0:T(8,128)(2,1)S(1)}, u32[]{:S(2)}, u32[]{:S(2)}) collective-permute-start(bf16[32,512]{1,0:T(8,128)(2,1)S(1)} %get-tuple-element.83), channel_id=1, source_target_pairs={{0,2},{1,3},{2,0},{3,1},{4,6},{5,7},{6,4},{7,5},{8,10},{9,11},{10,... | collective-permute-start | bytes 98312 | tf_op jit(solution)/shard_map/ppermute | solution.py:781
  143.4 4.9 %collective-permute-start.29 = (bf16[32,512]{1,0:T(8,128)(2,1)S(1)}, bf16[32,512]{1,0:T(8,128)(2,1)S(1)}, u32[]{:S(2)}, u32[]{:S(2)}) collective-permute-start(bf16[32,512]{1,0:T(8,128)(2,1)S(1)} %get-tuple-element.84), channel_id=1, source_target_pairs={{0,3},{1,2},{2,1},{3,0},{4,7},{5,6},{6,5},{7,4},{8,11},{9,10},{10,... | collective-permute-start | bytes 98312 | tf_op jit(solution)/shard_map/ppermute | solution.py:781

commit v13 on v12

--- a/solution.py
+++ b/solution.py
@@ -808,13 +808,13 @@
 ):
     axes = ("y", "z", "xl", "tp")
     slots = cache_keys.shape[0]
-    count = own_count(cache_count, cache_keys.shape[1])
-    other_count = swap(count, "xl")
     n, tp = lax.axis_size(axes), lax.axis_size("tp")
-    halo = lax.ppermute(tokens[-HALO:], axes, [(i, i + tp) for i in range(n - tp)])
     weight3 = jnp.transpose(project_weight, (1, 0, 2))
     q, pack = project(tokens, weight3, cache_keys, cache_values)
-    q, pack, other_count, halo = lax.optimization_barrier((q, pack, other_count, halo))
+    last, live, q, pack = lax.optimization_barrier((tokens, cache_count, q, pack))
+    halo = lax.ppermute(last[-HALO:], axes, [(i, i + tp) for i in range(n - tp)])
+    count = own_count(live, cache_keys.shape[1])
+    other_count = swap(count, "xl")
     marked = mark(halo, weight3, q, count, other_count)
     left, right = both_ways(pack, "y", 1)
     other, left, right, mate = lax.optimization_barrier(

time: 149 us -> 152 us (1.020)
  starting transfers between devices: 50.8 us -> 57.9 us
  waiting for transfers between devices: 37.9 us -> 34.8 us
    ppermute x13, starting transfers between devices: 26.3 us -> 31.7 us  [swap(): lax.ppermute(x, axis, [(i, i ^ flip) for i in range(lax.axis_size(axis))])]
    ppermute x16, waiting for transfers between devices: 22.1 us -> 16.9 us  [moved(): return lax.ppermute(x, axis, [(i, (i + by) % n) for i in range(n)])]
    ppermute x16, starting transfers between devices: 20.6 us -> 24.1 us  [moved(): return lax.ppermute(x, axis, [(i, (i + by) % n) for i in range(n)])]
    ppermute x13, waiting for transfers between devices: 15.8 us -> 17.9 us  [swap(): lax.ppermute(x, axis, [(i, i ^ flip) for i in range(lax.axis_size(axis))])]
    ppermute x1, starting transfers between devices: 3.94 us -> 2.16 us  [on_device(): lax.ppermute(last[-HALO:], axes, [(i, i + tp) for i in range(n - tp)])]
  transfers between devices with their start and end apart: 30 -> 30, of which waited for: 15 -> 13; matrix products, arithmetic and copies ran while one was open for 0% -> 0% of each run, Pallas kernels for 14% -> 11%
where the time goes in v13:
time: 152 us
  starting transfers between devices  57.9 us (38%)
  waiting for transfers between devices  34.8 us (23%)
  blocking collectives  30.2 us (20%)
  Pallas kernels  27 us (18%)
    ppermute x13, starting transfers between devices, swap(): lax.ppermute(x, axis, [(i, i ^ flip) for i in range(lax.axis_size(axis))])  31.7 us
    all_to_all x2, blocking collectives, exchange(): return lax.all_to_all(blocks, axis, 0, 0)  30.2 us
    ppermute x16, starting transfers between devices, moved(): return lax.ppermute(x, axis, [(i, (i + by) % n) for i in range(n)])  24.1 us
    ppermute x13, waiting for transfers between devices, swap(): lax.ppermute(x, axis, [(i, i ^ flip) for i in range(lax.axis_size(axis))])  17.9 us
    ppermute x16, waiting for transfers between devices, moved(): return lax.ppermute(x, axis, [(i, (i + by) % n) for i in range(n)])  16.9 us
    pallas_call x1, Pallas kernels, cache_attend(): pl.pallas_call(functools.partial(cache_kernel, slots), grid=(2,), in_spec...  9.79 us
    pallas_call x2, Pallas kernels, span_attend(): pl.pallas_call(functools.partial(span_kernel, tile, slots), in_specs=[pl....  6.32 us
    pallas_call x1, Pallas kernels, project(): pl.pallas_call(project_kernel, in_specs=[hbm] * 4, out_specs=[vmem, vmem]...  3.51 us
  transfers between devices with their start and end apart: 30, of which 13 were waited for; matrix products, arithmetic and copies ran while one was open for 0% of the time, Pallas kernels for 11%

profile of v13, /device:TPU:1, one launch (start us, length us, event | category | flops | bytes accessed | tf_op | source)
XLA Modules:
  0.0 151.7 jit_solution(15986830393566957876)
XLA Ops:
  0.0 3.5 %project.1 = (bf16[128,256]{1,0:T(8,128)(2,1)}, bf16[768,256]{1,0:T(8,128)(2,1)}) custom-call(bf16[128,2048]{1,0:T(8,128)(2,1)} %tok_hbm.3, bf16[3,2048,256]{2,1,0:T(8,128)(2,1)} %bitcast.2, bf16[256,256]{1,0:T(8,128)(2,1)} %ck_hbm.1, bf16[256,256]{1,0:T(8,128)(2,1)} %cv_hbm.1), custom_call_target="tpu_custom_call" | custom-call | flops 402653184 | bytes 3670016 | tf_op jit(solution)/shard_map/project/pallas_call | solution.py:84
  3.5 3.6 %collective-permute-start.4 = (bf16[768,256]{1,0:T(8,128)(2,1)}, bf16[768,256]{1,0:T(8,128)(2,1)S(1)}, u32[]{:S(2)}, u32[]{:S(2)}) collective-permute-start(bf16[768,256]{1,0:T(8,128)(2,1)} %get-tuple-element.50.refs_5_), channel_id=1, source_target_pairs={{0,192},{64,0},{128,64},{192,128},{1,193},{65,1},{129,65},{193,129... | collective-permute-start | bytes 1179656 | tf_op jit(solution)/shard_map/ppermute | solution.py:786
  7.2 1.2 collective-permute-start.2
  8.4 2.2 %collective-permute-start = (bf16[16,2048]{1,0:T(8,128)(2,1)S(1)}, bf16[16,2048]{1,0:T(8,128)(2,1)S(1)}, u32[]{:S(2)}, u32[]{:S(2)}) collective-permute-start(bf16[16,2048]{1,0:T(8,128)(2,1)S(1)} %slice.3), channel_id=1, source_target_pairs={{0,4},{1,5},{2,6},{3,7},{4,8},{5,9},{6,10},{7,11},{8,12},{9,13},{1... | collective-permute-start | bytes 196616 | tf_op jit(solution)/shard_map/ppermute | solution.py:815
  11.3 2.7 %collective-permute-start.1 = (bf16[16,256]{1,0:T(8,128)(2,1)S(1)}, bf16[16,256]{1,0:T(8,128)(2,1)S(1)}, u32[]{:S(2)}, u32[]{:S(2)}) collective-permute-start(bf16[16,256]{1,0:T(8,128)(2,1)S(1)} %own_count.1.a_hbm), channel_id=1, source_target_pairs={{0,4},{4,0},{1,5},{5,1},{2,6},{6,2},{3,7},{7,3},{8,12},{12,8},{9,1... | collective-permute-start | bytes 24584 | tf_op jit(solution)/shard_map/ppermute | solution.py:781
  13.9 3.7 %collective-permute-done.1.b_hbm = bf16[16,256]{1,0:T(8,128)(2,1)S(1)} collective-permute-done((bf16[16,256]{1,0:T(8,128)(2,1)S(1)}, bf16[16,256]{1,0:T(8,128)(2,1)S(1)}, u32[]{:S(2)}, u32[]{:S(2)}) %collective-permute-start.1) | collective-permute-done | bytes 8224 | tf_op jit(solution)/shard_map/ppermute | solution.py:781
  17.7 0.8 copy-done.6
  18.5 0.6 mark.1.a_ref
  19.1 2.7 %collective-permute-start.5 = (bf16[160,256]{1,0:T(8,128)(2,1)S(1)}, bf16[160,256]{1,0:T(8,128)(2,1)S(1)}, u32[]{:S(2)}, u32[]{:S(2)}) collective-permute-start(bf16[160,256]{1,0:T(8,128)(2,1)S(1)} %mark.1.a_ref), channel_id=1, source_target_pairs={{0,8},{8,0},{16,24},{24,16},{32,40},{40,32},{48,56},{56,48},{1,9},... | collective-permute-start | bytes 245768 | tf_op jit(solution)/shard_map/ppermute | solution.py:781
  21.8 1.8 %collective-permute-done.5.b_ref = bf16[160,256]{1,0:T(8,128)(2,1)S(1)} collective-permute-done((bf16[160,256]{1,0:T(8,128)(2,1)S(1)}, bf16[160,256]{1,0:T(8,128)(2,1)S(1)}, u32[]{:S(2)}, u32[]{:S(2)}) %collective-permute-start.5) | collective-permute-done | bytes 81952 | tf_op jit(solution)/shard_map/ppermute | solution.py:781
  23.7 2.5 %collective-permute-start.7 = (bf16[768,256]{1,0:T(8,128)(2,1)S(1)}, bf16[768,256]{1,0:T(8,128)(2,1)S(1)}, u32[]{:S(2)}, u32[]{:S(2)}) collective-permute-start(bf16[768,256]{1,0:T(8,128)(2,1)S(1)} %collective-permute-done.2.refs_6_), channel_id=1, source_target_pairs={{0,192},{64,0},{128,64},{192,128},{1,193},{65,1},{129,65},{193,129... | collective-permute-start | bytes 1179656 | tf_op jit(solution)/shard_map/ppermute | solution.py:786
  26.1 5.9 %collective-permute-start.9 = (bf16[320,256]{1,0:T(8,128)(2,1)S(1)}, bf16[320,256]{1,0:T(8,128)(2,1)S(1)}, u32[]{:S(2)}, u32[]{:S(2)}) collective-permute-start(bf16[320,256]{1,0:T(8,128)(2,1)S(1)} %join.3.own.refs_0_), channel_id=1, source_target_pairs={{0,48},{8,56},{16,0},{24,8},{32,16},{40,24},{48,32},{56,40},{1,49}... | collective-permute-start | bytes 491528 | tf_op jit(solution)/shard_map/ppermute | solution.py:786
  32.1 2.4 %collective-permute-done.9.right_ref.right.refs_2_ = bf16[320,256]{1,0:T(8,128)(2,1)S(1)} collective-permute-done((bf16[320,256]{1,0:T(8,128)(2,1)S(1)}, bf16[320,256]{1,0:T(8,128)(2,1)S(1)}, u32[]{:S(2)}, u32[]{:S(2)}) %collective-permute-start.9) | collective-permute-done | bytes 163872 | tf_op jit(solution)/shard_map/ppermute | solution.py:786
  34.4 5.1 %collective-permute-done.8.left_ref.left.refs_1_ = bf16[320,256]{1,0:T(8,128)(2,1)S(1)} collective-permute-done((bf16[320,256]{1,0:T(8,128)(2,1)S(1)}, bf16[320,256]{1,0:T(8,128)(2,1)S(1)}, u32[]{:S(2)}, u32[]{:S(2)}) %collective-permute-start.8) | collective-permute-done | bytes 163872 | tf_op jit(solution)/shard_map/ppermute | solution.py:786
  39.6 2.8 %collective-permute-start.16 = (bf16[256,2048]{1,0:T(8,128)(2,1)S(1)}, bf16[256,2048]{1,0:T(8,128)(2,1)S(1)}, u32[]{:S(2)}, u32[]{:S(2)}) collective-permute-start(bf16[256,2048]{1,0:T(8,128)(2,1)S(1)} %copy-done.5), channel_id=1, source_target_pairs={{0,2},{1,3},{2,0},{3,1},{4,6},{5,7},{6,4},{7,5},{8,10},{9,11},{10,... | collective-permute-start | bytes 3145736 | tf_op jit(solution)/shard_map/ppermute | solution.py:781
  42.4 2.7 %collective-permute-start.13 = (bf16[768,256]{1,0:T(8,128)(2,1)S(1)}, bf16[768,256]{1,0:T(8,128)(2,1)S(1)}, u32[]{:S(2)}, u32[]{:S(2)}) collective-permute-start(bf16[768,256]{1,0:T(8,128)(2,1)S(1)} %collective-permute-done.7.refs_10_), channel_id=1, source_target_pairs={{0,192},{64,0},{128,64},{192,128},{1,193},{65,1},{129,65},{193,129... | collective-permute-start | bytes 1179656 | tf_op jit(solution)/shard_map/ppermute | solution.py:786
  45.2 3.6 %collective-permute-start.11 = (bf16[160,256]{1,0:T(8,128)(2,1)S(1)}, bf16[160,256]{1,0:T(8,128)(2,1)S(1)}, u32[]{:S(2)}, u32[]{:S(2)}) collective-permute-start(bf16[160,256]{1,0:T(8,128)(2,1)S(1)} %get-tuple-element.57), channel_id=1, source_target_pairs={{0,48},{8,56},{16,0},{24,8},{32,16},{40,24},{48,32},{56,40},{1,49}... | collective-permute-start | bytes 245768 | tf_op jit(solution)/shard_map/ppermute | solution.py:786
  48.7 2.3 %collective-permute-done.10.far.refs_3_ = bf16[160,256]{1,0:T(8,128)(2,1)S(1)} collective-permute-done((bf16[160,256]{1,0:T(8,128)(2,1)S(1)}, bf16[160,256]{1,0:T(8,128)(2,1)S(1)}, u32[]{:S(2)}, u32[]{:S(2)}) %collective-permute-start.10) | collective-permute-done | bytes 81952 | tf_op jit(solution)/shard_map/ppermute | solution.py:786
  51.3 1.9 %collective-permute-done.12.refs_11_ = bf16[768,256]{1,0:T(8,128)(2,1)S(1)} collective-permute-done((bf16[768,256]{1,0:T(8,128)(2,1)S(1)}, bf16[768,256]{1,0:T(8,128)(2,1)S(1)}, u32[]{:S(2)}, u32[]{:S(2)}) %collective-permute-start.12) | collective-permute-done | bytes 393248 | tf_op jit(solution)/shard_map/ppermute | solution.py:786
  53.2 3.2 %span_attend.2 = (f32[576,256]{1,0:T(8,128)S(1)}, f32[576,128]{1,0:T(8,128)S(1)}) custom-call(f32[2]{0:T(128)S(1)} %copy-done.7, bf16[320,256]{1,0:T(8,128)(2,1)S(1)} %join.3.own.refs_0_, bf16[320,256]{1,0:T(8,128)(2,1)S(1)} %collective-permute-done.8.left_ref.left.refs_1_, bf16[320,256]{1,0:T(8,128)(2,1)S(1)} %collective-permute-done.9.right_ref.right.refs_2_, ...), custom_call_target="tpu_custom_call" | custom-call | flops 603979776 | bytes 1048576 | tf_op jit(solution)/shard_map/span_attend/pallas_call | solution.py:356
  56.4 2.0 %collective-permute-start.15 = (bf16[16,256]{1,0:T(8,128)(2,1)S(1)}, bf16[16,256]{1,0:T(8,128)(2,1)S(1)}, u32[]{:S(2)}, u32[]{:S(2)}) collective-permute-start(bf16[16,256]{1,0:T(8,128)(2,1)S(1)} %added.1.refs_13_), channel_id=1, source_target_pairs={{0,128},{64,192},{128,0},{192,64},{1,129},{65,193},{129,1},{193,65... | collective-permute-start | bytes 24584 | tf_op jit(solution)/shard_map/ppermute | solution.py:781
  58.5 3.2 %span_attend.3 = (f32[576,256]{1,0:T(8,128)S(1)}, f32[576,128]{1,0:T(8,128)S(1)}) custom-call(f32[2]{0:T(128)S(1)} %copy-done.7, bf16[320,256]{1,0:T(8,128)(2,1)S(1)} %join.3.own.refs_0_, bf16[320,256]{1,0:T(8,128)(2,1)S(1)} %collective-permute-done.8.left_ref.left.refs_1_, bf16[320,256]{1,0:T(8,128)(2,1)S(1)} %collective-permute-done.9.right_ref.right.refs_2_, ...), custom_call_target="tpu_custom_call" | custom-call | flops 603979776 | bytes 1048576 | tf_op jit(solution)/shard_map/span_attend/pallas_call | solution.py:356
  61.6 9.8 %cache_attend.1 = bf16[8,160,256]{2,1,0:T(8,128)(2,1)S(1)} custom-call(f32[2]{0:T(128)S(1)} %copy-done.7, bf16[320,256]{1,0:T(8,128)(2,1)S(1)} %join.3.own.refs_0_, bf16[320,256]{1,0:T(8,128)(2,1)S(1)} %collective-permute-done.8.left_ref.left.refs_1_, bf16[320,256]{1,0:T(8,128)(2,1)S(1)} %collective-permute-done.9.right_ref.right.refs_2_, ...), custom_call_target="tpu_custom_call" | custom-call | flops 2415919104 | bytes 2097152 | tf_op jit(solution)/shard_map/cache_attend/pallas_call | solution.py:453
  71.5 18.6 %all_to_all.10.parts_ref = bf16[8,160,256]{2,1,0:T(8,128)(2,1)S(1)} all-to-all(bf16[8,160,256]{2,1,0:T(8,128)(2,1)S(1)} %cache_attend.1), channel_id=1, replica_groups=mesh['y'=4,'z'=8,'xl'=2,'tp'=4] {'z'}, dimensions={0} | all-to-all | bytes 1310720 | tf_op jit(solution)/shard_map/all_to_all | solution.py:777
  90.0 1.4 merge.1.a_ref
  91.5 0.3 collective-permute-start.17
  91.8 5.0 %collective-permute-done.17.b_ref = bf16[144,256]{1,0:T(8,128)(2,1)S(1)} collective-permute-done((bf16[144,256]{1,0:T(8,128)(2,1)S(1)}, bf16[144,256]{1,0:T(8,128)(2,1)S(1)}, u32[]{:S(2)}, u32[]{:S(2)}) %collective-permute-start.17) | collective-permute-done | bytes 73760 | tf_op jit(solution)/shard_map/ppermute | solution.py:781
  96.8 1.4 layer_product.1
  98.2 10.0 %collective-permute-start.18 = (bf16[144,2048]{1,0:T(8,128)(2,1)S(1)}, bf16[144,2048]{1,0:T(8,128)(2,1)S(1)}, u32[]{:S(2)}, u32[]{:S(2)}) collective-permute-start(bf16[144,2048]{1,0:T(8,128)(2,1)S(1)} %get-tuple-element.77), channel_id=1, source_target_pairs={{0,1},{1,0},{2,3},{3,2},{4,5},{5,4},{6,7},{7,6},{8,9},{9,8},{10,11... | collective-permute-start | bytes 1769480 | tf_op jit(solution)/shard_map/ppermute | solution.py:781
  108.2 1.6 %collective-permute-done.18.term_ref = bf16[144,2048]{1,0:T(8,128)(2,1)S(1)} collective-permute-done((bf16[144,2048]{1,0:T(8,128)(2,1)S(1)}, bf16[144,2048]{1,0:T(8,128)(2,1)S(1)}, u32[]{:S(2)}, u32[]{:S(2)}) %collective-permute-start.18) | collective-permute-done | bytes 589856 | tf_op jit(solution)/shard_map/ppermute | solution.py:781
  109.9 1.2 short_project.1
  111.1 0.3 collective-permute-start.23
  111.7 2.3 %collective-permute-done.19.b_ref = bf16[32,256]{1,0:T(8,128)(2,1)S(1)} collective-permute-done((bf16[32,256]{1,0:T(8,128)(2,1)S(1)}, bf16[32,256]{1,0:T(8,128)(2,1)S(1)}, u32[]{:S(2)}, u32[]{:S(2)}) %collective-permute-start.19) | collective-permute-done | bytes 16416 | tf_op jit(solution)/shard_map/ppermute | solution.py:781
  114.1 0.6 collective-permute-start.26
  114.7 1.2 collective-permute-start.25
  115.9 0.8 collective-permute-start.24
  116.6 3.1 %collective-permute-start.21 = (bf16[64,256]{1,0:T(8,128)(2,1)S(1)}, bf16[64,256]{1,0:T(8,128)(2,1)S(1)}, u32[]{:S(2)}, u32[]{:S(2)}) collective-permute-start(bf16[64,256]{1,0:T(8,128)(2,1)S(1)} %join.4.refs_0_), channel_id=1, source_target_pairs={{0,32},{8,40},{16,48},{24,56},{32,0},{40,8},{48,16},{56,24},{1,33}... | collective-permute-start | bytes 98312 | tf_op jit(solution)/shard_map/ppermute | solution.py:786
  119.8 3.6 %collective-permute-done.21.refs_2_ = bf16[64,256]{1,0:T(8,128)(2,1)S(1)} collective-permute-done((bf16[64,256]{1,0:T(8,128)(2,1)S(1)}, bf16[64,256]{1,0:T(8,128)(2,1)S(1)}, u32[]{:S(2)}, u32[]{:S(2)}) %collective-permute-start.21) | collective-permute-done | bytes 32800 | tf_op jit(solution)/shard_map/ppermute | solution.py:786
  123.4 1.6 %collective-permute-done.20.refs_1_ = bf16[64,256]{1,0:T(8,128)(2,1)S(1)} collective-permute-done((bf16[64,256]{1,0:T(8,128)(2,1)S(1)}, bf16[64,256]{1,0:T(8,128)(2,1)S(1)}, u32[]{:S(2)}, u32[]{:S(2)}) %collective-permute-start.20) | collective-permute-done | bytes 32800 | tf_op jit(solution)/shard_map/ppermute | solution.py:786
  125.0 1.2 short_attend.1
  126.3 11.6 %all_to_all.11.parts_ref = bf16[8,32,384]{2,1,0:T(8,128)(2,1)S(1)} all-to-all(bf16[8,32,384]{2,1,0:T(8,128)(2,1)S(1)} %short_attend.1), channel_id=1, replica_groups=mesh['y'=4,'z'=8,'xl'=2,'tp'=4] {'z'}, dimensions={0} | all-to-all | bytes 393216 | tf_op jit(solution)/shard_map/all_to_all | solution.py:777
  137.9 0.5 short_merge.1
  138.4 5.8 %collective-permute-start.27 = (bf16[32,512]{1,0:T(8,128)(2,1)S(1)}, bf16[32,512]{1,0:T(8,128)(2,1)S(1)}, u32[]{:S(2)}, u32[]{:S(2)}) collective-permute-start(bf16[32,512]{1,0:T(8,128)(2,1)S(1)} %get-tuple-element.82), channel_id=1, source_target_pairs={{0,1},{1,0},{2,3},{3,2},{4,5},{5,4},{6,7},{7,6},{8,9},{9,8},{10,11... | collective-permute-start | bytes 98312 | tf_op jit(solution)/shard_map/ppermute | solution.py:781
  144.2 1.8 %collective-permute-start.28 = (bf16[32,512]{1,0:T(8,128)(2,1)S(1)}, bf16[32,512]{1,0:T(8,128)(2,1)S(1)}, u32[]{:S(2)}, u32[]{:S(2)}) collective-permute-start(bf16[32,512]{1,0:T(8,128)(2,1)S(1)} %get-tuple-element.83), channel_id=1, source_target_pairs={{0,2},{1,3},{2,0},{3,1},{4,6},{5,7},{6,4},{7,5},{8,10},{9,11},{10,... | collective-permute-start | bytes 98312 | tf_op jit(solution)/shard_map/ppermute | solution.py:781
  145.9 1.5 collective-permute-start.29
  147.4 1.0 collective-permute-done.28.refs_2_
  148.4 2.3 %collective-permute-done.29.refs_3_ = bf16[32,512]{1,0:T(8,128)(2,1)S(1)} collective-permute-done((bf16[32,512]{1,0:T(8,128)(2,1)S(1)}, bf16[32,512]{1,0:T(8,128)(2,1)S(1)}, u32[]{:S(2)}, u32[]{:S(2)}) %collective-permute-start.29) | collective-permute-done | bytes 32800 | tf_op jit(solution)/shard_map/ppermute | solution.py:781
  150.8 0.9 final_sum.1
  (51 shorter events, 0.8 us)
Async XLA Ops:
  0.0 8.4 %copy-start.2 = (bf16[128,2048]{1,0:T(8,128)(2,1)S(1)}, bf16[128,2048]{1,0:T(8,128)(2,1)}, u32[]{:S(2)}) copy-start(bf16[128,2048]{1,0:T(8,128)(2,1)} %tok_hbm.3) | copy-start | bytes 1572868
  0.0 17.7 %copy-start = (bf16[2048,3,256]{2,0,1:T(8,128)(2,1)S(1)}, bf16[2048,3,256]{2,0,1:T(8,128)(2,1)}, u32[]{:S(2)}) copy-start(bf16[2048,3,256]{2,0,1:T(8,128)(2,1)} %param.11) | copy-start | bytes 9437188
  0.0 53.2 %copy-start.7 = (f32[2]{0:T(128)S(1)}, f32[2]{0:T(128)}, u32[]{:S(2)}) copy-start(f32[2]{0:T(128)} %slope_ref.6) | copy-start | bytes 28
  3.5 36.0 %copy-start.5 = (bf16[256,2048]{1,0:T(8,128)(2,1)S(1)}, bf16[256,2048]{1,0:T(8,128)(2,1)}, u32[]{:S(2)}) copy-start(bf16[256,2048]{1,0:T(8,128)(2,1)} %wa_hbm.1) | copy-start | bytes 3145732
  3.5 49.7 %copy-start.3 = (bf16[768,256]{1,0:T(8,128)(2,1)S(1)}, bf16[768,256]{1,0:T(8,128)(2,1)}, u32[]{:S(2)}) copy-start(bf16[768,256]{1,0:T(8,128)(2,1)} %get-tuple-element.50.refs_5_) | copy-start | bytes 1179652
  3.5 20.1 %collective-permute-start.4 = (bf16[768,256]{1,0:T(8,128)(2,1)}, bf16[768,256]{1,0:T(8,128)(2,1)S(1)}, u32[]{:S(2)}, u32[]{:S(2)}) collective-permute-start(bf16[768,256]{1,0:T(8,128)(2,1)} %get-tuple-element.50.refs_5_), channel_id=1, source_target_pairs={{0,192},{64,0},{128,64},{192,128},{1,193},{65,1},{129,65},{193,129... | collective-permute-start | bytes 1179656 | tf_op jit(solution)/shard_map/ppermute | solution.py:786
  7.2 16.5 %collective-permute-start.3 = (bf16[768,256]{1,0:T(8,128)(2,1)}, bf16[768,256]{1,0:T(8,128)(2,1)S(1)}, u32[]{:S(2)}, u32[]{:S(2)}) collective-permute-start(bf16[768,256]{1,0:T(8,128)(2,1)} %get-tuple-element.50.refs_5_), channel_id=1, source_target_pairs={{0,64},{64,128},{128,192},{192,0},{1,65},{65,129},{129,193},{193,1... | collective-permute-start | bytes 1179656 | tf_op jit(solution)/shard_map/ppermute | solution.py:786
  7.2 16.5 %collective-permute-start.2 = (bf16[768,256]{1,0:T(8,128)(2,1)}, bf16[768,256]{1,0:T(8,128)(2,1)S(1)}, u32[]{:S(2)}, u32[]{:S(2)}) collective-permute-start(bf16[768,256]{1,0:T(8,128)(2,1)} %get-tuple-element.50.refs_5_), channel_id=1, source_target_pairs={{0,4},{4,0},{1,5},{5,1},{2,6},{6,2},{3,7},{7,3},{8,12},{12,8},{9,1... | collective-permute-start | bytes 1179656 | tf_op jit(solution)/shard_map/ppermute | solution.py:781
  8.4 9.2 %collective-permute-start = (bf16[16,2048]{1,0:T(8,128)(2,1)S(1)}, bf16[16,2048]{1,0:T(8,128)(2,1)S(1)}, u32[]{:S(2)}, u32[]{:S(2)}) collective-permute-start(bf16[16,2048]{1,0:T(8,128)(2,1)S(1)} %slice.3), channel_id=1, source_target_pairs={{0,4},{1,5},{2,6},{3,7},{4,8},{5,9},{6,10},{7,11},{8,12},{9,13},{1... | collective-permute-start | bytes 196616 | tf_op jit(solution)/shard_map/ppermute | solution.py:815
  11.3 6.4 %collective-permute-start.1 = (bf16[16,256]{1,0:T(8,128)(2,1)S(1)}, bf16[16,256]{1,0:T(8,128)(2,1)S(1)}, u32[]{:S(2)}, u32[]{:S(2)}) collective-permute-start(bf16[16,256]{1,0:T(8,128)(2,1)S(1)} %own_count.1.a_hbm), channel_id=1, source_target_pairs={{0,4},{4,0},{1,5},{5,1},{2,6},{6,2},{3,7},{7,3},{8,12},{12,8},{9,1... | collective-permute-start | bytes 24584 | tf_op jit(solution)/shard_map/ppermute | solution.py:781
  17.7 0.8 copy-start.6
  19.1 4.5 %collective-permute-start.5 = (bf16[160,256]{1,0:T(8,128)(2,1)S(1)}, bf16[160,256]{1,0:T(8,128)(2,1)S(1)}, u32[]{:S(2)}, u32[]{:S(2)}) collective-permute-start(bf16[160,256]{1,0:T(8,128)(2,1)S(1)} %mark.1.a_ref), channel_id=1, source_target_pairs={{0,8},{8,0},{16,24},{24,16},{32,40},{40,32},{48,56},{56,48},{1,9},... | collective-permute-start | bytes 245768 | tf_op jit(solution)/shard_map/ppermute | solution.py:781
  23.7 15.9 %collective-permute-start.7 = (bf16[768,256]{1,0:T(8,128)(2,1)S(1)}, bf16[768,256]{1,0:T(8,128)(2,1)S(1)}, u32[]{:S(2)}, u32[]{:S(2)}) collective-permute-start(bf16[768,256]{1,0:T(8,128)(2,1)S(1)} %collective-permute-done.2.refs_6_), channel_id=1, source_target_pairs={{0,192},{64,0},{128,64},{192,128},{1,193},{65,1},{129,65},{193,129... | collective-permute-start | bytes 1179656 | tf_op jit(solution)/shard_map/ppermute | solution.py:786
  26.1 13.4 %collective-permute-start.6 = (bf16[768,256]{1,0:T(8,128)(2,1)S(1)}, bf16[768,256]{1,0:T(8,128)(2,1)S(1)}, u32[]{:S(2)}, u32[]{:S(2)}) collective-permute-start(bf16[768,256]{1,0:T(8,128)(2,1)S(1)} %collective-permute-done.2.refs_6_), channel_id=1, source_target_pairs={{0,64},{64,128},{128,192},{192,0},{1,65},{65,129},{129,193},{193,1... | collective-permute-start | bytes 1179656 | tf_op jit(solution)/shard_map/ppermute | solution.py:786
  26.1 8.3 %collective-permute-start.9 = (bf16[320,256]{1,0:T(8,128)(2,1)S(1)}, bf16[320,256]{1,0:T(8,128)(2,1)S(1)}, u32[]{:S(2)}, u32[]{:S(2)}) collective-permute-start(bf16[320,256]{1,0:T(8,128)(2,1)S(1)} %join.3.own.refs_0_), channel_id=1, source_target_pairs={{0,48},{8,56},{16,0},{24,8},{32,16},{40,24},{48,32},{56,40},{1,49}... | collective-permute-start | bytes 491528 | tf_op jit(solution)/shard_map/ppermute | solution.py:786
  32.1 7.5 %collective-permute-start.8 = (bf16[320,256]{1,0:T(8,128)(2,1)S(1)}, bf16[320,256]{1,0:T(8,128)(2,1)S(1)}, u32[]{:S(2)}, u32[]{:S(2)}) collective-permute-start(bf16[320,256]{1,0:T(8,128)(2,1)S(1)} %join.3.own.refs_0_), channel_id=1, source_target_pairs={{0,16},{8,24},{16,32},{24,40},{32,48},{40,56},{48,0},{56,8},{1,17}... | collective-permute-start | bytes 491528 | tf_op jit(solution)/shard_map/ppermute | solution.py:786
  39.6 31.9 %collective-permute-start.16 = (bf16[256,2048]{1,0:T(8,128)(2,1)S(1)}, bf16[256,2048]{1,0:T(8,128)(2,1)S(1)}, u32[]{:S(2)}, u32[]{:S(2)}) collective-permute-start(bf16[256,2048]{1,0:T(8,128)(2,1)S(1)} %copy-done.5), channel_id=1, source_target_pairs={{0,2},{1,3},{2,0},{3,1},{4,6},{5,7},{6,4},{7,5},{8,10},{9,11},{10,... | collective-permute-start | bytes 3145736 | tf_op jit(solution)/shard_map/ppermute | solution.py:781
  42.4 8.9 %collective-permute-start.13 = (bf16[768,256]{1,0:T(8,128)(2,1)S(1)}, bf16[768,256]{1,0:T(8,128)(2,1)S(1)}, u32[]{:S(2)}, u32[]{:S(2)}) collective-permute-start(bf16[768,256]{1,0:T(8,128)(2,1)S(1)} %collective-permute-done.7.refs_10_), channel_id=1, source_target_pairs={{0,192},{64,0},{128,64},{192,128},{1,193},{65,1},{129,65},{193,129... | collective-permute-start | bytes 1179656 | tf_op jit(solution)/shard_map/ppermute | solution.py:786
  45.1 8.1 %collective-permute-start.12 = (bf16[768,256]{1,0:T(8,128)(2,1)S(1)}, bf16[768,256]{1,0:T(8,128)(2,1)S(1)}, u32[]{:S(2)}, u32[]{:S(2)}) collective-permute-start(bf16[768,256]{1,0:T(8,128)(2,1)S(1)} %collective-permute-done.3.refs_7_), channel_id=1, source_target_pairs={{0,64},{64,128},{128,192},{192,0},{1,65},{65,129},{129,193},{193,1... | collective-permute-start | bytes 1179656 | tf_op jit(solution)/shard_map/ppermute | solution.py:786
  45.1 5.9 %collective-permute-start.10 = (bf16[160,256]{1,0:T(8,128)(2,1)S(1)}, bf16[160,256]{1,0:T(8,128)(2,1)S(1)}, u32[]{:S(2)}, u32[]{:S(2)}) collective-permute-start(bf16[160,256]{1,0:T(8,128)(2,1)S(1)} %get-tuple-element.56), channel_id=1, source_target_pairs={{0,16},{8,24},{16,32},{24,40},{32,48},{40,56},{48,0},{56,8},{1,17}... | collective-permute-start | bytes 245768 | tf_op jit(solution)/shard_map/ppermute | solution.py:786
  45.2 5.8 %collective-permute-start.11 = (bf16[160,256]{1,0:T(8,128)(2,1)S(1)}, bf16[160,256]{1,0:T(8,128)(2,1)S(1)}, u32[]{:S(2)}, u32[]{:S(2)}) collective-permute-start(bf16[160,256]{1,0:T(8,128)(2,1)S(1)} %get-tuple-element.57), channel_id=1, source_target_pairs={{0,48},{8,56},{16,0},{24,8},{32,16},{40,24},{48,32},{56,40},{1,49}... | collective-permute-start | bytes 245768 | tf_op jit(solution)/shard_map/ppermute | solution.py:786
  51.0 5.4 %collective-permute-start.14 = (bf16[16,256]{1,0:T(8,128)(2,1)S(1)}, bf16[16,256]{1,0:T(8,128)(2,1)S(1)}, u32[]{:S(2)}, u32[]{:S(2)}) collective-permute-start(bf16[16,256]{1,0:T(8,128)(2,1)S(1)} %plane_counts.1.a_ref), channel_id=1, source_target_pairs={{0,64},{64,0},{128,192},{192,128},{1,65},{65,1},{129,193},{193,129... | collective-permute-start | bytes 24584 | tf_op jit(solution)/shard_map/ppermute | solution.py:781
  56.4 5.2 %collective-permute-start.15 = (bf16[16,256]{1,0:T(8,128)(2,1)S(1)}, bf16[16,256]{1,0:T(8,128)(2,1)S(1)}, u32[]{:S(2)}, u32[]{:S(2)}) collective-permute-start(bf16[16,256]{1,0:T(8,128)(2,1)S(1)} %added.1.refs_13_), channel_id=1, source_target_pairs={{0,128},{64,192},{128,0},{192,64},{1,129},{65,193},{129,1},{193,65... | collective-permute-start | bytes 24584 | tf_op jit(solution)/shard_map/ppermute | solution.py:781
  71.4 38.4 %copy-start.1 = (bf16[2048,3,256]{2,0,1:T(8,128)(2,1)S(1)}, bf16[2048,3,256]{2,0,1:T(8,128)(2,1)}, u32[]{:S(2)}) copy-start(bf16[2048,3,256]{2,0,1:T(8,128)(2,1)} %param.17) | copy-start | bytes 9437188
  91.5 5.3 %collective-permute-start.17 = (bf16[144,256]{1,0:T(8,128)(2,1)S(1)}, bf16[144,256]{1,0:T(8,128)(2,1)S(1)}, u32[]{:S(2)}, u32[]{:S(2)}) collective-permute-start(bf16[144,256]{1,0:T(8,128)(2,1)S(1)} %merge.1.a_ref), channel_id=1, source_target_pairs={{0,2},{1,3},{2,0},{3,1},{4,6},{5,7},{6,4},{7,5},{8,10},{9,11},{10,... | collective-permute-start | bytes 221192 | tf_op jit(solution)/shard_map/ppermute | solution.py:781
  98.2 26.8 %copy-start.8 = (f32[2]{0:T(128)S(1)}, f32[2]{0:T(128)}, u32[]{:S(2)}) copy-start(f32[2]{0:T(128)} %slope_ref.7) | copy-start | bytes 28
  98.2 39.6 %copy-start.4 = (bf16[256,2048]{1,0:T(8,128)(2,1)S(1)}, bf16[256,2048]{1,0:T(8,128)(2,1)}, u32[]{:S(2)}) copy-start(bf16[256,2048]{1,0:T(8,128)(2,1)} %w_ref.1) | copy-start | bytes 3145732
  98.2 11.6 %collective-permute-start.18 = (bf16[144,2048]{1,0:T(8,128)(2,1)S(1)}, bf16[144,2048]{1,0:T(8,128)(2,1)S(1)}, u32[]{:S(2)}, u32[]{:S(2)}) collective-permute-start(bf16[144,2048]{1,0:T(8,128)(2,1)S(1)} %get-tuple-element.77), channel_id=1, source_target_pairs={{0,1},{1,0},{2,3},{3,2},{4,5},{5,4},{6,7},{7,6},{8,9},{9,8},{10,11... | collective-permute-start | bytes 1769480 | tf_op jit(solution)/shard_map/ppermute | solution.py:781
  111.1 2.9 %collective-permute-start.23 = (bf16[32,512]{1,0:T(8,128)(2,1)S(1)}, bf16[32,512]{1,0:T(8,128)(2,1)S(1)}, u32[]{:S(2)}, u32[]{:S(2)}) collective-permute-start(bf16[32,512]{1,0:T(8,128)(2,1)S(1)} %get-tuple-element.80.a_ref), channel_id=1, source_target_pairs={{0,4},{4,0},{1,5},{5,1},{2,6},{6,2},{3,7},{7,3},{8,12},{12,8},{9,1... | collective-permute-start | bytes 98312 | tf_op jit(solution)/shard_map/ppermute | solution.py:781
  111.4 2.6 %collective-permute-start.19 = (bf16[32,256]{1,0:T(8,128)(2,1)S(1)}, bf16[32,256]{1,0:T(8,128)(2,1)S(1)}, u32[]{:S(2)}, u32[]{:S(2)}) collective-permute-start(bf16[32,256]{1,0:T(8,128)(2,1)S(1)} %get-tuple-element.79.a_ref), channel_id=1, source_target_pairs={{0,8},{8,0},{16,24},{24,16},{32,40},{40,32},{48,56},{56,48},{1,9},... | collective-permute-start | bytes 49160 | tf_op jit(solution)/shard_map/ppermute | solution.py:781
  114.0 5.8 %collective-permute-start.22 = (bf16[64,256]{1,0:T(8,128)(2,1)S(1)}, bf16[64,256]{1,0:T(8,128)(2,1)S(1)}, u32[]{:S(2)}, u32[]{:S(2)}) collective-permute-start(bf16[64,256]{1,0:T(8,128)(2,1)S(1)} %join.4.refs_0_), channel_id=1, source_target_pairs={{0,48},{8,56},{16,0},{24,8},{32,16},{40,24},{48,32},{56,40},{1,49}... | collective-permute-start | bytes 98312 | tf_op jit(solution)/shard_map/ppermute | solution.py:786
  114.1 11.0 %collective-permute-start.26 = (bf16[64,512]{1,0:T(8,128)(2,1)S(1)}, bf16[64,512]{1,0:T(8,128)(2,1)S(1)}, u32[]{:S(2)}, u32[]{:S(2)}) collective-permute-start(bf16[64,512]{1,0:T(8,128)(2,1)S(1)} %join.5.refs_4_), channel_id=1, source_target_pairs={{0,192},{64,0},{128,64},{192,128},{1,193},{65,1},{129,65},{193,129... | collective-permute-start | bytes 196616 | tf_op jit(solution)/shard_map/ppermute | solution.py:786
  114.7 10.3 %collective-permute-start.25 = (bf16[64,512]{1,0:T(8,128)(2,1)S(1)}, bf16[64,512]{1,0:T(8,128)(2,1)S(1)}, u32[]{:S(2)}, u32[]{:S(2)}) collective-permute-start(bf16[64,512]{1,0:T(8,128)(2,1)S(1)} %join.5.refs_4_), channel_id=1, source_target_pairs={{0,128},{64,192},{128,0},{192,64},{1,129},{65,193},{129,1},{193,65... | collective-permute-start | bytes 196616 | tf_op jit(solution)/shard_map/ppermute | solution.py:786
  115.9 9.1 %collective-permute-start.24 = (bf16[64,512]{1,0:T(8,128)(2,1)S(1)}, bf16[64,512]{1,0:T(8,128)(2,1)S(1)}, u32[]{:S(2)}, u32[]{:S(2)}) collective-permute-start(bf16[64,512]{1,0:T(8,128)(2,1)S(1)} %join.5.refs_4_), channel_id=1, source_target_pairs={{0,64},{64,128},{128,192},{192,0},{1,65},{65,129},{129,193},{193,1... | collective-permute-start | bytes 196616 | tf_op jit(solution)/shard_map/ppermute | solution.py:786
  116.6 6.8 %collective-permute-start.21 = (bf16[64,256]{1,0:T(8,128)(2,1)S(1)}, bf16[64,256]{1,0:T(8,128)(2,1)S(1)}, u32[]{:S(2)}, u32[]{:S(2)}) collective-permute-start(bf16[64,256]{1,0:T(8,128)(2,1)S(1)} %join.4.refs_0_), channel_id=1, source_target_pairs={{0,32},{8,40},{16,48},{24,56},{32,0},{40,8},{48,16},{56,24},{1,33}... | collective-permute-start | bytes 98312 | tf_op jit(solution)/shard_map/ppermute | solution.py:786
  119.8 5.2 %collective-permute-start.20 = (bf16[64,256]{1,0:T(8,128)(2,1)S(1)}, bf16[64,256]{1,0:T(8,128)(2,1)S(1)}, u32[]{:S(2)}, u32[]{:S(2)}) collective-permute-start(bf16[64,256]{1,0:T(8,128)(2,1)S(1)} %join.4.refs_0_), channel_id=1, source_target_pairs={{0,16},{8,24},{16,32},{24,40},{32,48},{40,56},{48,0},{56,8},{1,17}... | collective-permute-start | bytes 98312 | tf_op jit(solution)/shard_map/ppermute | solution.py:786
  138.4 9.0 %collective-permute-start.27 = (bf16[32,512]{1,0:T(8,128)(2,1)S(1)}, bf16[32,512]{1,0:T(8,128)(2,1)S(1)}, u32[]{:S(2)}, u32[]{:S(2)}) collective-permute-start(bf16[32,512]{1,0:T(8,128)(2,1)S(1)} %get-tuple-element.82), channel_id=1, source_target_pairs={{0,1},{1,0},{2,3},{3,2},{4,5},{5,4},{6,7},{7,6},{8,9},{9,8},{10,11... | collective-permute-start | bytes 98312 | tf_op jit(solution)/shard_map/ppermute | solution.py:781
  144.2 4.3 %collective-permute-start.28 = (bf16[32,512]{1,0:T(8,128)(2,1)S(1)}, bf16[32,512]{1,0:T(8,128)(2,1)S(1)}, u32[]{:S(2)}, u32[]{:S(2)}) collective-permute-start(bf16[32,512]{1,0:T(8,128)(2,1)S(1)} %get-tuple-element.83), channel_id=1, source_target_pairs={{0,2},{1,3},{2,0},{3,1},{4,6},{5,7},{6,4},{7,5},{8,10},{9,11},{10,... | collective-permute-start | bytes 98312 | tf_op jit(solution)/shard_map/ppermute | solution.py:781
  145.9 4.9 %collective-permute-start.29 = (bf16[32,512]{1,0:T(8,128)(2,1)S(1)}, bf16[32,512]{1,0:T(8,128)(2,1)S(1)}, u32[]{:S(2)}, u32[]{:S(2)}) collective-permute-start(bf16[32,512]{1,0:T(8,128)(2,1)S(1)} %get-tuple-element.84), channel_id=1, source_target_pairs={{0,3},{1,2},{2,1},{3,0},{4,7},{5,6},{6,5},{7,4},{8,11},{9,10},{10,... | collective-permute-start | bytes 98312 | tf_op jit(solution)/shard_map/ppermute | solution.py:781
